TPU v7x, 256 devices: a whole 4x4x8 slice. The times are simulated.
256 devices in a mesh: ctx: 32 (over z, y), head: 8 (over x, core).
Axes of the slice: x: 4, y: 4, z: 8, core: 2. Of those that a mesh axis runs over, the one named last changes fastest.
Arguments:
- queries: bfloat16 [16384, 8192], P('ctx', 'head'), may hold values from -40 to 40
- keys: bfloat16 [16384, 1024], P('ctx', 'head'), may hold values from -6 to 6
- values: bfloat16 [16384, 1024], P('ctx', 'head'), may hold values from -6 to 6
- sink_logits: float32 [64], P('head'), may hold values from 3 to 9
- vert_blocks: int32 [64, 8], P('head'), may hold values from -1 to 127, as said below
- slash_offsets: int32 [64, 3], P('head'), may hold values from 0 to 4, as said below
- output_weight: bfloat16 [8192, 4096], P('head'), may hold values from -0.0625 to 0.0625
Outputs:
- mixed: bfloat16 [16384, 4096], P(('ctx', 'head'))
Inputs may be any that keep to these rules, and one draw needn't show every extreme that they name: `vert_blocks`: in row h the valid entries are distinct block numbers and come first, the rest are -1; a row has 1 to 8 valid entries. The 8 heads that share a key-value head name exactly 24 distinct blocks together, and in each group some heads have 8 valid entries. `slash_offsets`: each row holds 3 distinct offsets, among them 0 and 4, in any order.
All inputs are finite; a program needn't handle non-finite values.
Results may differ from a plain program's by a relative error of at most 0.017.
Values may be sent and summed in bfloat16 or wider, within the bound.
No kernel may reach another device: no remote copies, remote signals or barrier semaphores. Data moves between devices by JAX's collectives and lax.ppermute only.
A program may use at most 128 MiB of HBM per device.

v0:
```python
import jax
import jax.numpy as jnp
from jax import lax
from jax.sharding import PartitionSpec as P

HEAD_SIZE = 128
KEY_BLOCK_ROWS = 128
VERTICAL_COUNT = 8
SLASH_BAND_COUNT = 3


def passed_along(value, axis, steps):
    count = lax.axis_size(axis)
    leading, last = (max(0, -steps), min(count, count - steps))
    return lax.ppermute(value, axis, [(source, source + steps) for source in range(leading, last)])


def per_device(queries, keys, values, sink_logits, vert_blocks, slash_offsets, output_weight):
    tok_rows = queries.shape[0]
    heads_here = sink_logits.shape[0]
    kv_here = keys.shape[1] // HEAD_SIZE
    heads_per_group = heads_here // kv_here
    local_blocks = tok_rows // KEY_BLOCK_ROWS
    logit_scale = HEAD_SIZE ** (-0.5)
    my_index = lax.axis_index("ctx")
    within = jnp.arange(KEY_BLOCK_ROWS, dtype=jnp.int32)
    head_kv = jnp.arange(heads_here, dtype=jnp.int32) // heads_per_group
    zero_half = jnp.zeros((), jnp.bfloat16)
    kv_local = jnp.concatenate(
        [keys.reshape(tok_rows, kv_here, HEAD_SIZE), values.reshape(tok_rows, kv_here, HEAD_SIZE)],
        axis=2,
    )
    kv_local = jnp.transpose(kv_local, (1, 0, 2))
    previous = passed_along(kv_local, "ctx", 1)
    local_index = vert_blocks - my_index * local_blocks
    owned_here = (vert_blocks >= 0) & (local_index >= 0) & (local_index < local_blocks)
    local_rows = (
        jnp.clip(local_index, 0, local_blocks - 1)[:, :, None] * KEY_BLOCK_ROWS
        + within[None, None, :]
    )
    picked = kv_local[head_kv[:, None, None], local_rows]
    contribution = jnp.where(owned_here[:, :, None, None], picked, zero_half)
    vertical = lax.psum(contribution, "ctx").astype(jnp.float32).astype(jnp.bfloat16)
    vertical = vertical.reshape(heads_here, VERTICAL_COUNT * KEY_BLOCK_ROWS, 2 * HEAD_SIZE)
    query_position = my_index * tok_rows + jnp.arange(tok_rows, dtype=jnp.int32)
    query_heads = queries.reshape(tok_rows, heads_here, HEAD_SIZE)
    score_vert = (
        jnp.einsum(
            "thd,hkd->htk",
            query_heads,
            vertical[:, :, :HEAD_SIZE],
            preferred_element_type=jnp.float32,
        )
        * logit_scale
    )
    vert_rows = (
        jnp.maximum(vert_blocks, 0)[:, :, None] * KEY_BLOCK_ROWS + within[None, None, :]
    ).reshape(heads_here, VERTICAL_COUNT * KEY_BLOCK_ROWS)
    vert_valid = jnp.repeat(vert_blocks >= 0, KEY_BLOCK_ROWS, axis=1)
    vert_mask = vert_valid[:, None, :] & (vert_rows[:, None, :] <= query_position[None, :, None])
    band_source = jnp.concatenate([previous, kv_local], axis=1).reshape(
        kv_here, 2 * local_blocks, KEY_BLOCK_ROWS, 2 * HEAD_SIZE
    )
    local_block = jnp.arange(local_blocks, dtype=jnp.int32)
    global_block = my_index * local_blocks + local_block[None, :, None] - slash_offsets[:, None, :]
    duplicate = jnp.any(global_block[:, :, :, None] == vert_blocks[:, None, None, :], axis=3)
    band_valid = (global_block >= 0) & jnp.logical_not(duplicate)
    band_index = local_blocks + local_block[None, :, None] - slash_offsets[:, None, :]
    band_rows = band_source[head_kv[:, None, None], band_index].reshape(
        heads_here, local_blocks, SLASH_BAND_COUNT * KEY_BLOCK_ROWS, 2 * HEAD_SIZE
    )
    query_block_rows = queries.reshape(local_blocks, KEY_BLOCK_ROWS, heads_here, HEAD_SIZE)
    slash_scores = (
        jnp.einsum(
            "lqhd,hlkd->hlqk",
            query_block_rows,
            band_rows[..., :HEAD_SIZE],
            preferred_element_type=jnp.float32,
        )
        * logit_scale
    )
    band_row = (
        jnp.maximum(global_block, 0)[:, :, :, None] * KEY_BLOCK_ROWS + within[None, None, None, :]
    ).reshape(heads_here, local_blocks, SLASH_BAND_COUNT * KEY_BLOCK_ROWS)
    position_blocks = query_position.reshape(local_blocks, KEY_BLOCK_ROWS)
    band_mask = jnp.repeat(band_valid, KEY_BLOCK_ROWS, axis=2)[:, :, None, :] & (
        band_row[:, :, None, :] <= position_blocks[None, :, :, None]
    )
    slash_scores = slash_scores.reshape(heads_here, tok_rows, SLASH_BAND_COUNT * KEY_BLOCK_ROWS)
    band_mask = band_mask.reshape(heads_here, tok_rows, SLASH_BAND_COUNT * KEY_BLOCK_ROWS)
    row_max = jnp.maximum(
        jnp.max(jnp.where(vert_mask, score_vert, -jnp.inf), axis=2),
        jnp.max(jnp.where(band_mask, slash_scores, -jnp.inf), axis=2),
    )
    row_max = jnp.maximum(row_max, sink_logits[:, None])
    exp_vert = jnp.where(vert_mask, jnp.exp(score_vert - row_max[:, :, None]), 0.0)
    exp_band = jnp.where(band_mask, jnp.exp(slash_scores - row_max[:, :, None]), 0.0)
    denominator = (
        jnp.exp(sink_logits[:, None] - row_max)
        + jnp.sum(exp_vert, axis=2)
        + jnp.sum(exp_band, axis=2)
    )
    weight_vert = (exp_vert / denominator[:, :, None]).astype(jnp.bfloat16)
    slash_weights = (exp_band / denominator[:, :, None]).astype(jnp.bfloat16)
    combined_output = jnp.einsum(
        "htk,hkd->thd", weight_vert, vertical[:, :, HEAD_SIZE:], preferred_element_type=jnp.float32
    )
    band_part = jnp.einsum(
        "hlqk,hlkd->lqhd",
        slash_weights.reshape(
            heads_here, local_blocks, KEY_BLOCK_ROWS, SLASH_BAND_COUNT * KEY_BLOCK_ROWS
        ),
        band_rows[..., HEAD_SIZE:],
        preferred_element_type=jnp.float32,
    )
    combined_output = combined_output + band_part.reshape(tok_rows, heads_here, HEAD_SIZE)
    attention = combined_output.astype(jnp.bfloat16).reshape(tok_rows, heads_here * HEAD_SIZE)
    return lax.psum_scatter(
        jnp.dot(attention, output_weight, preferred_element_type=jnp.float32).astype(jnp.bfloat16),
        "head",
        scatter_dimension=0,
        tiled=True,
    )


def solution(mesh):
    return jax.shard_map(
        per_device,
        mesh=mesh,
        in_specs=(
            P("ctx", "head"),
            P("ctx", "head"),
            P("ctx", "head"),
            P("head"),
            P("head", None),
            P("head", None),
            P("head", None),
        ),
        out_specs=P(("ctx", "head"), None),
        check_vma=False,
    )
```

profile of v0, /device:TPU:1, one launch (start us, length us, event | category | flops | bytes accessed | tf_op | source)
XLA Modules:
  0.0 346.8 jit_solution(18104807559748881144)
XLA Ops:
  6.5 0.7 broadcast_compare_fusion
  7.2 0.7 maximum_multiply_fusion.1
  8.0 1.0 maximum_bitcast_fusion
  9.0 70.3 %gather_fusion = bf16[8192,256]{1,0:T(8,128)(2,1)} fusion(bf16[1,512,256]{2,1,0:T(8,128)(2,1)S(1)} %maximum_bitcast_fusion, s32[8192]{0:T(1024)S(1)} %fusion.31), kind=kCustom, calls=%fused_computation | custom fusion | bytes 8454144 | tf_op jit(solution)/shard_map/gather | solution.py:41
  79.3 4.5 %broadcast_select_fusion = bf16[8,8,128,256]{3,2,1,0:T(8,128)(2,1)} fusion(bf16[8,8,128,256]{3,2,1,0:T(8,128)(2,1)} %bitcast.89, pred[8,8]{1,0:T(8,128)(4,1)S(1)} %get-tuple-element.6), kind=kLoop, calls=%fused_computation.19 | loop fusion | flops 2097152 | bytes 8388672 | tf_op jit(solution)/shard_map/jit(_where)/select_n | solution.py:42
  84.0 4.0 %collective-permute-start = (bf16[1,512,256]{2,1,0:T(8,128)(2,1)S(1)}, bf16[1,512,256]{2,1,0:T(8,128)(2,1)S(1)}, u32[]{:S(2)}, u32[]{:S(2)}) collective-permute-start(bf16[1,512,256]{2,1,0:T(8,128)(2,1)S(1)} %maximum_bitcast_fusion), channel_id=1, source_target_pairs={{0,8},{8,16},{16,24},{24,32},{32,40},{40,48},{48,56},{56,64},{64,7... | collective-permute-start | bytes 786440 | tf_op jit(solution)/shard_map/ppermute | solution.py:15
  88.6 0.4 compare_reduce_fusion
  89.3 0.1 reshape.235
  89.4 0.1 copy.40
  89.7 0.3 copy.58
  90.1 2.9 collective-permute-done
  93.0 6.2 %gather_fusion.1 = bf16[96,128,256]{2,1,0:T(8,128)(2,1)} fusion(bf16[1,8,128,256]{3,2,1,0:T(8,128)(2,1)S(1)} %bitcast.88, s32[96]{0:T(128)S(1)} %reshape.235), kind=kCustom, calls=%fused_computation.1 | custom fusion | bytes 12583680 | tf_op jit(solution)/shard_map/gather | solution.py:69
  99.2 8.6 %fusion.5 = (f32[8,4,128]{2,1,0:T(4,128)S(1)}, f32[8,4,384,128]{3,2,1,0:T(8,128)}) fusion(s32[4,128]{1,0:T(4,128)S(1)} %add_add_fusion, s32[8,4,384]{2,1,0:T(4,128)S(1)} %copy.43, pred[8,4,384]{2,1,0:T(4,128)(4,1)S(1)} %copy.41, bf16[4,128,8,128]{3,2,1,0:T(8,128)(2,1)S(1)} %bitcast.94, bf16[8,4,384,256]{3,2,1,0:T(8,128)(2,1)} %bitcast.91), kind=kOutput, calls=%fused_computation.13 | convolution fusion | flops 410513408 | bytes 10565632 | tf_op jit(solution)/shard_map/lqhd,hlkd->hlqk/dot_general | solution.py:74
  107.8 141.5 %all-reduce.2.cloned.1.call-done = bf16[8,1024,256]{2,1,0:T(8,128)(2,1)} async-done(((bf16[8,1024,256]{2,1,0:T(8,128)(2,1)}), bf16[8,1024,256]{2,1,0:T(8,128)(2,1)}) %all-reduce.2.cloned.1.call-update) | async-done | bytes 4194320 | tf_op jit(solution)/shard_map/psum | solution.py:43
  249.3 7.1 %fusion = (f32[8,512]{1,0:T(8,128)S(1)}, f32[8,1024,512]{2,1,0:T(8,128)S(1)}) fusion(s32[512]{0:T(512)S(1)} %iota_add_fusion, s32[8,1024]{1,0:T(8,128)S(1)} %bitcast_add_fusion.1, pred[8,1024]{1,0:T(8,128)(4,1)S(1)} %broadcast_bitcast_fusion, bf16[8,1024,256]{2,1,0:T(8,128)(2,1)} %all-reduce.2.cloned.1.call-done, bf16[512,1024]{1,0:T(8,128)(2,1)S(1)} %copy-done.3), kind=kOutput, calls=%fused_computation.4 | convolution fusion | flops 1094709248 | bytes 19982336 | tf_op jit(solution)/shard_map/thd,hkd->htk/dot_general | solution.py:48
  256.6 5.8 %fusion.3 = f32[8,512]{1,0:T(8,128)S(1)} fusion(f32[8,1024,512]{2,1,0:T(8,128)S(1)} %get-tuple-element.14, f32[8,512]{1,0:T(8,128)S(1)} %fusion.35, s32[512]{0:T(512)S(1)} %iota_add_fusion, s32[8,1024]{1,0:T(8,128)S(1)} %bitcast_add_fusion.1, pred[8,1024]{1,0:T(8,128)(4,1)S(1)} %broadcast_bitcast_fusion), kind=kLoop, calls=%fused_computation.9 | loop fusion | flops 25161728 | bytes 16852992 | tf_op jit(solution)/shard_map/reduce_sum | solution.py:100
  262.4 1.8 copy-done
  264.2 4.6 %fusion.8 = f32[8,4,128]{2,1,0:T(4,128)S(1)} fusion(f32[8,4,384,128]{3,2,1,0:T(8,128)S(1)} %copy-done.2, f32[8,4,128]{2,1,0:T(4,128)S(1)} %fusion.37, s32[4,128]{1,0:T(4,128)S(1)} %add_add_fusion, s32[8,4,384]{2,1,0:T(4,128)S(1)} %copy.43, pred[8,4,384]{2,1,0:T(4,128)(4,1)S(1)} %copy.41), kind=kLoop, calls=%fused_computation.20 | loop fusion | flops 9433088 | bytes 6387712 | tf_op jit(solution)/shard_map/reduce_sum | solution.py:101
  268.9 9.4 %fusion.18 = f32[4,128,8,128]{3,1,2,0:T(8,128)} fusion(bf16[8,4,384,256]{3,2,1,0:T(8,128)(2,1)S(1)} %bitcast.92, f32[8,4,384,128]{3,2,1,0:T(8,128)S(1)} %copy-done.2, f32[8,4,128]{2,1,0:T(4,128)S(1)} %fusion.36, f32[8,4,128]{2,1,0:T(4,128)S(1)} %fusion.37, s32[4,128]{1,0:T(4,128)S(1)} %add_add_fusion, s32[8,4,384]{2,1,0:T(4,128)S(1)} %copy.43, ...), kind=kOutput, calls=%fused_computation.31 | convolution fusion | flops 413663232 | bytes 11630592 | tf_op jit(solution)/shard_map/hlqk,hlkd->lqhd/dot_general | solution.py:108
  278.3 2.0 copy.52
  280.4 1.9 reshape.227
  282.3 10.7 %fusion.17 = bf16[512,8,128]{0,2,1:T(8,128)(2,1)S(1)} fusion(f32[512,8,128]{0,2,1:T(8,128)} %reshape.227, f32[8,1024,512]{2,1,0:T(8,128)} %copy-done, f32[8,512]{1,0:T(8,128)S(1)} %bitcast_add_fusion.2, f32[8,512]{1,0:T(8,128)S(1)} %fusion.35, s32[512]{0:T(512)S(1)} %iota_add_fusion, s32[8,1024]{1,0:T(8,128)S(1)} %bitcast_add_fusion.1, ...), kind=kOutput, calls=%fused_computation.30 | convolution fusion | flops 1104150528 | bytes 22095872 | tf_op jit(solution)/shard_map/htk,hkd->thd/dot_general | solution.py:105
  292.9 9.5 %convolution_convert_fusion = bf16[512,4096]{1,0:T(8,128)(2,1)} fusion(bf16[512,1024]{0,1:T(8,128)(2,1)S(1)} %bitcast.101, bf16[1024,4096]{1,0:T(8,128)(2,1)} %param.13), kind=kOutput, calls=%fused_computation.18 | convolution fusion | flops 4297064448 | bytes 13631488 | tf_op jit(solution)/shard_map/dot_general | solution.py:119
  302.5 37.5 %reduce-scatter.2.cloned.1.call-done = bf16[64,4096]{1,0:T(8,128)(2,1)} async-done(((bf16[512,4096]{1,0:T(8,128)(2,1)}), bf16[64,4096]{1,0:T(8,128)(2,1)}) %reduce-scatter.2.cloned.1.call-update) | async-done | bytes 524304 | tf_op jit(solution)/shard_map/reduce_scatter | solution.py:118
  (46 shorter events, 1.6 us)
Async XLA Ops:
  6.5 242.8 %all-reduce.2.cloned.1.call-start = ((), (), s32[]{:S(2)}) async-start(), calls=%async_computation.1 | async-start | bytes 8388608 | tf_op jit(solution)/shard_map/psum | solution.py:43
  79.3 8.8 %copy-start.5 = (s32[8,3]{0,1:T(4,128)S(1)}, s32[8,3]{0,1:T(4,128)}, u32[]{:S(2)}) copy-start(s32[8,3]{0,1:T(4,128)} %param.12) | copy-start | bytes 292
  79.3 9.2 %copy-start.4 = (s32[8,8]{1,0:T(8,128)S(1)}, s32[8,8]{1,0:T(8,128)}, u32[]{:S(2)}) copy-start(s32[8,8]{1,0:T(8,128)} %param.11) | copy-start | bytes 772
  79.3 10.4 %copy-start.3 = (bf16[512,1024]{1,0:T(8,128)(2,1)S(1)}, bf16[512,1024]{1,0:T(8,128)(2,1)}, u32[]{:S(2)}) copy-start(bf16[512,1024]{1,0:T(8,128)(2,1)} %param.7) | copy-start | bytes 3145732
  83.9 256.1 %reduce-scatter.2.cloned.1.call-start = ((), (), s32[]{:S(2)}) async-start(), calls=%async_computation.2 | async-start | bytes 4718592 | tf_op jit(solution)/shard_map/reduce_scatter | solution.py:118
  84.0 9.0 %collective-permute-start = (bf16[1,512,256]{2,1,0:T(8,128)(2,1)S(1)}, bf16[1,512,256]{2,1,0:T(8,128)(2,1)S(1)}, u32[]{:S(2)}, u32[]{:S(2)}) collective-permute-start(bf16[1,512,256]{2,1,0:T(8,128)(2,1)S(1)} %maximum_bitcast_fusion), channel_id=1, source_target_pairs={{0,8},{8,16},{16,24},{24,32},{32,40},{40,48},{48,56},{56,64},{64,7... | collective-permute-start | bytes 786440 | tf_op jit(solution)/shard_map/ppermute | solution.py:15
  107.8 148.6 %copy-start.6 = (f32[8]{0:T(128)S(1)}, f32[8]{0:T(128)}, u32[]{:S(2)}) copy-start(f32[8]{0:T(128)} %param.10) | copy-start | bytes 100
  256.4 7.8 %copy-start = (f32[8,1024,512]{2,1,0:T(8,128)}, f32[8,1024,512]{2,1,0:T(8,128)S(1)}, u32[]{:S(2)}) copy-start(f32[8,1024,512]{2,1,0:T(8,128)S(1)} %get-tuple-element.14) | copy-start | bytes 50331652
  256.6 7.6 %copy-start.2 = (f32[8,4,384,128]{3,2,1,0:T(8,128)S(1)}, f32[8,4,384,128]{3,2,1,0:T(8,128)}, u32[]{:S(2)}) copy-start(f32[8,4,384,128]{3,2,1,0:T(8,128)} %get-tuple-element.12) | copy-start | bytes 18874372
  264.2 4.8 %copy-start.1 = (bf16[96,128,256]{2,1,0:T(8,128)(2,1)S(1)}, bf16[96,128,256]{2,1,0:T(8,128)(2,1)}, u32[]{:S(2)}) copy-start(bf16[96,128,256]{2,1,0:T(8,128)(2,1)} %gather_fusion.1) | copy-start | bytes 18874372
Sparse Core Ops, SparseCore 0:
  84.0 165.2 all-reduce.1
  302.6 37.3 reduce-scatter.1
where the time goes:
time: 349 us; the launch traced here: 347 us
  waiting for transfers between devices  182 us (52%)
  local copies, waits for them, and re-layouts  83.5 us (24%)
  matrix products  45.2 us (13%)
  other arithmetic  18.4 us (5%)
  between operations  13.6 us (4%)
  starting transfers between devices  4.09 us (1%)
    psum x1, waiting for transfers between devices, per_device(): lax.psum(contribution, 'ctx').astype(jnp.float32).astype(jnp.bfloat16)  142 us
    gather x1, local copies, waits for them, and re-layouts, per_device(): picked = kv_local[head_kv[:, None, None], local_rows]  70.3 us
    reduce_scatter x1, waiting for transfers between devices, per_device(): lax.psum_scatter(jnp.dot(attention, output_weight, preferred_element_type...  37.5 us
    dot_general x1, matrix products, per_device(): jnp.einsum('htk,hkd->thd', weight_vert, vertical[:, :, HEAD_SIZE:], prefe...  10.7 us
    dot_general x1, matrix products, per_device(): jnp.dot(attention, output_weight, preferred_element_type=jnp.float32)  9.48 us
    dot_general x1, matrix products, per_device(): jnp.einsum('hlqk,hlkd->lqhd', slash_weights.reshape(heads_here, local_blo...  9.36 us
    dot_general x1, matrix products, per_device(): jnp.einsum('lqhd,hlkd->hlqk', query_block_rows, band_rows[..., :HEAD_SIZE...  8.6 us
    dot_general x1, matrix products, per_device(): jnp.einsum('thd,hkd->htk', query_heads, vertical[:, :, :HEAD_SIZE], prefe...  7.09 us
  transfers between devices with their start and end apart: 3, of which 3 were waited for; matrix products, arithmetic and copies ran while one was open for 5% of the time, Pallas kernels for 0%

commit v1 on v0

v1 whole, which is shorter than its diff:
```python
import functools

import jax
import jax.numpy as jnp
from jax import lax
from jax.experimental import pallas as pl
from jax.experimental.pallas import tpu as pltpu
from jax.sharding import PartitionSpec as P

HEAD = 128
ROWS = 128
SLOTS = 24
ENTRIES = 11
BLOCKS = 128
RUNS = 4
SCALE = HEAD ** -0.5
LOG2E = 1.4426950408889634
NEVER = 1 << 20
Z, Y, X = 8, 4, 4


def z_pairs(step):
    return [(Y * z + y, Y * ((z + step) % Z) + y) for z in range(Z) for y in range(Y)]


def y_pairs(flip):
    return [(Y * z + y, Y * z + (y ^ flip)) for z in range(Z) for y in range(Y)]


def x_pairs(step):
    return [(2 * x + k, 2 * ((x + step) % X) + k) for x in range(X) for k in range(2)]


CORE_PAIRS = [(h, h ^ 1) for h in range(8)]


def attend(meta, idx, sink, thr, q, a0, a2, b0, b2, a1, a3, b1, b3, kp, vp, kc, vc, w, dep, keep, give, token,
           kv, qs, ws, att, sems):
    run, core, odd = meta[0], meta[1], meta[2]
    copies = []

    def copy(src, dst):
        c = pltpu.make_async_copy(src, dst, sems.at[len(copies)])
        c.start()
        copies.append(c)

    copy(q.at[pl.ds(pl.multiple_of(run * ROWS + core * 64, 64), 64)], qs.at[pl.ds(0, 64)])
    copy(q.at[pl.ds(pl.multiple_of(run * ROWS + (1 - core) * 64, 64), 64)], qs.at[pl.ds(64, 64)])
    for kind, (prev, cur) in enumerate(((kp, kc), (vp, vc))):
        copy(prev, kv.at[kind, pl.ds(SLOTS, RUNS)])
        copy(cur, kv.at[kind, pl.ds(SLOTS + RUNS, RUNS)])
    for kind, parts in ((odd, (a0, a2, b0, b2)), (1 - odd, (a1, a3, b1, b3))):
        for p, part in enumerate(parts):
            copy(part, kv.at[kind, pl.ds(0, SLOTS), pl.ds(32 * p, 32)])
    first = len(copies)
    copy(w, ws)
    for c in copies[:first]:
        c.wait()
    place = lax.broadcasted_iota(jnp.int32, (ROWS, 1), 0)
    place = place + jnp.where(place < 64, core * 64, -core * 64)
    for h in range(8):
        cols = slice(h * HEAD, (h + 1) * HEAD)
        rows = [idx[run, h, e] for e in range(ENTRIES)]
        keys = jnp.concatenate([kv[0, r] for r in rows], axis=0)
        scores = lax.dot_general(qs[:, cols], keys, (((1,), (1,)), ((), ())), preferred_element_type=jnp.float32)
        limit = thr[run, pl.ds(h, 1), :]
        scores = jnp.where(place >= limit, scores, -1e30)
        sink_raw = sink[h] * (1.0 / SCALE)
        top = jnp.maximum(jnp.max(scores, axis=1, keepdims=True), sink_raw)
        weights = jnp.exp2((scores - top) * (SCALE * LOG2E))
        total = jnp.sum(weights, axis=1, keepdims=True) + jnp.exp2((sink_raw - top) * (SCALE * LOG2E))
        values = jnp.concatenate([kv[1, r] for r in rows], axis=0)
        mixed = jnp.dot(weights.astype(jnp.bfloat16), values, preferred_element_type=jnp.float32)
        att[:, cols] = (mixed / total).astype(jnp.bfloat16)
    copies[first].wait()
    tile = 512
    for n in range(w.shape[1] // tile):
        cols = slice(n * tile, (n + 1) * tile)
        out = jnp.dot(att[...], ws[:, cols], preferred_element_type=jnp.float32).astype(jnp.bfloat16)
        keep[:, cols] = out[:64]
        give[:, cols] = out[64:]
    token[0] = dep[0] + 1


def block_attention(meta, idx, sink, thr, q, parts, band, w, dep):
    smem = pl.BlockSpec(memory_space=pltpu.SMEM)
    vmem = pl.BlockSpec(memory_space=pltpu.VMEM)
    anyw = pl.BlockSpec(memory_space=pl.ANY)
    half = jax.ShapeDtypeStruct((64, w.shape[1]), jnp.bfloat16)
    return pl.pallas_call(
        attend,
        out_shape=(half, half, jax.ShapeDtypeStruct((1,), jnp.int32)),
        in_specs=[smem, smem, smem, vmem] + [anyw] * 14 + [smem],
        out_specs=(vmem, vmem, smem),
        scratch_shapes=[
            pltpu.VMEM((2, SLOTS + 2 * RUNS, ROWS, HEAD), jnp.bfloat16),
            pltpu.VMEM((ROWS, q.shape[1]), jnp.bfloat16),
            pltpu.VMEM(w.shape, jnp.bfloat16),
            pltpu.VMEM((ROWS, q.shape[1]), jnp.bfloat16),
            pltpu.SemaphoreType.DMA((15,)),
        ],
        compiler_params=pltpu.CompilerParams(vmem_limit_bytes=32 * 1024 * 1024),
        cost_estimate=pl.CostEstimate(flops=2 * 10 ** 9, bytes_accessed=12 * 2 ** 20, transcendentals=1408 * 1024),
    )(meta, idx, sink, thr, q, *parts, *band, w, dep)


def total_of(*terms):
    return functools.reduce(lambda a, b: a + b, [t.astype(jnp.float32) for t in terms]).astype(jnp.bfloat16)


def tables(c, vert_blocks, slash_offsets):
    z, y = c // Y, c % Y
    block = jnp.arange(BLOCKS, dtype=jnp.int32)
    present = jnp.any(vert_blocks.reshape(-1, 1) == block[None, :], axis=0).astype(jnp.int32)
    rank = jnp.sum(jnp.where(block[:, None] > block[None, :], present[None, :], 0), axis=1)
    place = jnp.where(present > 0, rank, -1)
    slot = jnp.sum(jnp.where(vert_blocks[:, :, None] == block, rank, 0), axis=2)
    run = jnp.arange(RUNS, dtype=jnp.int32)
    own = RUNS * c + run
    band = own[:, None, None] - slash_offsets[None]
    listed = jnp.any(band[:, :, :, None] == vert_blocks[None, :, None, :], axis=3)
    band_idx = SLOTS + RUNS + run[:, None, None] - slash_offsets[None]
    idx = jnp.concatenate([jnp.broadcast_to(slot[None], (RUNS,) + slot.shape), band_idx], axis=2)
    n = jnp.arange(ROWS, dtype=jnp.int32)
    part, inner, row = n // 32, (n // 8) % 4, n % 8
    z_of = jnp.where(part < 2, z + 2 * inner, z + jnp.where(inner < 2, -1 - 2 * inner, 2 * inner - 3)) % Z
    y_of = (y // 2) ^ (part % 2)
    key_row = (z_of * 2 + y_of) * 8 + row
    diag = vert_blocks[None] == own[:, None, None]
    seen = (vert_blocks[None] >= 0) & (vert_blocks[None] < own[:, None, None])
    thr_vert = jnp.where(diag[..., None], key_row, jnp.where(seen[..., None], -1, NEVER))
    ok = (band >= 0) & jnp.logical_not(listed)
    at_own = slash_offsets[None] == 0
    thr_band = jnp.where(ok[..., None], jnp.where(at_own[..., None], n, -1), NEVER)
    thr = jnp.concatenate([thr_vert, thr_band], axis=2).reshape(RUNS, vert_blocks.shape[0], ENTRIES * ROWS)
    return place, idx, thr


def per_device(queries, keys, values, sink_logits, vert_blocks, slash_offsets, output_weight):
    c = lax.axis_index("ctx")
    h = lax.axis_index("head")
    x, core = h // 2, h % 2
    keys = keys.reshape(RUNS, ROWS, HEAD)
    values = values.reshape(RUNS, ROWS, HEAD)
    step = [(s, s + 1) for s in range(Z * Y - 1)]
    k_prev = lax.ppermute(keys, "ctx", step)
    v_prev = lax.ppermute(values, "ctx", step)
    place, idx, thr = tables(c, vert_blocks, slash_offsets)

    def slices(a):
        return jnp.transpose(a.reshape(RUNS, 16, 8, HEAD), (1, 0, 2, 3))

    spread = jnp.stack([slices(keys), slices(values)], axis=1).reshape(Z * Y, RUNS * 8, HEAD)
    got = lax.all_to_all(spread, "ctx", 0, 0, tiled=True).reshape(BLOCKS * 8, HEAD)
    r = jnp.arange(SLOTS * 8, dtype=jnp.int32)[:, None]
    col = jnp.arange(BLOCKS * 8, dtype=jnp.int32)[None, :]
    pick = (jnp.repeat(place, 8)[None, :] == r // 8) & (col % 8 == r % 8)
    mine = jnp.dot(pick.astype(jnp.bfloat16), got, preferred_element_type=jnp.float32)
    mine = mine.astype(jnp.bfloat16).reshape(SLOTS, 8, HEAD)

    def from_z(a, offset):
        return lax.ppermute(a, "ctx", z_pairs(-offset))

    z2, z4, z6 = from_z(mine, 2), from_z(mine, 4), from_z(mine, 6)
    a0 = jnp.concatenate([mine, z2, z4, z6], axis=1)
    low = from_z(jnp.concatenate([mine, z6], axis=1), -1)
    high = from_z(jnp.concatenate([mine, z2], axis=1), 1)
    b0 = jnp.concatenate([low, high], axis=1)
    a1, a2, a3 = [lax.ppermute(a0, "ctx", y_pairs(f)) for f in (1, 2, 3)]
    b1, b2, b3 = [lax.ppermute(b0, "ctx", y_pairs(f)) for f in (1, 2, 3)]
    parts = (a0, a2, b0, b2, a1, a3, b1, b3)

    dep = jnp.zeros((1,), jnp.int32)
    band = (k_prev, v_prev, keys, values)
    sums = {}
    for d in (2, 1, 3, 0):
        meta = jnp.stack([(x + d) % X, core, c % 2]).astype(jnp.int32)
        keep, give, dep = block_attention(meta, idx, sink_logits, thr, queries, parts, band, output_weight, dep)
        sums[d] = (keep, lax.ppermute(give, "head", CORE_PAIRS))
    mid = output_weight.shape[1] // 2

    def left(pair):
        return tuple(p[:, :mid] for p in pair)

    def right(pair):
        return tuple(p[:, mid:] for p in pair)

    def to_x(a, step):
        return lax.ppermute(a, "head", x_pairs(step))

    relay_left = to_x(total_of(*left(sums[2])), 1)
    relay_right = to_x(total_of(*right(sums[2])), -1)
    right_below = to_x(total_of(*right(sums[1])), 1)
    left_above = to_x(total_of(*left(sums[3])), -1)
    left_below = to_x(total_of(*left(sums[1]), relay_left), 1)
    right_above = to_x(total_of(*right(sums[3]), relay_right), -1)
    out_left = total_of(*left(sums[0]), left_below, left_above)
    out_right = total_of(*right(sums[0]), right_below, right_above)
    return jnp.concatenate([out_left, out_right], axis=1)


def solution(mesh):
    return jax.shard_map(
        per_device,
        mesh=mesh,
        in_specs=(
            P("ctx", "head"),
            P("ctx", "head"),
            P("ctx", "head"),
            P("head"),
            P("head", None),
            P("head", None),
            P("head", None),
        ),
        out_specs=P(("ctx", "head"), None),
        check_vma=False,
    )
```

time: 349 us -> 138 us (0.40)
  waiting for transfers between devices: 182 us -> 33.6 us
  local copies, waits for them, and re-layouts: 83.5 us -> 14.9 us
  matrix products: 45.2 us -> 0.34 us
  starting transfers between devices: 4.09 us -> 45.3 us
  Pallas kernels: 0 us -> 33.4 us
  between operations: 13.6 us -> 0.4 us
  other arithmetic: 18.4 us -> 8.2 us
    psum x1 -> x0, waiting for transfers between devices: 142 us -> none  [per_device(): lax.psum(contribution, 'ctx').astype(jnp.float32).astype(jnp.bfloat16)]
    gather x2 -> x0, local copies, waits for them, and re-layouts: 76.5 us -> none  [the longest x1 70.3 us: per_device(): picked = kv_local[head_kv[:, None, None], local_rows]]
    dot_general x5 -> x1, matrix products: 45.2 us -> 0.34 us  [per_device(): jnp.dot(pick.astype(jnp.bfloat16), got, preferred_element_type=jnp.float32)]
    reduce_scatter x1 -> x0, waiting for transfers between devices: 37.5 us -> none  [per_device(): lax.psum_scatter(jnp.dot(attention, output_weight, preferred_element_type...]
    pallas_call x0 -> x4, Pallas kernels: none -> 33.4 us  [block_attention(): pl.pallas_call(attend, out_shape=(half, half, jax.ShapeDtypeStruct((1,),...]
    ppermute x1 -> x23, starting transfers between devices: 4.05 us -> 35.2 us  [the longest x6 7.16 us: to_x(): return lax.ppermute(a, 'head', x_pairs(step))]
    ppermute x1 -> x23, waiting for transfers between devices: 2.9 us -> 30.3 us  [the longest x6 14.4 us: to_x(): return lax.ppermute(a, 'head', x_pairs(step))]
    unnamed x16 -> x27, local copies, waits for them, and re-layouts: 2.18 us -> 12.8 us
  transfers between devices with their start and end apart: 3 -> 24, of which waited for: 3 -> 10; matrix products, arithmetic and copies ran while one was open for 5% -> 8% of each run, Pallas kernels for 0% -> 18%
where the time goes in v1:
time: 138 us; the launch traced here: 136 us
  starting transfers between devices  45.3 us (33%)
  waiting for transfers between devices  33.6 us (24%)
  Pallas kernels  33.4 us (24%)
  local copies, waits for them, and re-layouts  14.9 us (11%)
  other arithmetic  8.2 us (6%)
    pallas_call x4, Pallas kernels, block_attention(): pl.pallas_call(attend, out_shape=(half, half, jax.ShapeDtypeStruct((1,),...  33.4 us
    ppermute x6, waiting for transfers between devices, to_x(): return lax.ppermute(a, 'head', x_pairs(step))  14.4 us
    unnamed x27, local copies, waits for them, and re-layouts  12.8 us
    all_to_all x1, starting transfers between devices, per_device(): lax.all_to_all(spread, 'ctx', 0, 0, tiled=True).reshape(BLOCKS * 8, HEAD)  10.1 us
    ppermute x5, waiting for transfers between devices, from_z(): return lax.ppermute(a, 'ctx', z_pairs(-offset))  7.72 us
    ppermute x3, waiting for transfers between devices, per_device(): b1, b2, b3 = [lax.ppermute(b0, 'ctx', y_pairs(f)) for f in (1, 2, 3)]  7.63 us
    ppermute x6, starting transfers between devices, to_x(): return lax.ppermute(a, 'head', x_pairs(step))  7.16 us
    ppermute x5, starting transfers between devices, from_z(): return lax.ppermute(a, 'ctx', z_pairs(-offset))  6.29 us
  transfers between devices with their start and end apart: 24, of which 10 were waited for; matrix products, arithmetic and copies ran while one was open for 8% of the time, Pallas kernels for 18%

profile of v1, /device:TPU:1, one launch (start us, length us, event | category | flops | bytes accessed | tf_op | source)
XLA Modules:
  0.0 136.1 jit_solution(1140537638045480089)
XLA Ops:
  0.0 4.2 %collective-permute-start.11 = (bf16[4,128,128]{2,1,0:T(8,128)(2,1)}, bf16[4,128,128]{2,1,0:T(8,128)(2,1)S(1)}, u32[]{:S(2)}, u32[]{:S(2)}) collective-permute-start(bf16[4,128,128]{2,1,0:T(8,128)(2,1)} %bitcast.31), channel_id=1, source_target_pairs={{0,8},{8,16},{16,24},{24,32},{32,40},{40,48},{48,56},{56,64},{64,7... | collective-permute-start | bytes 393224 | tf_op jit(solution)/shard_map/ppermute | solution.py:146
  4.2 3.2 %collective-permute-start.12 = (bf16[4,128,128]{2,1,0:T(8,128)(2,1)}, bf16[4,128,128]{2,1,0:T(8,128)(2,1)S(1)}, u32[]{:S(2)}, u32[]{:S(2)}) collective-permute-start(bf16[4,128,128]{2,1,0:T(8,128)(2,1)} %bitcast.25), channel_id=1, source_target_pairs={{0,8},{8,16},{16,24},{24,32},{32,40},{40,48},{48,56},{56,64},{64,7... | collective-permute-start | bytes 393224 | tf_op jit(solution)/shard_map/ppermute | solution.py:147
  9.2 10.1 %all-to-all-start = ((bf16[32,32,128]{2,1,0:T(8,128)(2,1)}), bf16[32,32,128]{2,1,0:T(8,128)(2,1)S(1)}, u32[]{:S(2)}, u32[]{:S(2)}) async-start(bf16[32,32,128]{2,1,0:T(8,128)(2,1)} %bitcast.10), calls=%async_computation | async-start | bytes 524288 | tf_op jit(solution)/shard_map/all_to_all | solution.py:154
  26.7 3.2 %all-to-all-done = bf16[32,32,128]{2,1,0:T(8,128)(2,1)S(1)} async-done(((bf16[32,32,128]{2,1,0:T(8,128)(2,1)}), bf16[32,32,128]{2,1,0:T(8,128)(2,1)S(1)}, u32[]{:S(2)}, u32[]{:S(2)}) %all-to-all-start) | async-done | bytes 262176 | tf_op jit(solution)/shard_map/all_to_all | solution.py:154
  30.2 1.6 %collective-permute-start.2 = (bf16[24,8,128]{2,1,0:T(8,128)(2,1)S(1)}, bf16[24,8,128]{2,1,0:T(8,128)(2,1)S(1)}, u32[]{:S(2)}, u32[]{:S(2)}) collective-permute-start(bf16[24,8,128]{2,1,0:T(8,128)(2,1)S(1)} %fusion), channel_id=1, source_target_pairs={{0,64},{8,72},{16,80},{24,88},{32,96},{40,104},{48,112},{56,120},{... | collective-permute-start | bytes 147464 | tf_op jit(solution)/shard_map/ppermute | solution.py:162
  31.8 2.1 %collective-permute-start = (bf16[24,8,128]{2,1,0:T(8,128)(2,1)S(1)}, bf16[24,8,128]{2,1,0:T(8,128)(2,1)S(1)}, u32[]{:S(2)}, u32[]{:S(2)}) collective-permute-start(bf16[24,8,128]{2,1,0:T(8,128)(2,1)S(1)} %fusion), channel_id=1, source_target_pairs={{0,192},{8,200},{16,208},{24,216},{32,224},{40,232},{48,240},{56,2... | collective-permute-start | bytes 147464 | tf_op jit(solution)/shard_map/ppermute | solution.py:162
  34.0 1.9 %collective-permute-start.1 = (bf16[24,8,128]{2,1,0:T(8,128)(2,1)S(1)}, bf16[24,8,128]{2,1,0:T(8,128)(2,1)S(1)}, u32[]{:S(2)}, u32[]{:S(2)}) collective-permute-start(bf16[24,8,128]{2,1,0:T(8,128)(2,1)S(1)} %fusion), channel_id=1, source_target_pairs={{0,128},{8,136},{16,144},{24,152},{32,160},{40,168},{48,176},{56,1... | collective-permute-start | bytes 147464 | tf_op jit(solution)/shard_map/ppermute | solution.py:162
  37.0 3.9 %collective-permute-done.1 = bf16[24,8,128]{2,1,0:T(8,128)(2,1)S(1)} collective-permute-done((bf16[24,8,128]{2,1,0:T(8,128)(2,1)S(1)}, bf16[24,8,128]{2,1,0:T(8,128)(2,1)S(1)}, u32[]{:S(2)}, u32[]{:S(2)}) %collective-permute-start.1) | collective-permute-done | bytes 49184 | tf_op jit(solution)/shard_map/ppermute | solution.py:162
  43.0 3.5 %collective-permute-done.5 = bf16[24,16,128]{2,1,0:T(8,128)(2,1)S(1)} collective-permute-done((bf16[24,16,128]{2,1,0:T(8,128)(2,1)S(1)}, bf16[24,16,128]{2,1,0:T(8,128)(2,1)S(1)}, u32[]{:S(2)}, u32[]{:S(2)}) %collective-permute-start.5) | collective-permute-done | bytes 98336 | tf_op jit(solution)/shard_map/ppermute | solution.py:162
  46.5 2.3 %collective-permute-start.3 = (bf16[24,32,128]{2,1,0:T(8,128)(2,1)S(1)}, bf16[24,32,128]{2,1,0:T(8,128)(2,1)S(1)}, u32[]{:S(2)}, u32[]{:S(2)}) collective-permute-start(bf16[24,32,128]{2,1,0:T(8,128)(2,1)S(1)} %pad_maximum_fusion.2.a0), channel_id=1, source_target_pairs={{0,16},{8,24},{16,0},{24,8},{32,48},{40,56},{48,32},{56,40},{64,80... | collective-permute-start | bytes 589832 | tf_op jit(solution)/shard_map/ppermute | solution.py:169
  50.0 2.8 %collective-permute-start.6 = (bf16[24,32,128]{2,1,0:T(8,128)(2,1)S(1)}, bf16[24,32,128]{2,1,0:T(8,128)(2,1)S(1)}, u32[]{:S(2)}, u32[]{:S(2)}) collective-permute-start(bf16[24,32,128]{2,1,0:T(8,128)(2,1)S(1)} %constant_dynamic-update-slice_fusion.b0), channel_id=1, source_target_pairs={{0,16},{8,24},{16,0},{24,8},{32,48},{40,56},{48,32},{56,40},{64,80... | collective-permute-start | bytes 589832 | tf_op jit(solution)/shard_map/ppermute | solution.py:170
  53.4 3.2 %collective-permute-done.10.b3 = bf16[24,32,128]{2,1,0:T(8,128)(2,1)S(1)} collective-permute-done((bf16[24,32,128]{2,1,0:T(8,128)(2,1)S(1)}, bf16[24,32,128]{2,1,0:T(8,128)(2,1)S(1)}, u32[]{:S(2)}, u32[]{:S(2)}) %collective-permute-start.10) | collective-permute-done | bytes 196640 | tf_op jit(solution)/shard_map/ppermute | solution.py:170
  56.5 4.5 %collective-permute-done.6.b2 = bf16[24,32,128]{2,1,0:T(8,128)(2,1)S(1)} collective-permute-done((bf16[24,32,128]{2,1,0:T(8,128)(2,1)S(1)}, bf16[24,32,128]{2,1,0:T(8,128)(2,1)S(1)}, u32[]{:S(2)}, u32[]{:S(2)}) %collective-permute-start.6) | collective-permute-done | bytes 196640 | tf_op jit(solution)/shard_map/ppermute | solution.py:170
  61.0 3.4 %copy-done = bf16[1024,4096]{1,0:T(8,128)(2,1)S(1)} copy-done((bf16[1024,4096]{1,0:T(8,128)(2,1)S(1)}, bf16[1024,4096]{1,0:T(8,128)(2,1)}, u32[]{:S(2)}) %copy-start) | copy-done | bytes 8388632
  68.1 8.4 %shard_map.73 = (bf16[64,4096]{1,0:T(8,128)(2,1)S(1)}, bf16[64,4096]{1,0:T(8,128)(2,1)}, s32[1]{0:T(128)}) custom-call(s32[3]{0:T(128)S(1)} %get-tuple-element.42.meta, s32[4,8,11]{2,1,0:T(8,128)S(1)} %pad_add_fusion.idx, f32[8]{0:T(128)S(1)} %copy-done.10, s32[4,8,1408]{2,1,0:T(8,128)S(1)} %add_bitcast_fusion.thr, bf16[512,1024]{1,0:T(8,128)(2,1)S(1)} %copy-done.2, ...), custom_call_target="tpu_custom_call" | custom-call | flops 2000000000 | bytes 12582912 | tf_op jit(solution)/shard_map/pallas_call | solution.py:90
  77.3 5.0 %collective-permute-start.15 = (bf16[64,4096]{1,0:T(8,128)(2,1)}, bf16[64,4096]{1,0:T(8,128)(2,1)}, u32[]{:S(2)}, u32[]{:S(2)}) collective-permute-start(bf16[64,4096]{1,0:T(8,128)(2,1)} %get-tuple-element.24), channel_id=1, source_target_pairs={{0,1},{1,0},{2,3},{3,2},{4,5},{5,4},{6,7},{7,6},{8,9},{9,8},{10,11... | collective-permute-start | bytes 1572872 | tf_op jit(solution)/shard_map/ppermute | solution.py:179
  82.5 3.4 %copy-done.1 = bf16[1024,4096]{1,0:T(8,128)(2,1)S(1)} copy-done((bf16[1024,4096]{1,0:T(8,128)(2,1)S(1)}, bf16[1024,4096]{1,0:T(8,128)(2,1)}, u32[]{:S(2)}) %copy-start.1) | copy-done | bytes 8388632
  85.8 8.4 %shard_map.74 = (bf16[64,4096]{1,0:T(8,128)(2,1)S(1)}, bf16[64,4096]{1,0:T(8,128)(2,1)S(1)}, s32[1]{0:T(128)}) custom-call(s32[3]{0:T(128)S(1)} %get-tuple-element.41.meta, s32[4,8,11]{2,1,0:T(8,128)S(1)} %pad_add_fusion.idx, f32[8]{0:T(128)S(1)} %copy-done.11, s32[4,8,1408]{2,1,0:T(8,128)S(1)} %add_bitcast_fusion.thr, bf16[512,1024]{1,0:T(8,128)(2,1)S(1)} %copy-done.3, ...), custom_call_target="tpu_custom_call" | custom-call | flops 2000000000 | bytes 12582912 | tf_op jit(solution)/shard_map/pallas_call | solution.py:90
  97.0 8.3 %shard_map.75 = (bf16[64,4096]{1,0:T(8,128)(2,1)S(1)}, bf16[64,4096]{1,0:T(8,128)(2,1)S(1)}, s32[1]{0:T(128)}) custom-call(s32[3]{0:T(128)S(1)} %get-tuple-element.40.meta, s32[4,8,11]{2,1,0:T(8,128)S(1)} %pad_add_fusion.idx, f32[8]{0:T(128)S(1)} %copy-done.11, s32[4,8,1408]{2,1,0:T(8,128)S(1)} %add_bitcast_fusion.thr, bf16[512,1024]{1,0:T(8,128)(2,1)S(1)} %copy-done.3, ...), custom_call_target="tpu_custom_call" | custom-call | flops 2000000000 | bytes 12582912 | tf_op jit(solution)/shard_map/pallas_call | solution.py:90
  106.1 8.3 %shard_map.76 = (bf16[64,4096]{1,0:T(8,128)(2,1)S(1)}, bf16[64,4096]{1,0:T(8,128)(2,1)S(1)}, s32[1]{0:T(128)}) custom-call(s32[3]{0:T(128)S(1)} %get-tuple-element.39.meta, s32[4,8,11]{2,1,0:T(8,128)S(1)} %pad_add_fusion.idx, f32[8]{0:T(128)S(1)} %copy-done.11, s32[4,8,1408]{2,1,0:T(8,128)S(1)} %add_bitcast_fusion.thr, bf16[512,1024]{1,0:T(8,128)(2,1)S(1)} %copy-done.3, ...), custom_call_target="tpu_custom_call" | custom-call | flops 2000000000 | bytes 12582912 | tf_op jit(solution)/shard_map/pallas_call | solution.py:90
  117.6 4.5 %collective-permute-done.21 = bf16[64,2048]{1,0:T(8,128)(2,1)S(1)} collective-permute-done((bf16[64,2048]{1,0:T(8,128)(2,1)S(1)}, bf16[64,2048]{1,0:T(8,128)(2,1)S(1)}, u32[]{:S(2)}, u32[]{:S(2)}) %collective-permute-start.21) | collective-permute-done | bytes 262176 | tf_op jit(solution)/shard_map/ppermute | solution.py:189
  122.3 2.8 %collective-permute-start.19 = (bf16[64,2048]{1,0:T(8,128)(2,1)S(1)}, bf16[64,2048]{1,0:T(8,128)(2,1)S(1)}, u32[]{:S(2)}, u32[]{:S(2)}) collective-permute-start(bf16[64,2048]{1,0:T(8,128)(2,1)S(1)} %get-tuple-element.33), channel_id=1, source_target_pairs={{0,6},{1,7},{2,0},{3,1},{4,2},{5,3},{6,4},{7,5},{8,14},{9,15},{10,... | collective-permute-start | bytes 786440 | tf_op jit(solution)/shard_map/ppermute | solution.py:189
  125.1 5.2 %collective-permute-done.20 = bf16[64,2048]{1,0:T(8,128)(2,1)S(1)} collective-permute-done((bf16[64,2048]{1,0:T(8,128)(2,1)S(1)}, bf16[64,2048]{1,0:T(8,128)(2,1)S(1)}, u32[]{:S(2)}, u32[]{:S(2)}) %collective-permute-start.20) | collective-permute-done | bytes 262176 | tf_op jit(solution)/shard_map/ppermute | solution.py:189
  130.3 4.7 %collective-permute-done.22 = bf16[64,2048]{1,0:T(8,128)(2,1)S(1)} collective-permute-done((bf16[64,2048]{1,0:T(8,128)(2,1)S(1)}, bf16[64,2048]{1,0:T(8,128)(2,1)S(1)}, u32[]{:S(2)}, u32[]{:S(2)}) %collective-permute-start.22) | collective-permute-done | bytes 262176 | tf_op jit(solution)/shard_map/ppermute | solution.py:189
  (97 shorter events, 27.0 us)
Async XLA Ops:
  0.0 48.8 %collective-permute-start.11 = (bf16[4,128,128]{2,1,0:T(8,128)(2,1)}, bf16[4,128,128]{2,1,0:T(8,128)(2,1)S(1)}, u32[]{:S(2)}, u32[]{:S(2)}) collective-permute-start(bf16[4,128,128]{2,1,0:T(8,128)(2,1)} %bitcast.31), channel_id=1, source_target_pairs={{0,8},{8,16},{16,24},{24,32},{32,40},{40,48},{48,56},{56,64},{64,7... | collective-permute-start | bytes 393224 | tf_op jit(solution)/shard_map/ppermute | solution.py:146
  4.2 45.7 %collective-permute-start.12 = (bf16[4,128,128]{2,1,0:T(8,128)(2,1)}, bf16[4,128,128]{2,1,0:T(8,128)(2,1)S(1)}, u32[]{:S(2)}, u32[]{:S(2)}) collective-permute-start(bf16[4,128,128]{2,1,0:T(8,128)(2,1)} %bitcast.25), channel_id=1, source_target_pairs={{0,8},{8,16},{16,24},{24,32},{32,40},{40,48},{48,56},{56,64},{64,7... | collective-permute-start | bytes 393224 | tf_op jit(solution)/shard_map/ppermute | solution.py:147
  9.2 20.7 %all-to-all-start = ((bf16[32,32,128]{2,1,0:T(8,128)(2,1)}), bf16[32,32,128]{2,1,0:T(8,128)(2,1)S(1)}, u32[]{:S(2)}, u32[]{:S(2)}) async-start(bf16[32,32,128]{2,1,0:T(8,128)(2,1)} %bitcast.10), calls=%async_computation | async-start | bytes 524288 | tf_op jit(solution)/shard_map/all_to_all | solution.py:154
  30.2 5.7 %collective-permute-start.2 = (bf16[24,8,128]{2,1,0:T(8,128)(2,1)S(1)}, bf16[24,8,128]{2,1,0:T(8,128)(2,1)S(1)}, u32[]{:S(2)}, u32[]{:S(2)}) collective-permute-start(bf16[24,8,128]{2,1,0:T(8,128)(2,1)S(1)} %fusion), channel_id=1, source_target_pairs={{0,64},{8,72},{16,80},{24,88},{32,96},{40,104},{48,112},{56,120},{... | collective-permute-start | bytes 147464 | tf_op jit(solution)/shard_map/ppermute | solution.py:162
  31.8 4.4 %collective-permute-start = (bf16[24,8,128]{2,1,0:T(8,128)(2,1)S(1)}, bf16[24,8,128]{2,1,0:T(8,128)(2,1)S(1)}, u32[]{:S(2)}, u32[]{:S(2)}) collective-permute-start(bf16[24,8,128]{2,1,0:T(8,128)(2,1)S(1)} %fusion), channel_id=1, source_target_pairs={{0,192},{8,200},{16,208},{24,216},{32,224},{40,232},{48,240},{56,2... | collective-permute-start | bytes 147464 | tf_op jit(solution)/shard_map/ppermute | solution.py:162
  34.0 6.9 %collective-permute-start.1 = (bf16[24,8,128]{2,1,0:T(8,128)(2,1)S(1)}, bf16[24,8,128]{2,1,0:T(8,128)(2,1)S(1)}, u32[]{:S(2)}, u32[]{:S(2)}) collective-permute-start(bf16[24,8,128]{2,1,0:T(8,128)(2,1)S(1)} %fusion), channel_id=1, source_target_pairs={{0,128},{8,136},{16,144},{24,152},{32,160},{40,168},{48,176},{56,1... | collective-permute-start | bytes 147464 | tf_op jit(solution)/shard_map/ppermute | solution.py:162
  36.3 6.7 %collective-permute-start.4 = (bf16[24,16,128]{2,1,0:T(8,128)(2,1)S(1)}, bf16[24,16,128]{2,1,0:T(8,128)(2,1)S(1)}, u32[]{:S(2)}, u32[]{:S(2)}) collective-permute-start(bf16[24,16,128]{2,1,0:T(8,128)(2,1)S(1)} %get-tuple-element.36), channel_id=1, source_target_pairs={{0,32},{8,40},{16,48},{24,56},{32,64},{40,72},{48,80},{56,88},{64,... | collective-permute-start | bytes 294920 | tf_op jit(solution)/shard_map/ppermute | solution.py:162
  40.9 9.0 %collective-permute-start.8 = (bf16[24,32,128]{2,1,0:T(8,128)(2,1)S(1)}, bf16[24,32,128]{2,1,0:T(8,128)(2,1)S(1)}, u32[]{:S(2)}, u32[]{:S(2)}) collective-permute-start(bf16[24,32,128]{2,1,0:T(8,128)(2,1)S(1)} %pad_maximum_fusion.2.a0), channel_id=1, source_target_pairs={{0,24},{8,16},{16,8},{24,0},{32,56},{40,48},{48,40},{56,32},{64,88... | collective-permute-start | bytes 589832 | tf_op jit(solution)/shard_map/ppermute | solution.py:169
  42.4 10.4 %collective-permute-start.7 = (bf16[24,32,128]{2,1,0:T(8,128)(2,1)S(1)}, bf16[24,32,128]{2,1,0:T(8,128)(2,1)S(1)}, u32[]{:S(2)}, u32[]{:S(2)}) collective-permute-start(bf16[24,32,128]{2,1,0:T(8,128)(2,1)S(1)} %pad_maximum_fusion.2.a0), channel_id=1, source_target_pairs={{0,8},{8,0},{16,24},{24,16},{32,40},{40,32},{48,56},{56,48},{64,72... | collective-permute-start | bytes 589832 | tf_op jit(solution)/shard_map/ppermute | solution.py:169
  43.0 3.5 %collective-permute-start.5 = (bf16[24,16,128]{2,1,0:T(8,128)(2,1)S(1)}, bf16[24,16,128]{2,1,0:T(8,128)(2,1)S(1)}, u32[]{:S(2)}, u32[]{:S(2)}) collective-permute-start(bf16[24,16,128]{2,1,0:T(8,128)(2,1)S(1)} %get-tuple-element.35), channel_id=1, source_target_pairs={{0,224},{8,232},{16,240},{24,248},{32,0},{40,8},{48,16},{56,24},{6... | collective-permute-start | bytes 294920 | tf_op jit(solution)/shard_map/ppermute | solution.py:162
  46.5 6.9 %collective-permute-start.3 = (bf16[24,32,128]{2,1,0:T(8,128)(2,1)S(1)}, bf16[24,32,128]{2,1,0:T(8,128)(2,1)S(1)}, u32[]{:S(2)}, u32[]{:S(2)}) collective-permute-start(bf16[24,32,128]{2,1,0:T(8,128)(2,1)S(1)} %pad_maximum_fusion.2.a0), channel_id=1, source_target_pairs={{0,16},{8,24},{16,0},{24,8},{32,48},{40,56},{48,32},{56,40},{64,80... | collective-permute-start | bytes 589832 | tf_op jit(solution)/shard_map/ppermute | solution.py:169
  48.8 7.7 %collective-permute-start.10 = (bf16[24,32,128]{2,1,0:T(8,128)(2,1)S(1)}, bf16[24,32,128]{2,1,0:T(8,128)(2,1)S(1)}, u32[]{:S(2)}, u32[]{:S(2)}) collective-permute-start(bf16[24,32,128]{2,1,0:T(8,128)(2,1)S(1)} %constant_dynamic-update-slice_fusion.b0), channel_id=1, source_target_pairs={{0,24},{8,16},{16,8},{24,0},{32,56},{40,48},{48,40},{56,32},{64,88... | collective-permute-start | bytes 589832 | tf_op jit(solution)/shard_map/ppermute | solution.py:170
  49.9 6.6 %collective-permute-start.9 = (bf16[24,32,128]{2,1,0:T(8,128)(2,1)S(1)}, bf16[24,32,128]{2,1,0:T(8,128)(2,1)S(1)}, u32[]{:S(2)}, u32[]{:S(2)}) collective-permute-start(bf16[24,32,128]{2,1,0:T(8,128)(2,1)S(1)} %constant_dynamic-update-slice_fusion.b0), channel_id=1, source_target_pairs={{0,8},{8,0},{16,24},{24,16},{32,40},{40,32},{48,56},{56,48},{64,72... | collective-permute-start | bytes 589832 | tf_op jit(solution)/shard_map/ppermute | solution.py:170
  50.0 11.0 %collective-permute-start.6 = (bf16[24,32,128]{2,1,0:T(8,128)(2,1)S(1)}, bf16[24,32,128]{2,1,0:T(8,128)(2,1)S(1)}, u32[]{:S(2)}, u32[]{:S(2)}) collective-permute-start(bf16[24,32,128]{2,1,0:T(8,128)(2,1)S(1)} %constant_dynamic-update-slice_fusion.b0), channel_id=1, source_target_pairs={{0,16},{8,24},{16,0},{24,8},{32,48},{40,56},{48,32},{56,40},{64,80... | collective-permute-start | bytes 589832 | tf_op jit(solution)/shard_map/ppermute | solution.py:170
  77.3 17.0 %collective-permute-start.15 = (bf16[64,4096]{1,0:T(8,128)(2,1)}, bf16[64,4096]{1,0:T(8,128)(2,1)}, u32[]{:S(2)}, u32[]{:S(2)}) collective-permute-start(bf16[64,4096]{1,0:T(8,128)(2,1)} %get-tuple-element.24), channel_id=1, source_target_pairs={{0,1},{1,0},{2,3},{3,2},{4,5},{5,4},{6,7},{7,6},{8,9},{9,8},{10,11... | collective-permute-start | bytes 1572872 | tf_op jit(solution)/shard_map/ppermute | solution.py:179
  94.2 21.9 %collective-permute-start.14 = (bf16[64,4096]{1,0:T(8,128)(2,1)S(1)}, bf16[64,4096]{1,0:T(8,128)(2,1)S(1)}, u32[]{:S(2)}, u32[]{:S(2)}) collective-permute-start(bf16[64,4096]{1,0:T(8,128)(2,1)S(1)} %get-tuple-element.22), channel_id=1, source_target_pairs={{0,1},{1,0},{2,3},{3,2},{4,5},{5,4},{6,7},{7,6},{8,9},{9,8},{10,11... | collective-permute-start | bytes 1572872 | tf_op jit(solution)/shard_map/ppermute | solution.py:179
  95.5 20.6 %collective-permute-start.16 = (bf16[64,2048]{1,0:T(8,128)(2,1)S(1)}, bf16[64,2048]{1,0:T(8,128)(2,1)S(1)}, u32[]{:S(2)}, u32[]{:S(2)}) collective-permute-start(bf16[64,2048]{1,0:T(8,128)(2,1)S(1)} %get-tuple-element.31), channel_id=1, source_target_pairs={{0,2},{1,3},{2,4},{3,5},{4,6},{5,7},{6,0},{7,1},{8,10},{9,11},{10,... | collective-permute-start | bytes 786440 | tf_op jit(solution)/shard_map/ppermute | solution.py:189
  105.3 12.3 %collective-permute-start.18 = (bf16[64,4096]{1,0:T(8,128)(2,1)S(1)}, bf16[64,4096]{1,0:T(8,128)(2,1)S(1)}, u32[]{:S(2)}, u32[]{:S(2)}) collective-permute-start(bf16[64,4096]{1,0:T(8,128)(2,1)S(1)} %get-tuple-element.26), channel_id=1, source_target_pairs={{0,1},{1,0},{2,3},{3,2},{4,5},{5,4},{6,7},{7,6},{8,9},{9,8},{10,11... | collective-permute-start | bytes 1572872 | tf_op jit(solution)/shard_map/ppermute | solution.py:179
  114.4 10.7 %collective-permute-start.13 = (bf16[64,4096]{1,0:T(8,128)(2,1)S(1)}, bf16[64,4096]{1,0:T(8,128)(2,1)S(1)}, u32[]{:S(2)}, u32[]{:S(2)}) collective-permute-start(bf16[64,4096]{1,0:T(8,128)(2,1)S(1)} %get-tuple-element.20), channel_id=1, source_target_pairs={{0,1},{1,0},{2,3},{3,2},{4,5},{5,4},{6,7},{7,6},{8,9},{9,8},{10,11... | collective-permute-start | bytes 1572872 | tf_op jit(solution)/shard_map/ppermute | solution.py:179
  114.5 7.5 %collective-permute-start.21 = (bf16[64,2048]{1,0:T(8,128)(2,1)S(1)}, bf16[64,2048]{1,0:T(8,128)(2,1)S(1)}, u32[]{:S(2)}, u32[]{:S(2)}) collective-permute-start(bf16[64,2048]{1,0:T(8,128)(2,1)S(1)} %get-tuple-element.32), channel_id=1, source_target_pairs={{0,6},{1,7},{2,0},{3,1},{4,2},{5,3},{6,4},{7,5},{8,14},{9,15},{10,... | collective-permute-start | bytes 786440 | tf_op jit(solution)/shard_map/ppermute | solution.py:189
  116.3 8.8 %collective-permute-start.17 = (bf16[64,2048]{1,0:T(8,128)(2,1)S(1)}, bf16[64,2048]{1,0:T(8,128)(2,1)S(1)}, u32[]{:S(2)}, u32[]{:S(2)}) collective-permute-start(bf16[64,2048]{1,0:T(8,128)(2,1)S(1)} %get-tuple-element.29), channel_id=1, source_target_pairs={{0,2},{1,3},{2,4},{3,5},{4,6},{5,7},{6,0},{7,1},{8,10},{9,11},{10,... | collective-permute-start | bytes 786440 | tf_op jit(solution)/shard_map/ppermute | solution.py:189
  116.4 14.0 %collective-permute-start.20 = (bf16[64,2048]{1,0:T(8,128)(2,1)S(1)}, bf16[64,2048]{1,0:T(8,128)(2,1)S(1)}, u32[]{:S(2)}, u32[]{:S(2)}) collective-permute-start(bf16[64,2048]{1,0:T(8,128)(2,1)S(1)} %get-tuple-element.30), channel_id=1, source_target_pairs={{0,2},{1,3},{2,4},{3,5},{4,6},{5,7},{6,0},{7,1},{8,10},{9,11},{10,... | collective-permute-start | bytes 786440 | tf_op jit(solution)/shard_map/ppermute | solution.py:189
  122.3 8.1 %collective-permute-start.19 = (bf16[64,2048]{1,0:T(8,128)(2,1)S(1)}, bf16[64,2048]{1,0:T(8,128)(2,1)S(1)}, u32[]{:S(2)}, u32[]{:S(2)}) collective-permute-start(bf16[64,2048]{1,0:T(8,128)(2,1)S(1)} %get-tuple-element.33), channel_id=1, source_target_pairs={{0,6},{1,7},{2,0},{3,1},{4,2},{5,3},{6,4},{7,5},{8,14},{9,15},{10,... | collective-permute-start | bytes 786440 | tf_op jit(solution)/shard_map/ppermute | solution.py:189
  125.0 10.0 %collective-permute-start.22 = (bf16[64,2048]{1,0:T(8,128)(2,1)S(1)}, bf16[64,2048]{1,0:T(8,128)(2,1)S(1)}, u32[]{:S(2)}, u32[]{:S(2)}) collective-permute-start(bf16[64,2048]{1,0:T(8,128)(2,1)S(1)} %get-tuple-element.34), channel_id=1, source_target_pairs={{0,6},{1,7},{2,0},{3,1},{4,2},{5,3},{6,4},{7,5},{8,14},{9,15},{10,... | collective-permute-start | bytes 786440 | tf_op jit(solution)/shard_map/ppermute | solution.py:189
  (12 other events, 349.5 us)

commit v2 on v1

v2 whole, which is shorter than its diff:
```python
import functools

import jax
import jax.numpy as jnp
from jax import lax
from jax.experimental import pallas as pl
from jax.experimental.pallas import tpu as pltpu
from jax.sharding import PartitionSpec as P

HEAD = 128
ROWS = 128
HALF = 64
SLOTS = 24
LISTED = 8
BANDS = 3
BLOCKS = 128
RUNS = 4
HEADS = 8
TOKENS = RUNS * ROWS
SCALE = HEAD ** -0.5
FACTOR = SCALE * 1.4426950408889634
NEVER = 1 << 20
LOW = -1e30
Z, Y, X = 8, 4, 4
BF16, F32 = jnp.bfloat16, jnp.float32
SLOT, BASE, BAND, BAND_BASE, META = 0, 64, 128, 152, 248
TABLE = 256


def z_pairs(step):
    return [(Y * z + y, Y * ((z + step) % Z) + y) for z in range(Z) for y in range(Y)]


def y_pairs(flip):
    return [(Y * z + y, Y * z + (y ^ flip)) for z in range(Z) for y in range(Y)]


def x_pairs(step):
    return [(2 * x + k, 2 * ((x + step) % X) + k) for x in range(X) for k in range(2)]


CORE_PAIRS = [(h, h ^ 1) for h in range(HEADS)]


class Copies:
    def __init__(self, sems):
        self.sems, self.made = sems, []

    def start(self, src, dst):
        made = pltpu.make_async_copy(src, dst, self.sems.at[len(self.made)])
        made.start()
        self.made.append(made)

    def wait(self, count=None):
        for made in self.made[:count]:
            made.wait()
        self.made = [] if count is None else self.made[count:]


def key_places(table, late):
    z, y_half = table[META + 3], table[META + 4]
    n = lax.broadcasted_iota(jnp.int32, (1, HALF), 1)
    part, inner, row = n // 32, (n // 8) % 4, n % 8
    step = jnp.where(inner < 2, -1 - 2 * inner, 2 * inner - 3) if late else 2 * inner
    z_of = (z + step + Z) % Z
    return (z_of * 2 + (y_half ^ part)) * 8 + row


def load_half(copies, odd, own, far, near, cross, kv):
    for kind, parts in ((odd, (own, far)), (1 - odd, (near, cross))):
        for p, part in enumerate(parts):
            copies.start(part, kv.at[kind, :, pl.ds(32 * p, 32)])


def listed(table, kv, kind, h):
    return jnp.concatenate([kv[kind, table[SLOT + h * LISTED + e]] for e in range(LISTED)], axis=0)


def limits(table, places, h):
    return jnp.concatenate([places + table[BASE + h * LISTED + e] for e in range(LISTED)], axis=1)


def product(q, keys):
    return lax.dot_general(q, keys, (((1,), (1,)), ((), ())), preferred_element_type=F32)


def early_kernel(table, sink, q, w, a0, a2, a1, a3, kp, vp, kc, vc, acc, tops, sums, w_out, kv, band, qs, sems):
    copies = Copies(sems)
    copies.start(q, qs)
    for kind, (prev, cur) in enumerate(((kp, kc), (vp, vc))):
        copies.start(prev, band.at[kind, pl.ds(0, RUNS)])
        copies.start(cur, band.at[kind, pl.ds(RUNS, RUNS)])
    load_half(copies, table[META], a0, a2, a1, a3, kv)
    first = len(copies.made)
    copies.start(w, w_out)
    copies.wait(first)
    token = table[META + 2] + lax.broadcasted_iota(jnp.int32, (TOKENS, 1), 0)
    places = key_places(table, False)
    within = lax.broadcasted_iota(jnp.int32, (1, ROWS), 1)
    for h in range(HEADS):
        cols = slice(h * HEAD, (h + 1) * HEAD)
        qh = qs[:, cols]
        score = product(qh, listed(table, kv, 0, h))
        score = jnp.where(token >= limits(table, places, h), score, LOW)
        near = []
        for run in range(RUNS):
            rows = slice(run * ROWS, (run + 1) * ROWS)
            keys = jnp.concatenate([band[0, table[BAND + h * BANDS + j] + run] for j in range(BANDS)], axis=0)
            limit = jnp.concatenate(
                [within + table[BAND_BASE + (run * HEADS + h) * BANDS + j] for j in range(BANDS)], axis=1)
            near.append(jnp.where(token[rows] >= limit, product(qh[rows], keys), LOW))
        near = jnp.concatenate(near, axis=0)
        raw_sink = sink[h]
        top = jnp.maximum(jnp.max(score, axis=1, keepdims=True), jnp.max(near, axis=1, keepdims=True))
        top = jnp.maximum(top, raw_sink)
        weight = jnp.exp2((score - top) * FACTOR)
        near = jnp.exp2((near - top) * FACTOR)
        total = jnp.sum(weight, axis=1, keepdims=True) + jnp.sum(near, axis=1, keepdims=True)
        total = total + jnp.exp2((raw_sink - top) * FACTOR)
        mixed = jnp.dot(weight.astype(BF16), listed(table, kv, 1, h), preferred_element_type=F32)
        near = near.astype(BF16)
        for run in range(RUNS):
            rows = slice(run * ROWS, (run + 1) * ROWS)
            vals = jnp.concatenate([band[1, table[BAND + h * BANDS + j] + run] for j in range(BANDS)], axis=0)
            acc[rows, cols] = mixed[rows] + jnp.dot(near[rows], vals, preferred_element_type=F32)
        tops[:, h:h + 1] = top
        sums[:, h:h + 1] = total
    copies.wait()


def project(att, w, blocks, core, keeps, give):
    def rows(block, side):
        start = pl.multiple_of(block * ROWS + side * HALF, HALF)
        return att[pl.ds(start, HALF), :]

    lhs = jnp.concatenate([rows(b, core) for b in blocks] + [rows(b, 1 - core) for b in blocks], axis=0)
    tile = 512
    for n in range(w.shape[1] // tile):
        cols = slice(n * tile, (n + 1) * tile)
        out = jnp.dot(lhs, w[:, cols], preferred_element_type=F32).astype(BF16)
        for i, keep in enumerate(keeps):
            keep[:, cols] = out[i * HALF:(i + 1) * HALF]
        give[:, cols] = out[len(blocks) * HALF:]


def late_kernel(table, q, w, b0, b2, b1, b3, acc, tops, sums, att, keep, give, kv, qs, sems):
    copies = Copies(sems)
    copies.start(q, qs)
    load_half(copies, table[META], b0, b2, b1, b3, kv)
    copies.wait()
    token = table[META + 2] + lax.broadcasted_iota(jnp.int32, (TOKENS, 1), 0)
    places = key_places(table, True)
    for h in range(HEADS):
        cols = slice(h * HEAD, (h + 1) * HEAD)
        score = product(qs[:, cols], listed(table, kv, 0, h))
        score = jnp.where(token >= limits(table, places, h), score, LOW)
        before = tops[:, h:h + 1]
        top = jnp.maximum(jnp.max(score, axis=1, keepdims=True), before)
        weight = jnp.exp2((score - top) * FACTOR)
        fade = jnp.exp2((before - top) * FACTOR)
        total = jnp.sum(weight, axis=1, keepdims=True) + fade * sums[:, h:h + 1]
        mixed = jnp.dot(weight.astype(BF16), listed(table, kv, 1, h), preferred_element_type=F32)
        att[:, cols] = ((mixed + acc[:, cols] * fade) * (1.0 / total)).astype(BF16)
    project(att, w, [(table[META + 5] + 2) % X], table[META + 1], [keep], give)


def sides_kernel(table, att, w, keep_below, keep_above, give):
    x = table[META + 5]
    project(att, w, [(x + 1) % X, (x + 3) % X], table[META + 1], [keep_below, keep_above], give)


def own_kernel(table, att, w, after, keep, give):
    project(att, w, [table[META + 5]], table[META + 1], [keep], give)


SMEM = pl.BlockSpec(memory_space=pltpu.SMEM)
VMEM = pl.BlockSpec(memory_space=pltpu.VMEM)
ANY = pl.BlockSpec(memory_space=pl.ANY)


def call(body, ins, outs, scratch, micros, name):
    return pl.pallas_call(
        body,
        out_shape=tuple(pltpu.VMEM(shape, dtype) for shape, dtype in outs),
        in_specs=ins,
        out_specs=(VMEM,) * len(outs),
        scratch_shapes=scratch,
        compiler_params=pltpu.CompilerParams(vmem_limit_bytes=24 * 2 ** 20),
        cost_estimate=pl.CostEstimate(flops=int(micros * 1e9), bytes_accessed=2 ** 20, transcendentals=0),
        name=name,
    )


def total_of(*terms):
    return functools.reduce(lambda a, b: a + b, [t.astype(F32) for t in terms]).astype(BF16)


def tables(c, x, core, vert_blocks, slash_offsets):
    block = jnp.arange(BLOCKS, dtype=jnp.int32)
    ids = vert_blocks.reshape(-1)
    present = jnp.any(ids[:, None] == block[None, :], axis=0).astype(jnp.int32)
    rank = jnp.sum(jnp.where(block[:, None] > block[None, :], present[None, :], 0), axis=1)
    place = jnp.where(present > 0, rank, -1)
    slot = jnp.sum(jnp.where(ids[:, None] > block[None, :], present[None, :], 0), axis=1)
    slot = jnp.where(ids >= 0, slot, 0)
    base = jnp.where(ids >= 0, ids * ROWS, NEVER)
    run = jnp.arange(RUNS, dtype=jnp.int32)
    near = RUNS * c + run[:, None, None] - slash_offsets[None]
    dup = jnp.any(near[:, :, :, None] == vert_blocks[None, :, None, :], axis=3)
    near = jnp.where((near >= 0) & jnp.logical_not(dup), near * ROWS, NEVER)
    meta = jnp.stack([c % 2, core, TOKENS * c, c // Y, (c % Y) // 2, x, x * 0, x * 0]).astype(jnp.int32)
    parts = [slot, base, RUNS - slash_offsets.reshape(-1), near.reshape(-1), meta]
    return place, jnp.concatenate(parts)


def per_device(queries, keys, values, sink_logits, vert_blocks, slash_offsets, output_weight):
    c = lax.axis_index("ctx")
    h = lax.axis_index("head")
    x, core = h // 2, h % 2
    keys = keys.reshape(RUNS, ROWS, HEAD)
    values = values.reshape(RUNS, ROWS, HEAD)
    place, table = tables(c, x, core, vert_blocks, slash_offsets)

    def slices(a):
        return jnp.transpose(a.reshape(RUNS, 16, 8, HEAD), (1, 0, 2, 3))

    spread = jnp.stack([slices(keys), slices(values)], axis=1).reshape(Z * Y, RUNS * 8, HEAD)
    got = lax.all_to_all(spread, "ctx", 0, 0, tiled=True).reshape(BLOCKS * 8, HEAD)
    r = jnp.arange(SLOTS * 8, dtype=jnp.int32)[:, None]
    col = jnp.arange(BLOCKS * 8, dtype=jnp.int32)[None, :]
    pick = (jnp.repeat(place, 8)[None, :] == r // 8) & (col % 8 == r % 8)
    mine = jnp.dot(pick.astype(BF16), got, preferred_element_type=F32)
    mine = mine.astype(BF16).reshape(SLOTS, 8, HEAD)

    def from_z(a, offset):
        return lax.ppermute(a, "ctx", z_pairs(-offset))

    z2, z4, z6 = from_z(mine, 2), from_z(mine, 4), from_z(mine, 6)
    keys_late, values_late, z4 = lax.optimization_barrier((keys, values, z4))
    step = [(s, s + 1) for s in range(Z * Y - 1)]
    k_prev = lax.ppermute(keys_late, "ctx", step)
    v_prev = lax.ppermute(values_late, "ctx", step)
    a0 = jnp.concatenate([mine, z2, z4, z6], axis=1)
    low = from_z(jnp.concatenate([mine, z6], axis=1), -1)
    high = from_z(jnp.concatenate([mine, z2], axis=1), 1)
    b0 = jnp.concatenate([low, high], axis=1)
    a1, a2, a3 = [lax.ppermute(a0, "ctx", y_pairs(f)) for f in (1, 2, 3)]
    b1, b2, b3 = [lax.ppermute(b0, "ctx", y_pairs(f)) for f in (1, 2, 3)]

    width = output_weight.shape[1]
    kv = pltpu.VMEM((2, SLOTS, HALF, HEAD), BF16)
    held = pltpu.VMEM((TOKENS, HEADS * HEAD), BF16)
    part = ((HALF, width), BF16)
    far_queries = pltpu.with_memory_space_constraint(queries, pltpu.HBM)
    far_weight = pltpu.with_memory_space_constraint(output_weight, pltpu.HBM)
    acc, tops, sums, w = call(
        early_kernel, [SMEM, SMEM] + [ANY] * 10,
        [((TOKENS, HEADS * HEAD), F32), ((TOKENS, HEADS), F32), ((TOKENS, HEADS), F32), (output_weight.shape, BF16)],
        [kv, pltpu.VMEM((2, 2 * RUNS, ROWS, HEAD), BF16), held, pltpu.SemaphoreType.DMA((10,))], 8, "early",
    )(table, sink_logits * (1.0 / SCALE), far_queries, far_weight, a0, a2, a1, a3, k_prev, v_prev,
      *[pltpu.with_memory_space_constraint(a, pltpu.HBM) for a in (keys, values)])
    att, keep_far, give_far = call(
        late_kernel, [SMEM, ANY, VMEM] + [ANY] * 4 + [VMEM] * 3,
        [((TOKENS, HEADS * HEAD), BF16), part, part],
        [kv, held, pltpu.SemaphoreType.DMA((5,))], 1, "late",
    )(table, far_queries, w, b0, b2, b1, b3, acc, tops, sums)
    keep_below, keep_above, give_sides = call(
        sides_kernel, [SMEM, VMEM, VMEM], [part, part, ((2 * HALF, width), BF16)], [], 1, "sides",
    )(table, att, w)
    keep_own, give_own = call(
        own_kernel, [SMEM, VMEM, VMEM, ANY], [part, part], [], 1, "own",
    )(table, att, w, keep_below)

    def swap(a):
        return lax.ppermute(a, "head", CORE_PAIRS)

    def to_x(a, step):
        return lax.ppermute(a, "head", x_pairs(step))

    far, sides, own = swap(give_far), swap(give_sides), swap(give_own)
    below, above = sides[:HALF], sides[HALF:]
    mid = width // 2
    relay_left = to_x(total_of(keep_far[:, :mid], far[:, :mid]), 1)
    relay_right = to_x(total_of(keep_far[:, mid:], far[:, mid:]), -1)
    right_below = to_x(total_of(keep_below[:, mid:], below[:, mid:]), 1)
    left_above = to_x(total_of(keep_above[:, :mid], above[:, :mid]), -1)
    keep_below, keep_above, sides, relay_left, relay_right = lax.optimization_barrier(
        (keep_below, keep_above, sides, relay_left, relay_right))
    below, above = sides[:HALF], sides[HALF:]
    left_below = to_x(total_of(keep_below[:, :mid], below[:, :mid], relay_left), 1)
    right_above = to_x(total_of(keep_above[:, mid:], above[:, mid:], relay_right), -1)
    out_left = total_of(keep_own[:, :mid], own[:, :mid], left_below, left_above)
    out_right = total_of(keep_own[:, mid:], own[:, mid:], right_below, right_above)
    return jnp.concatenate([out_left, out_right], axis=1)


def solution(mesh):
    return jax.shard_map(
        per_device,
        mesh=mesh,
        in_specs=(
            P("ctx", "head"),
            P("ctx", "head"),
            P("ctx", "head"),
            P("head"),
            P("head", None),
            P("head", None),
            P("head", None),
        ),
        out_specs=P(("ctx", "head"), None),
        check_vma=False,
    )
```

time: 138 us -> 112 us (0.81)
  the two profiles are of different devices: /device:TPU:1 before, /device:TPU:70 now
where the time goes in v2:
time: 112 us; the launch traced here: 111 us
  starting transfers between devices  46.1 us (41%)
  waiting for transfers between devices  31.2 us (28%)
  Pallas kernels  24 us (21%)
  other arithmetic  7.02 us (6%)
  local copies, waits for them, and re-layouts  2.2 us (2%)
    ppermute x6, waiting for transfers between devices, to_x(): return lax.ppermute(a, 'head', x_pairs(step))  14.4 us
    all_to_all x1, starting transfers between devices, per_device(): lax.all_to_all(spread, 'ctx', 0, 0, tiled=True).reshape(BLOCKS * 8, HEAD)  10.9 us
    pallas_call x1, Pallas kernels, per_device(): call(late_kernel, [SMEM, ANY, VMEM] + [ANY] * 4 + [VMEM] * 3, [((TOKENS,...  10.6 us
    ppermute x6, starting transfers between devices, to_x(): return lax.ppermute(a, 'head', x_pairs(step))  9.74 us
    pallas_call x1, Pallas kernels, per_device(): call(early_kernel, [SMEM, SMEM] + [ANY] * 10, [((TOKENS, HEADS * HEAD), F...  8.67 us
    ppermute x3, starting transfers between devices, per_device(): b1, b2, b3 = [lax.ppermute(b0, 'ctx', y_pairs(f)) for f in (1, 2, 3)]  8 us
    ppermute x5, starting transfers between devices, from_z(): return lax.ppermute(a, 'ctx', z_pairs(-offset))  7.44 us
    all_to_all x1, waiting for transfers between devices, per_device(): lax.all_to_all(spread, 'ctx', 0, 0, tiled=True).reshape(BLOCKS * 8, HEAD)  6.72 us
  transfers between devices with their start and end apart: 23, of which 9 were waited for; matrix products, arithmetic and copies ran while one was open for 6% of the time, Pallas kernels for 12%

profile of v2, /device:TPU:70, one launch (start us, length us, event | category | flops | bytes accessed | tf_op | source)
XLA Modules:
  0.0 111.2 jit_solution(16442234987924886329)
XLA Ops:
  1.8 10.9 %all-to-all-start = ((bf16[32,32,128]{2,1,0:T(8,128)(2,1)}), bf16[32,32,128]{2,1,0:T(8,128)(2,1)S(1)}, u32[]{:S(2)}, u32[]{:S(2)}) async-start(bf16[32,32,128]{2,1,0:T(8,128)(2,1)} %bitcast.12), calls=%async_computation | async-start | bytes 524288 | tf_op jit(solution)/shard_map/all_to_all | solution.py:228
  17.3 6.7 %all-to-all-done = bf16[32,32,128]{2,1,0:T(8,128)(2,1)S(1)} async-done(((bf16[32,32,128]{2,1,0:T(8,128)(2,1)}), bf16[32,32,128]{2,1,0:T(8,128)(2,1)S(1)}, u32[]{:S(2)}, u32[]{:S(2)}) %all-to-all-start) | async-done | bytes 262176 | tf_op jit(solution)/shard_map/all_to_all | solution.py:228
  25.2 4.3 %collective-permute-start.1 = (bf16[24,8,128]{2,1,0:T(8,128)(2,1)S(1)}, bf16[24,8,128]{2,1,0:T(8,128)(2,1)S(1)}, u32[]{:S(2)}, u32[]{:S(2)}) collective-permute-start(bf16[24,8,128]{2,1,0:T(8,128)(2,1)S(1)} %fusion), channel_id=1, source_target_pairs={{0,128},{8,136},{16,144},{24,152},{32,160},{40,168},{48,176},{56,1... | collective-permute-start | bytes 147464 | tf_op jit(solution)/shard_map/ppermute | solution.py:236
  30.8 2.4 %collective-permute-done.1 = bf16[24,8,128]{2,1,0:T(8,128)(2,1)S(1)} collective-permute-done((bf16[24,8,128]{2,1,0:T(8,128)(2,1)S(1)}, bf16[24,8,128]{2,1,0:T(8,128)(2,1)S(1)}, u32[]{:S(2)}, u32[]{:S(2)}) %collective-permute-start.1) | collective-permute-done | bytes 49184 | tf_op jit(solution)/shard_map/ppermute | solution.py:236
  33.3 2.5 %collective-permute-done = bf16[24,8,128]{2,1,0:T(8,128)(2,1)S(1)} collective-permute-done((bf16[24,8,128]{2,1,0:T(8,128)(2,1)S(1)}, bf16[24,8,128]{2,1,0:T(8,128)(2,1)S(1)}, u32[]{:S(2)}, u32[]{:S(2)}) %collective-permute-start) | collective-permute-done | bytes 49184 | tf_op jit(solution)/shard_map/ppermute | solution.py:236
  35.9 2.1 %collective-permute-start.8 = (bf16[24,16,128]{2,1,0:T(8,128)(2,1)S(1)}, bf16[24,16,128]{2,1,0:T(8,128)(2,1)S(1)}, u32[]{:S(2)}, u32[]{:S(2)}) collective-permute-start(bf16[24,16,128]{2,1,0:T(8,128)(2,1)S(1)} %get-tuple-element.54), channel_id=1, source_target_pairs={{0,32},{8,40},{16,48},{24,56},{32,64},{40,72},{48,80},{56,88},{64,... | collective-permute-start | bytes 294920 | tf_op jit(solution)/shard_map/ppermute | solution.py:236
  38.1 1.7 %collective-permute-start.5 = (bf16[24,32,128]{2,1,0:T(8,128)(2,1)S(1)}, bf16[24,32,128]{2,1,0:T(8,128)(2,1)S(1)}, u32[]{:S(2)}, u32[]{:S(2)}) collective-permute-start(bf16[24,32,128]{2,1,0:T(8,128)(2,1)S(1)} %pad_maximum_fusion.2.a0), channel_id=1, source_target_pairs={{0,24},{8,16},{16,8},{24,0},{32,56},{40,48},{48,40},{56,32},{64,88... | collective-permute-start | bytes 589832 | tf_op jit(solution)/shard_map/ppermute | solution.py:247
  40.0 2.8 %collective-permute-start.3 = (bf16[24,32,128]{2,1,0:T(8,128)(2,1)S(1)}, bf16[24,32,128]{2,1,0:T(8,128)(2,1)S(1)}, u32[]{:S(2)}, u32[]{:S(2)}) collective-permute-start(bf16[24,32,128]{2,1,0:T(8,128)(2,1)S(1)} %pad_maximum_fusion.2.a0), channel_id=1, source_target_pairs={{0,16},{8,24},{16,0},{24,8},{32,48},{40,56},{48,32},{56,40},{64,80... | collective-permute-start | bytes 589832 | tf_op jit(solution)/shard_map/ppermute | solution.py:247
  42.9 1.9 %collective-permute-start.6 = (bf16[4,128,128]{2,1,0:T(8,128)(2,1)}, bf16[4,128,128]{2,1,0:T(8,128)(2,1)S(1)}, u32[]{:S(2)}, u32[]{:S(2)}) collective-permute-start(bf16[4,128,128]{2,1,0:T(8,128)(2,1)} %bitcast.28), channel_id=1, source_target_pairs={{0,8},{8,16},{16,24},{24,32},{32,40},{40,48},{48,56},{56,64},{64,7... | collective-permute-start | bytes 393224 | tf_op jit(solution)/shard_map/ppermute | solution.py:241
  44.8 2.6 %collective-permute-start.7 = (bf16[4,128,128]{2,1,0:T(8,128)(2,1)}, bf16[4,128,128]{2,1,0:T(8,128)(2,1)S(1)}, u32[]{:S(2)}, u32[]{:S(2)}) collective-permute-start(bf16[4,128,128]{2,1,0:T(8,128)(2,1)} %bitcast.25), channel_id=1, source_target_pairs={{0,8},{8,16},{16,24},{24,32},{32,40},{40,48},{48,56},{56,64},{64,7... | collective-permute-start | bytes 393224 | tf_op jit(solution)/shard_map/ppermute | solution.py:242
  47.4 5.0 %collective-permute-done.6.kp = bf16[4,128,128]{2,1,0:T(8,128)(2,1)S(1)} collective-permute-done((bf16[4,128,128]{2,1,0:T(8,128)(2,1)}, bf16[4,128,128]{2,1,0:T(8,128)(2,1)S(1)}, u32[]{:S(2)}, u32[]{:S(2)}) %collective-permute-start.6) | collective-permute-done | bytes 131104 | tf_op jit(solution)/shard_map/ppermute | solution.py:241
  52.4 1.5 %collective-permute-start.12 = (bf16[24,32,128]{2,1,0:T(8,128)(2,1)S(1)}, bf16[24,32,128]{2,1,0:T(8,128)(2,1)S(1)}, u32[]{:S(2)}, u32[]{:S(2)}) collective-permute-start(bf16[24,32,128]{2,1,0:T(8,128)(2,1)S(1)} %constant_dynamic-update-slice_fusion.b0), channel_id=1, source_target_pairs={{0,24},{8,16},{16,8},{24,0},{32,56},{40,48},{48,40},{56,32},{64,88... | collective-permute-start | bytes 589832 | tf_op jit(solution)/shard_map/ppermute | solution.py:248
  54.7 5.9 %collective-permute-start.10 = (bf16[24,32,128]{2,1,0:T(8,128)(2,1)S(1)}, bf16[24,32,128]{2,1,0:T(8,128)(2,1)S(1)}, u32[]{:S(2)}, u32[]{:S(2)}) collective-permute-start(bf16[24,32,128]{2,1,0:T(8,128)(2,1)S(1)} %constant_dynamic-update-slice_fusion.b0), channel_id=1, source_target_pairs={{0,16},{8,24},{16,0},{24,8},{32,48},{40,56},{48,32},{56,40},{64,80... | collective-permute-start | bytes 589832 | tf_op jit(solution)/shard_map/ppermute | solution.py:248
  60.5 8.7 %early.1 = (f32[512,1024]{1,0:T(8,128)S(1)}, f32[512,8]{1,0:T(8,128)S(1)}, f32[512,8]{1,0:T(8,128)S(1)}, bf16[1024,4096]{1,0:T(8,128)(2,1)S(1)}) custom-call(s32[256]{0:T(256)S(1)} %concatenate.18.table, f32[8]{0:T(128)S(1)} %broadcast_multiply_fusion.sink, bf16[512,1024]{1,0:T(8,128)(2,1)} %q.3, bf16[1024,4096]{1,0:T(8,128)(2,1)} %w.1, ...), custom_call_target="tpu_custom_call" | custom-call | flops 8000000000 | bytes 1048576 | tf_op jit(solution)/shard_map/early/pallas_call | solution.py:256
  69.3 10.6 %late.1 = (bf16[512,1024]{1,0:T(8,128)(2,1)S(1)}, bf16[64,4096]{1,0:T(8,128)(2,1)S(1)}, bf16[64,4096]{1,0:T(8,128)(2,1)S(1)}) custom-call(s32[256]{0:T(256)S(1)} %concatenate.18.table, bf16[512,1024]{1,0:T(8,128)(2,1)} %q.3, bf16[1024,4096]{1,0:T(8,128)(2,1)S(1)} %get-tuple-element.28.w, bf16[24,32,128]{2,1,0:T(8,128)(2,1)S(1)} %constant_dynamic-update-slice_fusion.b0, ...), custom_call_target="tpu_custom_call" | custom-call | flops 1000000000 | bytes 1048576 | tf_op jit(solution)/shard_map/late/pallas_call | solution.py:262
  79.9 2.9 %sides.1 = (bf16[64,4096]{1,0:T(8,128)(2,1)S(1)}, bf16[64,4096]{1,0:T(8,128)(2,1)S(1)}, bf16[128,4096]{1,0:T(8,128)(2,1)S(1)}) custom-call(s32[256]{0:T(256)S(1)} %concatenate.18.table, bf16[512,1024]{1,0:T(8,128)(2,1)S(1)} %get-tuple-element.32.att, bf16[1024,4096]{1,0:T(8,128)(2,1)S(1)} %get-tuple-element.28.w), custom_call_target="tpu_custom_call" | custom-call | flops 1000000000 | bytes 1048576 | tf_op jit(solution)/shard_map/sides/pallas_call | solution.py:267
  84.5 2.4 %collective-permute-start.16 = (bf16[64,2048]{1,0:T(8,128)(2,1)S(1)}, bf16[64,2048]{1,0:T(8,128)(2,1)S(1)}, u32[]{:S(2)}, u32[]{:S(2)}) collective-permute-start(bf16[64,2048]{1,0:T(8,128)(2,1)S(1)} %get-tuple-element.52), channel_id=1, source_target_pairs={{0,2},{1,3},{2,4},{3,5},{4,6},{5,7},{6,0},{7,1},{8,10},{9,11},{10,... | collective-permute-start | bytes 786440 | tf_op jit(solution)/shard_map/ppermute | solution.py:278
  86.9 1.8 %own.1 = (bf16[64,4096]{1,0:T(8,128)(2,1)S(1)}, bf16[64,4096]{1,0:T(8,128)(2,1)S(1)}) custom-call(s32[256]{0:T(256)S(1)} %concatenate.18.table, bf16[512,1024]{1,0:T(8,128)(2,1)S(1)} %get-tuple-element.32.att, bf16[1024,4096]{1,0:T(8,128)(2,1)S(1)} %get-tuple-element.28.w, bf16[64,4096]{1,0:T(8,128)(2,1)S(1)} %get-tuple-element.40.after), custom_call_target="tpu_custom_call" | custom-call | flops 1000000000 | bytes 1048576 | tf_op jit(solution)/shard_map/own/pallas_call | solution.py:270
  88.8 4.3 %collective-permute-done.17 = bf16[64,2048]{1,0:T(8,128)(2,1)S(1)} collective-permute-done((bf16[64,2048]{1,0:T(8,128)(2,1)S(1)}, bf16[64,2048]{1,0:T(8,128)(2,1)S(1)}, u32[]{:S(2)}, u32[]{:S(2)}) %collective-permute-start.17) | collective-permute-done | bytes 262176 | tf_op jit(solution)/shard_map/ppermute | solution.py:278
  93.3 3.0 %collective-permute-start.18 = (bf16[64,2048]{1,0:T(8,128)(2,1)S(1)}, bf16[64,2048]{1,0:T(8,128)(2,1)S(1)}, u32[]{:S(2)}, u32[]{:S(2)}) collective-permute-start(bf16[64,2048]{1,0:T(8,128)(2,1)S(1)} %get-tuple-element.47), channel_id=1, source_target_pairs={{0,2},{1,3},{2,4},{3,5},{4,6},{5,7},{6,0},{7,1},{8,10},{9,11},{10,... | collective-permute-start | bytes 786440 | tf_op jit(solution)/shard_map/ppermute | solution.py:278
  96.6 3.3 %collective-permute-start.20 = (bf16[64,2048]{1,0:T(8,128)(2,1)S(1)}, bf16[64,2048]{1,0:T(8,128)(2,1)S(1)}, u32[]{:S(2)}, u32[]{:S(2)}) collective-permute-start(bf16[64,2048]{1,0:T(8,128)(2,1)S(1)} %get-tuple-element.50), channel_id=1, source_target_pairs={{0,2},{1,3},{2,4},{3,5},{4,6},{5,7},{6,0},{7,1},{8,10},{9,11},{10,... | collective-permute-start | bytes 786440 | tf_op jit(solution)/shard_map/ppermute | solution.py:278
  99.9 3.2 %collective-permute-done.18 = bf16[64,2048]{1,0:T(8,128)(2,1)S(1)} collective-permute-done((bf16[64,2048]{1,0:T(8,128)(2,1)S(1)}, bf16[64,2048]{1,0:T(8,128)(2,1)S(1)}, u32[]{:S(2)}, u32[]{:S(2)}) %collective-permute-start.18) | collective-permute-done | bytes 262176 | tf_op jit(solution)/shard_map/ppermute | solution.py:278
  103.1 3.7 %collective-permute-done.21 = bf16[64,2048]{1,0:T(8,128)(2,1)S(1)} collective-permute-done((bf16[64,2048]{1,0:T(8,128)(2,1)S(1)}, bf16[64,2048]{1,0:T(8,128)(2,1)S(1)}, u32[]{:S(2)}, u32[]{:S(2)}) %collective-permute-start.21) | collective-permute-done | bytes 262176 | tf_op jit(solution)/shard_map/ppermute | solution.py:278
  106.8 3.2 %collective-permute-done.19 = bf16[64,2048]{1,0:T(8,128)(2,1)S(1)} collective-permute-done((bf16[64,2048]{1,0:T(8,128)(2,1)S(1)}, bf16[64,2048]{1,0:T(8,128)(2,1)S(1)}, u32[]{:S(2)}, u32[]{:S(2)}) %collective-permute-start.19) | collective-permute-done | bytes 262176 | tf_op jit(solution)/shard_map/ppermute | solution.py:278
  (61 shorter events, 13.4 us)
Async XLA Ops:
  1.8 22.3 %all-to-all-start = ((bf16[32,32,128]{2,1,0:T(8,128)(2,1)}), bf16[32,32,128]{2,1,0:T(8,128)(2,1)S(1)}, u32[]{:S(2)}, u32[]{:S(2)}) async-start(bf16[32,32,128]{2,1,0:T(8,128)(2,1)} %bitcast.12), calls=%async_computation | async-start | bytes 524288 | tf_op jit(solution)/shard_map/all_to_all | solution.py:228
  24.4 8.8 %collective-permute-start.2 = (bf16[24,8,128]{2,1,0:T(8,128)(2,1)S(1)}, bf16[24,8,128]{2,1,0:T(8,128)(2,1)S(1)}, u32[]{:S(2)}, u32[]{:S(2)}) collective-permute-start(bf16[24,8,128]{2,1,0:T(8,128)(2,1)S(1)} %fusion), channel_id=1, source_target_pairs={{0,64},{8,72},{16,80},{24,88},{32,96},{40,104},{48,112},{56,120},{... | collective-permute-start | bytes 147464 | tf_op jit(solution)/shard_map/ppermute | solution.py:236
  25.2 8.0 %collective-permute-start.1 = (bf16[24,8,128]{2,1,0:T(8,128)(2,1)S(1)}, bf16[24,8,128]{2,1,0:T(8,128)(2,1)S(1)}, u32[]{:S(2)}, u32[]{:S(2)}) collective-permute-start(bf16[24,8,128]{2,1,0:T(8,128)(2,1)S(1)} %fusion), channel_id=1, source_target_pairs={{0,128},{8,136},{16,144},{24,152},{32,160},{40,168},{48,176},{56,1... | collective-permute-start | bytes 147464 | tf_op jit(solution)/shard_map/ppermute | solution.py:236
  29.6 6.2 %collective-permute-start = (bf16[24,8,128]{2,1,0:T(8,128)(2,1)S(1)}, bf16[24,8,128]{2,1,0:T(8,128)(2,1)S(1)}, u32[]{:S(2)}, u32[]{:S(2)}) collective-permute-start(bf16[24,8,128]{2,1,0:T(8,128)(2,1)S(1)} %fusion), channel_id=1, source_target_pairs={{0,192},{8,200},{16,208},{24,216},{32,224},{40,232},{48,240},{56,2... | collective-permute-start | bytes 147464 | tf_op jit(solution)/shard_map/ppermute | solution.py:236
  35.8 7.0 %collective-permute-start.9 = (bf16[24,16,128]{2,1,0:T(8,128)(2,1)S(1)}, bf16[24,16,128]{2,1,0:T(8,128)(2,1)S(1)}, u32[]{:S(2)}, u32[]{:S(2)}) collective-permute-start(bf16[24,16,128]{2,1,0:T(8,128)(2,1)S(1)} %get-tuple-element.53), channel_id=1, source_target_pairs={{0,224},{8,232},{16,240},{24,248},{32,0},{40,8},{48,16},{56,24},{6... | collective-permute-start | bytes 294920 | tf_op jit(solution)/shard_map/ppermute | solution.py:236
  35.9 8.8 %collective-permute-start.8 = (bf16[24,16,128]{2,1,0:T(8,128)(2,1)S(1)}, bf16[24,16,128]{2,1,0:T(8,128)(2,1)S(1)}, u32[]{:S(2)}, u32[]{:S(2)}) collective-permute-start(bf16[24,16,128]{2,1,0:T(8,128)(2,1)S(1)} %get-tuple-element.54), channel_id=1, source_target_pairs={{0,32},{8,40},{16,48},{24,56},{32,64},{40,72},{48,80},{56,88},{64,... | collective-permute-start | bytes 294920 | tf_op jit(solution)/shard_map/ppermute | solution.py:236
  38.1 16.6 %collective-permute-start.5 = (bf16[24,32,128]{2,1,0:T(8,128)(2,1)S(1)}, bf16[24,32,128]{2,1,0:T(8,128)(2,1)S(1)}, u32[]{:S(2)}, u32[]{:S(2)}) collective-permute-start(bf16[24,32,128]{2,1,0:T(8,128)(2,1)S(1)} %pad_maximum_fusion.2.a0), channel_id=1, source_target_pairs={{0,24},{8,16},{16,8},{24,0},{32,56},{40,48},{48,40},{56,32},{64,88... | collective-permute-start | bytes 589832 | tf_op jit(solution)/shard_map/ppermute | solution.py:247
  39.8 20.8 %collective-permute-start.4 = (bf16[24,32,128]{2,1,0:T(8,128)(2,1)S(1)}, bf16[24,32,128]{2,1,0:T(8,128)(2,1)S(1)}, u32[]{:S(2)}, u32[]{:S(2)}) collective-permute-start(bf16[24,32,128]{2,1,0:T(8,128)(2,1)S(1)} %pad_maximum_fusion.2.a0), channel_id=1, source_target_pairs={{0,8},{8,0},{16,24},{24,16},{32,40},{40,32},{48,56},{56,48},{64,72... | collective-permute-start | bytes 589832 | tf_op jit(solution)/shard_map/ppermute | solution.py:247
  40.0 20.5 %collective-permute-start.3 = (bf16[24,32,128]{2,1,0:T(8,128)(2,1)S(1)}, bf16[24,32,128]{2,1,0:T(8,128)(2,1)S(1)}, u32[]{:S(2)}, u32[]{:S(2)}) collective-permute-start(bf16[24,32,128]{2,1,0:T(8,128)(2,1)S(1)} %pad_maximum_fusion.2.a0), channel_id=1, source_target_pairs={{0,16},{8,24},{16,0},{24,8},{32,48},{40,56},{48,32},{56,40},{64,80... | collective-permute-start | bytes 589832 | tf_op jit(solution)/shard_map/ppermute | solution.py:247
  42.9 9.5 %collective-permute-start.6 = (bf16[4,128,128]{2,1,0:T(8,128)(2,1)}, bf16[4,128,128]{2,1,0:T(8,128)(2,1)S(1)}, u32[]{:S(2)}, u32[]{:S(2)}) collective-permute-start(bf16[4,128,128]{2,1,0:T(8,128)(2,1)} %bitcast.28), channel_id=1, source_target_pairs={{0,8},{8,16},{16,24},{24,32},{32,40},{40,48},{48,56},{56,64},{64,7... | collective-permute-start | bytes 393224 | tf_op jit(solution)/shard_map/ppermute | solution.py:241
  44.8 9.2 %collective-permute-start.7 = (bf16[4,128,128]{2,1,0:T(8,128)(2,1)}, bf16[4,128,128]{2,1,0:T(8,128)(2,1)S(1)}, u32[]{:S(2)}, u32[]{:S(2)}) collective-permute-start(bf16[4,128,128]{2,1,0:T(8,128)(2,1)} %bitcast.25), channel_id=1, source_target_pairs={{0,8},{8,16},{16,24},{24,32},{32,40},{40,48},{48,56},{56,64},{64,7... | collective-permute-start | bytes 393224 | tf_op jit(solution)/shard_map/ppermute | solution.py:242
  52.4 16.8 %collective-permute-start.12 = (bf16[24,32,128]{2,1,0:T(8,128)(2,1)S(1)}, bf16[24,32,128]{2,1,0:T(8,128)(2,1)S(1)}, u32[]{:S(2)}, u32[]{:S(2)}) collective-permute-start(bf16[24,32,128]{2,1,0:T(8,128)(2,1)S(1)} %constant_dynamic-update-slice_fusion.b0), channel_id=1, source_target_pairs={{0,24},{8,16},{16,8},{24,0},{32,56},{40,48},{48,40},{56,32},{64,88... | collective-permute-start | bytes 589832 | tf_op jit(solution)/shard_map/ppermute | solution.py:248
  54.0 15.2 %collective-permute-start.11 = (bf16[24,32,128]{2,1,0:T(8,128)(2,1)S(1)}, bf16[24,32,128]{2,1,0:T(8,128)(2,1)S(1)}, u32[]{:S(2)}, u32[]{:S(2)}) collective-permute-start(bf16[24,32,128]{2,1,0:T(8,128)(2,1)S(1)} %constant_dynamic-update-slice_fusion.b0), channel_id=1, source_target_pairs={{0,8},{8,0},{16,24},{24,16},{32,40},{40,32},{48,56},{56,48},{64,72... | collective-permute-start | bytes 589832 | tf_op jit(solution)/shard_map/ppermute | solution.py:248
  54.7 14.6 %collective-permute-start.10 = (bf16[24,32,128]{2,1,0:T(8,128)(2,1)S(1)}, bf16[24,32,128]{2,1,0:T(8,128)(2,1)S(1)}, u32[]{:S(2)}, u32[]{:S(2)}) collective-permute-start(bf16[24,32,128]{2,1,0:T(8,128)(2,1)S(1)} %constant_dynamic-update-slice_fusion.b0), channel_id=1, source_target_pairs={{0,16},{8,24},{16,0},{24,8},{32,48},{40,56},{48,32},{56,40},{64,80... | collective-permute-start | bytes 589832 | tf_op jit(solution)/shard_map/ppermute | solution.py:248
  79.8 3.6 %collective-permute-start.15 = (bf16[64,4096]{1,0:T(8,128)(2,1)S(1)}, bf16[64,4096]{1,0:T(8,128)(2,1)S(1)}, u32[]{:S(2)}, u32[]{:S(2)}) collective-permute-start(bf16[64,4096]{1,0:T(8,128)(2,1)S(1)} %get-tuple-element.39), channel_id=1, source_target_pairs={{0,1},{1,0},{2,3},{3,2},{4,5},{5,4},{6,7},{7,6},{8,9},{9,8},{10,11... | collective-permute-start | bytes 1572872 | tf_op jit(solution)/shard_map/ppermute | solution.py:275
  82.8 10.2 %collective-permute-start.14 = (bf16[128,4096]{1,0:T(8,128)(2,1)S(1)}, bf16[128,4096]{1,0:T(8,128)(2,1)S(1)}, u32[]{:S(2)}, u32[]{:S(2)}) collective-permute-start(bf16[128,4096]{1,0:T(8,128)(2,1)S(1)} %get-tuple-element.37), channel_id=1, source_target_pairs={{0,1},{1,0},{2,3},{3,2},{4,5},{5,4},{6,7},{7,6},{8,9},{9,8},{10,11... | collective-permute-start | bytes 3145736 | tf_op jit(solution)/shard_map/ppermute | solution.py:275
  83.6 9.5 %collective-permute-start.17 = (bf16[64,2048]{1,0:T(8,128)(2,1)S(1)}, bf16[64,2048]{1,0:T(8,128)(2,1)S(1)}, u32[]{:S(2)}, u32[]{:S(2)}) collective-permute-start(bf16[64,2048]{1,0:T(8,128)(2,1)S(1)} %get-tuple-element.51), channel_id=1, source_target_pairs={{0,6},{1,7},{2,0},{3,1},{4,2},{5,3},{6,4},{7,5},{8,14},{9,15},{10,... | collective-permute-start | bytes 786440 | tf_op jit(solution)/shard_map/ppermute | solution.py:278
  84.5 8.6 %collective-permute-start.16 = (bf16[64,2048]{1,0:T(8,128)(2,1)S(1)}, bf16[64,2048]{1,0:T(8,128)(2,1)S(1)}, u32[]{:S(2)}, u32[]{:S(2)}) collective-permute-start(bf16[64,2048]{1,0:T(8,128)(2,1)S(1)} %get-tuple-element.52), channel_id=1, source_target_pairs={{0,2},{1,3},{2,4},{3,5},{4,6},{5,7},{6,0},{7,1},{8,10},{9,11},{10,... | collective-permute-start | bytes 786440 | tf_op jit(solution)/shard_map/ppermute | solution.py:278
  88.7 11.2 %collective-permute-start.13 = (bf16[64,4096]{1,0:T(8,128)(2,1)S(1)}, bf16[64,4096]{1,0:T(8,128)(2,1)S(1)}, u32[]{:S(2)}, u32[]{:S(2)}) collective-permute-start(bf16[64,4096]{1,0:T(8,128)(2,1)S(1)} %get-tuple-element.35), channel_id=1, source_target_pairs={{0,1},{1,0},{2,3},{3,2},{4,5},{5,4},{6,7},{7,6},{8,9},{9,8},{10,11... | collective-permute-start | bytes 1572872 | tf_op jit(solution)/shard_map/ppermute | solution.py:275
  93.3 9.8 %collective-permute-start.18 = (bf16[64,2048]{1,0:T(8,128)(2,1)S(1)}, bf16[64,2048]{1,0:T(8,128)(2,1)S(1)}, u32[]{:S(2)}, u32[]{:S(2)}) collective-permute-start(bf16[64,2048]{1,0:T(8,128)(2,1)S(1)} %get-tuple-element.47), channel_id=1, source_target_pairs={{0,2},{1,3},{2,4},{3,5},{4,6},{5,7},{6,0},{7,1},{8,10},{9,11},{10,... | collective-permute-start | bytes 786440 | tf_op jit(solution)/shard_map/ppermute | solution.py:278
  96.4 10.5 %collective-permute-start.21 = (bf16[64,2048]{1,0:T(8,128)(2,1)S(1)}, bf16[64,2048]{1,0:T(8,128)(2,1)S(1)}, u32[]{:S(2)}, u32[]{:S(2)}) collective-permute-start(bf16[64,2048]{1,0:T(8,128)(2,1)S(1)} %get-tuple-element.48), channel_id=1, source_target_pairs={{0,6},{1,7},{2,0},{3,1},{4,2},{5,3},{6,4},{7,5},{8,14},{9,15},{10,... | collective-permute-start | bytes 786440 | tf_op jit(solution)/shard_map/ppermute | solution.py:278
  96.5 13.5 %collective-permute-start.19 = (bf16[64,2048]{1,0:T(8,128)(2,1)S(1)}, bf16[64,2048]{1,0:T(8,128)(2,1)S(1)}, u32[]{:S(2)}, u32[]{:S(2)}) collective-permute-start(bf16[64,2048]{1,0:T(8,128)(2,1)S(1)} %get-tuple-element.49), channel_id=1, source_target_pairs={{0,6},{1,7},{2,0},{3,1},{4,2},{5,3},{6,4},{7,5},{8,14},{9,15},{10,... | collective-permute-start | bytes 786440 | tf_op jit(solution)/shard_map/ppermute | solution.py:278
  96.6 13.4 %collective-permute-start.20 = (bf16[64,2048]{1,0:T(8,128)(2,1)S(1)}, bf16[64,2048]{1,0:T(8,128)(2,1)S(1)}, u32[]{:S(2)}, u32[]{:S(2)}) collective-permute-start(bf16[64,2048]{1,0:T(8,128)(2,1)S(1)} %get-tuple-element.50), channel_id=1, source_target_pairs={{0,2},{1,3},{2,4},{3,5},{4,6},{5,7},{6,0},{7,1},{8,10},{9,11},{10,... | collective-permute-start | bytes 786440 | tf_op jit(solution)/shard_map/ppermute | solution.py:278

commit v3 on v2

--- a/solution.py
+++ b/solution.py
@@ -84,15 +84,28 @@
     return lax.dot_general(q, keys, (((1,), (1,)), ((), ())), preferred_element_type=F32)
 
 
-def early_kernel(table, sink, q, w, a0, a2, a1, a3, kp, vp, kc, vc, acc, tops, sums, w_out, kv, band, qs, sems):
+def wide(column):
+    return jnp.broadcast_to(column, (column.shape[0], HEAD))
+
+
+def across(column_block, count):
+    return jnp.concatenate([column_block] * count, axis=1)
+
+
+def early_kernel(table, sink, q, w, a0, a2, a1, a3, prev, kc, vc, acc, tops, sums, w_out, kv, band, qs, sems):
     copies = Copies(sems)
     copies.start(q, qs)
-    for kind, (prev, cur) in enumerate(((kp, kc), (vp, vc))):
-        copies.start(prev, band.at[kind, pl.ds(0, RUNS)])
+    for kind, cur in enumerate((kc, vc)):
         copies.start(cur, band.at[kind, pl.ds(RUNS, RUNS)])
     load_half(copies, table[META], a0, a2, a1, a3, kv)
     first = len(copies.made)
-    copies.start(w, w_out)
+    depth = w.shape[0] // 4
+    for n in range(4):
+        copies.start(w.at[pl.ds(n * depth, depth)], w_out.at[pl.ds(n * depth, depth)])
+    for kind in range(2):
+        for b in range(RUNS):
+            rows = [prev[r, kind, b].astype(F32) for r in range(16)]
+            band[kind, b] = jnp.concatenate(rows, axis=0).astype(BF16)
     copies.wait(first)
     token = table[META + 2] + lax.broadcasted_iota(jnp.int32, (TOKENS, 1), 0)
     places = key_places(table, False)
@@ -123,8 +136,8 @@
             rows = slice(run * ROWS, (run + 1) * ROWS)
             vals = jnp.concatenate([band[1, table[BAND + h * BANDS + j] + run] for j in range(BANDS)], axis=0)
             acc[rows, cols] = mixed[rows] + jnp.dot(near[rows], vals, preferred_element_type=F32)
-        tops[:, h:h + 1] = top
-        sums[:, h:h + 1] = total
+        tops[:, cols] = wide(top)
+        sums[:, cols] = wide(total)
     copies.wait()
 
 
@@ -140,7 +153,7 @@
         out = jnp.dot(lhs, w[:, cols], preferred_element_type=F32).astype(BF16)
         for i, keep in enumerate(keeps):
             keep[:, cols] = out[i * HALF:(i + 1) * HALF]
-        give[:, cols] = out[len(blocks) * HALF:]
+        give(n * tile, tile, out[len(blocks) * HALF:])
 
 
 def late_kernel(table, q, w, b0, b2, b1, b3, acc, tops, sums, att, keep, give, kv, qs, sems):
@@ -154,23 +167,46 @@
         cols = slice(h * HEAD, (h + 1) * HEAD)
         score = product(qs[:, cols], listed(table, kv, 0, h))
         score = jnp.where(token >= limits(table, places, h), score, LOW)
-        before = tops[:, h:h + 1]
-        top = jnp.maximum(jnp.max(score, axis=1, keepdims=True), before)
-        weight = jnp.exp2((score - top) * FACTOR)
+        before = tops[:, cols]
+        top = jnp.maximum(wide(jnp.max(score, axis=1, keepdims=True)), before)
+        weight = jnp.exp2((score - across(top, LISTED * HALF // HEAD)) * FACTOR)
         fade = jnp.exp2((before - top) * FACTOR)
-        total = jnp.sum(weight, axis=1, keepdims=True) + fade * sums[:, h:h + 1]
+        total = wide(jnp.sum(weight, axis=1, keepdims=True)) + fade * sums[:, cols]
         mixed = jnp.dot(weight.astype(BF16), listed(table, kv, 1, h), preferred_element_type=F32)
         att[:, cols] = ((mixed + acc[:, cols] * fade) * (1.0 / total)).astype(BF16)
-    project(att, w, [(table[META + 5] + 2) % X], table[META + 1], [keep], give)
-
-
-def sides_kernel(table, att, w, keep_below, keep_above, give):
-    x = table[META + 5]
+    project(att, w, [(table[META + 5] + 2) % X], table[META + 1], [keep], functools.partial(store, give))
+
+
+def store(give, start, size, rows):
+    give[:, start:start + size] = rows
+
+
+def sides_kernel(table, att, w, keep_below, keep_above, direct, relayed):
+    x, mid = table[META + 5], w.shape[1] // 2
+
+    def give(start, size, rows):
+        below, above = rows[:HALF], rows[HALF:]
+        at = slice(start % mid, start % mid + size)
+        if start < mid:
+            relayed[:HALF, at], direct[HALF:, at] = below, above
+        else:
+            direct[:HALF, at], relayed[HALF:, at] = below, above
+
     project(att, w, [(x + 1) % X, (x + 3) % X], table[META + 1], [keep_below, keep_above], give)
 
 
 def own_kernel(table, att, w, after, keep, give):
-    project(att, w, [table[META + 5]], table[META + 1], [keep], give)
+    project(att, w, [table[META + 5]], table[META + 1], [keep], functools.partial(store, give))
+
+
+def final_kernel(keep, swapped, left_below, left_above, right_below, right_above, out):
+    mid = out.shape[1] // 2
+    for start, pair in ((0, (left_below, left_above)), (mid, (right_below, right_above))):
+        cols = slice(start, start + mid)
+        total = keep[:, cols].astype(F32) + swapped[:, cols].astype(F32)
+        for part in pair:
+            total = total + part[...].astype(F32)
+        out[:, cols] = total.astype(BF16)
 
 
 SMEM = pl.BlockSpec(memory_space=pltpu.SMEM)
@@ -225,6 +261,7 @@
         return jnp.transpose(a.reshape(RUNS, 16, 8, HEAD), (1, 0, 2, 3))
 
     spread = jnp.stack([slices(keys), slices(values)], axis=1).reshape(Z * Y, RUNS * 8, HEAD)
+    prev = lax.ppermute(spread, "ctx", [(s, s + 1) for s in range(Z * Y - 1)]).reshape(16, 2, RUNS, 8, HEAD)
     got = lax.all_to_all(spread, "ctx", 0, 0, tiled=True).reshape(BLOCKS * 8, HEAD)
     r = jnp.arange(SLOTS * 8, dtype=jnp.int32)[:, None]
     col = jnp.arange(BLOCKS * 8, dtype=jnp.int32)[None, :]
@@ -236,10 +273,6 @@
         return lax.ppermute(a, "ctx", z_pairs(-offset))
 
     z2, z4, z6 = from_z(mine, 2), from_z(mine, 4), from_z(mine, 6)
-    keys_late, values_late, z4 = lax.optimization_barrier((keys, values, z4))
-    step = [(s, s + 1) for s in range(Z * Y - 1)]
-    k_prev = lax.ppermute(keys_late, "ctx", step)
-    v_prev = lax.ppermute(values_late, "ctx", step)
     a0 = jnp.concatenate([mine, z2, z4, z6], axis=1)
     low = from_z(jnp.concatenate([mine, z6], axis=1), -1)
     high = from_z(jnp.concatenate([mine, z2], axis=1), 1)
@@ -254,44 +287,50 @@
     far_queries = pltpu.with_memory_space_constraint(queries, pltpu.HBM)
     far_weight = pltpu.with_memory_space_constraint(output_weight, pltpu.HBM)
     acc, tops, sums, w = call(
-        early_kernel, [SMEM, SMEM] + [ANY] * 10,
-        [((TOKENS, HEADS * HEAD), F32), ((TOKENS, HEADS), F32), ((TOKENS, HEADS), F32), (output_weight.shape, BF16)],
-        [kv, pltpu.VMEM((2, 2 * RUNS, ROWS, HEAD), BF16), held, pltpu.SemaphoreType.DMA((10,))], 8, "early",
-    )(table, sink_logits * (1.0 / SCALE), far_queries, far_weight, a0, a2, a1, a3, k_prev, v_prev,
+        early_kernel, [SMEM, SMEM] + [ANY] * 6 + [VMEM, ANY, ANY],
+        [((TOKENS, HEADS * HEAD), F32)] * 3 + [(output_weight.shape, BF16)],
+        [kv, pltpu.VMEM((2, 2 * RUNS, ROWS, HEAD), BF16), held, pltpu.SemaphoreType.DMA((11,))], 8, "early",
+    )(table, sink_logits * (1.0 / SCALE), far_queries, far_weight, a0, a2, a1, a3, prev,
       *[pltpu.with_memory_space_constraint(a, pltpu.HBM) for a in (keys, values)])
     att, keep_far, give_far = call(
         late_kernel, [SMEM, ANY, VMEM] + [ANY] * 4 + [VMEM] * 3,
         [((TOKENS, HEADS * HEAD), BF16), part, part],
         [kv, held, pltpu.SemaphoreType.DMA((5,))], 1, "late",
     )(table, far_queries, w, b0, b2, b1, b3, acc, tops, sums)
-    keep_below, keep_above, give_sides = call(
-        sides_kernel, [SMEM, VMEM, VMEM], [part, part, ((2 * HALF, width), BF16)], [], 1, "sides",
+    halves = ((2 * HALF, width // 2), BF16)
+    keep_below, keep_above, give_direct, give_relayed = call(
+        sides_kernel, [SMEM, VMEM, VMEM], [part, part, halves, halves], [], 1, "sides",
     )(table, att, w)
+    def swap(a):
+        return lax.ppermute(a, "head", CORE_PAIRS)
+
+    def to_x(a, step):
+        return lax.ppermute(a, "head", x_pairs(step))
+
+    far, direct, relayed = swap(give_far), swap(give_direct), swap(give_relayed)
+    mid = width // 2
+    far_left = total_of(keep_far[:, :mid], far[:, :mid])
+    far_right = total_of(keep_far[:, mid:], far[:, mid:])
+    relay_left, relay_right = to_x(far_left, 1), to_x(far_right, -1)
     keep_own, give_own = call(
         own_kernel, [SMEM, VMEM, VMEM, ANY], [part, part], [], 1, "own",
-    )(table, att, w, keep_below)
-
-    def swap(a):
-        return lax.ppermute(a, "head", CORE_PAIRS)
-
-    def to_x(a, step):
-        return lax.ppermute(a, "head", x_pairs(step))
-
-    far, sides, own = swap(give_far), swap(give_sides), swap(give_own)
-    below, above = sides[:HALF], sides[HALF:]
-    mid = width // 2
-    relay_left = to_x(total_of(keep_far[:, :mid], far[:, :mid]), 1)
-    relay_right = to_x(total_of(keep_far[:, mid:], far[:, mid:]), -1)
-    right_below = to_x(total_of(keep_below[:, mid:], below[:, mid:]), 1)
-    left_above = to_x(total_of(keep_above[:, :mid], above[:, :mid]), -1)
-    keep_below, keep_above, sides, relay_left, relay_right = lax.optimization_barrier(
-        (keep_below, keep_above, sides, relay_left, relay_right))
-    below, above = sides[:HALF], sides[HALF:]
-    left_below = to_x(total_of(keep_below[:, :mid], below[:, :mid], relay_left), 1)
-    right_above = to_x(total_of(keep_above[:, mid:], above[:, mid:], relay_right), -1)
-    out_left = total_of(keep_own[:, :mid], own[:, :mid], left_below, left_above)
-    out_right = total_of(keep_own[:, mid:], own[:, mid:], right_below, right_above)
-    return jnp.concatenate([out_left, out_right], axis=1)
+    )(table, att, w, far_left)
+
+    own = swap(give_own)
+    right_below = to_x(total_of(keep_below[:, mid:], direct[:HALF]), 1)
+    left_above = to_x(total_of(keep_above[:, :mid], direct[HALF:]), -1)
+    keep_below, keep_above, relayed, relay_left, relay_right = lax.optimization_barrier(
+        (keep_below, keep_above, relayed, relay_left, relay_right))
+    left_below = to_x(total_of(keep_below[:, :mid], relayed[:HALF], relay_left), 1)
+    right_above = to_x(total_of(keep_above[:, mid:], relayed[HALF:], relay_right), -1)
+    return pl.pallas_call(
+        final_kernel,
+        out_shape=jax.ShapeDtypeStruct((HALF, width), BF16),
+        in_specs=[VMEM] * 6,
+        out_specs=VMEM,
+        compiler_params=pltpu.CompilerParams(vmem_limit_bytes=8 * 2 ** 20),
+        name="final",
+    )(keep_own, own, left_below, left_above, right_below, right_above)
 
 
 def solution(mesh):

time: 112 us -> 99.6 us (0.89)
  the two profiles are of different devices: /device:TPU:70 before, /device:TPU:1 now
where the time goes in v3:
time: 99.6 us; the launch traced here: 99.2 us
  starting transfers between devices  46.8 us (47%)
  waiting for transfers between devices  22.5 us (23%)
  Pallas kernels  21.8 us (22%)
  other arithmetic  5.21 us (5%)
  local copies, waits for them, and re-layouts  2.2 us (2%)
    all_to_all x1, starting transfers between devices, per_device(): lax.all_to_all(spread, 'ctx', 0, 0, tiled=True).reshape(BLOCKS * 8, HEAD)  12 us
    ppermute x6, waiting for transfers between devices, to_x(): return lax.ppermute(a, 'head', x_pairs(step))  10.8 us
    ppermute x4, starting transfers between devices, swap(): return lax.ppermute(a, 'head', CORE_PAIRS)  9.17 us
    pallas_call x1, Pallas kernels, per_device(): call(early_kernel, [SMEM, SMEM] + [ANY] * 6 + [VMEM, ANY, ANY], [((TOKENS...  8.9 us
    ppermute x5, waiting for transfers between devices, from_z(): return lax.ppermute(a, 'ctx', z_pairs(-offset))  8.36 us
    ppermute x6, starting transfers between devices, to_x(): return lax.ppermute(a, 'head', x_pairs(step))  8.32 us
    pallas_call x1, Pallas kernels, per_device(): call(late_kernel, [SMEM, ANY, VMEM] + [ANY] * 4 + [VMEM] * 3, [((TOKENS,...  7.08 us
    ppermute x5, starting transfers between devices, from_z(): return lax.ppermute(a, 'ctx', z_pairs(-offset))  6.28 us
  transfers between devices with their start and end apart: 23, of which 7 were waited for; matrix products, arithmetic and copies ran while one was open for 6% of the time, Pallas kernels for 14%

profile of v3, /device:TPU:1, one launch (start us, length us, event | category | flops | bytes accessed | tf_op | source)
XLA Modules:
  0.0 99.2 jit_solution(2820703670931207650)
XLA Ops:
  1.8 12.0 %all-to-all-start = ((bf16[32,32,128]{2,1,0:T(8,128)(2,1)}), bf16[32,32,128]{2,1,0:T(8,128)(2,1)S(1)}, u32[]{:S(2)}, u32[]{:S(2)}) async-start(bf16[32,32,128]{2,1,0:T(8,128)(2,1)} %bitcast.12), calls=%async_computation | async-start | bytes 524288 | tf_op jit(solution)/shard_map/all_to_all | solution.py:265
  13.8 3.1 %collective-permute-start.6 = (bf16[32,32,128]{2,1,0:T(8,128)(2,1)}, bf16[32,32,128]{2,1,0:T(8,128)(2,1)S(1)}, u32[]{:S(2)}, u32[]{:S(2)}) collective-permute-start(bf16[32,32,128]{2,1,0:T(8,128)(2,1)} %bitcast.12), channel_id=1, source_target_pairs={{0,8},{8,16},{16,24},{24,32},{32,40},{40,48},{48,56},{56,64},{64,7... | collective-permute-start | bytes 786440 | tf_op jit(solution)/shard_map/ppermute | solution.py:264
  21.6 3.4 %all-to-all-done = bf16[32,32,128]{2,1,0:T(8,128)(2,1)S(1)} async-done(((bf16[32,32,128]{2,1,0:T(8,128)(2,1)}), bf16[32,32,128]{2,1,0:T(8,128)(2,1)S(1)}, u32[]{:S(2)}, u32[]{:S(2)}) %all-to-all-start) | async-done | bytes 262176 | tf_op jit(solution)/shard_map/all_to_all | solution.py:265
  25.4 1.6 %collective-permute-start.2 = (bf16[24,8,128]{2,1,0:T(8,128)(2,1)S(1)}, bf16[24,8,128]{2,1,0:T(8,128)(2,1)S(1)}, u32[]{:S(2)}, u32[]{:S(2)}) collective-permute-start(bf16[24,8,128]{2,1,0:T(8,128)(2,1)S(1)} %fusion), channel_id=1, source_target_pairs={{0,64},{8,72},{16,80},{24,88},{32,96},{40,104},{48,112},{56,120},{... | collective-permute-start | bytes 147464 | tf_op jit(solution)/shard_map/ppermute | solution.py:273
  27.0 2.0 %collective-permute-start = (bf16[24,8,128]{2,1,0:T(8,128)(2,1)S(1)}, bf16[24,8,128]{2,1,0:T(8,128)(2,1)S(1)}, u32[]{:S(2)}, u32[]{:S(2)}) collective-permute-start(bf16[24,8,128]{2,1,0:T(8,128)(2,1)S(1)} %fusion), channel_id=1, source_target_pairs={{0,192},{8,200},{16,208},{24,216},{32,224},{40,232},{48,240},{56,2... | collective-permute-start | bytes 147464 | tf_op jit(solution)/shard_map/ppermute | solution.py:273
  29.5 2.1 %collective-permute-start.1 = (bf16[24,8,128]{2,1,0:T(8,128)(2,1)S(1)}, bf16[24,8,128]{2,1,0:T(8,128)(2,1)S(1)}, u32[]{:S(2)}, u32[]{:S(2)}) collective-permute-start(bf16[24,8,128]{2,1,0:T(8,128)(2,1)S(1)} %fusion), channel_id=1, source_target_pairs={{0,128},{8,136},{16,144},{24,152},{32,160},{40,168},{48,176},{56,1... | collective-permute-start | bytes 147464 | tf_op jit(solution)/shard_map/ppermute | solution.py:273
  32.2 4.9 %collective-permute-done.1 = bf16[24,8,128]{2,1,0:T(8,128)(2,1)S(1)} collective-permute-done((bf16[24,8,128]{2,1,0:T(8,128)(2,1)S(1)}, bf16[24,8,128]{2,1,0:T(8,128)(2,1)S(1)}, u32[]{:S(2)}, u32[]{:S(2)}) %collective-permute-start.1) | collective-permute-done | bytes 49184 | tf_op jit(solution)/shard_map/ppermute | solution.py:273
  37.1 1.5 %collective-permute-start.5 = (bf16[24,32,128]{2,1,0:T(8,128)(2,1)S(1)}, bf16[24,32,128]{2,1,0:T(8,128)(2,1)S(1)}, u32[]{:S(2)}, u32[]{:S(2)}) collective-permute-start(bf16[24,32,128]{2,1,0:T(8,128)(2,1)S(1)} %pad_maximum_fusion.1.a0), channel_id=1, source_target_pairs={{0,24},{8,16},{16,8},{24,0},{32,56},{40,48},{48,40},{56,32},{64,88... | collective-permute-start | bytes 589832 | tf_op jit(solution)/shard_map/ppermute | solution.py:280
  38.6 2.5 %collective-permute-start.3 = (bf16[24,32,128]{2,1,0:T(8,128)(2,1)S(1)}, bf16[24,32,128]{2,1,0:T(8,128)(2,1)S(1)}, u32[]{:S(2)}, u32[]{:S(2)}) collective-permute-start(bf16[24,32,128]{2,1,0:T(8,128)(2,1)S(1)} %pad_maximum_fusion.1.a0), channel_id=1, source_target_pairs={{0,16},{8,24},{16,0},{24,8},{32,48},{40,56},{48,32},{56,40},{64,80... | collective-permute-start | bytes 589832 | tf_op jit(solution)/shard_map/ppermute | solution.py:280
  41.1 3.5 %collective-permute-done.8 = bf16[24,16,128]{2,1,0:T(8,128)(2,1)S(1)} collective-permute-done((bf16[24,16,128]{2,1,0:T(8,128)(2,1)S(1)}, bf16[24,16,128]{2,1,0:T(8,128)(2,1)S(1)}, u32[]{:S(2)}, u32[]{:S(2)}) %collective-permute-start.8) | collective-permute-done | bytes 98336 | tf_op jit(solution)/shard_map/ppermute | solution.py:273
  44.6 1.5 %collective-permute-start.11 = (bf16[24,32,128]{2,1,0:T(8,128)(2,1)S(1)}, bf16[24,32,128]{2,1,0:T(8,128)(2,1)S(1)}, u32[]{:S(2)}, u32[]{:S(2)}) collective-permute-start(bf16[24,32,128]{2,1,0:T(8,128)(2,1)S(1)} %constant_dynamic-update-slice_fusion.b0), channel_id=1, source_target_pairs={{0,24},{8,16},{16,8},{24,0},{32,56},{40,48},{48,40},{56,32},{64,88... | collective-permute-start | bytes 589832 | tf_op jit(solution)/shard_map/ppermute | solution.py:281
  46.1 2.5 %collective-permute-start.9 = (bf16[24,32,128]{2,1,0:T(8,128)(2,1)S(1)}, bf16[24,32,128]{2,1,0:T(8,128)(2,1)S(1)}, u32[]{:S(2)}, u32[]{:S(2)}) collective-permute-start(bf16[24,32,128]{2,1,0:T(8,128)(2,1)S(1)} %constant_dynamic-update-slice_fusion.b0), channel_id=1, source_target_pairs={{0,16},{8,24},{16,0},{24,8},{32,48},{40,56},{48,32},{56,40},{64,80... | collective-permute-start | bytes 589832 | tf_op jit(solution)/shard_map/ppermute | solution.py:281
  48.5 8.9 %early.1 = (f32[512,1024]{1,0:T(8,128)S(1)}, f32[512,1024]{1,0:T(8,128)S(1)}, f32[512,1024]{1,0:T(8,128)S(1)}, bf16[1024,4096]{1,0:T(8,128)(2,1)S(1)}) custom-call(s32[256]{0:T(256)S(1)} %concatenate.15.table, f32[8]{0:T(128)S(1)} %broadcast_multiply_fusion.sink, bf16[512,1024]{1,0:T(8,128)(2,1)} %q.3, bf16[1024,4096]{1,0:T(8,128)(2,1)} %w.1, ...), custom_call_target="tpu_custom_call" | custom-call | flops 8000000000 | bytes 1048576 | tf_op jit(solution)/shard_map/early/pallas_call | solution.py:289
  57.5 7.1 %late.1 = (bf16[512,1024]{1,0:T(8,128)(2,1)S(1)}, bf16[64,4096]{1,0:T(8,128)(2,1)S(1)}, bf16[64,4096]{1,0:T(8,128)(2,1)S(1)}) custom-call(s32[256]{0:T(256)S(1)} %concatenate.15.table, bf16[512,1024]{1,0:T(8,128)(2,1)} %q.3, bf16[1024,4096]{1,0:T(8,128)(2,1)S(1)} %get-tuple-element.23.w, bf16[24,32,128]{2,1,0:T(8,128)(2,1)S(1)} %constant_dynamic-update-slice_fusion.b0, ...), custom_call_target="tpu_custom_call" | custom-call | flops 1000000000 | bytes 1048576 | tf_op jit(solution)/shard_map/late/pallas_call | solution.py:295
  64.6 7.9 %collective-permute-start.12 = (bf16[64,4096]{1,0:T(8,128)(2,1)S(1)}, bf16[64,4096]{1,0:T(8,128)(2,1)S(1)}, u32[]{:S(2)}, u32[]{:S(2)}) collective-permute-start(bf16[64,4096]{1,0:T(8,128)(2,1)S(1)} %get-tuple-element.29), channel_id=1, source_target_pairs={{0,1},{1,0},{2,3},{3,2},{4,5},{5,4},{6,7},{7,6},{8,9},{9,8},{10,11... | collective-permute-start | bytes 1572872 | tf_op jit(solution)/shard_map/ppermute | solution.py:305
  72.5 2.9 %sides.1 = (bf16[64,4096]{1,0:T(8,128)(2,1)S(1)}, bf16[64,4096]{1,0:T(8,128)(2,1)S(1)}, bf16[128,2048]{1,0:T(8,128)(2,1)S(1)}, bf16[128,2048]{1,0:T(8,128)(2,1)S(1)}) custom-call(s32[256]{0:T(256)S(1)} %concatenate.15.table, bf16[512,1024]{1,0:T(8,128)(2,1)S(1)} %get-tuple-element.27.att, bf16[1024,4096]{1,0:T(8,128)(2,1)S(1)} %get-tuple-element.23.w), custom_call_target="tpu_custom_call" | custom-call | flops 1000000000 | bytes 1048576 | tf_op jit(solution)/shard_map/sides/pallas_call | solution.py:301
  76.1 1.3 %collective-permute-start.15 = (bf16[64,2048]{1,0:T(8,128)(2,1)S(1)}, bf16[64,2048]{1,0:T(8,128)(2,1)S(1)}, u32[]{:S(2)}, u32[]{:S(2)}) collective-permute-start(bf16[64,2048]{1,0:T(8,128)(2,1)S(1)} %get-tuple-element.42.after), channel_id=1, source_target_pairs={{0,2},{1,3},{2,4},{3,5},{4,6},{5,7},{6,0},{7,1},{8,10},{9,11},{10,... | collective-permute-start | bytes 786440 | tf_op jit(solution)/shard_map/ppermute | solution.py:308
  77.4 1.8 %own.1 = (bf16[64,4096]{1,0:T(8,128)(2,1)S(1)}, bf16[64,4096]{1,0:T(8,128)(2,1)S(1)}) custom-call(s32[256]{0:T(256)S(1)} %concatenate.15.table, bf16[512,1024]{1,0:T(8,128)(2,1)S(1)} %get-tuple-element.27.att, bf16[1024,4096]{1,0:T(8,128)(2,1)S(1)} %get-tuple-element.23.w, bf16[64,2048]{1,0:T(8,128)(2,1)S(1)} %get-tuple-element.42.after), custom_call_target="tpu_custom_call" | custom-call | flops 1000000000 | bytes 1048576 | tf_op jit(solution)/shard_map/own/pallas_call | solution.py:315
  79.3 1.5 %collective-permute-start.16 = (bf16[64,2048]{1,0:T(8,128)(2,1)S(1)}, bf16[64,2048]{1,0:T(8,128)(2,1)S(1)}, u32[]{:S(2)}, u32[]{:S(2)}) collective-permute-start(bf16[64,2048]{1,0:T(8,128)(2,1)S(1)} %get-tuple-element.41), channel_id=1, source_target_pairs={{0,6},{1,7},{2,0},{3,1},{4,2},{5,3},{6,4},{7,5},{8,14},{9,15},{10,... | collective-permute-start | bytes 786440 | tf_op jit(solution)/shard_map/ppermute | solution.py:308
  81.7 2.7 %collective-permute-start.19 = (bf16[64,2048]{1,0:T(8,128)(2,1)S(1)}, bf16[64,2048]{1,0:T(8,128)(2,1)S(1)}, u32[]{:S(2)}, u32[]{:S(2)}) collective-permute-start(bf16[64,2048]{1,0:T(8,128)(2,1)S(1)} %get-tuple-element.46), channel_id=1, source_target_pairs={{0,6},{1,7},{2,0},{3,1},{4,2},{5,3},{6,4},{7,5},{8,14},{9,15},{10,... | collective-permute-start | bytes 786440 | tf_op jit(solution)/shard_map/ppermute | solution.py:308
  84.4 2.5 %collective-permute-done.16 = bf16[64,2048]{1,0:T(8,128)(2,1)S(1)} collective-permute-done((bf16[64,2048]{1,0:T(8,128)(2,1)S(1)}, bf16[64,2048]{1,0:T(8,128)(2,1)S(1)}, u32[]{:S(2)}, u32[]{:S(2)}) %collective-permute-start.16) | collective-permute-done | bytes 262176 | tf_op jit(solution)/shard_map/ppermute | solution.py:308
  87.1 2.7 %collective-permute-start.21 = (bf16[64,2048]{1,0:T(8,128)(2,1)S(1)}, bf16[64,2048]{1,0:T(8,128)(2,1)S(1)}, u32[]{:S(2)}, u32[]{:S(2)}) collective-permute-start(bf16[64,2048]{1,0:T(8,128)(2,1)S(1)} %get-tuple-element.43), channel_id=1, source_target_pairs={{0,6},{1,7},{2,0},{3,1},{4,2},{5,3},{6,4},{7,5},{8,14},{9,15},{10,... | collective-permute-start | bytes 786440 | tf_op jit(solution)/shard_map/ppermute | solution.py:308
  91.1 1.4 %collective-permute-done.19.left_above = bf16[64,2048]{1,0:T(8,128)(2,1)S(1)} collective-permute-done((bf16[64,2048]{1,0:T(8,128)(2,1)S(1)}, bf16[64,2048]{1,0:T(8,128)(2,1)S(1)}, u32[]{:S(2)}, u32[]{:S(2)}) %collective-permute-start.19) | collective-permute-done | bytes 262176 | tf_op jit(solution)/shard_map/ppermute | solution.py:308
  92.5 5.6 %collective-permute-done.21.right_above = bf16[64,2048]{1,0:T(8,128)(2,1)S(1)} collective-permute-done((bf16[64,2048]{1,0:T(8,128)(2,1)S(1)}, bf16[64,2048]{1,0:T(8,128)(2,1)S(1)}, u32[]{:S(2)}, u32[]{:S(2)}) %collective-permute-start.21) | collective-permute-done | bytes 262176 | tf_op jit(solution)/shard_map/ppermute | solution.py:308
  (62 shorter events, 11.9 us)
Async XLA Ops:
  0.0 29.0 %copy-start = (f32[8]{0:T(128)S(1)}, f32[8]{0:T(128)}, u32[]{:S(2)}) copy-start(f32[8]{0:T(128)} %param.10) | copy-start | bytes 100
  1.8 23.2 %all-to-all-start = ((bf16[32,32,128]{2,1,0:T(8,128)(2,1)}), bf16[32,32,128]{2,1,0:T(8,128)(2,1)S(1)}, u32[]{:S(2)}, u32[]{:S(2)}) async-start(bf16[32,32,128]{2,1,0:T(8,128)(2,1)} %bitcast.12), calls=%async_computation | async-start | bytes 524288 | tf_op jit(solution)/shard_map/all_to_all | solution.py:265
  13.8 32.2 %collective-permute-start.6 = (bf16[32,32,128]{2,1,0:T(8,128)(2,1)}, bf16[32,32,128]{2,1,0:T(8,128)(2,1)S(1)}, u32[]{:S(2)}, u32[]{:S(2)}) collective-permute-start(bf16[32,32,128]{2,1,0:T(8,128)(2,1)} %bitcast.12), channel_id=1, source_target_pairs={{0,8},{8,16},{16,24},{24,32},{32,40},{40,48},{48,56},{56,64},{64,7... | collective-permute-start | bytes 786440 | tf_op jit(solution)/shard_map/ppermute | solution.py:264
  25.4 6.3 %collective-permute-start.2 = (bf16[24,8,128]{2,1,0:T(8,128)(2,1)S(1)}, bf16[24,8,128]{2,1,0:T(8,128)(2,1)S(1)}, u32[]{:S(2)}, u32[]{:S(2)}) collective-permute-start(bf16[24,8,128]{2,1,0:T(8,128)(2,1)S(1)} %fusion), channel_id=1, source_target_pairs={{0,64},{8,72},{16,80},{24,88},{32,96},{40,104},{48,112},{56,120},{... | collective-permute-start | bytes 147464 | tf_op jit(solution)/shard_map/ppermute | solution.py:273
  27.0 4.7 %collective-permute-start = (bf16[24,8,128]{2,1,0:T(8,128)(2,1)S(1)}, bf16[24,8,128]{2,1,0:T(8,128)(2,1)S(1)}, u32[]{:S(2)}, u32[]{:S(2)}) collective-permute-start(bf16[24,8,128]{2,1,0:T(8,128)(2,1)S(1)} %fusion), channel_id=1, source_target_pairs={{0,192},{8,200},{16,208},{24,216},{32,224},{40,232},{48,240},{56,2... | collective-permute-start | bytes 147464 | tf_op jit(solution)/shard_map/ppermute | solution.py:273
  29.5 7.6 %collective-permute-start.1 = (bf16[24,8,128]{2,1,0:T(8,128)(2,1)S(1)}, bf16[24,8,128]{2,1,0:T(8,128)(2,1)S(1)}, u32[]{:S(2)}, u32[]{:S(2)}) collective-permute-start(bf16[24,8,128]{2,1,0:T(8,128)(2,1)S(1)} %fusion), channel_id=1, source_target_pairs={{0,128},{8,136},{16,144},{24,152},{32,160},{40,168},{48,176},{56,1... | collective-permute-start | bytes 147464 | tf_op jit(solution)/shard_map/ppermute | solution.py:273
  31.7 9.4 %collective-permute-start.7 = (bf16[24,16,128]{2,1,0:T(8,128)(2,1)S(1)}, bf16[24,16,128]{2,1,0:T(8,128)(2,1)S(1)}, u32[]{:S(2)}, u32[]{:S(2)}) collective-permute-start(bf16[24,16,128]{2,1,0:T(8,128)(2,1)S(1)} %get-tuple-element.48), channel_id=1, source_target_pairs={{0,32},{8,40},{16,48},{24,56},{32,64},{40,72},{48,80},{56,88},{64,... | collective-permute-start | bytes 294920 | tf_op jit(solution)/shard_map/ppermute | solution.py:273
  37.1 8.9 %collective-permute-start.5 = (bf16[24,32,128]{2,1,0:T(8,128)(2,1)S(1)}, bf16[24,32,128]{2,1,0:T(8,128)(2,1)S(1)}, u32[]{:S(2)}, u32[]{:S(2)}) collective-permute-start(bf16[24,32,128]{2,1,0:T(8,128)(2,1)S(1)} %pad_maximum_fusion.1.a0), channel_id=1, source_target_pairs={{0,24},{8,16},{16,8},{24,0},{32,56},{40,48},{48,40},{56,32},{64,88... | collective-permute-start | bytes 589832 | tf_op jit(solution)/shard_map/ppermute | solution.py:280
  38.6 9.9 %collective-permute-start.4 = (bf16[24,32,128]{2,1,0:T(8,128)(2,1)S(1)}, bf16[24,32,128]{2,1,0:T(8,128)(2,1)S(1)}, u32[]{:S(2)}, u32[]{:S(2)}) collective-permute-start(bf16[24,32,128]{2,1,0:T(8,128)(2,1)S(1)} %pad_maximum_fusion.1.a0), channel_id=1, source_target_pairs={{0,8},{8,0},{16,24},{24,16},{32,40},{40,32},{48,56},{56,48},{64,72... | collective-permute-start | bytes 589832 | tf_op jit(solution)/shard_map/ppermute | solution.py:280
  38.6 9.9 %collective-permute-start.3 = (bf16[24,32,128]{2,1,0:T(8,128)(2,1)S(1)}, bf16[24,32,128]{2,1,0:T(8,128)(2,1)S(1)}, u32[]{:S(2)}, u32[]{:S(2)}) collective-permute-start(bf16[24,32,128]{2,1,0:T(8,128)(2,1)S(1)} %pad_maximum_fusion.1.a0), channel_id=1, source_target_pairs={{0,16},{8,24},{16,0},{24,8},{32,48},{40,56},{48,32},{56,40},{64,80... | collective-permute-start | bytes 589832 | tf_op jit(solution)/shard_map/ppermute | solution.py:280
  41.1 3.5 %collective-permute-start.8 = (bf16[24,16,128]{2,1,0:T(8,128)(2,1)S(1)}, bf16[24,16,128]{2,1,0:T(8,128)(2,1)S(1)}, u32[]{:S(2)}, u32[]{:S(2)}) collective-permute-start(bf16[24,16,128]{2,1,0:T(8,128)(2,1)S(1)} %get-tuple-element.47), channel_id=1, source_target_pairs={{0,224},{8,232},{16,240},{24,248},{32,0},{40,8},{48,16},{56,24},{6... | collective-permute-start | bytes 294920 | tf_op jit(solution)/shard_map/ppermute | solution.py:273
  44.6 12.9 %collective-permute-start.11 = (bf16[24,32,128]{2,1,0:T(8,128)(2,1)S(1)}, bf16[24,32,128]{2,1,0:T(8,128)(2,1)S(1)}, u32[]{:S(2)}, u32[]{:S(2)}) collective-permute-start(bf16[24,32,128]{2,1,0:T(8,128)(2,1)S(1)} %constant_dynamic-update-slice_fusion.b0), channel_id=1, source_target_pairs={{0,24},{8,16},{16,8},{24,0},{32,56},{40,48},{48,40},{56,32},{64,88... | collective-permute-start | bytes 589832 | tf_op jit(solution)/shard_map/ppermute | solution.py:281
  46.0 11.4 %collective-permute-start.10 = (bf16[24,32,128]{2,1,0:T(8,128)(2,1)S(1)}, bf16[24,32,128]{2,1,0:T(8,128)(2,1)S(1)}, u32[]{:S(2)}, u32[]{:S(2)}) collective-permute-start(bf16[24,32,128]{2,1,0:T(8,128)(2,1)S(1)} %constant_dynamic-update-slice_fusion.b0), channel_id=1, source_target_pairs={{0,8},{8,0},{16,24},{24,16},{32,40},{40,32},{48,56},{56,48},{64,72... | collective-permute-start | bytes 589832 | tf_op jit(solution)/shard_map/ppermute | solution.py:281
  46.1 11.4 %collective-permute-start.9 = (bf16[24,32,128]{2,1,0:T(8,128)(2,1)S(1)}, bf16[24,32,128]{2,1,0:T(8,128)(2,1)S(1)}, u32[]{:S(2)}, u32[]{:S(2)}) collective-permute-start(bf16[24,32,128]{2,1,0:T(8,128)(2,1)S(1)} %constant_dynamic-update-slice_fusion.b0), channel_id=1, source_target_pairs={{0,16},{8,24},{16,0},{24,8},{32,48},{40,56},{48,32},{56,40},{64,80... | collective-permute-start | bytes 589832 | tf_op jit(solution)/shard_map/ppermute | solution.py:281
  64.6 11.5 %collective-permute-start.12 = (bf16[64,4096]{1,0:T(8,128)(2,1)S(1)}, bf16[64,4096]{1,0:T(8,128)(2,1)S(1)}, u32[]{:S(2)}, u32[]{:S(2)}) collective-permute-start(bf16[64,4096]{1,0:T(8,128)(2,1)S(1)} %get-tuple-element.29), channel_id=1, source_target_pairs={{0,1},{1,0},{2,3},{3,2},{4,5},{5,4},{6,7},{7,6},{8,9},{9,8},{10,11... | collective-permute-start | bytes 1572872 | tf_op jit(solution)/shard_map/ppermute | solution.py:305
  75.4 6.3 %collective-permute-start.14 = (bf16[128,2048]{1,0:T(8,128)(2,1)S(1)}, bf16[128,2048]{1,0:T(8,128)(2,1)S(1)}, u32[]{:S(2)}, u32[]{:S(2)}) collective-permute-start(bf16[128,2048]{1,0:T(8,128)(2,1)S(1)} %get-tuple-element.34), channel_id=1, source_target_pairs={{0,1},{1,0},{2,3},{3,2},{4,5},{5,4},{6,7},{7,6},{8,9},{9,8},{10,11... | collective-permute-start | bytes 1572872 | tf_op jit(solution)/shard_map/ppermute | solution.py:305
  75.5 6.0 %collective-permute-start.18 = (bf16[128,2048]{1,0:T(8,128)(2,1)S(1)}, bf16[128,2048]{1,0:T(8,128)(2,1)S(1)}, u32[]{:S(2)}, u32[]{:S(2)}) collective-permute-start(bf16[128,2048]{1,0:T(8,128)(2,1)S(1)} %get-tuple-element.38), channel_id=1, source_target_pairs={{0,1},{1,0},{2,3},{3,2},{4,5},{5,4},{6,7},{7,6},{8,9},{9,8},{10,11... | collective-permute-start | bytes 1572872 | tf_op jit(solution)/shard_map/ppermute | solution.py:305
  76.1 10.8 %collective-permute-start.15 = (bf16[64,2048]{1,0:T(8,128)(2,1)S(1)}, bf16[64,2048]{1,0:T(8,128)(2,1)S(1)}, u32[]{:S(2)}, u32[]{:S(2)}) collective-permute-start(bf16[64,2048]{1,0:T(8,128)(2,1)S(1)} %get-tuple-element.42.after), channel_id=1, source_target_pairs={{0,2},{1,3},{2,4},{3,5},{4,6},{5,7},{6,0},{7,1},{8,10},{9,11},{10,... | collective-permute-start | bytes 786440 | tf_op jit(solution)/shard_map/ppermute | solution.py:308
  79.3 7.6 %collective-permute-start.16 = (bf16[64,2048]{1,0:T(8,128)(2,1)S(1)}, bf16[64,2048]{1,0:T(8,128)(2,1)S(1)}, u32[]{:S(2)}, u32[]{:S(2)}) collective-permute-start(bf16[64,2048]{1,0:T(8,128)(2,1)S(1)} %get-tuple-element.41), channel_id=1, source_target_pairs={{0,6},{1,7},{2,0},{3,1},{4,2},{5,3},{6,4},{7,5},{8,14},{9,15},{10,... | collective-permute-start | bytes 786440 | tf_op jit(solution)/shard_map/ppermute | solution.py:308
  80.8 17.3 %collective-permute-start.13 = (bf16[64,4096]{1,0:T(8,128)(2,1)S(1)}, bf16[64,4096]{1,0:T(8,128)(2,1)S(1)}, u32[]{:S(2)}, u32[]{:S(2)}) collective-permute-start(bf16[64,4096]{1,0:T(8,128)(2,1)S(1)} %get-tuple-element.31), channel_id=1, source_target_pairs={{0,1},{1,0},{2,3},{3,2},{4,5},{5,4},{6,7},{7,6},{8,9},{9,8},{10,11... | collective-permute-start | bytes 1572872 | tf_op jit(solution)/shard_map/ppermute | solution.py:305
  81.6 9.5 %collective-permute-start.20 = (bf16[64,2048]{1,0:T(8,128)(2,1)S(1)}, bf16[64,2048]{1,0:T(8,128)(2,1)S(1)}, u32[]{:S(2)}, u32[]{:S(2)}) collective-permute-start(bf16[64,2048]{1,0:T(8,128)(2,1)S(1)} %get-tuple-element.45), channel_id=1, source_target_pairs={{0,2},{1,3},{2,4},{3,5},{4,6},{5,7},{6,0},{7,1},{8,10},{9,11},{10,... | collective-permute-start | bytes 786440 | tf_op jit(solution)/shard_map/ppermute | solution.py:308
  81.7 10.8 %collective-permute-start.19 = (bf16[64,2048]{1,0:T(8,128)(2,1)S(1)}, bf16[64,2048]{1,0:T(8,128)(2,1)S(1)}, u32[]{:S(2)}, u32[]{:S(2)}) collective-permute-start(bf16[64,2048]{1,0:T(8,128)(2,1)S(1)} %get-tuple-element.46), channel_id=1, source_target_pairs={{0,6},{1,7},{2,0},{3,1},{4,2},{5,3},{6,4},{7,5},{8,14},{9,15},{10,... | collective-permute-start | bytes 786440 | tf_op jit(solution)/shard_map/ppermute | solution.py:308
  87.1 11.0 %collective-permute-start.21 = (bf16[64,2048]{1,0:T(8,128)(2,1)S(1)}, bf16[64,2048]{1,0:T(8,128)(2,1)S(1)}, u32[]{:S(2)}, u32[]{:S(2)}) collective-permute-start(bf16[64,2048]{1,0:T(8,128)(2,1)S(1)} %get-tuple-element.43), channel_id=1, source_target_pairs={{0,6},{1,7},{2,0},{3,1},{4,2},{5,3},{6,4},{7,5},{8,14},{9,15},{10,... | collective-permute-start | bytes 786440 | tf_op jit(solution)/shard_map/ppermute | solution.py:308
  89.9 8.2 %collective-permute-start.17 = (bf16[64,2048]{1,0:T(8,128)(2,1)S(1)}, bf16[64,2048]{1,0:T(8,128)(2,1)S(1)}, u32[]{:S(2)}, u32[]{:S(2)}) collective-permute-start(bf16[64,2048]{1,0:T(8,128)(2,1)S(1)} %get-tuple-element.44), channel_id=1, source_target_pairs={{0,2},{1,3},{2,4},{3,5},{4,6},{5,7},{6,0},{7,1},{8,10},{9,11},{10,... | collective-permute-start | bytes 786440 | tf_op jit(solution)/shard_map/ppermute | solution.py:308

commit v4 on v3

--- a/solution.py
+++ b/solution.py
@@ -23,8 +23,7 @@
 LOW = -1e30
 Z, Y, X = 8, 4, 4
 BF16, F32 = jnp.bfloat16, jnp.float32
-SLOT, BASE, BAND, BAND_BASE, META = 0, 64, 128, 152, 248
-TABLE = 256
+META = BLOCKS
 
 
 def z_pairs(step):
@@ -72,12 +71,25 @@
             copies.start(part, kv.at[kind, :, pl.ds(32 * p, 32)])
 
 
-def listed(table, kv, kind, h):
-    return jnp.concatenate([kv[kind, table[SLOT + h * LISTED + e]] for e in range(LISTED)], axis=0)
-
-
-def limits(table, places, h):
-    return jnp.concatenate([places + table[BASE + h * LISTED + e] for e in range(LISTED)], axis=1)
+def slots_of(table, vert, h):
+    return [table[jnp.maximum(vert[h, e], 0)] for e in range(LISTED)]
+
+
+def listed(kv, kind, slots):
+    return jnp.concatenate([kv[kind, slot] for slot in slots], axis=0)
+
+
+def limits(vert, places, h):
+    ids = [vert[h, e] for e in range(LISTED)]
+    return jnp.concatenate([places + jnp.where(i >= 0, i * ROWS, NEVER) for i in ids], axis=1)
+
+
+def near_base(table, vert, slash, h, run, j):
+    block = table[META + 2] + run - slash[h, j]
+    use = block >= 0
+    for e in range(LISTED):
+        use = jnp.logical_and(use, vert[h, e] != block)
+    return jnp.where(use, block * ROWS, NEVER)
 
 
 def product(q, keys):
@@ -92,7 +104,7 @@
     return jnp.concatenate([column_block] * count, axis=1)
 
 
-def early_kernel(table, sink, q, w, a0, a2, a1, a3, prev, kc, vc, acc, tops, sums, w_out, kv, band, qs, sems):
+def early_kernel(table, vert, slash, sink, q, w, a0, a2, a1, a3, prev, kc, vc, acc, tops, sums, w_out, qs, kv, band, sems):
     copies = Copies(sems)
     copies.start(q, qs)
     for kind, cur in enumerate((kc, vc)):
@@ -107,34 +119,35 @@
             rows = [prev[r, kind, b].astype(F32) for r in range(16)]
             band[kind, b] = jnp.concatenate(rows, axis=0).astype(BF16)
     copies.wait(first)
-    token = table[META + 2] + lax.broadcasted_iota(jnp.int32, (TOKENS, 1), 0)
+    token = TOKENS // RUNS * table[META + 2] + lax.broadcasted_iota(jnp.int32, (TOKENS, 1), 0)
     places = key_places(table, False)
     within = lax.broadcasted_iota(jnp.int32, (1, ROWS), 1)
     for h in range(HEADS):
         cols = slice(h * HEAD, (h + 1) * HEAD)
         qh = qs[:, cols]
-        score = product(qh, listed(table, kv, 0, h))
-        score = jnp.where(token >= limits(table, places, h), score, LOW)
+        slots = slots_of(table, vert, h)
+        score = product(qh, listed(kv, 0, slots))
+        score = jnp.where(token >= limits(vert, places, h), score, LOW)
         near = []
         for run in range(RUNS):
             rows = slice(run * ROWS, (run + 1) * ROWS)
-            keys = jnp.concatenate([band[0, table[BAND + h * BANDS + j] + run] for j in range(BANDS)], axis=0)
+            keys = jnp.concatenate([band[0, RUNS + run - slash[h, j]] for j in range(BANDS)], axis=0)
             limit = jnp.concatenate(
-                [within + table[BAND_BASE + (run * HEADS + h) * BANDS + j] for j in range(BANDS)], axis=1)
+                [within + near_base(table, vert, slash, h, run, j) for j in range(BANDS)], axis=1)
             near.append(jnp.where(token[rows] >= limit, product(qh[rows], keys), LOW))
         near = jnp.concatenate(near, axis=0)
-        raw_sink = sink[h]
+        raw_sink = sink[h] * (1.0 / SCALE)
         top = jnp.maximum(jnp.max(score, axis=1, keepdims=True), jnp.max(near, axis=1, keepdims=True))
         top = jnp.maximum(top, raw_sink)
         weight = jnp.exp2((score - top) * FACTOR)
         near = jnp.exp2((near - top) * FACTOR)
         total = jnp.sum(weight, axis=1, keepdims=True) + jnp.sum(near, axis=1, keepdims=True)
         total = total + jnp.exp2((raw_sink - top) * FACTOR)
-        mixed = jnp.dot(weight.astype(BF16), listed(table, kv, 1, h), preferred_element_type=F32)
+        mixed = jnp.dot(weight.astype(BF16), listed(kv, 1, slots), preferred_element_type=F32)
         near = near.astype(BF16)
         for run in range(RUNS):
             rows = slice(run * ROWS, (run + 1) * ROWS)
-            vals = jnp.concatenate([band[1, table[BAND + h * BANDS + j] + run] for j in range(BANDS)], axis=0)
+            vals = jnp.concatenate([band[1, RUNS + run - slash[h, j]] for j in range(BANDS)], axis=0)
             acc[rows, cols] = mixed[rows] + jnp.dot(near[rows], vals, preferred_element_type=F32)
         tops[:, cols] = wide(top)
         sums[:, cols] = wide(total)
@@ -156,23 +169,23 @@
         give(n * tile, tile, out[len(blocks) * HALF:])
 
 
-def late_kernel(table, q, w, b0, b2, b1, b3, acc, tops, sums, att, keep, give, kv, qs, sems):
+def late_kernel(table, vert, qs, w, b0, b2, b1, b3, acc, tops, sums, att, keep, give, kv, sems):
     copies = Copies(sems)
-    copies.start(q, qs)
     load_half(copies, table[META], b0, b2, b1, b3, kv)
     copies.wait()
-    token = table[META + 2] + lax.broadcasted_iota(jnp.int32, (TOKENS, 1), 0)
+    token = TOKENS // RUNS * table[META + 2] + lax.broadcasted_iota(jnp.int32, (TOKENS, 1), 0)
     places = key_places(table, True)
     for h in range(HEADS):
         cols = slice(h * HEAD, (h + 1) * HEAD)
-        score = product(qs[:, cols], listed(table, kv, 0, h))
-        score = jnp.where(token >= limits(table, places, h), score, LOW)
+        slots = slots_of(table, vert, h)
+        score = product(qs[:, cols], listed(kv, 0, slots))
+        score = jnp.where(token >= limits(vert, places, h), score, LOW)
         before = tops[:, cols]
         top = jnp.maximum(wide(jnp.max(score, axis=1, keepdims=True)), before)
         weight = jnp.exp2((score - across(top, LISTED * HALF // HEAD)) * FACTOR)
         fade = jnp.exp2((before - top) * FACTOR)
         total = wide(jnp.sum(weight, axis=1, keepdims=True)) + fade * sums[:, cols]
-        mixed = jnp.dot(weight.astype(BF16), listed(table, kv, 1, h), preferred_element_type=F32)
+        mixed = jnp.dot(weight.astype(BF16), listed(kv, 1, slots), preferred_element_type=F32)
         att[:, cols] = ((mixed + acc[:, cols] * fade) * (1.0 / total)).astype(BF16)
     project(att, w, [(table[META + 5] + 2) % X], table[META + 1], [keep], functools.partial(store, give))
 
@@ -222,7 +235,7 @@
         out_specs=(VMEM,) * len(outs),
         scratch_shapes=scratch,
         compiler_params=pltpu.CompilerParams(vmem_limit_bytes=24 * 2 ** 20),
-        cost_estimate=pl.CostEstimate(flops=int(micros * 1e9), bytes_accessed=2 ** 20, transcendentals=0),
+        cost_estimate=pl.CostEstimate(flops=int(micros * 1e9), bytes_accessed=int(micros * 2 ** 20), transcendentals=0),
         name=name,
     )
 
@@ -231,22 +244,20 @@
     return functools.reduce(lambda a, b: a + b, [t.astype(F32) for t in terms]).astype(BF16)
 
 
-def tables(c, x, core, vert_blocks, slash_offsets):
+def tables(c, x, core, vert_blocks):
     block = jnp.arange(BLOCKS, dtype=jnp.int32)
-    ids = vert_blocks.reshape(-1)
-    present = jnp.any(ids[:, None] == block[None, :], axis=0).astype(jnp.int32)
+    present = jnp.any(vert_blocks[:, :, None] == block, axis=(0, 1)).astype(jnp.int32)
     rank = jnp.sum(jnp.where(block[:, None] > block[None, :], present[None, :], 0), axis=1)
-    place = jnp.where(present > 0, rank, -1)
-    slot = jnp.sum(jnp.where(ids[:, None] > block[None, :], present[None, :], 0), axis=1)
-    slot = jnp.where(ids >= 0, slot, 0)
-    base = jnp.where(ids >= 0, ids * ROWS, NEVER)
-    run = jnp.arange(RUNS, dtype=jnp.int32)
-    near = RUNS * c + run[:, None, None] - slash_offsets[None]
-    dup = jnp.any(near[:, :, :, None] == vert_blocks[None, :, None, :], axis=3)
-    near = jnp.where((near >= 0) & jnp.logical_not(dup), near * ROWS, NEVER)
-    meta = jnp.stack([c % 2, core, TOKENS * c, c // Y, (c % Y) // 2, x, x * 0, x * 0]).astype(jnp.int32)
-    parts = [slot, base, RUNS - slash_offsets.reshape(-1), near.reshape(-1), meta]
-    return place, jnp.concatenate(parts)
+    meta = jnp.stack([c % 2, core, RUNS * c, c // Y, (c % Y) // 2, x]).astype(jnp.int32)
+    return jnp.where(present > 0, rank, -1), jnp.concatenate([rank, meta])
+
+
+def spread_kernel(keys, values, out, sems):
+    copies = Copies(sems)
+    for kind, a in enumerate((keys, values)):
+        for b in range(RUNS):
+            copies.start(a.at[b], out.at[:, kind, b])
+    copies.wait()
 
 
 def per_device(queries, keys, values, sink_logits, vert_blocks, slash_offsets, output_weight):
@@ -255,12 +266,13 @@
     x, core = h // 2, h % 2
     keys = keys.reshape(RUNS, ROWS, HEAD)
     values = values.reshape(RUNS, ROWS, HEAD)
-    place, table = tables(c, x, core, vert_blocks, slash_offsets)
-
-    def slices(a):
-        return jnp.transpose(a.reshape(RUNS, 16, 8, HEAD), (1, 0, 2, 3))
-
-    spread = jnp.stack([slices(keys), slices(values)], axis=1).reshape(Z * Y, RUNS * 8, HEAD)
+    place, table = tables(c, x, core, vert_blocks)
+    far_keys, far_values = [pltpu.with_memory_space_constraint(a.reshape(RUNS, 16, 8, HEAD), pltpu.HBM)
+                            for a in (keys, values)]
+    (spread,) = call(
+        spread_kernel, [ANY, ANY], [((16, 2, RUNS, 8, HEAD), BF16)], [pltpu.SemaphoreType.DMA((2 * RUNS,))], 1, "spread",
+    )(far_keys, far_values)
+    spread = spread.reshape(Z * Y, RUNS * 8, HEAD)
     prev = lax.ppermute(spread, "ctx", [(s, s + 1) for s in range(Z * Y - 1)]).reshape(16, 2, RUNS, 8, HEAD)
     got = lax.all_to_all(spread, "ctx", 0, 0, tiled=True).reshape(BLOCKS * 8, HEAD)
     r = jnp.arange(SLOTS * 8, dtype=jnp.int32)[:, None]
@@ -282,24 +294,23 @@
 
     width = output_weight.shape[1]
     kv = pltpu.VMEM((2, SLOTS, HALF, HEAD), BF16)
-    held = pltpu.VMEM((TOKENS, HEADS * HEAD), BF16)
+    rows = ((TOKENS, HEADS * HEAD), BF16)
     part = ((HALF, width), BF16)
     far_queries = pltpu.with_memory_space_constraint(queries, pltpu.HBM)
     far_weight = pltpu.with_memory_space_constraint(output_weight, pltpu.HBM)
-    acc, tops, sums, w = call(
-        early_kernel, [SMEM, SMEM] + [ANY] * 6 + [VMEM, ANY, ANY],
-        [((TOKENS, HEADS * HEAD), F32)] * 3 + [(output_weight.shape, BF16)],
-        [kv, pltpu.VMEM((2, 2 * RUNS, ROWS, HEAD), BF16), held, pltpu.SemaphoreType.DMA((11,))], 8, "early",
-    )(table, sink_logits * (1.0 / SCALE), far_queries, far_weight, a0, a2, a1, a3, prev,
+    acc, tops, sums, w, q = call(
+        early_kernel, [SMEM] * 4 + [ANY] * 6 + [VMEM, ANY, ANY],
+        [((TOKENS, HEADS * HEAD), F32)] * 3 + [(output_weight.shape, BF16), rows],
+        [kv, pltpu.VMEM((2, 2 * RUNS, ROWS, HEAD), BF16), pltpu.SemaphoreType.DMA((11,))], 8, "early",
+    )(table, vert_blocks, slash_offsets, sink_logits, far_queries, far_weight, a0, a2, a1, a3, prev,
       *[pltpu.with_memory_space_constraint(a, pltpu.HBM) for a in (keys, values)])
     att, keep_far, give_far = call(
-        late_kernel, [SMEM, ANY, VMEM] + [ANY] * 4 + [VMEM] * 3,
-        [((TOKENS, HEADS * HEAD), BF16), part, part],
-        [kv, held, pltpu.SemaphoreType.DMA((5,))], 1, "late",
-    )(table, far_queries, w, b0, b2, b1, b3, acc, tops, sums)
+        late_kernel, [SMEM, SMEM, VMEM, VMEM] + [ANY] * 4 + [VMEM] * 3,
+        [rows, part, part], [kv, pltpu.SemaphoreType.DMA((4,))], 0.01, "late",
+    )(table, vert_blocks, q, w, b0, b2, b1, b3, acc, tops, sums)
     halves = ((2 * HALF, width // 2), BF16)
     keep_below, keep_above, give_direct, give_relayed = call(
-        sides_kernel, [SMEM, VMEM, VMEM], [part, part, halves, halves], [], 1, "sides",
+        sides_kernel, [SMEM, VMEM, VMEM], [part, part, halves, halves], [], 0.01, "sides",
     )(table, att, w)
     def swap(a):
         return lax.ppermute(a, "head", CORE_PAIRS)
@@ -313,7 +324,7 @@
     far_right = total_of(keep_far[:, mid:], far[:, mid:])
     relay_left, relay_right = to_x(far_left, 1), to_x(far_right, -1)
     keep_own, give_own = call(
-        own_kernel, [SMEM, VMEM, VMEM, ANY], [part, part], [], 1, "own",
+        own_kernel, [SMEM, VMEM, VMEM, ANY], [part, part], [], 0.01, "own",
     )(table, att, w, far_left)
 
     own = swap(give_own)

time: 99.6 us -> 100 us (level)
  waiting for transfers between devices: 22.5 us -> 31.7 us
  other arithmetic: 5.21 us -> 0.77 us
  starting transfers between devices: 46.8 us -> 44.4 us
  local copies, waits for them, and re-layouts: 2.2 us -> 0.38 us
    all_to_all x1, waiting for transfers between devices: 3.37 us -> 10.7 us  [per_device(): lax.all_to_all(spread, 'ctx', 0, 0, tiled=True).reshape(BLOCKS * 8, HEAD)]
    ppermute x6, waiting for transfers between devices: 10.8 us -> 12.6 us  [to_x(): return lax.ppermute(a, 'head', x_pairs(step))]
    ppermute x4, starting transfers between devices: 9.17 us -> 7.67 us  [swap(): return lax.ppermute(a, 'head', CORE_PAIRS)]
    sub x2 -> x0, other arithmetic: 1.44 us -> none  [the longest x1 0.75 us: tables(): near = RUNS * c + run[:, None, None] - slash_offsets[None]]
    ppermute x1, starting transfers between devices: 3.15 us -> 1.98 us  [per_device(): lax.ppermute(spread, 'ctx', [(s, s + 1) for s in range(Z * Y - 1)])]
    ppermute x6, starting transfers between devices: 8.32 us -> 7.25 us  [to_x(): return lax.ppermute(a, 'head', x_pairs(step))]
    reduce_or x2 -> x1, other arithmetic: 1.14 us -> 0.09 us  [tables(): jnp.any(vert_blocks[:, :, None] == block, axis=(0, 1)).astype(jnp.int32)]
    another operation x1 -> x0, other arithmetic: 1.01 us -> none  [per_device(): jnp.stack([slices(keys), slices(values)], axis=1)]
  transfers between devices with their start and end apart: 23 -> 23, of which waited for: 7 -> 8; matrix products, arithmetic and copies ran while one was open for 6% -> 1% of each run, Pallas kernels for 14% -> 14%
where the time goes in v4:
time: 100 us; the launch traced here: 99.8 us
  starting transfers between devices  44.4 us (44%)
  waiting for transfers between devices  31.7 us (32%)
  Pallas kernels  22 us (22%)
    ppermute x6, waiting for transfers between devices, to_x(): return lax.ppermute(a, 'head', x_pairs(step))  12.6 us
    all_to_all x1, starting transfers between devices, per_device(): lax.all_to_all(spread, 'ctx', 0, 0, tiled=True).reshape(BLOCKS * 8, HEAD)  12 us
    all_to_all x1, waiting for transfers between devices, per_device(): lax.all_to_all(spread, 'ctx', 0, 0, tiled=True).reshape(BLOCKS * 8, HEAD)  10.7 us
    pallas_call x1, Pallas kernels, per_device(): call(early_kernel, [SMEM] * 4 + [ANY] * 6 + [VMEM, ANY, ANY], [((TOKENS,...  8.79 us
    ppermute x5, waiting for transfers between devices, from_z(): return lax.ppermute(a, 'ctx', z_pairs(-offset))  8.25 us
    ppermute x4, starting transfers between devices, swap(): return lax.ppermute(a, 'head', CORE_PAIRS)  7.67 us
    ppermute x6, starting transfers between devices, to_x(): return lax.ppermute(a, 'head', x_pairs(step))  7.25 us
    ppermute x5, starting transfers between devices, from_z(): return lax.ppermute(a, 'ctx', z_pairs(-offset))  6.33 us
  transfers between devices with their start and end apart: 23, of which 8 were waited for; matrix products, arithmetic and copies ran while one was open for 1% of the time, Pallas kernels for 14%

profile of v4, /device:TPU:1, one launch (start us, length us, event | category | flops | bytes accessed | tf_op | source)
XLA Modules:
  0.0 99.8 jit_solution(10042477540937159237)
XLA Ops:
  0.0 1.7 %spread.1 = bf16[16,2,4,8,128]{4,3,2,1,0:T(8,128)(2,1)} custom-call(bf16[4,16,8,128]{3,2,1,0:T(8,128)(2,1)} %bitcast.18, bf16[4,16,8,128]{3,2,1,0:T(8,128)(2,1)} %bitcast.20), custom_call_target="tpu_custom_call" | custom-call | flops 1000000000 | bytes 1048576 | tf_op jit(solution)/shard_map/spread/pallas_call | solution.py:272
  1.7 12.0 %all-to-all-start = ((bf16[32,32,128]{2,1,0:T(8,128)(2,1)}), bf16[32,32,128]{2,1,0:T(8,128)(2,1)S(1)}, u32[]{:S(2)}, u32[]{:S(2)}) async-start(bf16[32,32,128]{2,1,0:T(8,128)(2,1)} %bitcast.8), calls=%async_computation | async-start | bytes 524288 | tf_op jit(solution)/shard_map/all_to_all | solution.py:277
  14.2 10.7 %all-to-all-done = bf16[32,32,128]{2,1,0:T(8,128)(2,1)S(1)} async-done(((bf16[32,32,128]{2,1,0:T(8,128)(2,1)}), bf16[32,32,128]{2,1,0:T(8,128)(2,1)S(1)}, u32[]{:S(2)}, u32[]{:S(2)}) %all-to-all-start) | async-done | bytes 262176 | tf_op jit(solution)/shard_map/all_to_all | solution.py:277
  25.3 1.6 %collective-permute-start.2 = (bf16[24,8,128]{2,1,0:T(8,128)(2,1)S(1)}, bf16[24,8,128]{2,1,0:T(8,128)(2,1)S(1)}, u32[]{:S(2)}, u32[]{:S(2)}) collective-permute-start(bf16[24,8,128]{2,1,0:T(8,128)(2,1)S(1)} %fusion), channel_id=1, source_target_pairs={{0,64},{8,72},{16,80},{24,88},{32,96},{40,104},{48,112},{56,120},{... | collective-permute-start | bytes 147464 | tf_op jit(solution)/shard_map/ppermute | solution.py:285
  26.9 2.0 %collective-permute-start = (bf16[24,8,128]{2,1,0:T(8,128)(2,1)S(1)}, bf16[24,8,128]{2,1,0:T(8,128)(2,1)S(1)}, u32[]{:S(2)}, u32[]{:S(2)}) collective-permute-start(bf16[24,8,128]{2,1,0:T(8,128)(2,1)S(1)} %fusion), channel_id=1, source_target_pairs={{0,192},{8,200},{16,208},{24,216},{32,224},{40,232},{48,240},{56,2... | collective-permute-start | bytes 147464 | tf_op jit(solution)/shard_map/ppermute | solution.py:285
  28.9 2.0 %collective-permute-start.6 = (bf16[32,32,128]{2,1,0:T(8,128)(2,1)}, bf16[32,32,128]{2,1,0:T(8,128)(2,1)S(1)}, u32[]{:S(2)}, u32[]{:S(2)}) collective-permute-start(bf16[32,32,128]{2,1,0:T(8,128)(2,1)} %bitcast.8), channel_id=1, source_target_pairs={{0,8},{8,16},{16,24},{24,32},{32,40},{40,48},{48,56},{56,64},{64,7... | collective-permute-start | bytes 786440 | tf_op jit(solution)/shard_map/ppermute | solution.py:276
  31.2 2.0 %collective-permute-start.1 = (bf16[24,8,128]{2,1,0:T(8,128)(2,1)S(1)}, bf16[24,8,128]{2,1,0:T(8,128)(2,1)S(1)}, u32[]{:S(2)}, u32[]{:S(2)}) collective-permute-start(bf16[24,8,128]{2,1,0:T(8,128)(2,1)S(1)} %fusion), channel_id=1, source_target_pairs={{0,128},{8,136},{16,144},{24,152},{32,160},{40,168},{48,176},{56,1... | collective-permute-start | bytes 147464 | tf_op jit(solution)/shard_map/ppermute | solution.py:285
  33.9 4.8 %collective-permute-done.1 = bf16[24,8,128]{2,1,0:T(8,128)(2,1)S(1)} collective-permute-done((bf16[24,8,128]{2,1,0:T(8,128)(2,1)S(1)}, bf16[24,8,128]{2,1,0:T(8,128)(2,1)S(1)}, u32[]{:S(2)}, u32[]{:S(2)}) %collective-permute-start.1) | collective-permute-done | bytes 49184 | tf_op jit(solution)/shard_map/ppermute | solution.py:285
  38.7 3.6 %collective-permute-start.5 = (bf16[24,32,128]{2,1,0:T(8,128)(2,1)S(1)}, bf16[24,32,128]{2,1,0:T(8,128)(2,1)S(1)}, u32[]{:S(2)}, u32[]{:S(2)}) collective-permute-start(bf16[24,32,128]{2,1,0:T(8,128)(2,1)S(1)} %pad_maximum_fusion.a0), channel_id=1, source_target_pairs={{0,24},{8,16},{16,8},{24,0},{32,56},{40,48},{48,40},{56,32},{64,88... | collective-permute-start | bytes 589832 | tf_op jit(solution)/shard_map/ppermute | solution.py:292
  42.3 1.3 %collective-permute-start.3 = (bf16[24,32,128]{2,1,0:T(8,128)(2,1)S(1)}, bf16[24,32,128]{2,1,0:T(8,128)(2,1)S(1)}, u32[]{:S(2)}, u32[]{:S(2)}) collective-permute-start(bf16[24,32,128]{2,1,0:T(8,128)(2,1)S(1)} %pad_maximum_fusion.a0), channel_id=1, source_target_pairs={{0,16},{8,24},{16,0},{24,8},{32,48},{40,56},{48,32},{56,40},{64,80... | collective-permute-start | bytes 589832 | tf_op jit(solution)/shard_map/ppermute | solution.py:292
  43.6 3.5 %collective-permute-done.8 = bf16[24,16,128]{2,1,0:T(8,128)(2,1)S(1)} collective-permute-done((bf16[24,16,128]{2,1,0:T(8,128)(2,1)S(1)}, bf16[24,16,128]{2,1,0:T(8,128)(2,1)S(1)}, u32[]{:S(2)}, u32[]{:S(2)}) %collective-permute-start.8) | collective-permute-done | bytes 98336 | tf_op jit(solution)/shard_map/ppermute | solution.py:285
  47.1 3.0 %collective-permute-start.11 = (bf16[24,32,128]{2,1,0:T(8,128)(2,1)S(1)}, bf16[24,32,128]{2,1,0:T(8,128)(2,1)S(1)}, u32[]{:S(2)}, u32[]{:S(2)}) collective-permute-start(bf16[24,32,128]{2,1,0:T(8,128)(2,1)S(1)} %constant_dynamic-update-slice_fusion.b0), channel_id=1, source_target_pairs={{0,24},{8,16},{16,8},{24,0},{32,56},{40,48},{48,40},{56,32},{64,88... | collective-permute-start | bytes 589832 | tf_op jit(solution)/shard_map/ppermute | solution.py:293
  50.1 1.3 %collective-permute-start.9 = (bf16[24,32,128]{2,1,0:T(8,128)(2,1)S(1)}, bf16[24,32,128]{2,1,0:T(8,128)(2,1)S(1)}, u32[]{:S(2)}, u32[]{:S(2)}) collective-permute-start(bf16[24,32,128]{2,1,0:T(8,128)(2,1)S(1)} %constant_dynamic-update-slice_fusion.b0), channel_id=1, source_target_pairs={{0,16},{8,24},{16,0},{24,8},{32,48},{40,56},{48,32},{56,40},{64,80... | collective-permute-start | bytes 589832 | tf_op jit(solution)/shard_map/ppermute | solution.py:293
  51.4 8.8 %early.1 = (f32[512,1024]{1,0:T(8,128)S(1)}, f32[512,1024]{1,0:T(8,128)S(1)}, f32[512,1024]{1,0:T(8,128)S(1)}, bf16[1024,4096]{1,0:T(8,128)(2,1)S(1)}, bf16[512,1024]{1,0:T(8,128)(2,1)S(1)}) custom-call(s32[134]{0:T(256)S(1)} %concatenate.15.table, s32[8,8]{1,0:T(8,128)S(1)} %copy-done, s32[8,3]{1,0:T(8,128)S(1)} %copy.10.slash, f32[8]{0:T(128)S(1)} %copy-done.1, ...), custom_call_target="tpu_custom_call" | custom-call | flops 8000000000 | bytes 8388608 | tf_op jit(solution)/shard_map/early/pallas_call | solution.py:301
  60.2 5.7 %late.1 = (bf16[512,1024]{1,0:T(8,128)(2,1)S(1)}, bf16[64,4096]{1,0:T(8,128)(2,1)S(1)}, bf16[64,4096]{1,0:T(8,128)(2,1)S(1)}) custom-call(s32[134]{0:T(256)S(1)} %concatenate.15.table, s32[8,8]{1,0:T(8,128)S(1)} %copy-done, bf16[512,1024]{1,0:T(8,128)(2,1)S(1)} %get-tuple-element.24.qs, bf16[1024,4096]{1,0:T(8,128)(2,1)S(1)} %get-tuple-element.25.w, ...), custom_call_target="tpu_custom_call" | custom-call | flops 10000000 | bytes 10485 | tf_op jit(solution)/shard_map/late/pallas_call | solution.py:307
  65.9 6.6 %collective-permute-start.12 = (bf16[64,4096]{1,0:T(8,128)(2,1)S(1)}, bf16[64,4096]{1,0:T(8,128)(2,1)S(1)}, u32[]{:S(2)}, u32[]{:S(2)}) collective-permute-start(bf16[64,4096]{1,0:T(8,128)(2,1)S(1)} %get-tuple-element.31), channel_id=1, source_target_pairs={{0,1},{1,0},{2,3},{3,2},{4,5},{5,4},{6,7},{7,6},{8,9},{9,8},{10,11... | collective-permute-start | bytes 1572872 | tf_op jit(solution)/shard_map/ppermute | solution.py:316
  72.6 2.9 %sides.1 = (bf16[64,4096]{1,0:T(8,128)(2,1)S(1)}, bf16[64,4096]{1,0:T(8,128)(2,1)S(1)}, bf16[128,2048]{1,0:T(8,128)(2,1)S(1)}, bf16[128,2048]{1,0:T(8,128)(2,1)S(1)}) custom-call(s32[134]{0:T(256)S(1)} %concatenate.15.table, bf16[512,1024]{1,0:T(8,128)(2,1)S(1)} %get-tuple-element.29.att, bf16[1024,4096]{1,0:T(8,128)(2,1)S(1)} %get-tuple-element.25.w), custom_call_target="tpu_custom_call" | custom-call | flops 10000000 | bytes 10485 | tf_op jit(solution)/shard_map/sides/pallas_call | solution.py:312
  76.2 2.6 %collective-permute-start.16 = (bf16[64,2048]{1,0:T(8,128)(2,1)S(1)}, bf16[64,2048]{1,0:T(8,128)(2,1)S(1)}, u32[]{:S(2)}, u32[]{:S(2)}) collective-permute-start(bf16[64,2048]{1,0:T(8,128)(2,1)S(1)} %get-tuple-element.43), channel_id=1, source_target_pairs={{0,6},{1,7},{2,0},{3,1},{4,2},{5,3},{6,4},{7,5},{8,14},{9,15},{10,... | collective-permute-start | bytes 786440 | tf_op jit(solution)/shard_map/ppermute | solution.py:319
  78.8 1.8 %own.1 = (bf16[64,4096]{1,0:T(8,128)(2,1)S(1)}, bf16[64,4096]{1,0:T(8,128)(2,1)S(1)}) custom-call(s32[134]{0:T(256)S(1)} %concatenate.15.table, bf16[512,1024]{1,0:T(8,128)(2,1)S(1)} %get-tuple-element.29.att, bf16[1024,4096]{1,0:T(8,128)(2,1)S(1)} %get-tuple-element.25.w, bf16[64,2048]{1,0:T(8,128)(2,1)S(1)} %get-tuple-element.44.after), custom_call_target="tpu_custom_call" | custom-call | flops 10000000 | bytes 10485 | tf_op jit(solution)/shard_map/own/pallas_call | solution.py:326
  81.8 2.6 %collective-permute-start.19 = (bf16[64,2048]{1,0:T(8,128)(2,1)S(1)}, bf16[64,2048]{1,0:T(8,128)(2,1)S(1)}, u32[]{:S(2)}, u32[]{:S(2)}) collective-permute-start(bf16[64,2048]{1,0:T(8,128)(2,1)S(1)} %get-tuple-element.48), channel_id=1, source_target_pairs={{0,6},{1,7},{2,0},{3,1},{4,2},{5,3},{6,4},{7,5},{8,14},{9,15},{10,... | collective-permute-start | bytes 786440 | tf_op jit(solution)/shard_map/ppermute | solution.py:319
  84.4 3.1 %collective-permute-done.15 = bf16[64,2048]{1,0:T(8,128)(2,1)S(1)} collective-permute-done((bf16[64,2048]{1,0:T(8,128)(2,1)S(1)}, bf16[64,2048]{1,0:T(8,128)(2,1)S(1)}, u32[]{:S(2)}, u32[]{:S(2)}) %collective-permute-start.15) | collective-permute-done | bytes 262176 | tf_op jit(solution)/shard_map/ppermute | solution.py:319
  89.3 3.8 %collective-permute-done.20.right_below = bf16[64,2048]{1,0:T(8,128)(2,1)S(1)} collective-permute-done((bf16[64,2048]{1,0:T(8,128)(2,1)S(1)}, bf16[64,2048]{1,0:T(8,128)(2,1)S(1)}, u32[]{:S(2)}, u32[]{:S(2)}) %collective-permute-start.20) | collective-permute-done | bytes 262176 | tf_op jit(solution)/shard_map/ppermute | solution.py:319
  93.1 2.6 %collective-permute-done.21.right_above = bf16[64,2048]{1,0:T(8,128)(2,1)S(1)} collective-permute-done((bf16[64,2048]{1,0:T(8,128)(2,1)S(1)}, bf16[64,2048]{1,0:T(8,128)(2,1)S(1)}, u32[]{:S(2)}, u32[]{:S(2)}) %collective-permute-start.21) | collective-permute-done | bytes 262176 | tf_op jit(solution)/shard_map/ppermute | solution.py:319
  95.7 3.0 %collective-permute-done.17.left_below = bf16[64,2048]{1,0:T(8,128)(2,1)S(1)} collective-permute-done((bf16[64,2048]{1,0:T(8,128)(2,1)S(1)}, bf16[64,2048]{1,0:T(8,128)(2,1)S(1)}, u32[]{:S(2)}, u32[]{:S(2)}) %collective-permute-start.17) | collective-permute-done | bytes 262176 | tf_op jit(solution)/shard_map/ppermute | solution.py:319
  (52 shorter events, 6.5 us)
Async XLA Ops:
  1.7 49.7 %copy-start.1 = (f32[8]{0:T(128)S(1)}, f32[8]{0:T(128)}, u32[]{:S(2)}) copy-start(f32[8]{0:T(128)} %sink.1) | copy-start | bytes 100
  1.7 23.2 %all-to-all-start = ((bf16[32,32,128]{2,1,0:T(8,128)(2,1)}), bf16[32,32,128]{2,1,0:T(8,128)(2,1)S(1)}, u32[]{:S(2)}, u32[]{:S(2)}) async-start(bf16[32,32,128]{2,1,0:T(8,128)(2,1)} %bitcast.8), calls=%async_computation | async-start | bytes 524288 | tf_op jit(solution)/shard_map/all_to_all | solution.py:277
  25.3 7.9 %collective-permute-start.2 = (bf16[24,8,128]{2,1,0:T(8,128)(2,1)S(1)}, bf16[24,8,128]{2,1,0:T(8,128)(2,1)S(1)}, u32[]{:S(2)}, u32[]{:S(2)}) collective-permute-start(bf16[24,8,128]{2,1,0:T(8,128)(2,1)S(1)} %fusion), channel_id=1, source_target_pairs={{0,64},{8,72},{16,80},{24,88},{32,96},{40,104},{48,112},{56,120},{... | collective-permute-start | bytes 147464 | tf_op jit(solution)/shard_map/ppermute | solution.py:285
  26.9 6.3 %collective-permute-start = (bf16[24,8,128]{2,1,0:T(8,128)(2,1)S(1)}, bf16[24,8,128]{2,1,0:T(8,128)(2,1)S(1)}, u32[]{:S(2)}, u32[]{:S(2)}) collective-permute-start(bf16[24,8,128]{2,1,0:T(8,128)(2,1)S(1)} %fusion), channel_id=1, source_target_pairs={{0,192},{8,200},{16,208},{24,216},{32,224},{40,232},{48,240},{56,2... | collective-permute-start | bytes 147464 | tf_op jit(solution)/shard_map/ppermute | solution.py:285
  28.9 21.1 %collective-permute-start.6 = (bf16[32,32,128]{2,1,0:T(8,128)(2,1)}, bf16[32,32,128]{2,1,0:T(8,128)(2,1)S(1)}, u32[]{:S(2)}, u32[]{:S(2)}) collective-permute-start(bf16[32,32,128]{2,1,0:T(8,128)(2,1)} %bitcast.8), channel_id=1, source_target_pairs={{0,8},{8,16},{16,24},{24,32},{32,40},{40,48},{48,56},{56,64},{64,7... | collective-permute-start | bytes 786440 | tf_op jit(solution)/shard_map/ppermute | solution.py:276
  31.2 7.5 %collective-permute-start.1 = (bf16[24,8,128]{2,1,0:T(8,128)(2,1)S(1)}, bf16[24,8,128]{2,1,0:T(8,128)(2,1)S(1)}, u32[]{:S(2)}, u32[]{:S(2)}) collective-permute-start(bf16[24,8,128]{2,1,0:T(8,128)(2,1)S(1)} %fusion), channel_id=1, source_target_pairs={{0,128},{8,136},{16,144},{24,152},{32,160},{40,168},{48,176},{56,1... | collective-permute-start | bytes 147464 | tf_op jit(solution)/shard_map/ppermute | solution.py:285
  33.2 10.4 %collective-permute-start.7 = (bf16[24,16,128]{2,1,0:T(8,128)(2,1)S(1)}, bf16[24,16,128]{2,1,0:T(8,128)(2,1)S(1)}, u32[]{:S(2)}, u32[]{:S(2)}) collective-permute-start(bf16[24,16,128]{2,1,0:T(8,128)(2,1)S(1)} %get-tuple-element.50), channel_id=1, source_target_pairs={{0,32},{8,40},{16,48},{24,56},{32,64},{40,72},{48,80},{56,88},{64,... | collective-permute-start | bytes 294920 | tf_op jit(solution)/shard_map/ppermute | solution.py:285
  38.7 11.3 %collective-permute-start.5 = (bf16[24,32,128]{2,1,0:T(8,128)(2,1)S(1)}, bf16[24,32,128]{2,1,0:T(8,128)(2,1)S(1)}, u32[]{:S(2)}, u32[]{:S(2)}) collective-permute-start(bf16[24,32,128]{2,1,0:T(8,128)(2,1)S(1)} %pad_maximum_fusion.a0), channel_id=1, source_target_pairs={{0,24},{8,16},{16,8},{24,0},{32,56},{40,48},{48,40},{56,32},{64,88... | collective-permute-start | bytes 589832 | tf_op jit(solution)/shard_map/ppermute | solution.py:292
  42.3 9.0 %collective-permute-start.4 = (bf16[24,32,128]{2,1,0:T(8,128)(2,1)S(1)}, bf16[24,32,128]{2,1,0:T(8,128)(2,1)S(1)}, u32[]{:S(2)}, u32[]{:S(2)}) collective-permute-start(bf16[24,32,128]{2,1,0:T(8,128)(2,1)S(1)} %pad_maximum_fusion.a0), channel_id=1, source_target_pairs={{0,8},{8,0},{16,24},{24,16},{32,40},{40,32},{48,56},{56,48},{64,72... | collective-permute-start | bytes 589832 | tf_op jit(solution)/shard_map/ppermute | solution.py:292
  42.3 9.0 %collective-permute-start.3 = (bf16[24,32,128]{2,1,0:T(8,128)(2,1)S(1)}, bf16[24,32,128]{2,1,0:T(8,128)(2,1)S(1)}, u32[]{:S(2)}, u32[]{:S(2)}) collective-permute-start(bf16[24,32,128]{2,1,0:T(8,128)(2,1)S(1)} %pad_maximum_fusion.a0), channel_id=1, source_target_pairs={{0,16},{8,24},{16,0},{24,8},{32,48},{40,56},{48,32},{56,40},{64,80... | collective-permute-start | bytes 589832 | tf_op jit(solution)/shard_map/ppermute | solution.py:292
  43.6 3.5 %collective-permute-start.8 = (bf16[24,16,128]{2,1,0:T(8,128)(2,1)S(1)}, bf16[24,16,128]{2,1,0:T(8,128)(2,1)S(1)}, u32[]{:S(2)}, u32[]{:S(2)}) collective-permute-start(bf16[24,16,128]{2,1,0:T(8,128)(2,1)S(1)} %get-tuple-element.49), channel_id=1, source_target_pairs={{0,224},{8,232},{16,240},{24,248},{32,0},{40,8},{48,16},{56,24},{6... | collective-permute-start | bytes 294920 | tf_op jit(solution)/shard_map/ppermute | solution.py:285
  47.1 13.1 %collective-permute-start.11 = (bf16[24,32,128]{2,1,0:T(8,128)(2,1)S(1)}, bf16[24,32,128]{2,1,0:T(8,128)(2,1)S(1)}, u32[]{:S(2)}, u32[]{:S(2)}) collective-permute-start(bf16[24,32,128]{2,1,0:T(8,128)(2,1)S(1)} %constant_dynamic-update-slice_fusion.b0), channel_id=1, source_target_pairs={{0,24},{8,16},{16,8},{24,0},{32,56},{40,48},{48,40},{56,32},{64,88... | collective-permute-start | bytes 589832 | tf_op jit(solution)/shard_map/ppermute | solution.py:293
  50.1 10.1 %collective-permute-start.10 = (bf16[24,32,128]{2,1,0:T(8,128)(2,1)S(1)}, bf16[24,32,128]{2,1,0:T(8,128)(2,1)S(1)}, u32[]{:S(2)}, u32[]{:S(2)}) collective-permute-start(bf16[24,32,128]{2,1,0:T(8,128)(2,1)S(1)} %constant_dynamic-update-slice_fusion.b0), channel_id=1, source_target_pairs={{0,8},{8,0},{16,24},{24,16},{32,40},{40,32},{48,56},{56,48},{64,72... | collective-permute-start | bytes 589832 | tf_op jit(solution)/shard_map/ppermute | solution.py:293
  50.1 10.1 %collective-permute-start.9 = (bf16[24,32,128]{2,1,0:T(8,128)(2,1)S(1)}, bf16[24,32,128]{2,1,0:T(8,128)(2,1)S(1)}, u32[]{:S(2)}, u32[]{:S(2)}) collective-permute-start(bf16[24,32,128]{2,1,0:T(8,128)(2,1)S(1)} %constant_dynamic-update-slice_fusion.b0), channel_id=1, source_target_pairs={{0,16},{8,24},{16,0},{24,8},{32,48},{40,56},{48,32},{56,40},{64,80... | collective-permute-start | bytes 589832 | tf_op jit(solution)/shard_map/ppermute | solution.py:293
  65.9 10.1 %collective-permute-start.12 = (bf16[64,4096]{1,0:T(8,128)(2,1)S(1)}, bf16[64,4096]{1,0:T(8,128)(2,1)S(1)}, u32[]{:S(2)}, u32[]{:S(2)}) collective-permute-start(bf16[64,4096]{1,0:T(8,128)(2,1)S(1)} %get-tuple-element.31), channel_id=1, source_target_pairs={{0,1},{1,0},{2,3},{3,2},{4,5},{5,4},{6,7},{7,6},{8,9},{9,8},{10,11... | collective-permute-start | bytes 1572872 | tf_op jit(solution)/shard_map/ppermute | solution.py:316
  75.5 5.6 %collective-permute-start.18 = (bf16[128,2048]{1,0:T(8,128)(2,1)S(1)}, bf16[128,2048]{1,0:T(8,128)(2,1)S(1)}, u32[]{:S(2)}, u32[]{:S(2)}) collective-permute-start(bf16[128,2048]{1,0:T(8,128)(2,1)S(1)} %get-tuple-element.40), channel_id=1, source_target_pairs={{0,1},{1,0},{2,3},{3,2},{4,5},{5,4},{6,7},{7,6},{8,9},{9,8},{10,11... | collective-permute-start | bytes 1572872 | tf_op jit(solution)/shard_map/ppermute | solution.py:316
  75.6 6.2 %collective-permute-start.14 = (bf16[128,2048]{1,0:T(8,128)(2,1)S(1)}, bf16[128,2048]{1,0:T(8,128)(2,1)S(1)}, u32[]{:S(2)}, u32[]{:S(2)}) collective-permute-start(bf16[128,2048]{1,0:T(8,128)(2,1)S(1)} %get-tuple-element.36), channel_id=1, source_target_pairs={{0,1},{1,0},{2,3},{3,2},{4,5},{5,4},{6,7},{7,6},{8,9},{9,8},{10,11... | collective-permute-start | bytes 1572872 | tf_op jit(solution)/shard_map/ppermute | solution.py:316
  76.2 8.2 %collective-permute-start.16 = (bf16[64,2048]{1,0:T(8,128)(2,1)S(1)}, bf16[64,2048]{1,0:T(8,128)(2,1)S(1)}, u32[]{:S(2)}, u32[]{:S(2)}) collective-permute-start(bf16[64,2048]{1,0:T(8,128)(2,1)S(1)} %get-tuple-element.43), channel_id=1, source_target_pairs={{0,6},{1,7},{2,0},{3,1},{4,2},{5,3},{6,4},{7,5},{8,14},{9,15},{10,... | collective-permute-start | bytes 786440 | tf_op jit(solution)/shard_map/ppermute | solution.py:319
  78.8 8.7 %collective-permute-start.15 = (bf16[64,2048]{1,0:T(8,128)(2,1)S(1)}, bf16[64,2048]{1,0:T(8,128)(2,1)S(1)}, u32[]{:S(2)}, u32[]{:S(2)}) collective-permute-start(bf16[64,2048]{1,0:T(8,128)(2,1)S(1)} %get-tuple-element.44.after), channel_id=1, source_target_pairs={{0,2},{1,3},{2,4},{3,5},{4,6},{5,7},{6,0},{7,1},{8,10},{9,11},{10,... | collective-permute-start | bytes 786440 | tf_op jit(solution)/shard_map/ppermute | solution.py:319
  80.6 18.1 %collective-permute-start.13 = (bf16[64,4096]{1,0:T(8,128)(2,1)S(1)}, bf16[64,4096]{1,0:T(8,128)(2,1)S(1)}, u32[]{:S(2)}, u32[]{:S(2)}) collective-permute-start(bf16[64,4096]{1,0:T(8,128)(2,1)S(1)} %get-tuple-element.33), channel_id=1, source_target_pairs={{0,1},{1,0},{2,3},{3,2},{4,5},{5,4},{6,7},{7,6},{8,9},{9,8},{10,11... | collective-permute-start | bytes 1572872 | tf_op jit(solution)/shard_map/ppermute | solution.py:316
  81.2 11.9 %collective-permute-start.20 = (bf16[64,2048]{1,0:T(8,128)(2,1)S(1)}, bf16[64,2048]{1,0:T(8,128)(2,1)S(1)}, u32[]{:S(2)}, u32[]{:S(2)}) collective-permute-start(bf16[64,2048]{1,0:T(8,128)(2,1)S(1)} %get-tuple-element.47), channel_id=1, source_target_pairs={{0,2},{1,3},{2,4},{3,5},{4,6},{5,7},{6,0},{7,1},{8,10},{9,11},{10,... | collective-permute-start | bytes 786440 | tf_op jit(solution)/shard_map/ppermute | solution.py:319
  81.8 11.4 %collective-permute-start.19 = (bf16[64,2048]{1,0:T(8,128)(2,1)S(1)}, bf16[64,2048]{1,0:T(8,128)(2,1)S(1)}, u32[]{:S(2)}, u32[]{:S(2)}) collective-permute-start(bf16[64,2048]{1,0:T(8,128)(2,1)S(1)} %get-tuple-element.48), channel_id=1, source_target_pairs={{0,6},{1,7},{2,0},{3,1},{4,2},{5,3},{6,4},{7,5},{8,14},{9,15},{10,... | collective-permute-start | bytes 786440 | tf_op jit(solution)/shard_map/ppermute | solution.py:319
  87.8 8.0 %collective-permute-start.21 = (bf16[64,2048]{1,0:T(8,128)(2,1)S(1)}, bf16[64,2048]{1,0:T(8,128)(2,1)S(1)}, u32[]{:S(2)}, u32[]{:S(2)}) collective-permute-start(bf16[64,2048]{1,0:T(8,128)(2,1)S(1)} %get-tuple-element.45), channel_id=1, source_target_pairs={{0,6},{1,7},{2,0},{3,1},{4,2},{5,3},{6,4},{7,5},{8,14},{9,15},{10,... | collective-permute-start | bytes 786440 | tf_op jit(solution)/shard_map/ppermute | solution.py:319
  88.2 10.6 %collective-permute-start.17 = (bf16[64,2048]{1,0:T(8,128)(2,1)S(1)}, bf16[64,2048]{1,0:T(8,128)(2,1)S(1)}, u32[]{:S(2)}, u32[]{:S(2)}) collective-permute-start(bf16[64,2048]{1,0:T(8,128)(2,1)S(1)} %get-tuple-element.46), channel_id=1, source_target_pairs={{0,2},{1,3},{2,4},{3,5},{4,6},{5,7},{6,0},{7,1},{8,10},{9,11},{10,... | collective-permute-start | bytes 786440 | tf_op jit(solution)/shard_map/ppermute | solution.py:319
  (2 other events, 44.7 us)

commit v5 on v4

--- a/solution.py
+++ b/solution.py
@@ -26,8 +26,8 @@
 META = BLOCKS
 
 
-def z_pairs(step):
-    return [(Y * z + y, Y * ((z + step) % Z) + y) for z in range(Z) for y in range(Y)]
+def z_pairs(flip):
+    return [(Y * z + y, Y * (z ^ flip) + y) for z in range(Z) for y in range(Y)]
 
 
 def y_pairs(flip):
@@ -60,8 +60,7 @@
     z, y_half = table[META + 3], table[META + 4]
     n = lax.broadcasted_iota(jnp.int32, (1, HALF), 1)
     part, inner, row = n // 32, (n // 8) % 4, n % 8
-    step = jnp.where(inner < 2, -1 - 2 * inner, 2 * inner - 3) if late else 2 * inner
-    z_of = (z + step + Z) % Z
+    z_of = z ^ ((inner % 2) * 4 + (inner // 2) * 2 + int(late))
     return (z_of * 2 + (y_half ^ part)) * 8 + row
 
 
@@ -275,20 +274,19 @@
     spread = spread.reshape(Z * Y, RUNS * 8, HEAD)
     prev = lax.ppermute(spread, "ctx", [(s, s + 1) for s in range(Z * Y - 1)]).reshape(16, 2, RUNS, 8, HEAD)
     got = lax.all_to_all(spread, "ctx", 0, 0, tiled=True).reshape(BLOCKS * 8, HEAD)
+    prev, place = lax.optimization_barrier((prev, place))
     r = jnp.arange(SLOTS * 8, dtype=jnp.int32)[:, None]
     col = jnp.arange(BLOCKS * 8, dtype=jnp.int32)[None, :]
     pick = (jnp.repeat(place, 8)[None, :] == r // 8) & (col % 8 == r % 8)
     mine = jnp.dot(pick.astype(BF16), got, preferred_element_type=F32)
     mine = mine.astype(BF16).reshape(SLOTS, 8, HEAD)
 
-    def from_z(a, offset):
-        return lax.ppermute(a, "ctx", z_pairs(-offset))
-
-    z2, z4, z6 = from_z(mine, 2), from_z(mine, 4), from_z(mine, 6)
-    a0 = jnp.concatenate([mine, z2, z4, z6], axis=1)
-    low = from_z(jnp.concatenate([mine, z6], axis=1), -1)
-    high = from_z(jnp.concatenate([mine, z2], axis=1), 1)
-    b0 = jnp.concatenate([low, high], axis=1)
+    def from_z(a, flip):
+        return lax.ppermute(a, "ctx", z_pairs(flip))
+
+    pair = jnp.concatenate([mine, from_z(mine, 4)], axis=1)
+    a0 = jnp.concatenate([pair, from_z(pair, 2)], axis=1)
+    b0 = from_z(a0, 1)
     a1, a2, a3 = [lax.ppermute(a0, "ctx", y_pairs(f)) for f in (1, 2, 3)]
     b1, b2, b3 = [lax.ppermute(b0, "ctx", y_pairs(f)) for f in (1, 2, 3)]
 

time: 100 us -> 103 us (1.030)
  starting transfers between devices: 44.4 us -> 51.1 us
  waiting for transfers between devices: 31.7 us -> 27.6 us
    all_to_all x1, waiting for transfers between devices: 10.7 us -> 0.86 us  [per_device(): lax.all_to_all(spread, 'ctx', 0, 0, tiled=True).reshape(BLOCKS * 8, HEAD)]
    ppermute x1, waiting for transfers between devices: 0.01 us -> 6.74 us  [per_device(): lax.ppermute(spread, 'ctx', [(s, s + 1) for s in range(Z * Y - 1)])]
    ppermute x5 -> x3, starting transfers between devices: 6.33 us -> 12.4 us  [from_z(): return lax.ppermute(a, 'ctx', z_pairs(flip))]
    ppermute x5 -> x3, waiting for transfers between devices: 8.25 us -> 4.54 us  [from_z(): return lax.ppermute(a, 'ctx', z_pairs(flip))]
    ppermute x3, waiting for transfers between devices: 0.01 us -> 2.84 us  [per_device(): a1, a2, a3 = [lax.ppermute(a0, 'ctx', y_pairs(f)) for f in (1, 2, 3)]]
    ppermute x4, starting transfers between devices: 7.67 us -> 10.1 us  [swap(): return lax.ppermute(a, 'head', CORE_PAIRS)]
    ppermute x3, starting transfers between devices: 4.25 us -> 2.36 us  [per_device(): b1, b2, b3 = [lax.ppermute(b0, 'ctx', y_pairs(f)) for f in (1, 2, 3)]]
    ppermute x1, starting transfers between devices: 1.98 us -> 3.15 us  [per_device(): lax.ppermute(spread, 'ctx', [(s, s + 1) for s in range(Z * Y - 1)])]
  transfers between devices with their start and end apart: 23 -> 21, of which waited for: 8 -> 11; matrix products, arithmetic and copies ran while one was open for 1% -> 1% of each run, Pallas kernels for 14% -> 13%
where the time goes in v5:
time: 103 us; the launch traced here: 102 us
  starting transfers between devices  51.1 us (50%)
  waiting for transfers between devices  27.6 us (27%)
  Pallas kernels  22 us (21%)
    ppermute x6, waiting for transfers between devices, to_x(): return lax.ppermute(a, 'head', x_pairs(step))  12.6 us
    ppermute x3, starting transfers between devices, from_z(): return lax.ppermute(a, 'ctx', z_pairs(flip))  12.4 us
    all_to_all x1, starting transfers between devices, per_device(): lax.all_to_all(spread, 'ctx', 0, 0, tiled=True).reshape(BLOCKS * 8, HEAD)  12 us
    ppermute x4, starting transfers between devices, swap(): return lax.ppermute(a, 'head', CORE_PAIRS)  10.1 us
    pallas_call x1, Pallas kernels, per_device(): call(early_kernel, [SMEM] * 4 + [ANY] * 6 + [VMEM, ANY, ANY], [((TOKENS,...  8.77 us
    ppermute x6, starting transfers between devices, to_x(): return lax.ppermute(a, 'head', x_pairs(step))  7.26 us
    ppermute x1, waiting for transfers between devices, per_device(): lax.ppermute(spread, 'ctx', [(s, s + 1) for s in range(Z * Y - 1)])  6.74 us
    pallas_call x1, Pallas kernels, per_device(): call(late_kernel, [SMEM, SMEM, VMEM, VMEM] + [ANY] * 4 + [VMEM] * 3, [row...  5.73 us
  transfers between devices with their start and end apart: 21, of which 11 were waited for; matrix products, arithmetic and copies ran while one was open for 1% of the time, Pallas kernels for 13%

profile of v5, /device:TPU:1, one launch (start us, length us, event | category | flops | bytes accessed | tf_op | source)
XLA Modules:
  0.0 102.4 jit_solution(13956576324333131633)
XLA Ops:
  0.0 1.7 %spread.1 = bf16[16,2,4,8,128]{4,3,2,1,0:T(8,128)(2,1)} custom-call(bf16[4,16,8,128]{3,2,1,0:T(8,128)(2,1)} %bitcast.18, bf16[4,16,8,128]{3,2,1,0:T(8,128)(2,1)} %bitcast.20), custom_call_target="tpu_custom_call" | custom-call | flops 1000000000 | bytes 1048576 | tf_op jit(solution)/shard_map/spread/pallas_call | solution.py:271
  1.7 12.0 %all-to-all-start = ((bf16[32,32,128]{2,1,0:T(8,128)(2,1)}), bf16[32,32,128]{2,1,0:T(8,128)(2,1)S(1)}, u32[]{:S(2)}, u32[]{:S(2)}) async-start(bf16[32,32,128]{2,1,0:T(8,128)(2,1)} %bitcast.8), calls=%async_computation | async-start | bytes 524288 | tf_op jit(solution)/shard_map/all_to_all | solution.py:276
  13.7 3.1 %collective-permute-start = (bf16[32,32,128]{2,1,0:T(8,128)(2,1)}, bf16[32,32,128]{2,1,0:T(8,128)(2,1)S(1)}, u32[]{:S(2)}, u32[]{:S(2)}) collective-permute-start(bf16[32,32,128]{2,1,0:T(8,128)(2,1)} %bitcast.8), channel_id=1, source_target_pairs={{0,8},{8,16},{16,24},{24,32},{32,40},{40,48},{48,56},{56,64},{64,7... | collective-permute-start | bytes 786440 | tf_op jit(solution)/shard_map/ppermute | solution.py:275
  17.2 6.7 %collective-permute-done = bf16[32,32,128]{2,1,0:T(8,128)(2,1)S(1)} collective-permute-done((bf16[32,32,128]{2,1,0:T(8,128)(2,1)}, bf16[32,32,128]{2,1,0:T(8,128)(2,1)S(1)}, u32[]{:S(2)}, u32[]{:S(2)}) %collective-permute-start) | collective-permute-done | bytes 262176 | tf_op jit(solution)/shard_map/ppermute | solution.py:275
  25.3 8.6 %collective-permute-start.1 = (bf16[24,8,128]{2,1,0:T(8,128)(2,1)S(1)}, bf16[24,8,128]{2,1,0:T(8,128)(2,1)S(1)}, u32[]{:S(2)}, u32[]{:S(2)}) collective-permute-start(bf16[24,8,128]{2,1,0:T(8,128)(2,1)S(1)} %fusion), channel_id=1, source_target_pairs={{0,128},{8,136},{16,144},{24,152},{32,160},{40,168},{48,176},{56,1... | collective-permute-start | bytes 147464 | tf_op jit(solution)/shard_map/ppermute | solution.py:285
  33.9 1.5 %collective-permute-done.1 = bf16[24,8,128]{2,1,0:T(8,128)(2,1)S(1)} collective-permute-done((bf16[24,8,128]{2,1,0:T(8,128)(2,1)S(1)}, bf16[24,8,128]{2,1,0:T(8,128)(2,1)S(1)}, u32[]{:S(2)}, u32[]{:S(2)}) %collective-permute-start.1) | collective-permute-done | bytes 49184 | tf_op jit(solution)/shard_map/ppermute | solution.py:285
  35.4 2.9 %collective-permute-start.2 = (bf16[24,16,128]{2,1,0:T(8,128)(2,1)S(1)}, bf16[24,16,128]{2,1,0:T(8,128)(2,1)S(1)}, u32[]{:S(2)}, u32[]{:S(2)}) collective-permute-start(bf16[24,16,128]{2,1,0:T(8,128)(2,1)S(1)} %pad_maximum_fusion.1), channel_id=1, source_target_pairs={{0,64},{8,72},{16,80},{24,88},{32,96},{40,104},{48,112},{56,120},{... | collective-permute-start | bytes 294920 | tf_op jit(solution)/shard_map/ppermute | solution.py:285
  38.4 3.1 %collective-permute-done.2 = bf16[24,16,128]{2,1,0:T(8,128)(2,1)S(1)} collective-permute-done((bf16[24,16,128]{2,1,0:T(8,128)(2,1)S(1)}, bf16[24,16,128]{2,1,0:T(8,128)(2,1)S(1)}, u32[]{:S(2)}, u32[]{:S(2)}) %collective-permute-start.2) | collective-permute-done | bytes 98336 | tf_op jit(solution)/shard_map/ppermute | solution.py:285
  42.3 3.9 %collective-permute-start.3 = (bf16[24,32,128]{2,1,0:T(8,128)(2,1)S(1)}, bf16[24,32,128]{2,1,0:T(8,128)(2,1)S(1)}, u32[]{:S(2)}, u32[]{:S(2)}) collective-permute-start(bf16[24,32,128]{2,1,0:T(8,128)(2,1)S(1)} %pad_maximum_fusion.a0), channel_id=1, source_target_pairs={{0,16},{8,24},{16,0},{24,8},{32,48},{40,56},{48,32},{56,40},{64,80... | collective-permute-start | bytes 589832 | tf_op jit(solution)/shard_map/ppermute | solution.py:290
  46.5 1.5 %collective-permute-done.5.a3 = bf16[24,32,128]{2,1,0:T(8,128)(2,1)S(1)} collective-permute-done((bf16[24,32,128]{2,1,0:T(8,128)(2,1)S(1)}, bf16[24,32,128]{2,1,0:T(8,128)(2,1)S(1)}, u32[]{:S(2)}, u32[]{:S(2)}) %collective-permute-start.5) | collective-permute-done | bytes 196640 | tf_op jit(solution)/shard_map/ppermute | solution.py:290
  48.0 2.2 %collective-permute-start.7 = (bf16[24,32,128]{2,1,0:T(8,128)(2,1)S(1)}, bf16[24,32,128]{2,1,0:T(8,128)(2,1)S(1)}, u32[]{:S(2)}, u32[]{:S(2)}) collective-permute-start(bf16[24,32,128]{2,1,0:T(8,128)(2,1)S(1)} %collective-permute-done.6.b0), channel_id=1, source_target_pairs={{0,16},{8,24},{16,0},{24,8},{32,48},{40,56},{48,32},{56,40},{64,80... | collective-permute-start | bytes 589832 | tf_op jit(solution)/shard_map/ppermute | solution.py:291
  50.2 1.3 %collective-permute-done.3.a2 = bf16[24,32,128]{2,1,0:T(8,128)(2,1)S(1)} collective-permute-done((bf16[24,32,128]{2,1,0:T(8,128)(2,1)S(1)}, bf16[24,32,128]{2,1,0:T(8,128)(2,1)S(1)}, u32[]{:S(2)}, u32[]{:S(2)}) %collective-permute-start.3) | collective-permute-done | bytes 196640 | tf_op jit(solution)/shard_map/ppermute | solution.py:290
  51.5 8.8 %early.1 = (f32[512,1024]{1,0:T(8,128)S(1)}, f32[512,1024]{1,0:T(8,128)S(1)}, f32[512,1024]{1,0:T(8,128)S(1)}, bf16[1024,4096]{1,0:T(8,128)(2,1)S(1)}, bf16[512,1024]{1,0:T(8,128)(2,1)S(1)}) custom-call(s32[134]{0:T(256)S(1)} %concatenate.10.table, s32[8,8]{1,0:T(8,128)S(1)} %copy-done, s32[8,3]{1,0:T(8,128)S(1)} %copy.10.slash, f32[8]{0:T(128)S(1)} %copy-done.1, ...), custom_call_target="tpu_custom_call" | custom-call | flops 8000000000 | bytes 8388608 | tf_op jit(solution)/shard_map/early/pallas_call | solution.py:299
  60.3 5.7 %late.1 = (bf16[512,1024]{1,0:T(8,128)(2,1)S(1)}, bf16[64,4096]{1,0:T(8,128)(2,1)S(1)}, bf16[64,4096]{1,0:T(8,128)(2,1)S(1)}) custom-call(s32[134]{0:T(256)S(1)} %concatenate.10.table, s32[8,8]{1,0:T(8,128)S(1)} %copy-done, bf16[512,1024]{1,0:T(8,128)(2,1)S(1)} %get-tuple-element.28.qs, bf16[1024,4096]{1,0:T(8,128)(2,1)S(1)} %get-tuple-element.29.w, ...), custom_call_target="tpu_custom_call" | custom-call | flops 10000000 | bytes 10485 | tf_op jit(solution)/shard_map/late/pallas_call | solution.py:305
  66.1 9.0 %collective-permute-start.10 = (bf16[64,4096]{1,0:T(8,128)(2,1)S(1)}, bf16[64,4096]{1,0:T(8,128)(2,1)S(1)}, u32[]{:S(2)}, u32[]{:S(2)}) collective-permute-start(bf16[64,4096]{1,0:T(8,128)(2,1)S(1)} %get-tuple-element.35), channel_id=1, source_target_pairs={{0,1},{1,0},{2,3},{3,2},{4,5},{5,4},{6,7},{7,6},{8,9},{9,8},{10,11... | collective-permute-start | bytes 1572872 | tf_op jit(solution)/shard_map/ppermute | solution.py:314
  75.1 2.9 %sides.1 = (bf16[64,4096]{1,0:T(8,128)(2,1)S(1)}, bf16[64,4096]{1,0:T(8,128)(2,1)S(1)}, bf16[128,2048]{1,0:T(8,128)(2,1)S(1)}, bf16[128,2048]{1,0:T(8,128)(2,1)S(1)}) custom-call(s32[134]{0:T(256)S(1)} %concatenate.10.table, bf16[512,1024]{1,0:T(8,128)(2,1)S(1)} %get-tuple-element.33.att, bf16[1024,4096]{1,0:T(8,128)(2,1)S(1)} %get-tuple-element.29.w), custom_call_target="tpu_custom_call" | custom-call | flops 10000000 | bytes 10485 | tf_op jit(solution)/shard_map/sides/pallas_call | solution.py:310
  78.8 2.6 %collective-permute-start.14 = (bf16[64,2048]{1,0:T(8,128)(2,1)S(1)}, bf16[64,2048]{1,0:T(8,128)(2,1)S(1)}, u32[]{:S(2)}, u32[]{:S(2)}) collective-permute-start(bf16[64,2048]{1,0:T(8,128)(2,1)S(1)} %get-tuple-element.47), channel_id=1, source_target_pairs={{0,6},{1,7},{2,0},{3,1},{4,2},{5,3},{6,4},{7,5},{8,14},{9,15},{10,... | collective-permute-start | bytes 786440 | tf_op jit(solution)/shard_map/ppermute | solution.py:317
  81.4 1.8 %own.1 = (bf16[64,4096]{1,0:T(8,128)(2,1)S(1)}, bf16[64,4096]{1,0:T(8,128)(2,1)S(1)}) custom-call(s32[134]{0:T(256)S(1)} %concatenate.10.table, bf16[512,1024]{1,0:T(8,128)(2,1)S(1)} %get-tuple-element.33.att, bf16[1024,4096]{1,0:T(8,128)(2,1)S(1)} %get-tuple-element.29.w, bf16[64,2048]{1,0:T(8,128)(2,1)S(1)} %get-tuple-element.48.after), custom_call_target="tpu_custom_call" | custom-call | flops 10000000 | bytes 10485 | tf_op jit(solution)/shard_map/own/pallas_call | solution.py:324
  84.4 2.6 %collective-permute-start.17 = (bf16[64,2048]{1,0:T(8,128)(2,1)S(1)}, bf16[64,2048]{1,0:T(8,128)(2,1)S(1)}, u32[]{:S(2)}, u32[]{:S(2)}) collective-permute-start(bf16[64,2048]{1,0:T(8,128)(2,1)S(1)} %get-tuple-element.52), channel_id=1, source_target_pairs={{0,6},{1,7},{2,0},{3,1},{4,2},{5,3},{6,4},{7,5},{8,14},{9,15},{10,... | collective-permute-start | bytes 786440 | tf_op jit(solution)/shard_map/ppermute | solution.py:317
  87.0 3.1 %collective-permute-done.13 = bf16[64,2048]{1,0:T(8,128)(2,1)S(1)} collective-permute-done((bf16[64,2048]{1,0:T(8,128)(2,1)S(1)}, bf16[64,2048]{1,0:T(8,128)(2,1)S(1)}, u32[]{:S(2)}, u32[]{:S(2)}) %collective-permute-start.13) | collective-permute-done | bytes 262176 | tf_op jit(solution)/shard_map/ppermute | solution.py:317
  90.8 1.1 %collective-permute-start.15 = (bf16[64,2048]{1,0:T(8,128)(2,1)S(1)}, bf16[64,2048]{1,0:T(8,128)(2,1)S(1)}, u32[]{:S(2)}, u32[]{:S(2)}) collective-permute-start(bf16[64,2048]{1,0:T(8,128)(2,1)S(1)} %get-tuple-element.50), channel_id=1, source_target_pairs={{0,2},{1,3},{2,4},{3,5},{4,6},{5,7},{6,0},{7,1},{8,10},{9,11},{10,... | collective-permute-start | bytes 786440 | tf_op jit(solution)/shard_map/ppermute | solution.py:317
  91.9 3.8 %collective-permute-done.18.right_below = bf16[64,2048]{1,0:T(8,128)(2,1)S(1)} collective-permute-done((bf16[64,2048]{1,0:T(8,128)(2,1)S(1)}, bf16[64,2048]{1,0:T(8,128)(2,1)S(1)}, u32[]{:S(2)}, u32[]{:S(2)}) %collective-permute-start.18) | collective-permute-done | bytes 262176 | tf_op jit(solution)/shard_map/ppermute | solution.py:317
  95.7 2.6 %collective-permute-done.19.right_above = bf16[64,2048]{1,0:T(8,128)(2,1)S(1)} collective-permute-done((bf16[64,2048]{1,0:T(8,128)(2,1)S(1)}, bf16[64,2048]{1,0:T(8,128)(2,1)S(1)}, u32[]{:S(2)}, u32[]{:S(2)}) %collective-permute-start.19) | collective-permute-done | bytes 262176 | tf_op jit(solution)/shard_map/ppermute | solution.py:317
  98.3 3.0 %collective-permute-done.15.left_below = bf16[64,2048]{1,0:T(8,128)(2,1)S(1)} collective-permute-done((bf16[64,2048]{1,0:T(8,128)(2,1)S(1)}, bf16[64,2048]{1,0:T(8,128)(2,1)S(1)}, u32[]{:S(2)}, u32[]{:S(2)}) %collective-permute-start.15) | collective-permute-done | bytes 262176 | tf_op jit(solution)/shard_map/ppermute | solution.py:317
  (46 shorter events, 6.4 us)
Async XLA Ops:
  0.0 16.9 %copy-start = (s32[8,8]{1,0:T(8,128)S(1)}, s32[8,8]{1,0:T(8,128)}, u32[]{:S(2)}) copy-start(s32[8,8]{1,0:T(8,128)} %vert.3) | copy-start | bytes 772
  0.0 46.1 %copy-start.2 = (s32[8,3]{0,1:T(4,128)S(1)}, s32[8,3]{0,1:T(4,128)}, u32[]{:S(2)}) copy-start(s32[8,3]{0,1:T(4,128)} %param.12) | copy-start | bytes 292
  0.0 51.5 %copy-start.1 = (f32[8]{0:T(128)S(1)}, f32[8]{0:T(128)}, u32[]{:S(2)}) copy-start(f32[8]{0:T(128)} %sink.1) | copy-start | bytes 100
  1.7 23.2 %all-to-all-start = ((bf16[32,32,128]{2,1,0:T(8,128)(2,1)}), bf16[32,32,128]{2,1,0:T(8,128)(2,1)S(1)}, u32[]{:S(2)}, u32[]{:S(2)}) async-start(bf16[32,32,128]{2,1,0:T(8,128)(2,1)} %bitcast.8), calls=%async_computation | async-start | bytes 524288 | tf_op jit(solution)/shard_map/all_to_all | solution.py:276
  13.7 10.1 %collective-permute-start = (bf16[32,32,128]{2,1,0:T(8,128)(2,1)}, bf16[32,32,128]{2,1,0:T(8,128)(2,1)S(1)}, u32[]{:S(2)}, u32[]{:S(2)}) collective-permute-start(bf16[32,32,128]{2,1,0:T(8,128)(2,1)} %bitcast.8), channel_id=1, source_target_pairs={{0,8},{8,16},{16,24},{24,32},{32,40},{40,48},{48,56},{56,64},{64,7... | collective-permute-start | bytes 786440 | tf_op jit(solution)/shard_map/ppermute | solution.py:275
  25.3 10.1 %collective-permute-start.1 = (bf16[24,8,128]{2,1,0:T(8,128)(2,1)S(1)}, bf16[24,8,128]{2,1,0:T(8,128)(2,1)S(1)}, u32[]{:S(2)}, u32[]{:S(2)}) collective-permute-start(bf16[24,8,128]{2,1,0:T(8,128)(2,1)S(1)} %fusion), channel_id=1, source_target_pairs={{0,128},{8,136},{16,144},{24,152},{32,160},{40,168},{48,176},{56,1... | collective-permute-start | bytes 147464 | tf_op jit(solution)/shard_map/ppermute | solution.py:285
  35.4 6.0 %collective-permute-start.2 = (bf16[24,16,128]{2,1,0:T(8,128)(2,1)S(1)}, bf16[24,16,128]{2,1,0:T(8,128)(2,1)S(1)}, u32[]{:S(2)}, u32[]{:S(2)}) collective-permute-start(bf16[24,16,128]{2,1,0:T(8,128)(2,1)S(1)} %pad_maximum_fusion.1), channel_id=1, source_target_pairs={{0,64},{8,72},{16,80},{24,88},{32,96},{40,104},{48,112},{56,120},{... | collective-permute-start | bytes 294920 | tf_op jit(solution)/shard_map/ppermute | solution.py:285
  41.5 4.8 %collective-permute-start.6 = (bf16[24,32,128]{2,1,0:T(8,128)(2,1)S(1)}, bf16[24,32,128]{2,1,0:T(8,128)(2,1)S(1)}, u32[]{:S(2)}, u32[]{:S(2)}) collective-permute-start(bf16[24,32,128]{2,1,0:T(8,128)(2,1)S(1)} %pad_maximum_fusion.a0), channel_id=1, source_target_pairs={{0,32},{8,40},{16,48},{24,56},{32,0},{40,8},{48,16},{56,24},{64,96... | collective-permute-start | bytes 589832 | tf_op jit(solution)/shard_map/ppermute | solution.py:285
  42.3 5.7 %collective-permute-start.5 = (bf16[24,32,128]{2,1,0:T(8,128)(2,1)S(1)}, bf16[24,32,128]{2,1,0:T(8,128)(2,1)S(1)}, u32[]{:S(2)}, u32[]{:S(2)}) collective-permute-start(bf16[24,32,128]{2,1,0:T(8,128)(2,1)S(1)} %pad_maximum_fusion.a0), channel_id=1, source_target_pairs={{0,24},{8,16},{16,8},{24,0},{32,56},{40,48},{48,40},{56,32},{64,88... | collective-permute-start | bytes 589832 | tf_op jit(solution)/shard_map/ppermute | solution.py:290
  42.3 7.9 %collective-permute-start.4 = (bf16[24,32,128]{2,1,0:T(8,128)(2,1)S(1)}, bf16[24,32,128]{2,1,0:T(8,128)(2,1)S(1)}, u32[]{:S(2)}, u32[]{:S(2)}) collective-permute-start(bf16[24,32,128]{2,1,0:T(8,128)(2,1)S(1)} %pad_maximum_fusion.a0), channel_id=1, source_target_pairs={{0,8},{8,0},{16,24},{24,16},{32,40},{40,32},{48,56},{56,48},{64,72... | collective-permute-start | bytes 589832 | tf_op jit(solution)/shard_map/ppermute | solution.py:290
  42.3 9.3 %collective-permute-start.3 = (bf16[24,32,128]{2,1,0:T(8,128)(2,1)S(1)}, bf16[24,32,128]{2,1,0:T(8,128)(2,1)S(1)}, u32[]{:S(2)}, u32[]{:S(2)}) collective-permute-start(bf16[24,32,128]{2,1,0:T(8,128)(2,1)S(1)} %pad_maximum_fusion.a0), channel_id=1, source_target_pairs={{0,16},{8,24},{16,0},{24,8},{32,48},{40,56},{48,32},{56,40},{64,80... | collective-permute-start | bytes 589832 | tf_op jit(solution)/shard_map/ppermute | solution.py:290
  46.3 14.0 %collective-permute-start.9 = (bf16[24,32,128]{2,1,0:T(8,128)(2,1)S(1)}, bf16[24,32,128]{2,1,0:T(8,128)(2,1)S(1)}, u32[]{:S(2)}, u32[]{:S(2)}) collective-permute-start(bf16[24,32,128]{2,1,0:T(8,128)(2,1)S(1)} %collective-permute-done.6.b0), channel_id=1, source_target_pairs={{0,24},{8,16},{16,8},{24,0},{32,56},{40,48},{48,40},{56,32},{64,88... | collective-permute-start | bytes 589832 | tf_op jit(solution)/shard_map/ppermute | solution.py:291
  46.4 14.0 %collective-permute-start.8 = (bf16[24,32,128]{2,1,0:T(8,128)(2,1)S(1)}, bf16[24,32,128]{2,1,0:T(8,128)(2,1)S(1)}, u32[]{:S(2)}, u32[]{:S(2)}) collective-permute-start(bf16[24,32,128]{2,1,0:T(8,128)(2,1)S(1)} %collective-permute-done.6.b0), channel_id=1, source_target_pairs={{0,8},{8,0},{16,24},{24,16},{32,40},{40,32},{48,56},{56,48},{64,72... | collective-permute-start | bytes 589832 | tf_op jit(solution)/shard_map/ppermute | solution.py:291
  48.0 12.3 %collective-permute-start.7 = (bf16[24,32,128]{2,1,0:T(8,128)(2,1)S(1)}, bf16[24,32,128]{2,1,0:T(8,128)(2,1)S(1)}, u32[]{:S(2)}, u32[]{:S(2)}) collective-permute-start(bf16[24,32,128]{2,1,0:T(8,128)(2,1)S(1)} %collective-permute-done.6.b0), channel_id=1, source_target_pairs={{0,16},{8,24},{16,0},{24,8},{32,48},{40,56},{48,32},{56,40},{64,80... | collective-permute-start | bytes 589832 | tf_op jit(solution)/shard_map/ppermute | solution.py:291
  66.1 12.6 %collective-permute-start.10 = (bf16[64,4096]{1,0:T(8,128)(2,1)S(1)}, bf16[64,4096]{1,0:T(8,128)(2,1)S(1)}, u32[]{:S(2)}, u32[]{:S(2)}) collective-permute-start(bf16[64,4096]{1,0:T(8,128)(2,1)S(1)} %get-tuple-element.35), channel_id=1, source_target_pairs={{0,1},{1,0},{2,3},{3,2},{4,5},{5,4},{6,7},{7,6},{8,9},{9,8},{10,11... | collective-permute-start | bytes 1572872 | tf_op jit(solution)/shard_map/ppermute | solution.py:314
  78.0 5.6 %collective-permute-start.16 = (bf16[128,2048]{1,0:T(8,128)(2,1)S(1)}, bf16[128,2048]{1,0:T(8,128)(2,1)S(1)}, u32[]{:S(2)}, u32[]{:S(2)}) collective-permute-start(bf16[128,2048]{1,0:T(8,128)(2,1)S(1)} %get-tuple-element.44), channel_id=1, source_target_pairs={{0,1},{1,0},{2,3},{3,2},{4,5},{5,4},{6,7},{7,6},{8,9},{9,8},{10,11... | collective-permute-start | bytes 1572872 | tf_op jit(solution)/shard_map/ppermute | solution.py:314
  78.1 6.2 %collective-permute-start.12 = (bf16[128,2048]{1,0:T(8,128)(2,1)S(1)}, bf16[128,2048]{1,0:T(8,128)(2,1)S(1)}, u32[]{:S(2)}, u32[]{:S(2)}) collective-permute-start(bf16[128,2048]{1,0:T(8,128)(2,1)S(1)} %get-tuple-element.40), channel_id=1, source_target_pairs={{0,1},{1,0},{2,3},{3,2},{4,5},{5,4},{6,7},{7,6},{8,9},{9,8},{10,11... | collective-permute-start | bytes 1572872 | tf_op jit(solution)/shard_map/ppermute | solution.py:314
  78.8 8.2 %collective-permute-start.14 = (bf16[64,2048]{1,0:T(8,128)(2,1)S(1)}, bf16[64,2048]{1,0:T(8,128)(2,1)S(1)}, u32[]{:S(2)}, u32[]{:S(2)}) collective-permute-start(bf16[64,2048]{1,0:T(8,128)(2,1)S(1)} %get-tuple-element.47), channel_id=1, source_target_pairs={{0,6},{1,7},{2,0},{3,1},{4,2},{5,3},{6,4},{7,5},{8,14},{9,15},{10,... | collective-permute-start | bytes 786440 | tf_op jit(solution)/shard_map/ppermute | solution.py:317
  81.4 8.7 %collective-permute-start.13 = (bf16[64,2048]{1,0:T(8,128)(2,1)S(1)}, bf16[64,2048]{1,0:T(8,128)(2,1)S(1)}, u32[]{:S(2)}, u32[]{:S(2)}) collective-permute-start(bf16[64,2048]{1,0:T(8,128)(2,1)S(1)} %get-tuple-element.48.after), channel_id=1, source_target_pairs={{0,2},{1,3},{2,4},{3,5},{4,6},{5,7},{6,0},{7,1},{8,10},{9,11},{10,... | collective-permute-start | bytes 786440 | tf_op jit(solution)/shard_map/ppermute | solution.py:317
  83.2 18.1 %collective-permute-start.11 = (bf16[64,4096]{1,0:T(8,128)(2,1)S(1)}, bf16[64,4096]{1,0:T(8,128)(2,1)S(1)}, u32[]{:S(2)}, u32[]{:S(2)}) collective-permute-start(bf16[64,4096]{1,0:T(8,128)(2,1)S(1)} %get-tuple-element.37), channel_id=1, source_target_pairs={{0,1},{1,0},{2,3},{3,2},{4,5},{5,4},{6,7},{7,6},{8,9},{9,8},{10,11... | collective-permute-start | bytes 1572872 | tf_op jit(solution)/shard_map/ppermute | solution.py:314
  83.8 11.9 %collective-permute-start.18 = (bf16[64,2048]{1,0:T(8,128)(2,1)S(1)}, bf16[64,2048]{1,0:T(8,128)(2,1)S(1)}, u32[]{:S(2)}, u32[]{:S(2)}) collective-permute-start(bf16[64,2048]{1,0:T(8,128)(2,1)S(1)} %get-tuple-element.51), channel_id=1, source_target_pairs={{0,2},{1,3},{2,4},{3,5},{4,6},{5,7},{6,0},{7,1},{8,10},{9,11},{10,... | collective-permute-start | bytes 786440 | tf_op jit(solution)/shard_map/ppermute | solution.py:317
  84.4 11.4 %collective-permute-start.17 = (bf16[64,2048]{1,0:T(8,128)(2,1)S(1)}, bf16[64,2048]{1,0:T(8,128)(2,1)S(1)}, u32[]{:S(2)}, u32[]{:S(2)}) collective-permute-start(bf16[64,2048]{1,0:T(8,128)(2,1)S(1)} %get-tuple-element.52), channel_id=1, source_target_pairs={{0,6},{1,7},{2,0},{3,1},{4,2},{5,3},{6,4},{7,5},{8,14},{9,15},{10,... | collective-permute-start | bytes 786440 | tf_op jit(solution)/shard_map/ppermute | solution.py:317
  90.4 8.0 %collective-permute-start.19 = (bf16[64,2048]{1,0:T(8,128)(2,1)S(1)}, bf16[64,2048]{1,0:T(8,128)(2,1)S(1)}, u32[]{:S(2)}, u32[]{:S(2)}) collective-permute-start(bf16[64,2048]{1,0:T(8,128)(2,1)S(1)} %get-tuple-element.49), channel_id=1, source_target_pairs={{0,6},{1,7},{2,0},{3,1},{4,2},{5,3},{6,4},{7,5},{8,14},{9,15},{10,... | collective-permute-start | bytes 786440 | tf_op jit(solution)/shard_map/ppermute | solution.py:317
  90.8 10.6 %collective-permute-start.15 = (bf16[64,2048]{1,0:T(8,128)(2,1)S(1)}, bf16[64,2048]{1,0:T(8,128)(2,1)S(1)}, u32[]{:S(2)}, u32[]{:S(2)}) collective-permute-start(bf16[64,2048]{1,0:T(8,128)(2,1)S(1)} %get-tuple-element.50), channel_id=1, source_target_pairs={{0,2},{1,3},{2,4},{3,5},{4,6},{5,7},{6,0},{7,1},{8,10},{9,11},{10,... | collective-permute-start | bytes 786440 | tf_op jit(solution)/shard_map/ppermute | solution.py:317

commit v6 on v4

--- a/solution.py
+++ b/solution.py
@@ -285,6 +285,7 @@
         return lax.ppermute(a, "ctx", z_pairs(-offset))
 
     z2, z4, z6 = from_z(mine, 2), from_z(mine, 4), from_z(mine, 6)
+    prev, z2, z4, z6 = lax.optimization_barrier((prev, z2, z4, z6))
     a0 = jnp.concatenate([mine, z2, z4, z6], axis=1)
     low = from_z(jnp.concatenate([mine, z6], axis=1), -1)
     high = from_z(jnp.concatenate([mine, z2], axis=1), 1)

time: 100 us -> 97.5 us (0.975)
  waiting for transfers between devices: 31.7 us -> 25.4 us
  starting transfers between devices: 44.4 us -> 48.1 us
    all_to_all x1, waiting for transfers between devices: 10.7 us -> 7.59 us  [per_device(): lax.all_to_all(spread, 'ctx', 0, 0, tiled=True).reshape(BLOCKS * 8, HEAD)]
    ppermute x5, waiting for transfers between devices: 8.25 us -> 5.18 us  [from_z(): return lax.ppermute(a, 'ctx', z_pairs(-offset))]
    ppermute x5, starting transfers between devices: 6.33 us -> 8.45 us  [from_z(): return lax.ppermute(a, 'ctx', z_pairs(-offset))]
    ppermute x4, starting transfers between devices: 7.67 us -> 9.36 us  [swap(): return lax.ppermute(a, 'head', CORE_PAIRS)]
    ppermute x1, starting transfers between devices: 1.98 us -> 3.15 us  [per_device(): lax.ppermute(spread, 'ctx', [(s, s + 1) for s in range(Z * Y - 1)])]
  transfers between devices with their start and end apart: 23 -> 23, of which waited for: 8 -> 9; matrix products, arithmetic and copies ran while one was open for 1% -> 1% of each run, Pallas kernels for 14% -> 14%
where the time goes in v6:
time: 97.5 us; the launch traced here: 97.3 us
  starting transfers between devices  48.1 us (49%)
  waiting for transfers between devices  25.4 us (26%)
  Pallas kernels  22 us (23%)
    ppermute x6, waiting for transfers between devices, to_x(): return lax.ppermute(a, 'head', x_pairs(step))  12.6 us
    all_to_all x1, starting transfers between devices, per_device(): lax.all_to_all(spread, 'ctx', 0, 0, tiled=True).reshape(BLOCKS * 8, HEAD)  12 us
    ppermute x4, starting transfers between devices, swap(): return lax.ppermute(a, 'head', CORE_PAIRS)  9.36 us
    pallas_call x1, Pallas kernels, per_device(): call(early_kernel, [SMEM] * 4 + [ANY] * 6 + [VMEM, ANY, ANY], [((TOKENS,...  8.79 us
    ppermute x5, starting transfers between devices, from_z(): return lax.ppermute(a, 'ctx', z_pairs(-offset))  8.45 us
    all_to_all x1, waiting for transfers between devices, per_device(): lax.all_to_all(spread, 'ctx', 0, 0, tiled=True).reshape(BLOCKS * 8, HEAD)  7.59 us
    ppermute x6, starting transfers between devices, to_x(): return lax.ppermute(a, 'head', x_pairs(step))  7.25 us
    pallas_call x1, Pallas kernels, per_device(): call(late_kernel, [SMEM, SMEM, VMEM, VMEM] + [ANY] * 4 + [VMEM] * 3, [row...  5.74 us
  transfers between devices with their start and end apart: 23, of which 9 were waited for; matrix products, arithmetic and copies ran while one was open for 1% of the time, Pallas kernels for 14%

profile of v6, /device:TPU:1, one launch (start us, length us, event | category | flops | bytes accessed | tf_op | source)
XLA Modules:
  0.0 97.3 jit_solution(5231323135927571433)
XLA Ops:
  0.0 1.7 %spread.1 = bf16[16,2,4,8,128]{4,3,2,1,0:T(8,128)(2,1)} custom-call(bf16[4,16,8,128]{3,2,1,0:T(8,128)(2,1)} %bitcast.18, bf16[4,16,8,128]{3,2,1,0:T(8,128)(2,1)} %bitcast.20), custom_call_target="tpu_custom_call" | custom-call | flops 1000000000 | bytes 1048576 | tf_op jit(solution)/shard_map/spread/pallas_call | solution.py:272
  1.7 12.0 %all-to-all-start = ((bf16[32,32,128]{2,1,0:T(8,128)(2,1)}), bf16[32,32,128]{2,1,0:T(8,128)(2,1)S(1)}, u32[]{:S(2)}, u32[]{:S(2)}) async-start(bf16[32,32,128]{2,1,0:T(8,128)(2,1)} %bitcast.8), calls=%async_computation | async-start | bytes 524288 | tf_op jit(solution)/shard_map/all_to_all | solution.py:277
  13.7 3.1 %collective-permute-start = (bf16[32,32,128]{2,1,0:T(8,128)(2,1)}, bf16[32,32,128]{2,1,0:T(8,128)(2,1)S(1)}, u32[]{:S(2)}, u32[]{:S(2)}) collective-permute-start(bf16[32,32,128]{2,1,0:T(8,128)(2,1)} %bitcast.8), channel_id=1, source_target_pairs={{0,8},{8,16},{16,24},{24,32},{32,40},{40,48},{48,56},{56,64},{64,7... | collective-permute-start | bytes 786440 | tf_op jit(solution)/shard_map/ppermute | solution.py:276
  17.3 7.6 %all-to-all-done = bf16[32,32,128]{2,1,0:T(8,128)(2,1)S(1)} async-done(((bf16[32,32,128]{2,1,0:T(8,128)(2,1)}), bf16[32,32,128]{2,1,0:T(8,128)(2,1)S(1)}, u32[]{:S(2)}, u32[]{:S(2)}) %all-to-all-start) | async-done | bytes 262176 | tf_op jit(solution)/shard_map/all_to_all | solution.py:277
  25.3 1.6 %collective-permute-start.3 = (bf16[24,8,128]{2,1,0:T(8,128)(2,1)S(1)}, bf16[24,8,128]{2,1,0:T(8,128)(2,1)S(1)}, u32[]{:S(2)}, u32[]{:S(2)}) collective-permute-start(bf16[24,8,128]{2,1,0:T(8,128)(2,1)S(1)} %fusion), channel_id=1, source_target_pairs={{0,64},{8,72},{16,80},{24,88},{32,96},{40,104},{48,112},{56,120},{... | collective-permute-start | bytes 147464 | tf_op jit(solution)/shard_map/ppermute | solution.py:285
  26.9 2.1 %collective-permute-start.2 = (bf16[24,8,128]{2,1,0:T(8,128)(2,1)S(1)}, bf16[24,8,128]{2,1,0:T(8,128)(2,1)S(1)}, u32[]{:S(2)}, u32[]{:S(2)}) collective-permute-start(bf16[24,8,128]{2,1,0:T(8,128)(2,1)S(1)} %fusion), channel_id=1, source_target_pairs={{0,128},{8,136},{16,144},{24,152},{32,160},{40,168},{48,176},{56,1... | collective-permute-start | bytes 147464 | tf_op jit(solution)/shard_map/ppermute | solution.py:285
  29.0 2.0 %collective-permute-start.1 = (bf16[24,8,128]{2,1,0:T(8,128)(2,1)S(1)}, bf16[24,8,128]{2,1,0:T(8,128)(2,1)S(1)}, u32[]{:S(2)}, u32[]{:S(2)}) collective-permute-start(bf16[24,8,128]{2,1,0:T(8,128)(2,1)S(1)} %fusion), channel_id=1, source_target_pairs={{0,192},{8,200},{16,208},{24,216},{32,224},{40,232},{48,240},{56,2... | collective-permute-start | bytes 147464 | tf_op jit(solution)/shard_map/ppermute | solution.py:285
  31.2 3.0 %collective-permute-done.2 = bf16[24,8,128]{2,1,0:T(8,128)(2,1)S(1)} collective-permute-done((bf16[24,8,128]{2,1,0:T(8,128)(2,1)S(1)}, bf16[24,8,128]{2,1,0:T(8,128)(2,1)S(1)}, u32[]{:S(2)}, u32[]{:S(2)}) %collective-permute-start.2) | collective-permute-done | bytes 49184 | tf_op jit(solution)/shard_map/ppermute | solution.py:285
  34.9 1.4 %collective-permute-start.6 = (bf16[24,32,128]{2,1,0:T(8,128)(2,1)S(1)}, bf16[24,32,128]{2,1,0:T(8,128)(2,1)S(1)}, u32[]{:S(2)}, u32[]{:S(2)}) collective-permute-start(bf16[24,32,128]{2,1,0:T(8,128)(2,1)S(1)} %pad_maximum_fusion.a0), channel_id=1, source_target_pairs={{0,24},{8,16},{16,8},{24,0},{32,56},{40,48},{48,40},{56,32},{64,88... | collective-permute-start | bytes 589832 | tf_op jit(solution)/shard_map/ppermute | solution.py:293
  36.3 2.6 %collective-permute-start.4 = (bf16[24,32,128]{2,1,0:T(8,128)(2,1)S(1)}, bf16[24,32,128]{2,1,0:T(8,128)(2,1)S(1)}, u32[]{:S(2)}, u32[]{:S(2)}) collective-permute-start(bf16[24,32,128]{2,1,0:T(8,128)(2,1)S(1)} %pad_maximum_fusion.a0), channel_id=1, source_target_pairs={{0,16},{8,24},{16,0},{24,8},{32,48},{40,56},{48,32},{56,40},{64,80... | collective-permute-start | bytes 589832 | tf_op jit(solution)/shard_map/ppermute | solution.py:293
  38.8 2.7 %collective-permute-start.8 = (bf16[24,16,128]{2,1,0:T(8,128)(2,1)S(1)}, bf16[24,16,128]{2,1,0:T(8,128)(2,1)S(1)}, u32[]{:S(2)}, u32[]{:S(2)}) collective-permute-start(bf16[24,16,128]{2,1,0:T(8,128)(2,1)S(1)} %get-tuple-element.57), channel_id=1, source_target_pairs={{0,224},{8,232},{16,240},{24,248},{32,0},{40,8},{48,16},{56,24},{6... | collective-permute-start | bytes 294920 | tf_op jit(solution)/shard_map/ppermute | solution.py:285
  41.5 1.6 %collective-permute-done.8 = bf16[24,16,128]{2,1,0:T(8,128)(2,1)S(1)} collective-permute-done((bf16[24,16,128]{2,1,0:T(8,128)(2,1)S(1)}, bf16[24,16,128]{2,1,0:T(8,128)(2,1)S(1)}, u32[]{:S(2)}, u32[]{:S(2)}) %collective-permute-start.8) | collective-permute-done | bytes 98336 | tf_op jit(solution)/shard_map/ppermute | solution.py:285
  44.5 2.6 %collective-permute-start.9 = (bf16[24,32,128]{2,1,0:T(8,128)(2,1)S(1)}, bf16[24,32,128]{2,1,0:T(8,128)(2,1)S(1)}, u32[]{:S(2)}, u32[]{:S(2)}) collective-permute-start(bf16[24,32,128]{2,1,0:T(8,128)(2,1)S(1)} %constant_dynamic-update-slice_fusion.b0), channel_id=1, source_target_pairs={{0,16},{8,24},{16,0},{24,8},{32,48},{40,56},{48,32},{56,40},{64,80... | collective-permute-start | bytes 589832 | tf_op jit(solution)/shard_map/ppermute | solution.py:294
  47.1 8.8 %early.1 = (f32[512,1024]{1,0:T(8,128)S(1)}, f32[512,1024]{1,0:T(8,128)S(1)}, f32[512,1024]{1,0:T(8,128)S(1)}, bf16[1024,4096]{1,0:T(8,128)(2,1)S(1)}, bf16[512,1024]{1,0:T(8,128)(2,1)S(1)}) custom-call(s32[134]{0:T(256)S(1)} %concatenate.15.table, s32[8,8]{1,0:T(8,128)S(1)} %copy-done, s32[8,3]{1,0:T(8,128)S(1)} %copy.10.slash, f32[8]{0:T(128)S(1)} %copy-done.1, ...), custom_call_target="tpu_custom_call" | custom-call | flops 8000000000 | bytes 8388608 | tf_op jit(solution)/shard_map/early/pallas_call | solution.py:302
  55.9 5.7 %late.1 = (bf16[512,1024]{1,0:T(8,128)(2,1)S(1)}, bf16[64,4096]{1,0:T(8,128)(2,1)S(1)}, bf16[64,4096]{1,0:T(8,128)(2,1)S(1)}) custom-call(s32[134]{0:T(256)S(1)} %concatenate.15.table, s32[8,8]{1,0:T(8,128)S(1)} %copy-done, bf16[512,1024]{1,0:T(8,128)(2,1)S(1)} %get-tuple-element.32.qs, bf16[1024,4096]{1,0:T(8,128)(2,1)S(1)} %get-tuple-element.33.w, ...), custom_call_target="tpu_custom_call" | custom-call | flops 10000000 | bytes 10485 | tf_op jit(solution)/shard_map/late/pallas_call | solution.py:308
  61.7 8.3 %collective-permute-start.12 = (bf16[64,4096]{1,0:T(8,128)(2,1)S(1)}, bf16[64,4096]{1,0:T(8,128)(2,1)S(1)}, u32[]{:S(2)}, u32[]{:S(2)}) collective-permute-start(bf16[64,4096]{1,0:T(8,128)(2,1)S(1)} %get-tuple-element.39), channel_id=1, source_target_pairs={{0,1},{1,0},{2,3},{3,2},{4,5},{5,4},{6,7},{7,6},{8,9},{9,8},{10,11... | collective-permute-start | bytes 1572872 | tf_op jit(solution)/shard_map/ppermute | solution.py:317
  70.0 2.9 %sides.1 = (bf16[64,4096]{1,0:T(8,128)(2,1)S(1)}, bf16[64,4096]{1,0:T(8,128)(2,1)S(1)}, bf16[128,2048]{1,0:T(8,128)(2,1)S(1)}, bf16[128,2048]{1,0:T(8,128)(2,1)S(1)}) custom-call(s32[134]{0:T(256)S(1)} %concatenate.15.table, bf16[512,1024]{1,0:T(8,128)(2,1)S(1)} %get-tuple-element.37.att, bf16[1024,4096]{1,0:T(8,128)(2,1)S(1)} %get-tuple-element.33.w), custom_call_target="tpu_custom_call" | custom-call | flops 10000000 | bytes 10485 | tf_op jit(solution)/shard_map/sides/pallas_call | solution.py:313
  73.7 2.6 %collective-permute-start.16 = (bf16[64,2048]{1,0:T(8,128)(2,1)S(1)}, bf16[64,2048]{1,0:T(8,128)(2,1)S(1)}, u32[]{:S(2)}, u32[]{:S(2)}) collective-permute-start(bf16[64,2048]{1,0:T(8,128)(2,1)S(1)} %get-tuple-element.51), channel_id=1, source_target_pairs={{0,6},{1,7},{2,0},{3,1},{4,2},{5,3},{6,4},{7,5},{8,14},{9,15},{10,... | collective-permute-start | bytes 786440 | tf_op jit(solution)/shard_map/ppermute | solution.py:320
  76.2 1.8 %own.1 = (bf16[64,4096]{1,0:T(8,128)(2,1)S(1)}, bf16[64,4096]{1,0:T(8,128)(2,1)S(1)}) custom-call(s32[134]{0:T(256)S(1)} %concatenate.15.table, bf16[512,1024]{1,0:T(8,128)(2,1)S(1)} %get-tuple-element.37.att, bf16[1024,4096]{1,0:T(8,128)(2,1)S(1)} %get-tuple-element.33.w, bf16[64,2048]{1,0:T(8,128)(2,1)S(1)} %get-tuple-element.52.after), custom_call_target="tpu_custom_call" | custom-call | flops 10000000 | bytes 10485 | tf_op jit(solution)/shard_map/own/pallas_call | solution.py:327
  79.2 2.6 %collective-permute-start.19 = (bf16[64,2048]{1,0:T(8,128)(2,1)S(1)}, bf16[64,2048]{1,0:T(8,128)(2,1)S(1)}, u32[]{:S(2)}, u32[]{:S(2)}) collective-permute-start(bf16[64,2048]{1,0:T(8,128)(2,1)S(1)} %get-tuple-element.56), channel_id=1, source_target_pairs={{0,6},{1,7},{2,0},{3,1},{4,2},{5,3},{6,4},{7,5},{8,14},{9,15},{10,... | collective-permute-start | bytes 786440 | tf_op jit(solution)/shard_map/ppermute | solution.py:320
  81.9 3.1 %collective-permute-done.15 = bf16[64,2048]{1,0:T(8,128)(2,1)S(1)} collective-permute-done((bf16[64,2048]{1,0:T(8,128)(2,1)S(1)}, bf16[64,2048]{1,0:T(8,128)(2,1)S(1)}, u32[]{:S(2)}, u32[]{:S(2)}) %collective-permute-start.15) | collective-permute-done | bytes 262176 | tf_op jit(solution)/shard_map/ppermute | solution.py:320
  86.8 3.8 %collective-permute-done.20.right_below = bf16[64,2048]{1,0:T(8,128)(2,1)S(1)} collective-permute-done((bf16[64,2048]{1,0:T(8,128)(2,1)S(1)}, bf16[64,2048]{1,0:T(8,128)(2,1)S(1)}, u32[]{:S(2)}, u32[]{:S(2)}) %collective-permute-start.20) | collective-permute-done | bytes 262176 | tf_op jit(solution)/shard_map/ppermute | solution.py:320
  90.6 2.6 %collective-permute-done.21.right_above = bf16[64,2048]{1,0:T(8,128)(2,1)S(1)} collective-permute-done((bf16[64,2048]{1,0:T(8,128)(2,1)S(1)}, bf16[64,2048]{1,0:T(8,128)(2,1)S(1)}, u32[]{:S(2)}, u32[]{:S(2)}) %collective-permute-start.21) | collective-permute-done | bytes 262176 | tf_op jit(solution)/shard_map/ppermute | solution.py:320
  93.2 3.0 %collective-permute-done.17.left_below = bf16[64,2048]{1,0:T(8,128)(2,1)S(1)} collective-permute-done((bf16[64,2048]{1,0:T(8,128)(2,1)S(1)}, bf16[64,2048]{1,0:T(8,128)(2,1)S(1)}, u32[]{:S(2)}, u32[]{:S(2)}) %collective-permute-start.17) | collective-permute-done | bytes 262176 | tf_op jit(solution)/shard_map/ppermute | solution.py:320
  (52 shorter events, 7.8 us)
Async XLA Ops:
  1.7 45.4 %copy-start.1 = (f32[8]{0:T(128)S(1)}, f32[8]{0:T(128)}, u32[]{:S(2)}) copy-start(f32[8]{0:T(128)} %sink.1) | copy-start | bytes 100
  1.7 23.2 %all-to-all-start = ((bf16[32,32,128]{2,1,0:T(8,128)(2,1)}), bf16[32,32,128]{2,1,0:T(8,128)(2,1)S(1)}, u32[]{:S(2)}, u32[]{:S(2)}) async-start(bf16[32,32,128]{2,1,0:T(8,128)(2,1)} %bitcast.8), calls=%async_computation | async-start | bytes 524288 | tf_op jit(solution)/shard_map/all_to_all | solution.py:277
  13.7 17.4 %collective-permute-start = (bf16[32,32,128]{2,1,0:T(8,128)(2,1)}, bf16[32,32,128]{2,1,0:T(8,128)(2,1)S(1)}, u32[]{:S(2)}, u32[]{:S(2)}) collective-permute-start(bf16[32,32,128]{2,1,0:T(8,128)(2,1)} %bitcast.8), channel_id=1, source_target_pairs={{0,8},{8,16},{16,24},{24,32},{32,40},{40,48},{48,56},{56,64},{64,7... | collective-permute-start | bytes 786440 | tf_op jit(solution)/shard_map/ppermute | solution.py:276
  25.3 5.9 %collective-permute-start.3 = (bf16[24,8,128]{2,1,0:T(8,128)(2,1)S(1)}, bf16[24,8,128]{2,1,0:T(8,128)(2,1)S(1)}, u32[]{:S(2)}, u32[]{:S(2)}) collective-permute-start(bf16[24,8,128]{2,1,0:T(8,128)(2,1)S(1)} %fusion), channel_id=1, source_target_pairs={{0,64},{8,72},{16,80},{24,88},{32,96},{40,104},{48,112},{56,120},{... | collective-permute-start | bytes 147464 | tf_op jit(solution)/shard_map/ppermute | solution.py:285
  26.9 7.3 %collective-permute-start.2 = (bf16[24,8,128]{2,1,0:T(8,128)(2,1)S(1)}, bf16[24,8,128]{2,1,0:T(8,128)(2,1)S(1)}, u32[]{:S(2)}, u32[]{:S(2)}) collective-permute-start(bf16[24,8,128]{2,1,0:T(8,128)(2,1)S(1)} %fusion), channel_id=1, source_target_pairs={{0,128},{8,136},{16,144},{24,152},{32,160},{40,168},{48,176},{56,1... | collective-permute-start | bytes 147464 | tf_op jit(solution)/shard_map/ppermute | solution.py:285
  29.0 5.7 %collective-permute-start.1 = (bf16[24,8,128]{2,1,0:T(8,128)(2,1)S(1)}, bf16[24,8,128]{2,1,0:T(8,128)(2,1)S(1)}, u32[]{:S(2)}, u32[]{:S(2)}) collective-permute-start(bf16[24,8,128]{2,1,0:T(8,128)(2,1)S(1)} %fusion), channel_id=1, source_target_pairs={{0,192},{8,200},{16,208},{24,216},{32,224},{40,232},{48,240},{56,2... | collective-permute-start | bytes 147464 | tf_op jit(solution)/shard_map/ppermute | solution.py:285
  34.8 6.7 %collective-permute-start.7 = (bf16[24,16,128]{2,1,0:T(8,128)(2,1)S(1)}, bf16[24,16,128]{2,1,0:T(8,128)(2,1)S(1)}, u32[]{:S(2)}, u32[]{:S(2)}) collective-permute-start(bf16[24,16,128]{2,1,0:T(8,128)(2,1)S(1)} %get-tuple-element.58), channel_id=1, source_target_pairs={{0,32},{8,40},{16,48},{24,56},{32,64},{40,72},{48,80},{56,88},{64,... | collective-permute-start | bytes 294920 | tf_op jit(solution)/shard_map/ppermute | solution.py:285
  34.9 9.6 %collective-permute-start.6 = (bf16[24,32,128]{2,1,0:T(8,128)(2,1)S(1)}, bf16[24,32,128]{2,1,0:T(8,128)(2,1)S(1)}, u32[]{:S(2)}, u32[]{:S(2)}) collective-permute-start(bf16[24,32,128]{2,1,0:T(8,128)(2,1)S(1)} %pad_maximum_fusion.a0), channel_id=1, source_target_pairs={{0,24},{8,16},{16,8},{24,0},{32,56},{40,48},{48,40},{56,32},{64,88... | collective-permute-start | bytes 589832 | tf_op jit(solution)/shard_map/ppermute | solution.py:293
  36.3 10.8 %collective-permute-start.5 = (bf16[24,32,128]{2,1,0:T(8,128)(2,1)S(1)}, bf16[24,32,128]{2,1,0:T(8,128)(2,1)S(1)}, u32[]{:S(2)}, u32[]{:S(2)}) collective-permute-start(bf16[24,32,128]{2,1,0:T(8,128)(2,1)S(1)} %pad_maximum_fusion.a0), channel_id=1, source_target_pairs={{0,8},{8,0},{16,24},{24,16},{32,40},{40,32},{48,56},{56,48},{64,72... | collective-permute-start | bytes 589832 | tf_op jit(solution)/shard_map/ppermute | solution.py:293
  36.3 10.8 %collective-permute-start.4 = (bf16[24,32,128]{2,1,0:T(8,128)(2,1)S(1)}, bf16[24,32,128]{2,1,0:T(8,128)(2,1)S(1)}, u32[]{:S(2)}, u32[]{:S(2)}) collective-permute-start(bf16[24,32,128]{2,1,0:T(8,128)(2,1)S(1)} %pad_maximum_fusion.a0), channel_id=1, source_target_pairs={{0,16},{8,24},{16,0},{24,8},{32,48},{40,56},{48,32},{56,40},{64,80... | collective-permute-start | bytes 589832 | tf_op jit(solution)/shard_map/ppermute | solution.py:293
  38.8 4.3 %collective-permute-start.8 = (bf16[24,16,128]{2,1,0:T(8,128)(2,1)S(1)}, bf16[24,16,128]{2,1,0:T(8,128)(2,1)S(1)}, u32[]{:S(2)}, u32[]{:S(2)}) collective-permute-start(bf16[24,16,128]{2,1,0:T(8,128)(2,1)S(1)} %get-tuple-element.57), channel_id=1, source_target_pairs={{0,224},{8,232},{16,240},{24,248},{32,0},{40,8},{48,16},{56,24},{6... | collective-permute-start | bytes 294920 | tf_op jit(solution)/shard_map/ppermute | solution.py:285
  43.2 12.8 %collective-permute-start.11 = (bf16[24,32,128]{2,1,0:T(8,128)(2,1)S(1)}, bf16[24,32,128]{2,1,0:T(8,128)(2,1)S(1)}, u32[]{:S(2)}, u32[]{:S(2)}) collective-permute-start(bf16[24,32,128]{2,1,0:T(8,128)(2,1)S(1)} %constant_dynamic-update-slice_fusion.b0), channel_id=1, source_target_pairs={{0,24},{8,16},{16,8},{24,0},{32,56},{40,48},{48,40},{56,32},{64,88... | collective-permute-start | bytes 589832 | tf_op jit(solution)/shard_map/ppermute | solution.py:294
  44.5 11.4 %collective-permute-start.10 = (bf16[24,32,128]{2,1,0:T(8,128)(2,1)S(1)}, bf16[24,32,128]{2,1,0:T(8,128)(2,1)S(1)}, u32[]{:S(2)}, u32[]{:S(2)}) collective-permute-start(bf16[24,32,128]{2,1,0:T(8,128)(2,1)S(1)} %constant_dynamic-update-slice_fusion.b0), channel_id=1, source_target_pairs={{0,8},{8,0},{16,24},{24,16},{32,40},{40,32},{48,56},{56,48},{64,72... | collective-permute-start | bytes 589832 | tf_op jit(solution)/shard_map/ppermute | solution.py:294
  44.5 11.4 %collective-permute-start.9 = (bf16[24,32,128]{2,1,0:T(8,128)(2,1)S(1)}, bf16[24,32,128]{2,1,0:T(8,128)(2,1)S(1)}, u32[]{:S(2)}, u32[]{:S(2)}) collective-permute-start(bf16[24,32,128]{2,1,0:T(8,128)(2,1)S(1)} %constant_dynamic-update-slice_fusion.b0), channel_id=1, source_target_pairs={{0,16},{8,24},{16,0},{24,8},{32,48},{40,56},{48,32},{56,40},{64,80... | collective-permute-start | bytes 589832 | tf_op jit(solution)/shard_map/ppermute | solution.py:294
  61.7 11.8 %collective-permute-start.12 = (bf16[64,4096]{1,0:T(8,128)(2,1)S(1)}, bf16[64,4096]{1,0:T(8,128)(2,1)S(1)}, u32[]{:S(2)}, u32[]{:S(2)}) collective-permute-start(bf16[64,4096]{1,0:T(8,128)(2,1)S(1)} %get-tuple-element.39), channel_id=1, source_target_pairs={{0,1},{1,0},{2,3},{3,2},{4,5},{5,4},{6,7},{7,6},{8,9},{9,8},{10,11... | collective-permute-start | bytes 1572872 | tf_op jit(solution)/shard_map/ppermute | solution.py:317
  72.9 5.6 %collective-permute-start.18 = (bf16[128,2048]{1,0:T(8,128)(2,1)S(1)}, bf16[128,2048]{1,0:T(8,128)(2,1)S(1)}, u32[]{:S(2)}, u32[]{:S(2)}) collective-permute-start(bf16[128,2048]{1,0:T(8,128)(2,1)S(1)} %get-tuple-element.48), channel_id=1, source_target_pairs={{0,1},{1,0},{2,3},{3,2},{4,5},{5,4},{6,7},{7,6},{8,9},{9,8},{10,11... | collective-permute-start | bytes 1572872 | tf_op jit(solution)/shard_map/ppermute | solution.py:317
  73.0 6.2 %collective-permute-start.14 = (bf16[128,2048]{1,0:T(8,128)(2,1)S(1)}, bf16[128,2048]{1,0:T(8,128)(2,1)S(1)}, u32[]{:S(2)}, u32[]{:S(2)}) collective-permute-start(bf16[128,2048]{1,0:T(8,128)(2,1)S(1)} %get-tuple-element.44), channel_id=1, source_target_pairs={{0,1},{1,0},{2,3},{3,2},{4,5},{5,4},{6,7},{7,6},{8,9},{9,8},{10,11... | collective-permute-start | bytes 1572872 | tf_op jit(solution)/shard_map/ppermute | solution.py:317
  73.7 8.2 %collective-permute-start.16 = (bf16[64,2048]{1,0:T(8,128)(2,1)S(1)}, bf16[64,2048]{1,0:T(8,128)(2,1)S(1)}, u32[]{:S(2)}, u32[]{:S(2)}) collective-permute-start(bf16[64,2048]{1,0:T(8,128)(2,1)S(1)} %get-tuple-element.51), channel_id=1, source_target_pairs={{0,6},{1,7},{2,0},{3,1},{4,2},{5,3},{6,4},{7,5},{8,14},{9,15},{10,... | collective-permute-start | bytes 786440 | tf_op jit(solution)/shard_map/ppermute | solution.py:320
  76.2 8.7 %collective-permute-start.15 = (bf16[64,2048]{1,0:T(8,128)(2,1)S(1)}, bf16[64,2048]{1,0:T(8,128)(2,1)S(1)}, u32[]{:S(2)}, u32[]{:S(2)}) collective-permute-start(bf16[64,2048]{1,0:T(8,128)(2,1)S(1)} %get-tuple-element.52.after), channel_id=1, source_target_pairs={{0,2},{1,3},{2,4},{3,5},{4,6},{5,7},{6,0},{7,1},{8,10},{9,11},{10,... | collective-permute-start | bytes 786440 | tf_op jit(solution)/shard_map/ppermute | solution.py:320
  78.1 18.1 %collective-permute-start.13 = (bf16[64,4096]{1,0:T(8,128)(2,1)S(1)}, bf16[64,4096]{1,0:T(8,128)(2,1)S(1)}, u32[]{:S(2)}, u32[]{:S(2)}) collective-permute-start(bf16[64,4096]{1,0:T(8,128)(2,1)S(1)} %get-tuple-element.41), channel_id=1, source_target_pairs={{0,1},{1,0},{2,3},{3,2},{4,5},{5,4},{6,7},{7,6},{8,9},{9,8},{10,11... | collective-permute-start | bytes 1572872 | tf_op jit(solution)/shard_map/ppermute | solution.py:317
  78.7 11.9 %collective-permute-start.20 = (bf16[64,2048]{1,0:T(8,128)(2,1)S(1)}, bf16[64,2048]{1,0:T(8,128)(2,1)S(1)}, u32[]{:S(2)}, u32[]{:S(2)}) collective-permute-start(bf16[64,2048]{1,0:T(8,128)(2,1)S(1)} %get-tuple-element.55), channel_id=1, source_target_pairs={{0,2},{1,3},{2,4},{3,5},{4,6},{5,7},{6,0},{7,1},{8,10},{9,11},{10,... | collective-permute-start | bytes 786440 | tf_op jit(solution)/shard_map/ppermute | solution.py:320
  79.2 11.4 %collective-permute-start.19 = (bf16[64,2048]{1,0:T(8,128)(2,1)S(1)}, bf16[64,2048]{1,0:T(8,128)(2,1)S(1)}, u32[]{:S(2)}, u32[]{:S(2)}) collective-permute-start(bf16[64,2048]{1,0:T(8,128)(2,1)S(1)} %get-tuple-element.56), channel_id=1, source_target_pairs={{0,6},{1,7},{2,0},{3,1},{4,2},{5,3},{6,4},{7,5},{8,14},{9,15},{10,... | collective-permute-start | bytes 786440 | tf_op jit(solution)/shard_map/ppermute | solution.py:320
  85.2 8.0 %collective-permute-start.21 = (bf16[64,2048]{1,0:T(8,128)(2,1)S(1)}, bf16[64,2048]{1,0:T(8,128)(2,1)S(1)}, u32[]{:S(2)}, u32[]{:S(2)}) collective-permute-start(bf16[64,2048]{1,0:T(8,128)(2,1)S(1)} %get-tuple-element.53), channel_id=1, source_target_pairs={{0,6},{1,7},{2,0},{3,1},{4,2},{5,3},{6,4},{7,5},{8,14},{9,15},{10,... | collective-permute-start | bytes 786440 | tf_op jit(solution)/shard_map/ppermute | solution.py:320
  85.6 10.6 %collective-permute-start.17 = (bf16[64,2048]{1,0:T(8,128)(2,1)S(1)}, bf16[64,2048]{1,0:T(8,128)(2,1)S(1)}, u32[]{:S(2)}, u32[]{:S(2)}) collective-permute-start(bf16[64,2048]{1,0:T(8,128)(2,1)S(1)} %get-tuple-element.54), channel_id=1, source_target_pairs={{0,2},{1,3},{2,4},{3,5},{4,6},{5,7},{6,0},{7,1},{8,10},{9,11},{10,... | collective-permute-start | bytes 786440 | tf_op jit(solution)/shard_map/ppermute | solution.py:320
  (2 other events, 47.9 us)

commit v7 on v6

--- a/solution.py
+++ b/solution.py
@@ -324,13 +324,14 @@
     far_left = total_of(keep_far[:, :mid], far[:, :mid])
     far_right = total_of(keep_far[:, mid:], far[:, mid:])
     relay_left, relay_right = to_x(far_left, 1), to_x(far_right, -1)
+    direct_right = total_of(keep_below[:, mid:], direct[:HALF])
+    direct_left = total_of(keep_above[:, :mid], direct[HALF:])
+    right_below, left_above = to_x(direct_right, 1), to_x(direct_left, -1)
     keep_own, give_own = call(
         own_kernel, [SMEM, VMEM, VMEM, ANY], [part, part], [], 0.01, "own",
-    )(table, att, w, far_left)
+    )(table, att, w, direct_right)
 
     own = swap(give_own)
-    right_below = to_x(total_of(keep_below[:, mid:], direct[:HALF]), 1)
-    left_above = to_x(total_of(keep_above[:, :mid], direct[HALF:]), -1)
     keep_below, keep_above, relayed, relay_left, relay_right = lax.optimization_barrier(
         (keep_below, keep_above, relayed, relay_left, relay_right))
     left_below = to_x(total_of(keep_below[:, :mid], relayed[:HALF], relay_left), 1)

time: 97.5 us -> 97.5 us (level)
  no operation moved by 1% of the time
where the time goes in v7:
time: 97.5 us; the launch traced here: 97.3 us
  starting transfers between devices  48.3 us (50%)
  waiting for transfers between devices  25.2 us (26%)
  Pallas kernels  22 us (23%)
    ppermute x6, waiting for transfers between devices, to_x(): return lax.ppermute(a, 'head', x_pairs(step))  12.4 us
    all_to_all x1, starting transfers between devices, per_device(): lax.all_to_all(spread, 'ctx', 0, 0, tiled=True).reshape(BLOCKS * 8, HEAD)  12 us
    ppermute x4, starting transfers between devices, swap(): return lax.ppermute(a, 'head', CORE_PAIRS)  9.92 us
    pallas_call x1, Pallas kernels, per_device(): call(early_kernel, [SMEM] * 4 + [ANY] * 6 + [VMEM, ANY, ANY], [((TOKENS,...  8.79 us
    ppermute x5, starting transfers between devices, from_z(): return lax.ppermute(a, 'ctx', z_pairs(-offset))  8.45 us
    all_to_all x1, waiting for transfers between devices, per_device(): lax.all_to_all(spread, 'ctx', 0, 0, tiled=True).reshape(BLOCKS * 8, HEAD)  7.59 us
    ppermute x6, starting transfers between devices, to_x(): return lax.ppermute(a, 'head', x_pairs(step))  6.88 us
    pallas_call x1, Pallas kernels, per_device(): call(late_kernel, [SMEM, SMEM, VMEM, VMEM] + [ANY] * 4 + [VMEM] * 3, [row...  5.74 us
  transfers between devices with their start and end apart: 23, of which 9 were waited for; matrix products, arithmetic and copies ran while one was open for 1% of the time, Pallas kernels for 14%

profile of v7, /device:TPU:1, one launch (start us, length us, event | category | flops | bytes accessed | tf_op | source)
XLA Modules:
  0.0 97.3 jit_solution(5973635812009845016)
XLA Ops:
  0.0 1.7 %spread.1 = bf16[16,2,4,8,128]{4,3,2,1,0:T(8,128)(2,1)} custom-call(bf16[4,16,8,128]{3,2,1,0:T(8,128)(2,1)} %bitcast.18, bf16[4,16,8,128]{3,2,1,0:T(8,128)(2,1)} %bitcast.20), custom_call_target="tpu_custom_call" | custom-call | flops 1000000000 | bytes 1048576 | tf_op jit(solution)/shard_map/spread/pallas_call | solution.py:272
  1.7 12.0 %all-to-all-start = ((bf16[32,32,128]{2,1,0:T(8,128)(2,1)}), bf16[32,32,128]{2,1,0:T(8,128)(2,1)S(1)}, u32[]{:S(2)}, u32[]{:S(2)}) async-start(bf16[32,32,128]{2,1,0:T(8,128)(2,1)} %bitcast.8), calls=%async_computation | async-start | bytes 524288 | tf_op jit(solution)/shard_map/all_to_all | solution.py:277
  13.7 3.1 %collective-permute-start = (bf16[32,32,128]{2,1,0:T(8,128)(2,1)}, bf16[32,32,128]{2,1,0:T(8,128)(2,1)S(1)}, u32[]{:S(2)}, u32[]{:S(2)}) collective-permute-start(bf16[32,32,128]{2,1,0:T(8,128)(2,1)} %bitcast.8), channel_id=1, source_target_pairs={{0,8},{8,16},{16,24},{24,32},{32,40},{40,48},{48,56},{56,64},{64,7... | collective-permute-start | bytes 786440 | tf_op jit(solution)/shard_map/ppermute | solution.py:276
  17.3 7.6 %all-to-all-done = bf16[32,32,128]{2,1,0:T(8,128)(2,1)S(1)} async-done(((bf16[32,32,128]{2,1,0:T(8,128)(2,1)}), bf16[32,32,128]{2,1,0:T(8,128)(2,1)S(1)}, u32[]{:S(2)}, u32[]{:S(2)}) %all-to-all-start) | async-done | bytes 262176 | tf_op jit(solution)/shard_map/all_to_all | solution.py:277
  25.3 1.6 %collective-permute-start.3 = (bf16[24,8,128]{2,1,0:T(8,128)(2,1)S(1)}, bf16[24,8,128]{2,1,0:T(8,128)(2,1)S(1)}, u32[]{:S(2)}, u32[]{:S(2)}) collective-permute-start(bf16[24,8,128]{2,1,0:T(8,128)(2,1)S(1)} %fusion), channel_id=1, source_target_pairs={{0,64},{8,72},{16,80},{24,88},{32,96},{40,104},{48,112},{56,120},{... | collective-permute-start | bytes 147464 | tf_op jit(solution)/shard_map/ppermute | solution.py:285
  26.9 2.1 %collective-permute-start.2 = (bf16[24,8,128]{2,1,0:T(8,128)(2,1)S(1)}, bf16[24,8,128]{2,1,0:T(8,128)(2,1)S(1)}, u32[]{:S(2)}, u32[]{:S(2)}) collective-permute-start(bf16[24,8,128]{2,1,0:T(8,128)(2,1)S(1)} %fusion), channel_id=1, source_target_pairs={{0,128},{8,136},{16,144},{24,152},{32,160},{40,168},{48,176},{56,1... | collective-permute-start | bytes 147464 | tf_op jit(solution)/shard_map/ppermute | solution.py:285
  29.0 2.0 %collective-permute-start.1 = (bf16[24,8,128]{2,1,0:T(8,128)(2,1)S(1)}, bf16[24,8,128]{2,1,0:T(8,128)(2,1)S(1)}, u32[]{:S(2)}, u32[]{:S(2)}) collective-permute-start(bf16[24,8,128]{2,1,0:T(8,128)(2,1)S(1)} %fusion), channel_id=1, source_target_pairs={{0,192},{8,200},{16,208},{24,216},{32,224},{40,232},{48,240},{56,2... | collective-permute-start | bytes 147464 | tf_op jit(solution)/shard_map/ppermute | solution.py:285
  31.2 3.0 %collective-permute-done.2 = bf16[24,8,128]{2,1,0:T(8,128)(2,1)S(1)} collective-permute-done((bf16[24,8,128]{2,1,0:T(8,128)(2,1)S(1)}, bf16[24,8,128]{2,1,0:T(8,128)(2,1)S(1)}, u32[]{:S(2)}, u32[]{:S(2)}) %collective-permute-start.2) | collective-permute-done | bytes 49184 | tf_op jit(solution)/shard_map/ppermute | solution.py:285
  34.9 1.4 %collective-permute-start.6 = (bf16[24,32,128]{2,1,0:T(8,128)(2,1)S(1)}, bf16[24,32,128]{2,1,0:T(8,128)(2,1)S(1)}, u32[]{:S(2)}, u32[]{:S(2)}) collective-permute-start(bf16[24,32,128]{2,1,0:T(8,128)(2,1)S(1)} %pad_maximum_fusion.a0), channel_id=1, source_target_pairs={{0,24},{8,16},{16,8},{24,0},{32,56},{40,48},{48,40},{56,32},{64,88... | collective-permute-start | bytes 589832 | tf_op jit(solution)/shard_map/ppermute | solution.py:293
  36.3 2.6 %collective-permute-start.4 = (bf16[24,32,128]{2,1,0:T(8,128)(2,1)S(1)}, bf16[24,32,128]{2,1,0:T(8,128)(2,1)S(1)}, u32[]{:S(2)}, u32[]{:S(2)}) collective-permute-start(bf16[24,32,128]{2,1,0:T(8,128)(2,1)S(1)} %pad_maximum_fusion.a0), channel_id=1, source_target_pairs={{0,16},{8,24},{16,0},{24,8},{32,48},{40,56},{48,32},{56,40},{64,80... | collective-permute-start | bytes 589832 | tf_op jit(solution)/shard_map/ppermute | solution.py:293
  38.8 2.7 %collective-permute-start.8 = (bf16[24,16,128]{2,1,0:T(8,128)(2,1)S(1)}, bf16[24,16,128]{2,1,0:T(8,128)(2,1)S(1)}, u32[]{:S(2)}, u32[]{:S(2)}) collective-permute-start(bf16[24,16,128]{2,1,0:T(8,128)(2,1)S(1)} %get-tuple-element.57), channel_id=1, source_target_pairs={{0,224},{8,232},{16,240},{24,248},{32,0},{40,8},{48,16},{56,24},{6... | collective-permute-start | bytes 294920 | tf_op jit(solution)/shard_map/ppermute | solution.py:285
  41.5 1.6 %collective-permute-done.8 = bf16[24,16,128]{2,1,0:T(8,128)(2,1)S(1)} collective-permute-done((bf16[24,16,128]{2,1,0:T(8,128)(2,1)S(1)}, bf16[24,16,128]{2,1,0:T(8,128)(2,1)S(1)}, u32[]{:S(2)}, u32[]{:S(2)}) %collective-permute-start.8) | collective-permute-done | bytes 98336 | tf_op jit(solution)/shard_map/ppermute | solution.py:285
  44.5 2.6 %collective-permute-start.9 = (bf16[24,32,128]{2,1,0:T(8,128)(2,1)S(1)}, bf16[24,32,128]{2,1,0:T(8,128)(2,1)S(1)}, u32[]{:S(2)}, u32[]{:S(2)}) collective-permute-start(bf16[24,32,128]{2,1,0:T(8,128)(2,1)S(1)} %constant_dynamic-update-slice_fusion.b0), channel_id=1, source_target_pairs={{0,16},{8,24},{16,0},{24,8},{32,48},{40,56},{48,32},{56,40},{64,80... | collective-permute-start | bytes 589832 | tf_op jit(solution)/shard_map/ppermute | solution.py:294
  47.1 8.8 %early.1 = (f32[512,1024]{1,0:T(8,128)S(1)}, f32[512,1024]{1,0:T(8,128)S(1)}, f32[512,1024]{1,0:T(8,128)S(1)}, bf16[1024,4096]{1,0:T(8,128)(2,1)S(1)}, bf16[512,1024]{1,0:T(8,128)(2,1)S(1)}) custom-call(s32[134]{0:T(256)S(1)} %concatenate.15.table, s32[8,8]{1,0:T(8,128)S(1)} %copy-done, s32[8,3]{1,0:T(8,128)S(1)} %copy.10.slash, f32[8]{0:T(128)S(1)} %copy-done.1, ...), custom_call_target="tpu_custom_call" | custom-call | flops 8000000000 | bytes 8388608 | tf_op jit(solution)/shard_map/early/pallas_call | solution.py:302
  55.9 5.7 %late.1 = (bf16[512,1024]{1,0:T(8,128)(2,1)S(1)}, bf16[64,4096]{1,0:T(8,128)(2,1)S(1)}, bf16[64,4096]{1,0:T(8,128)(2,1)S(1)}) custom-call(s32[134]{0:T(256)S(1)} %concatenate.15.table, s32[8,8]{1,0:T(8,128)S(1)} %copy-done, bf16[512,1024]{1,0:T(8,128)(2,1)S(1)} %get-tuple-element.32.qs, bf16[1024,4096]{1,0:T(8,128)(2,1)S(1)} %get-tuple-element.33.w, ...), custom_call_target="tpu_custom_call" | custom-call | flops 10000000 | bytes 10485 | tf_op jit(solution)/shard_map/late/pallas_call | solution.py:308
  61.7 8.3 %collective-permute-start.15 = (bf16[64,4096]{1,0:T(8,128)(2,1)S(1)}, bf16[64,4096]{1,0:T(8,128)(2,1)S(1)}, u32[]{:S(2)}, u32[]{:S(2)}) collective-permute-start(bf16[64,4096]{1,0:T(8,128)(2,1)S(1)} %get-tuple-element.45), channel_id=1, source_target_pairs={{0,1},{1,0},{2,3},{3,2},{4,5},{5,4},{6,7},{7,6},{8,9},{9,8},{10,11... | collective-permute-start | bytes 1572872 | tf_op jit(solution)/shard_map/ppermute | solution.py:317
  70.0 2.9 %sides.1 = (bf16[64,4096]{1,0:T(8,128)(2,1)S(1)}, bf16[64,4096]{1,0:T(8,128)(2,1)S(1)}, bf16[128,2048]{1,0:T(8,128)(2,1)S(1)}, bf16[128,2048]{1,0:T(8,128)(2,1)S(1)}) custom-call(s32[134]{0:T(256)S(1)} %concatenate.15.table, bf16[512,1024]{1,0:T(8,128)(2,1)S(1)} %get-tuple-element.37.att, bf16[1024,4096]{1,0:T(8,128)(2,1)S(1)} %get-tuple-element.33.w), custom_call_target="tpu_custom_call" | custom-call | flops 10000000 | bytes 10485 | tf_op jit(solution)/shard_map/sides/pallas_call | solution.py:313
  73.7 2.6 %collective-permute-start.17 = (bf16[64,2048]{1,0:T(8,128)(2,1)S(1)}, bf16[64,2048]{1,0:T(8,128)(2,1)S(1)}, u32[]{:S(2)}, u32[]{:S(2)}) collective-permute-start(bf16[64,2048]{1,0:T(8,128)(2,1)S(1)} %get-tuple-element.51), channel_id=1, source_target_pairs={{0,6},{1,7},{2,0},{3,1},{4,2},{5,3},{6,4},{7,5},{8,14},{9,15},{10,... | collective-permute-start | bytes 786440 | tf_op jit(solution)/shard_map/ppermute | solution.py:320
  76.4 2.8 %collective-permute-start.19 = (bf16[64,2048]{1,0:T(8,128)(2,1)S(1)}, bf16[64,2048]{1,0:T(8,128)(2,1)S(1)}, u32[]{:S(2)}, u32[]{:S(2)}) collective-permute-start(bf16[64,2048]{1,0:T(8,128)(2,1)S(1)} %get-tuple-element.55), channel_id=1, source_target_pairs={{0,6},{1,7},{2,0},{3,1},{4,2},{5,3},{6,4},{7,5},{8,14},{9,15},{10,... | collective-permute-start | bytes 786440 | tf_op jit(solution)/shard_map/ppermute | solution.py:320
  79.1 1.8 %own.1 = (bf16[64,4096]{1,0:T(8,128)(2,1)S(1)}, bf16[64,4096]{1,0:T(8,128)(2,1)S(1)}) custom-call(s32[134]{0:T(256)S(1)} %concatenate.15.table, bf16[512,1024]{1,0:T(8,128)(2,1)S(1)} %get-tuple-element.37.att, bf16[1024,4096]{1,0:T(8,128)(2,1)S(1)} %get-tuple-element.33.w, bf16[64,2048]{1,0:T(8,128)(2,1)S(1)} %get-tuple-element.56.after), custom_call_target="tpu_custom_call" | custom-call | flops 10000000 | bytes 10485 | tf_op jit(solution)/shard_map/own/pallas_call | solution.py:330
  82.0 3.0 %collective-permute-done.16 = bf16[64,2048]{1,0:T(8,128)(2,1)S(1)} collective-permute-done((bf16[64,2048]{1,0:T(8,128)(2,1)S(1)}, bf16[64,2048]{1,0:T(8,128)(2,1)S(1)}, u32[]{:S(2)}, u32[]{:S(2)}) %collective-permute-start.16) | collective-permute-done | bytes 262176 | tf_op jit(solution)/shard_map/ppermute | solution.py:320
  87.5 3.1 %collective-permute-done.20.right_below = bf16[64,2048]{1,0:T(8,128)(2,1)S(1)} collective-permute-done((bf16[64,2048]{1,0:T(8,128)(2,1)S(1)}, bf16[64,2048]{1,0:T(8,128)(2,1)S(1)}, u32[]{:S(2)}, u32[]{:S(2)}) %collective-permute-start.20) | collective-permute-done | bytes 262176 | tf_op jit(solution)/shard_map/ppermute | solution.py:320
  90.6 2.5 %collective-permute-done.21.right_above = bf16[64,2048]{1,0:T(8,128)(2,1)S(1)} collective-permute-done((bf16[64,2048]{1,0:T(8,128)(2,1)S(1)}, bf16[64,2048]{1,0:T(8,128)(2,1)S(1)}, u32[]{:S(2)}, u32[]{:S(2)}) %collective-permute-start.21) | collective-permute-done | bytes 262176 | tf_op jit(solution)/shard_map/ppermute | solution.py:320
  93.1 3.1 %collective-permute-done.18.left_below = bf16[64,2048]{1,0:T(8,128)(2,1)S(1)} collective-permute-done((bf16[64,2048]{1,0:T(8,128)(2,1)S(1)}, bf16[64,2048]{1,0:T(8,128)(2,1)S(1)}, u32[]{:S(2)}, u32[]{:S(2)}) %collective-permute-start.18) | collective-permute-done | bytes 262176 | tf_op jit(solution)/shard_map/ppermute | solution.py:320
  (52 shorter events, 8.5 us)
Async XLA Ops:
  1.7 45.4 %copy-start.1 = (f32[8]{0:T(128)S(1)}, f32[8]{0:T(128)}, u32[]{:S(2)}) copy-start(f32[8]{0:T(128)} %sink.1) | copy-start | bytes 100
  1.7 23.2 %all-to-all-start = ((bf16[32,32,128]{2,1,0:T(8,128)(2,1)}), bf16[32,32,128]{2,1,0:T(8,128)(2,1)S(1)}, u32[]{:S(2)}, u32[]{:S(2)}) async-start(bf16[32,32,128]{2,1,0:T(8,128)(2,1)} %bitcast.8), calls=%async_computation | async-start | bytes 524288 | tf_op jit(solution)/shard_map/all_to_all | solution.py:277
  13.7 17.4 %collective-permute-start = (bf16[32,32,128]{2,1,0:T(8,128)(2,1)}, bf16[32,32,128]{2,1,0:T(8,128)(2,1)S(1)}, u32[]{:S(2)}, u32[]{:S(2)}) collective-permute-start(bf16[32,32,128]{2,1,0:T(8,128)(2,1)} %bitcast.8), channel_id=1, source_target_pairs={{0,8},{8,16},{16,24},{24,32},{32,40},{40,48},{48,56},{56,64},{64,7... | collective-permute-start | bytes 786440 | tf_op jit(solution)/shard_map/ppermute | solution.py:276
  25.3 5.9 %collective-permute-start.3 = (bf16[24,8,128]{2,1,0:T(8,128)(2,1)S(1)}, bf16[24,8,128]{2,1,0:T(8,128)(2,1)S(1)}, u32[]{:S(2)}, u32[]{:S(2)}) collective-permute-start(bf16[24,8,128]{2,1,0:T(8,128)(2,1)S(1)} %fusion), channel_id=1, source_target_pairs={{0,64},{8,72},{16,80},{24,88},{32,96},{40,104},{48,112},{56,120},{... | collective-permute-start | bytes 147464 | tf_op jit(solution)/shard_map/ppermute | solution.py:285
  26.9 7.3 %collective-permute-start.2 = (bf16[24,8,128]{2,1,0:T(8,128)(2,1)S(1)}, bf16[24,8,128]{2,1,0:T(8,128)(2,1)S(1)}, u32[]{:S(2)}, u32[]{:S(2)}) collective-permute-start(bf16[24,8,128]{2,1,0:T(8,128)(2,1)S(1)} %fusion), channel_id=1, source_target_pairs={{0,128},{8,136},{16,144},{24,152},{32,160},{40,168},{48,176},{56,1... | collective-permute-start | bytes 147464 | tf_op jit(solution)/shard_map/ppermute | solution.py:285
  29.0 5.7 %collective-permute-start.1 = (bf16[24,8,128]{2,1,0:T(8,128)(2,1)S(1)}, bf16[24,8,128]{2,1,0:T(8,128)(2,1)S(1)}, u32[]{:S(2)}, u32[]{:S(2)}) collective-permute-start(bf16[24,8,128]{2,1,0:T(8,128)(2,1)S(1)} %fusion), channel_id=1, source_target_pairs={{0,192},{8,200},{16,208},{24,216},{32,224},{40,232},{48,240},{56,2... | collective-permute-start | bytes 147464 | tf_op jit(solution)/shard_map/ppermute | solution.py:285
  34.8 6.7 %collective-permute-start.7 = (bf16[24,16,128]{2,1,0:T(8,128)(2,1)S(1)}, bf16[24,16,128]{2,1,0:T(8,128)(2,1)S(1)}, u32[]{:S(2)}, u32[]{:S(2)}) collective-permute-start(bf16[24,16,128]{2,1,0:T(8,128)(2,1)S(1)} %get-tuple-element.58), channel_id=1, source_target_pairs={{0,32},{8,40},{16,48},{24,56},{32,64},{40,72},{48,80},{56,88},{64,... | collective-permute-start | bytes 294920 | tf_op jit(solution)/shard_map/ppermute | solution.py:285
  34.9 9.6 %collective-permute-start.6 = (bf16[24,32,128]{2,1,0:T(8,128)(2,1)S(1)}, bf16[24,32,128]{2,1,0:T(8,128)(2,1)S(1)}, u32[]{:S(2)}, u32[]{:S(2)}) collective-permute-start(bf16[24,32,128]{2,1,0:T(8,128)(2,1)S(1)} %pad_maximum_fusion.a0), channel_id=1, source_target_pairs={{0,24},{8,16},{16,8},{24,0},{32,56},{40,48},{48,40},{56,32},{64,88... | collective-permute-start | bytes 589832 | tf_op jit(solution)/shard_map/ppermute | solution.py:293
  36.3 10.8 %collective-permute-start.5 = (bf16[24,32,128]{2,1,0:T(8,128)(2,1)S(1)}, bf16[24,32,128]{2,1,0:T(8,128)(2,1)S(1)}, u32[]{:S(2)}, u32[]{:S(2)}) collective-permute-start(bf16[24,32,128]{2,1,0:T(8,128)(2,1)S(1)} %pad_maximum_fusion.a0), channel_id=1, source_target_pairs={{0,8},{8,0},{16,24},{24,16},{32,40},{40,32},{48,56},{56,48},{64,72... | collective-permute-start | bytes 589832 | tf_op jit(solution)/shard_map/ppermute | solution.py:293
  36.3 10.8 %collective-permute-start.4 = (bf16[24,32,128]{2,1,0:T(8,128)(2,1)S(1)}, bf16[24,32,128]{2,1,0:T(8,128)(2,1)S(1)}, u32[]{:S(2)}, u32[]{:S(2)}) collective-permute-start(bf16[24,32,128]{2,1,0:T(8,128)(2,1)S(1)} %pad_maximum_fusion.a0), channel_id=1, source_target_pairs={{0,16},{8,24},{16,0},{24,8},{32,48},{40,56},{48,32},{56,40},{64,80... | collective-permute-start | bytes 589832 | tf_op jit(solution)/shard_map/ppermute | solution.py:293
  38.8 4.3 %collective-permute-start.8 = (bf16[24,16,128]{2,1,0:T(8,128)(2,1)S(1)}, bf16[24,16,128]{2,1,0:T(8,128)(2,1)S(1)}, u32[]{:S(2)}, u32[]{:S(2)}) collective-permute-start(bf16[24,16,128]{2,1,0:T(8,128)(2,1)S(1)} %get-tuple-element.57), channel_id=1, source_target_pairs={{0,224},{8,232},{16,240},{24,248},{32,0},{40,8},{48,16},{56,24},{6... | collective-permute-start | bytes 294920 | tf_op jit(solution)/shard_map/ppermute | solution.py:285
  43.2 12.8 %collective-permute-start.11 = (bf16[24,32,128]{2,1,0:T(8,128)(2,1)S(1)}, bf16[24,32,128]{2,1,0:T(8,128)(2,1)S(1)}, u32[]{:S(2)}, u32[]{:S(2)}) collective-permute-start(bf16[24,32,128]{2,1,0:T(8,128)(2,1)S(1)} %constant_dynamic-update-slice_fusion.b0), channel_id=1, source_target_pairs={{0,24},{8,16},{16,8},{24,0},{32,56},{40,48},{48,40},{56,32},{64,88... | collective-permute-start | bytes 589832 | tf_op jit(solution)/shard_map/ppermute | solution.py:294
  44.5 11.4 %collective-permute-start.10 = (bf16[24,32,128]{2,1,0:T(8,128)(2,1)S(1)}, bf16[24,32,128]{2,1,0:T(8,128)(2,1)S(1)}, u32[]{:S(2)}, u32[]{:S(2)}) collective-permute-start(bf16[24,32,128]{2,1,0:T(8,128)(2,1)S(1)} %constant_dynamic-update-slice_fusion.b0), channel_id=1, source_target_pairs={{0,8},{8,0},{16,24},{24,16},{32,40},{40,32},{48,56},{56,48},{64,72... | collective-permute-start | bytes 589832 | tf_op jit(solution)/shard_map/ppermute | solution.py:294
  44.5 11.4 %collective-permute-start.9 = (bf16[24,32,128]{2,1,0:T(8,128)(2,1)S(1)}, bf16[24,32,128]{2,1,0:T(8,128)(2,1)S(1)}, u32[]{:S(2)}, u32[]{:S(2)}) collective-permute-start(bf16[24,32,128]{2,1,0:T(8,128)(2,1)S(1)} %constant_dynamic-update-slice_fusion.b0), channel_id=1, source_target_pairs={{0,16},{8,24},{16,0},{24,8},{32,48},{40,56},{48,32},{56,40},{64,80... | collective-permute-start | bytes 589832 | tf_op jit(solution)/shard_map/ppermute | solution.py:294
  61.7 11.8 %collective-permute-start.15 = (bf16[64,4096]{1,0:T(8,128)(2,1)S(1)}, bf16[64,4096]{1,0:T(8,128)(2,1)S(1)}, u32[]{:S(2)}, u32[]{:S(2)}) collective-permute-start(bf16[64,4096]{1,0:T(8,128)(2,1)S(1)} %get-tuple-element.45), channel_id=1, source_target_pairs={{0,1},{1,0},{2,3},{3,2},{4,5},{5,4},{6,7},{7,6},{8,9},{9,8},{10,11... | collective-permute-start | bytes 1572872 | tf_op jit(solution)/shard_map/ppermute | solution.py:317
  72.9 3.3 %collective-permute-start.12 = (bf16[128,2048]{1,0:T(8,128)(2,1)S(1)}, bf16[128,2048]{1,0:T(8,128)(2,1)S(1)}, u32[]{:S(2)}, u32[]{:S(2)}) collective-permute-start(bf16[128,2048]{1,0:T(8,128)(2,1)S(1)} %get-tuple-element.39), channel_id=1, source_target_pairs={{0,1},{1,0},{2,3},{3,2},{4,5},{5,4},{6,7},{7,6},{8,9},{9,8},{10,11... | collective-permute-start | bytes 1572872 | tf_op jit(solution)/shard_map/ppermute | solution.py:317
  73.0 7.9 %collective-permute-start.14 = (bf16[128,2048]{1,0:T(8,128)(2,1)S(1)}, bf16[128,2048]{1,0:T(8,128)(2,1)S(1)}, u32[]{:S(2)}, u32[]{:S(2)}) collective-permute-start(bf16[128,2048]{1,0:T(8,128)(2,1)S(1)} %get-tuple-element.43), channel_id=1, source_target_pairs={{0,1},{1,0},{2,3},{3,2},{4,5},{5,4},{6,7},{7,6},{8,9},{9,8},{10,11... | collective-permute-start | bytes 1572872 | tf_op jit(solution)/shard_map/ppermute | solution.py:317
  73.7 8.3 %collective-permute-start.17 = (bf16[64,2048]{1,0:T(8,128)(2,1)S(1)}, bf16[64,2048]{1,0:T(8,128)(2,1)S(1)}, u32[]{:S(2)}, u32[]{:S(2)}) collective-permute-start(bf16[64,2048]{1,0:T(8,128)(2,1)S(1)} %get-tuple-element.51), channel_id=1, source_target_pairs={{0,6},{1,7},{2,0},{3,1},{4,2},{5,3},{6,4},{7,5},{8,14},{9,15},{10,... | collective-permute-start | bytes 786440 | tf_op jit(solution)/shard_map/ppermute | solution.py:320
  76.2 8.7 %collective-permute-start.16 = (bf16[64,2048]{1,0:T(8,128)(2,1)S(1)}, bf16[64,2048]{1,0:T(8,128)(2,1)S(1)}, u32[]{:S(2)}, u32[]{:S(2)}) collective-permute-start(bf16[64,2048]{1,0:T(8,128)(2,1)S(1)} %get-tuple-element.52), channel_id=1, source_target_pairs={{0,2},{1,3},{2,4},{3,5},{4,6},{5,7},{6,0},{7,1},{8,10},{9,11},{10,... | collective-permute-start | bytes 786440 | tf_op jit(solution)/shard_map/ppermute | solution.py:320
  76.4 11.1 %collective-permute-start.19 = (bf16[64,2048]{1,0:T(8,128)(2,1)S(1)}, bf16[64,2048]{1,0:T(8,128)(2,1)S(1)}, u32[]{:S(2)}, u32[]{:S(2)}) collective-permute-start(bf16[64,2048]{1,0:T(8,128)(2,1)S(1)} %get-tuple-element.55), channel_id=1, source_target_pairs={{0,6},{1,7},{2,0},{3,1},{4,2},{5,3},{6,4},{7,5},{8,14},{9,15},{10,... | collective-permute-start | bytes 786440 | tf_op jit(solution)/shard_map/ppermute | solution.py:320
  79.1 11.5 %collective-permute-start.20 = (bf16[64,2048]{1,0:T(8,128)(2,1)S(1)}, bf16[64,2048]{1,0:T(8,128)(2,1)S(1)}, u32[]{:S(2)}, u32[]{:S(2)}) collective-permute-start(bf16[64,2048]{1,0:T(8,128)(2,1)S(1)} %get-tuple-element.56.after), channel_id=1, source_target_pairs={{0,2},{1,3},{2,4},{3,5},{4,6},{5,7},{6,0},{7,1},{8,10},{9,11},{10,... | collective-permute-start | bytes 786440 | tf_op jit(solution)/shard_map/ppermute | solution.py:320
  81.0 15.2 %collective-permute-start.13 = (bf16[64,4096]{1,0:T(8,128)(2,1)S(1)}, bf16[64,4096]{1,0:T(8,128)(2,1)S(1)}, u32[]{:S(2)}, u32[]{:S(2)}) collective-permute-start(bf16[64,4096]{1,0:T(8,128)(2,1)S(1)} %get-tuple-element.41), channel_id=1, source_target_pairs={{0,1},{1,0},{2,3},{3,2},{4,5},{5,4},{6,7},{7,6},{8,9},{9,8},{10,11... | collective-permute-start | bytes 1572872 | tf_op jit(solution)/shard_map/ppermute | solution.py:317
  85.2 7.9 %collective-permute-start.21 = (bf16[64,2048]{1,0:T(8,128)(2,1)S(1)}, bf16[64,2048]{1,0:T(8,128)(2,1)S(1)}, u32[]{:S(2)}, u32[]{:S(2)}) collective-permute-start(bf16[64,2048]{1,0:T(8,128)(2,1)S(1)} %get-tuple-element.53), channel_id=1, source_target_pairs={{0,6},{1,7},{2,0},{3,1},{4,2},{5,3},{6,4},{7,5},{8,14},{9,15},{10,... | collective-permute-start | bytes 786440 | tf_op jit(solution)/shard_map/ppermute | solution.py:320
  85.6 10.6 %collective-permute-start.18 = (bf16[64,2048]{1,0:T(8,128)(2,1)S(1)}, bf16[64,2048]{1,0:T(8,128)(2,1)S(1)}, u32[]{:S(2)}, u32[]{:S(2)}) collective-permute-start(bf16[64,2048]{1,0:T(8,128)(2,1)S(1)} %get-tuple-element.54), channel_id=1, source_target_pairs={{0,2},{1,3},{2,4},{3,5},{4,6},{5,7},{6,0},{7,1},{8,10},{9,11},{10,... | collective-permute-start | bytes 786440 | tf_op jit(solution)/shard_map/ppermute | solution.py:320
  (2 other events, 47.9 us)

commit v8 on v7

--- a/solution.py
+++ b/solution.py
@@ -60,8 +60,7 @@
     z, y_half = table[META + 3], table[META + 4]
     n = lax.broadcasted_iota(jnp.int32, (1, HALF), 1)
     part, inner, row = n // 32, (n // 8) % 4, n % 8
-    step = jnp.where(inner < 2, -1 - 2 * inner, 2 * inner - 3) if late else 2 * inner
-    z_of = (z + step + Z) % Z
+    z_of = ((z ^ int(late)) + 2 * inner) % Z
     return (z_of * 2 + (y_half ^ part)) * 8 + row
 
 
@@ -287,9 +286,7 @@
     z2, z4, z6 = from_z(mine, 2), from_z(mine, 4), from_z(mine, 6)
     prev, z2, z4, z6 = lax.optimization_barrier((prev, z2, z4, z6))
     a0 = jnp.concatenate([mine, z2, z4, z6], axis=1)
-    low = from_z(jnp.concatenate([mine, z6], axis=1), -1)
-    high = from_z(jnp.concatenate([mine, z2], axis=1), 1)
-    b0 = jnp.concatenate([low, high], axis=1)
+    b0 = lax.ppermute(a0, "ctx", [(Y * z + y, Y * (z ^ 1) + y) for z in range(Z) for y in range(Y)])
     a1, a2, a3 = [lax.ppermute(a0, "ctx", y_pairs(f)) for f in (1, 2, 3)]
     b1, b2, b3 = [lax.ppermute(b0, "ctx", y_pairs(f)) for f in (1, 2, 3)]
 

time: 97.5 us -> 96.2 us (0.987)
  starting transfers between devices: 48.3 us -> 46.9 us
    ppermute x5 -> x3, starting transfers between devices: 8.45 us -> 5.71 us  [from_z(): return lax.ppermute(a, 'ctx', z_pairs(-offset))]
    ppermute x5 -> x3, waiting for transfers between devices: 5.18 us -> 3.72 us  [from_z(): return lax.ppermute(a, 'ctx', z_pairs(-offset))]
    ppermute x4, starting transfers between devices: 9.92 us -> 11.3 us  [swap(): return lax.ppermute(a, 'head', CORE_PAIRS)]
  transfers between devices with their start and end apart: 23 -> 22, of which waited for: 9 -> 11; matrix products, arithmetic and copies ran while one was open for 1% -> 1% of each run, Pallas kernels for 14% -> 14%
where the time goes in v8:
time: 96.2 us; the launch traced here: 96 us
  starting transfers between devices  46.9 us (49%)
  waiting for transfers between devices  25.4 us (26%)
  Pallas kernels  22 us (23%)
    ppermute x6, waiting for transfers between devices, to_x(): return lax.ppermute(a, 'head', x_pairs(step))  12.4 us
    all_to_all x1, starting transfers between devices, per_device(): lax.all_to_all(spread, 'ctx', 0, 0, tiled=True).reshape(BLOCKS * 8, HEAD)  12 us
    ppermute x4, starting transfers between devices, swap(): return lax.ppermute(a, 'head', CORE_PAIRS)  11.3 us
    pallas_call x1, Pallas kernels, per_device(): call(early_kernel, [SMEM] * 4 + [ANY] * 6 + [VMEM, ANY, ANY], [((TOKENS,...  8.77 us
    all_to_all x1, waiting for transfers between devices, per_device(): lax.all_to_all(spread, 'ctx', 0, 0, tiled=True).reshape(BLOCKS * 8, HEAD)  7.59 us
    ppermute x6, starting transfers between devices, to_x(): return lax.ppermute(a, 'head', x_pairs(step))  6.87 us
    pallas_call x1, Pallas kernels, per_device(): call(late_kernel, [SMEM, SMEM, VMEM, VMEM] + [ANY] * 4 + [VMEM] * 3, [row...  5.72 us
    ppermute x3, starting transfers between devices, from_z(): return lax.ppermute(a, 'ctx', z_pairs(-offset))  5.71 us
  transfers between devices with their start and end apart: 22, of which 11 were waited for; matrix products, arithmetic and copies ran while one was open for 1% of the time, Pallas kernels for 14%

profile of v8, /device:TPU:1, one launch (start us, length us, event | category | flops | bytes accessed | tf_op | source)
XLA Modules:
  0.0 96.0 jit_solution(1198278268938230931)
XLA Ops:
  0.0 1.7 %spread.1 = bf16[16,2,4,8,128]{4,3,2,1,0:T(8,128)(2,1)} custom-call(bf16[4,16,8,128]{3,2,1,0:T(8,128)(2,1)} %bitcast.18, bf16[4,16,8,128]{3,2,1,0:T(8,128)(2,1)} %bitcast.20), custom_call_target="tpu_custom_call" | custom-call | flops 1000000000 | bytes 1048576 | tf_op jit(solution)/shard_map/spread/pallas_call | solution.py:271
  1.7 12.0 %all-to-all-start = ((bf16[32,32,128]{2,1,0:T(8,128)(2,1)}), bf16[32,32,128]{2,1,0:T(8,128)(2,1)S(1)}, u32[]{:S(2)}, u32[]{:S(2)}) async-start(bf16[32,32,128]{2,1,0:T(8,128)(2,1)} %bitcast.8), calls=%async_computation | async-start | bytes 524288 | tf_op jit(solution)/shard_map/all_to_all | solution.py:276
  13.7 3.1 %collective-permute-start = (bf16[32,32,128]{2,1,0:T(8,128)(2,1)}, bf16[32,32,128]{2,1,0:T(8,128)(2,1)S(1)}, u32[]{:S(2)}, u32[]{:S(2)}) collective-permute-start(bf16[32,32,128]{2,1,0:T(8,128)(2,1)} %bitcast.8), channel_id=1, source_target_pairs={{0,8},{8,16},{16,24},{24,32},{32,40},{40,48},{48,56},{56,64},{64,7... | collective-permute-start | bytes 786440 | tf_op jit(solution)/shard_map/ppermute | solution.py:275
  17.3 7.6 %all-to-all-done = bf16[32,32,128]{2,1,0:T(8,128)(2,1)S(1)} async-done(((bf16[32,32,128]{2,1,0:T(8,128)(2,1)}), bf16[32,32,128]{2,1,0:T(8,128)(2,1)S(1)}, u32[]{:S(2)}, u32[]{:S(2)}) %all-to-all-start) | async-done | bytes 262176 | tf_op jit(solution)/shard_map/all_to_all | solution.py:276
  25.3 1.6 %collective-permute-start.3 = (bf16[24,8,128]{2,1,0:T(8,128)(2,1)S(1)}, bf16[24,8,128]{2,1,0:T(8,128)(2,1)S(1)}, u32[]{:S(2)}, u32[]{:S(2)}) collective-permute-start(bf16[24,8,128]{2,1,0:T(8,128)(2,1)S(1)} %fusion), channel_id=1, source_target_pairs={{0,64},{8,72},{16,80},{24,88},{32,96},{40,104},{48,112},{56,120},{... | collective-permute-start | bytes 147464 | tf_op jit(solution)/shard_map/ppermute | solution.py:284
  26.9 2.1 %collective-permute-start.2 = (bf16[24,8,128]{2,1,0:T(8,128)(2,1)S(1)}, bf16[24,8,128]{2,1,0:T(8,128)(2,1)S(1)}, u32[]{:S(2)}, u32[]{:S(2)}) collective-permute-start(bf16[24,8,128]{2,1,0:T(8,128)(2,1)S(1)} %fusion), channel_id=1, source_target_pairs={{0,128},{8,136},{16,144},{24,152},{32,160},{40,168},{48,176},{56,1... | collective-permute-start | bytes 147464 | tf_op jit(solution)/shard_map/ppermute | solution.py:284
  29.0 2.0 %collective-permute-start.1 = (bf16[24,8,128]{2,1,0:T(8,128)(2,1)S(1)}, bf16[24,8,128]{2,1,0:T(8,128)(2,1)S(1)}, u32[]{:S(2)}, u32[]{:S(2)}) collective-permute-start(bf16[24,8,128]{2,1,0:T(8,128)(2,1)S(1)} %fusion), channel_id=1, source_target_pairs={{0,192},{8,200},{16,208},{24,216},{32,224},{40,232},{48,240},{56,2... | collective-permute-start | bytes 147464 | tf_op jit(solution)/shard_map/ppermute | solution.py:284
  31.0 3.1 %collective-permute-done.2 = bf16[24,8,128]{2,1,0:T(8,128)(2,1)S(1)} collective-permute-done((bf16[24,8,128]{2,1,0:T(8,128)(2,1)S(1)}, bf16[24,8,128]{2,1,0:T(8,128)(2,1)S(1)}, u32[]{:S(2)}, u32[]{:S(2)}) %collective-permute-start.2) | collective-permute-done | bytes 49184 | tf_op jit(solution)/shard_map/ppermute | solution.py:284
  34.9 1.4 %collective-permute-start.6 = (bf16[24,32,128]{2,1,0:T(8,128)(2,1)S(1)}, bf16[24,32,128]{2,1,0:T(8,128)(2,1)S(1)}, u32[]{:S(2)}, u32[]{:S(2)}) collective-permute-start(bf16[24,32,128]{2,1,0:T(8,128)(2,1)S(1)} %pad_maximum_fusion.a0), channel_id=1, source_target_pairs={{0,24},{8,16},{16,8},{24,0},{32,56},{40,48},{48,40},{56,32},{64,88... | collective-permute-start | bytes 589832 | tf_op jit(solution)/shard_map/ppermute | solution.py:290
  36.3 2.6 %collective-permute-start.4 = (bf16[24,32,128]{2,1,0:T(8,128)(2,1)S(1)}, bf16[24,32,128]{2,1,0:T(8,128)(2,1)S(1)}, u32[]{:S(2)}, u32[]{:S(2)}) collective-permute-start(bf16[24,32,128]{2,1,0:T(8,128)(2,1)S(1)} %pad_maximum_fusion.a0), channel_id=1, source_target_pairs={{0,16},{8,24},{16,0},{24,8},{32,48},{40,56},{48,32},{56,40},{64,80... | collective-permute-start | bytes 589832 | tf_op jit(solution)/shard_map/ppermute | solution.py:290
  39.8 1.3 %collective-permute-start.10 = (bf16[24,32,128]{2,1,0:T(8,128)(2,1)S(1)}, bf16[24,32,128]{2,1,0:T(8,128)(2,1)S(1)}, u32[]{:S(2)}, u32[]{:S(2)}) collective-permute-start(bf16[24,32,128]{2,1,0:T(8,128)(2,1)S(1)} %collective-permute-done.7.b0), channel_id=1, source_target_pairs={{0,24},{8,16},{16,8},{24,0},{32,56},{40,48},{48,40},{56,32},{64,88... | collective-permute-start | bytes 589832 | tf_op jit(solution)/shard_map/ppermute | solution.py:291
  41.1 2.6 %collective-permute-start.8 = (bf16[24,32,128]{2,1,0:T(8,128)(2,1)S(1)}, bf16[24,32,128]{2,1,0:T(8,128)(2,1)S(1)}, u32[]{:S(2)}, u32[]{:S(2)}) collective-permute-start(bf16[24,32,128]{2,1,0:T(8,128)(2,1)S(1)} %collective-permute-done.7.b0), channel_id=1, source_target_pairs={{0,16},{8,24},{16,0},{24,8},{32,48},{40,56},{48,32},{56,40},{64,80... | collective-permute-start | bytes 589832 | tf_op jit(solution)/shard_map/ppermute | solution.py:291
  44.1 8.8 %early.1 = (f32[512,1024]{1,0:T(8,128)S(1)}, f32[512,1024]{1,0:T(8,128)S(1)}, f32[512,1024]{1,0:T(8,128)S(1)}, bf16[1024,4096]{1,0:T(8,128)(2,1)S(1)}, bf16[512,1024]{1,0:T(8,128)(2,1)S(1)}) custom-call(s32[134]{0:T(256)S(1)} %concatenate.6.table, s32[8,8]{1,0:T(8,128)S(1)} %copy-done, s32[8,3]{1,0:T(8,128)S(1)} %copy.10.slash, f32[8]{0:T(128)S(1)} %copy-done.1, ...), custom_call_target="tpu_custom_call" | custom-call | flops 8000000000 | bytes 8388608 | tf_op jit(solution)/shard_map/early/pallas_call | solution.py:299
  53.3 5.7 %late.1 = (bf16[512,1024]{1,0:T(8,128)(2,1)S(1)}, bf16[64,4096]{1,0:T(8,128)(2,1)S(1)}, bf16[64,4096]{1,0:T(8,128)(2,1)S(1)}) custom-call(s32[134]{0:T(256)S(1)} %concatenate.6.table, s32[8,8]{1,0:T(8,128)S(1)} %copy-done, bf16[512,1024]{1,0:T(8,128)(2,1)S(1)} %get-tuple-element.32.qs, bf16[1024,4096]{1,0:T(8,128)(2,1)S(1)} %get-tuple-element.33.w, ...), custom_call_target="tpu_custom_call" | custom-call | flops 10000000 | bytes 10485 | tf_op jit(solution)/shard_map/late/pallas_call | solution.py:305
  59.0 9.7 %collective-permute-start.14 = (bf16[64,4096]{1,0:T(8,128)(2,1)S(1)}, bf16[64,4096]{1,0:T(8,128)(2,1)S(1)}, u32[]{:S(2)}, u32[]{:S(2)}) collective-permute-start(bf16[64,4096]{1,0:T(8,128)(2,1)S(1)} %get-tuple-element.45), channel_id=1, source_target_pairs={{0,1},{1,0},{2,3},{3,2},{4,5},{5,4},{6,7},{7,6},{8,9},{9,8},{10,11... | collective-permute-start | bytes 1572872 | tf_op jit(solution)/shard_map/ppermute | solution.py:314
  68.7 2.9 %sides.1 = (bf16[64,4096]{1,0:T(8,128)(2,1)S(1)}, bf16[64,4096]{1,0:T(8,128)(2,1)S(1)}, bf16[128,2048]{1,0:T(8,128)(2,1)S(1)}, bf16[128,2048]{1,0:T(8,128)(2,1)S(1)}) custom-call(s32[134]{0:T(256)S(1)} %concatenate.6.table, bf16[512,1024]{1,0:T(8,128)(2,1)S(1)} %get-tuple-element.37.att, bf16[1024,4096]{1,0:T(8,128)(2,1)S(1)} %get-tuple-element.33.w), custom_call_target="tpu_custom_call" | custom-call | flops 10000000 | bytes 10485 | tf_op jit(solution)/shard_map/sides/pallas_call | solution.py:310
  72.4 2.6 %collective-permute-start.16 = (bf16[64,2048]{1,0:T(8,128)(2,1)S(1)}, bf16[64,2048]{1,0:T(8,128)(2,1)S(1)}, u32[]{:S(2)}, u32[]{:S(2)}) collective-permute-start(bf16[64,2048]{1,0:T(8,128)(2,1)S(1)} %get-tuple-element.51), channel_id=1, source_target_pairs={{0,6},{1,7},{2,0},{3,1},{4,2},{5,3},{6,4},{7,5},{8,14},{9,15},{10,... | collective-permute-start | bytes 786440 | tf_op jit(solution)/shard_map/ppermute | solution.py:317
  75.1 2.8 %collective-permute-start.18 = (bf16[64,2048]{1,0:T(8,128)(2,1)S(1)}, bf16[64,2048]{1,0:T(8,128)(2,1)S(1)}, u32[]{:S(2)}, u32[]{:S(2)}) collective-permute-start(bf16[64,2048]{1,0:T(8,128)(2,1)S(1)} %get-tuple-element.55), channel_id=1, source_target_pairs={{0,6},{1,7},{2,0},{3,1},{4,2},{5,3},{6,4},{7,5},{8,14},{9,15},{10,... | collective-permute-start | bytes 786440 | tf_op jit(solution)/shard_map/ppermute | solution.py:317
  77.8 1.8 %own.1 = (bf16[64,4096]{1,0:T(8,128)(2,1)S(1)}, bf16[64,4096]{1,0:T(8,128)(2,1)S(1)}) custom-call(s32[134]{0:T(256)S(1)} %concatenate.6.table, bf16[512,1024]{1,0:T(8,128)(2,1)S(1)} %get-tuple-element.37.att, bf16[1024,4096]{1,0:T(8,128)(2,1)S(1)} %get-tuple-element.33.w, bf16[64,2048]{1,0:T(8,128)(2,1)S(1)} %get-tuple-element.56.after), custom_call_target="tpu_custom_call" | custom-call | flops 10000000 | bytes 10485 | tf_op jit(solution)/shard_map/own/pallas_call | solution.py:327
  80.7 3.0 %collective-permute-done.15 = bf16[64,2048]{1,0:T(8,128)(2,1)S(1)} collective-permute-done((bf16[64,2048]{1,0:T(8,128)(2,1)S(1)}, bf16[64,2048]{1,0:T(8,128)(2,1)S(1)}, u32[]{:S(2)}, u32[]{:S(2)}) %collective-permute-start.15) | collective-permute-done | bytes 262176 | tf_op jit(solution)/shard_map/ppermute | solution.py:317
  84.3 1.1 %collective-permute-start.17 = (bf16[64,2048]{1,0:T(8,128)(2,1)S(1)}, bf16[64,2048]{1,0:T(8,128)(2,1)S(1)}, u32[]{:S(2)}, u32[]{:S(2)}) collective-permute-start(bf16[64,2048]{1,0:T(8,128)(2,1)S(1)} %get-tuple-element.54), channel_id=1, source_target_pairs={{0,2},{1,3},{2,4},{3,5},{4,6},{5,7},{6,0},{7,1},{8,10},{9,11},{10,... | collective-permute-start | bytes 786440 | tf_op jit(solution)/shard_map/ppermute | solution.py:317
  86.2 3.1 %collective-permute-done.19.right_below = bf16[64,2048]{1,0:T(8,128)(2,1)S(1)} collective-permute-done((bf16[64,2048]{1,0:T(8,128)(2,1)S(1)}, bf16[64,2048]{1,0:T(8,128)(2,1)S(1)}, u32[]{:S(2)}, u32[]{:S(2)}) %collective-permute-start.19) | collective-permute-done | bytes 262176 | tf_op jit(solution)/shard_map/ppermute | solution.py:317
  89.3 2.5 %collective-permute-done.20.right_above = bf16[64,2048]{1,0:T(8,128)(2,1)S(1)} collective-permute-done((bf16[64,2048]{1,0:T(8,128)(2,1)S(1)}, bf16[64,2048]{1,0:T(8,128)(2,1)S(1)}, u32[]{:S(2)}, u32[]{:S(2)}) %collective-permute-start.20) | collective-permute-done | bytes 262176 | tf_op jit(solution)/shard_map/ppermute | solution.py:317
  91.8 3.1 %collective-permute-done.17.left_below = bf16[64,2048]{1,0:T(8,128)(2,1)S(1)} collective-permute-done((bf16[64,2048]{1,0:T(8,128)(2,1)S(1)}, bf16[64,2048]{1,0:T(8,128)(2,1)S(1)}, u32[]{:S(2)}, u32[]{:S(2)}) %collective-permute-start.17) | collective-permute-done | bytes 262176 | tf_op jit(solution)/shard_map/ppermute | solution.py:317
  (47 shorter events, 7.6 us)
Async XLA Ops:
  0.0 38.8 %copy-start.2 = (s32[8,3]{0,1:T(4,128)S(1)}, s32[8,3]{0,1:T(4,128)}, u32[]{:S(2)}) copy-start(s32[8,3]{0,1:T(4,128)} %param.12) | copy-start | bytes 292
  0.0 44.1 %copy-start.1 = (f32[8]{0:T(128)S(1)}, f32[8]{0:T(128)}, u32[]{:S(2)}) copy-start(f32[8]{0:T(128)} %sink.1) | copy-start | bytes 100
  1.7 23.2 %all-to-all-start = ((bf16[32,32,128]{2,1,0:T(8,128)(2,1)}), bf16[32,32,128]{2,1,0:T(8,128)(2,1)S(1)}, u32[]{:S(2)}, u32[]{:S(2)}) async-start(bf16[32,32,128]{2,1,0:T(8,128)(2,1)} %bitcast.8), calls=%async_computation | async-start | bytes 524288 | tf_op jit(solution)/shard_map/all_to_all | solution.py:276
  13.7 17.3 %collective-permute-start = (bf16[32,32,128]{2,1,0:T(8,128)(2,1)}, bf16[32,32,128]{2,1,0:T(8,128)(2,1)S(1)}, u32[]{:S(2)}, u32[]{:S(2)}) collective-permute-start(bf16[32,32,128]{2,1,0:T(8,128)(2,1)} %bitcast.8), channel_id=1, source_target_pairs={{0,8},{8,16},{16,24},{24,32},{32,40},{40,48},{48,56},{56,64},{64,7... | collective-permute-start | bytes 786440 | tf_op jit(solution)/shard_map/ppermute | solution.py:275
  25.3 5.7 %collective-permute-start.3 = (bf16[24,8,128]{2,1,0:T(8,128)(2,1)S(1)}, bf16[24,8,128]{2,1,0:T(8,128)(2,1)S(1)}, u32[]{:S(2)}, u32[]{:S(2)}) collective-permute-start(bf16[24,8,128]{2,1,0:T(8,128)(2,1)S(1)} %fusion), channel_id=1, source_target_pairs={{0,64},{8,72},{16,80},{24,88},{32,96},{40,104},{48,112},{56,120},{... | collective-permute-start | bytes 147464 | tf_op jit(solution)/shard_map/ppermute | solution.py:284
  26.9 7.3 %collective-permute-start.2 = (bf16[24,8,128]{2,1,0:T(8,128)(2,1)S(1)}, bf16[24,8,128]{2,1,0:T(8,128)(2,1)S(1)}, u32[]{:S(2)}, u32[]{:S(2)}) collective-permute-start(bf16[24,8,128]{2,1,0:T(8,128)(2,1)S(1)} %fusion), channel_id=1, source_target_pairs={{0,128},{8,136},{16,144},{24,152},{32,160},{40,168},{48,176},{56,1... | collective-permute-start | bytes 147464 | tf_op jit(solution)/shard_map/ppermute | solution.py:284
  29.0 5.7 %collective-permute-start.1 = (bf16[24,8,128]{2,1,0:T(8,128)(2,1)S(1)}, bf16[24,8,128]{2,1,0:T(8,128)(2,1)S(1)}, u32[]{:S(2)}, u32[]{:S(2)}) collective-permute-start(bf16[24,8,128]{2,1,0:T(8,128)(2,1)S(1)} %fusion), channel_id=1, source_target_pairs={{0,192},{8,200},{16,208},{24,216},{32,224},{40,232},{48,240},{56,2... | collective-permute-start | bytes 147464 | tf_op jit(solution)/shard_map/ppermute | solution.py:284
  34.8 5.0 %collective-permute-start.7 = (bf16[24,32,128]{2,1,0:T(8,128)(2,1)S(1)}, bf16[24,32,128]{2,1,0:T(8,128)(2,1)S(1)}, u32[]{:S(2)}, u32[]{:S(2)}) collective-permute-start(bf16[24,32,128]{2,1,0:T(8,128)(2,1)S(1)} %pad_maximum_fusion.a0), channel_id=1, source_target_pairs={{0,32},{8,40},{16,48},{24,56},{32,0},{40,8},{48,16},{56,24},{64,96... | collective-permute-start | bytes 589832 | tf_op jit(solution)/shard_map/ppermute | solution.py:289
  34.9 6.2 %collective-permute-start.6 = (bf16[24,32,128]{2,1,0:T(8,128)(2,1)S(1)}, bf16[24,32,128]{2,1,0:T(8,128)(2,1)S(1)}, u32[]{:S(2)}, u32[]{:S(2)}) collective-permute-start(bf16[24,32,128]{2,1,0:T(8,128)(2,1)S(1)} %pad_maximum_fusion.a0), channel_id=1, source_target_pairs={{0,24},{8,16},{16,8},{24,0},{32,56},{40,48},{48,40},{56,32},{64,88... | collective-permute-start | bytes 589832 | tf_op jit(solution)/shard_map/ppermute | solution.py:290
  36.2 7.4 %collective-permute-start.5 = (bf16[24,32,128]{2,1,0:T(8,128)(2,1)S(1)}, bf16[24,32,128]{2,1,0:T(8,128)(2,1)S(1)}, u32[]{:S(2)}, u32[]{:S(2)}) collective-permute-start(bf16[24,32,128]{2,1,0:T(8,128)(2,1)S(1)} %pad_maximum_fusion.a0), channel_id=1, source_target_pairs={{0,8},{8,0},{16,24},{24,16},{32,40},{40,32},{48,56},{56,48},{64,72... | collective-permute-start | bytes 589832 | tf_op jit(solution)/shard_map/ppermute | solution.py:290
  36.3 7.8 %collective-permute-start.4 = (bf16[24,32,128]{2,1,0:T(8,128)(2,1)S(1)}, bf16[24,32,128]{2,1,0:T(8,128)(2,1)S(1)}, u32[]{:S(2)}, u32[]{:S(2)}) collective-permute-start(bf16[24,32,128]{2,1,0:T(8,128)(2,1)S(1)} %pad_maximum_fusion.a0), channel_id=1, source_target_pairs={{0,16},{8,24},{16,0},{24,8},{32,48},{40,56},{48,32},{56,40},{64,80... | collective-permute-start | bytes 589832 | tf_op jit(solution)/shard_map/ppermute | solution.py:290
  39.8 13.0 %collective-permute-start.10 = (bf16[24,32,128]{2,1,0:T(8,128)(2,1)S(1)}, bf16[24,32,128]{2,1,0:T(8,128)(2,1)S(1)}, u32[]{:S(2)}, u32[]{:S(2)}) collective-permute-start(bf16[24,32,128]{2,1,0:T(8,128)(2,1)S(1)} %collective-permute-done.7.b0), channel_id=1, source_target_pairs={{0,24},{8,16},{16,8},{24,0},{32,56},{40,48},{48,40},{56,32},{64,88... | collective-permute-start | bytes 589832 | tf_op jit(solution)/shard_map/ppermute | solution.py:291
  41.1 11.8 %collective-permute-start.9 = (bf16[24,32,128]{2,1,0:T(8,128)(2,1)S(1)}, bf16[24,32,128]{2,1,0:T(8,128)(2,1)S(1)}, u32[]{:S(2)}, u32[]{:S(2)}) collective-permute-start(bf16[24,32,128]{2,1,0:T(8,128)(2,1)S(1)} %collective-permute-done.7.b0), channel_id=1, source_target_pairs={{0,8},{8,0},{16,24},{24,16},{32,40},{40,32},{48,56},{56,48},{64,72... | collective-permute-start | bytes 589832 | tf_op jit(solution)/shard_map/ppermute | solution.py:291
  41.1 12.2 %collective-permute-start.8 = (bf16[24,32,128]{2,1,0:T(8,128)(2,1)S(1)}, bf16[24,32,128]{2,1,0:T(8,128)(2,1)S(1)}, u32[]{:S(2)}, u32[]{:S(2)}) collective-permute-start(bf16[24,32,128]{2,1,0:T(8,128)(2,1)S(1)} %collective-permute-done.7.b0), channel_id=1, source_target_pairs={{0,16},{8,24},{16,0},{24,8},{32,48},{40,56},{48,32},{56,40},{64,80... | collective-permute-start | bytes 589832 | tf_op jit(solution)/shard_map/ppermute | solution.py:291
  59.0 13.2 %collective-permute-start.14 = (bf16[64,4096]{1,0:T(8,128)(2,1)S(1)}, bf16[64,4096]{1,0:T(8,128)(2,1)S(1)}, u32[]{:S(2)}, u32[]{:S(2)}) collective-permute-start(bf16[64,4096]{1,0:T(8,128)(2,1)S(1)} %get-tuple-element.45), channel_id=1, source_target_pairs={{0,1},{1,0},{2,3},{3,2},{4,5},{5,4},{6,7},{7,6},{8,9},{9,8},{10,11... | collective-permute-start | bytes 1572872 | tf_op jit(solution)/shard_map/ppermute | solution.py:314
  71.6 3.3 %collective-permute-start.11 = (bf16[128,2048]{1,0:T(8,128)(2,1)S(1)}, bf16[128,2048]{1,0:T(8,128)(2,1)S(1)}, u32[]{:S(2)}, u32[]{:S(2)}) collective-permute-start(bf16[128,2048]{1,0:T(8,128)(2,1)S(1)} %get-tuple-element.39), channel_id=1, source_target_pairs={{0,1},{1,0},{2,3},{3,2},{4,5},{5,4},{6,7},{7,6},{8,9},{9,8},{10,11... | collective-permute-start | bytes 1572872 | tf_op jit(solution)/shard_map/ppermute | solution.py:314
  71.7 7.9 %collective-permute-start.13 = (bf16[128,2048]{1,0:T(8,128)(2,1)S(1)}, bf16[128,2048]{1,0:T(8,128)(2,1)S(1)}, u32[]{:S(2)}, u32[]{:S(2)}) collective-permute-start(bf16[128,2048]{1,0:T(8,128)(2,1)S(1)} %get-tuple-element.43), channel_id=1, source_target_pairs={{0,1},{1,0},{2,3},{3,2},{4,5},{5,4},{6,7},{7,6},{8,9},{9,8},{10,11... | collective-permute-start | bytes 1572872 | tf_op jit(solution)/shard_map/ppermute | solution.py:314
  72.4 8.3 %collective-permute-start.16 = (bf16[64,2048]{1,0:T(8,128)(2,1)S(1)}, bf16[64,2048]{1,0:T(8,128)(2,1)S(1)}, u32[]{:S(2)}, u32[]{:S(2)}) collective-permute-start(bf16[64,2048]{1,0:T(8,128)(2,1)S(1)} %get-tuple-element.51), channel_id=1, source_target_pairs={{0,6},{1,7},{2,0},{3,1},{4,2},{5,3},{6,4},{7,5},{8,14},{9,15},{10,... | collective-permute-start | bytes 786440 | tf_op jit(solution)/shard_map/ppermute | solution.py:317
  74.9 8.7 %collective-permute-start.15 = (bf16[64,2048]{1,0:T(8,128)(2,1)S(1)}, bf16[64,2048]{1,0:T(8,128)(2,1)S(1)}, u32[]{:S(2)}, u32[]{:S(2)}) collective-permute-start(bf16[64,2048]{1,0:T(8,128)(2,1)S(1)} %get-tuple-element.52), channel_id=1, source_target_pairs={{0,2},{1,3},{2,4},{3,5},{4,6},{5,7},{6,0},{7,1},{8,10},{9,11},{10,... | collective-permute-start | bytes 786440 | tf_op jit(solution)/shard_map/ppermute | solution.py:317
  75.1 11.1 %collective-permute-start.18 = (bf16[64,2048]{1,0:T(8,128)(2,1)S(1)}, bf16[64,2048]{1,0:T(8,128)(2,1)S(1)}, u32[]{:S(2)}, u32[]{:S(2)}) collective-permute-start(bf16[64,2048]{1,0:T(8,128)(2,1)S(1)} %get-tuple-element.55), channel_id=1, source_target_pairs={{0,6},{1,7},{2,0},{3,1},{4,2},{5,3},{6,4},{7,5},{8,14},{9,15},{10,... | collective-permute-start | bytes 786440 | tf_op jit(solution)/shard_map/ppermute | solution.py:317
  77.8 11.5 %collective-permute-start.19 = (bf16[64,2048]{1,0:T(8,128)(2,1)S(1)}, bf16[64,2048]{1,0:T(8,128)(2,1)S(1)}, u32[]{:S(2)}, u32[]{:S(2)}) collective-permute-start(bf16[64,2048]{1,0:T(8,128)(2,1)S(1)} %get-tuple-element.56.after), channel_id=1, source_target_pairs={{0,2},{1,3},{2,4},{3,5},{4,6},{5,7},{6,0},{7,1},{8,10},{9,11},{10,... | collective-permute-start | bytes 786440 | tf_op jit(solution)/shard_map/ppermute | solution.py:317
  79.7 15.2 %collective-permute-start.12 = (bf16[64,4096]{1,0:T(8,128)(2,1)S(1)}, bf16[64,4096]{1,0:T(8,128)(2,1)S(1)}, u32[]{:S(2)}, u32[]{:S(2)}) collective-permute-start(bf16[64,4096]{1,0:T(8,128)(2,1)S(1)} %get-tuple-element.41), channel_id=1, source_target_pairs={{0,1},{1,0},{2,3},{3,2},{4,5},{5,4},{6,7},{7,6},{8,9},{9,8},{10,11... | collective-permute-start | bytes 1572872 | tf_op jit(solution)/shard_map/ppermute | solution.py:314
  83.9 7.9 %collective-permute-start.20 = (bf16[64,2048]{1,0:T(8,128)(2,1)S(1)}, bf16[64,2048]{1,0:T(8,128)(2,1)S(1)}, u32[]{:S(2)}, u32[]{:S(2)}) collective-permute-start(bf16[64,2048]{1,0:T(8,128)(2,1)S(1)} %get-tuple-element.53), channel_id=1, source_target_pairs={{0,6},{1,7},{2,0},{3,1},{4,2},{5,3},{6,4},{7,5},{8,14},{9,15},{10,... | collective-permute-start | bytes 786440 | tf_op jit(solution)/shard_map/ppermute | solution.py:317
  84.3 10.6 %collective-permute-start.17 = (bf16[64,2048]{1,0:T(8,128)(2,1)S(1)}, bf16[64,2048]{1,0:T(8,128)(2,1)S(1)}, u32[]{:S(2)}, u32[]{:S(2)}) collective-permute-start(bf16[64,2048]{1,0:T(8,128)(2,1)S(1)} %get-tuple-element.54), channel_id=1, source_target_pairs={{0,2},{1,3},{2,4},{3,5},{4,6},{5,7},{6,0},{7,1},{8,10},{9,11},{10,... | collective-permute-start | bytes 786440 | tf_op jit(solution)/shard_map/ppermute | solution.py:317
  (1 other events, 16.9 us)

commit v9 on v8

--- a/solution.py
+++ b/solution.py
@@ -103,12 +103,11 @@
     return jnp.concatenate([column_block] * count, axis=1)
 
 
-def early_kernel(table, vert, slash, sink, q, w, a0, a2, a1, a3, prev, kc, vc, acc, tops, sums, w_out, qs, kv, band, sems):
+def band_kernel(table, vert, slash, sink, q, w, prev, kc, vc, acc, tops, sums, w_out, qs, band, sems):
     copies = Copies(sems)
     copies.start(q, qs)
     for kind, cur in enumerate((kc, vc)):
         copies.start(cur, band.at[kind, pl.ds(RUNS, RUNS)])
-    load_half(copies, table[META], a0, a2, a1, a3, kv)
     first = len(copies.made)
     depth = w.shape[0] // 4
     for n in range(4):
@@ -119,61 +118,34 @@
             band[kind, b] = jnp.concatenate(rows, axis=0).astype(BF16)
     copies.wait(first)
     token = TOKENS // RUNS * table[META + 2] + lax.broadcasted_iota(jnp.int32, (TOKENS, 1), 0)
-    places = key_places(table, False)
     within = lax.broadcasted_iota(jnp.int32, (1, ROWS), 1)
     for h in range(HEADS):
         cols = slice(h * HEAD, (h + 1) * HEAD)
-        qh = qs[:, cols]
-        slots = slots_of(table, vert, h)
-        score = product(qh, listed(kv, 0, slots))
-        score = jnp.where(token >= limits(vert, places, h), score, LOW)
-        near = []
+        raw_sink = sink[h] * (1.0 / SCALE)
+        score = []
         for run in range(RUNS):
             rows = slice(run * ROWS, (run + 1) * ROWS)
             keys = jnp.concatenate([band[0, RUNS + run - slash[h, j]] for j in range(BANDS)], axis=0)
             limit = jnp.concatenate(
                 [within + near_base(table, vert, slash, h, run, j) for j in range(BANDS)], axis=1)
-            near.append(jnp.where(token[rows] >= limit, product(qh[rows], keys), LOW))
-        near = jnp.concatenate(near, axis=0)
-        raw_sink = sink[h] * (1.0 / SCALE)
-        top = jnp.maximum(jnp.max(score, axis=1, keepdims=True), jnp.max(near, axis=1, keepdims=True))
-        top = jnp.maximum(top, raw_sink)
+            score.append(jnp.where(token[rows] >= limit, product(qs[rows, cols], keys), LOW))
+        score = jnp.concatenate(score, axis=0)
+        top = jnp.maximum(jnp.max(score, axis=1, keepdims=True), raw_sink)
         weight = jnp.exp2((score - top) * FACTOR)
-        near = jnp.exp2((near - top) * FACTOR)
-        total = jnp.sum(weight, axis=1, keepdims=True) + jnp.sum(near, axis=1, keepdims=True)
-        total = total + jnp.exp2((raw_sink - top) * FACTOR)
-        mixed = jnp.dot(weight.astype(BF16), listed(kv, 1, slots), preferred_element_type=F32)
-        near = near.astype(BF16)
+        total = jnp.sum(weight, axis=1, keepdims=True) + jnp.exp2((raw_sink - top) * FACTOR)
+        weight = weight.astype(BF16)
         for run in range(RUNS):
             rows = slice(run * ROWS, (run + 1) * ROWS)
             vals = jnp.concatenate([band[1, RUNS + run - slash[h, j]] for j in range(BANDS)], axis=0)
-            acc[rows, cols] = mixed[rows] + jnp.dot(near[rows], vals, preferred_element_type=F32)
+            acc[rows, cols] = jnp.dot(weight[rows], vals, preferred_element_type=F32)
         tops[:, cols] = wide(top)
         sums[:, cols] = wide(total)
     copies.wait()
 
 
-def project(att, w, blocks, core, keeps, give):
-    def rows(block, side):
-        start = pl.multiple_of(block * ROWS + side * HALF, HALF)
-        return att[pl.ds(start, HALF), :]
-
-    lhs = jnp.concatenate([rows(b, core) for b in blocks] + [rows(b, 1 - core) for b in blocks], axis=0)
-    tile = 512
-    for n in range(w.shape[1] // tile):
-        cols = slice(n * tile, (n + 1) * tile)
-        out = jnp.dot(lhs, w[:, cols], preferred_element_type=F32).astype(BF16)
-        for i, keep in enumerate(keeps):
-            keep[:, cols] = out[i * HALF:(i + 1) * HALF]
-        give(n * tile, tile, out[len(blocks) * HALF:])
-
-
-def late_kernel(table, vert, qs, w, b0, b2, b1, b3, acc, tops, sums, att, keep, give, kv, sems):
-    copies = Copies(sems)
-    load_half(copies, table[META], b0, b2, b1, b3, kv)
-    copies.wait()
+def add_listed(table, vert, qs, kv, late, acc, tops, sums, put):
     token = TOKENS // RUNS * table[META + 2] + lax.broadcasted_iota(jnp.int32, (TOKENS, 1), 0)
-    places = key_places(table, True)
+    places = key_places(table, late)
     for h in range(HEADS):
         cols = slice(h * HEAD, (h + 1) * HEAD)
         slots = slots_of(table, vert, h)
@@ -185,7 +157,44 @@
         fade = jnp.exp2((before - top) * FACTOR)
         total = wide(jnp.sum(weight, axis=1, keepdims=True)) + fade * sums[:, cols]
         mixed = jnp.dot(weight.astype(BF16), listed(kv, 1, slots), preferred_element_type=F32)
-        att[:, cols] = ((mixed + acc[:, cols] * fade) * (1.0 / total)).astype(BF16)
+        put(cols, mixed + acc[:, cols] * fade, top, total)
+
+
+def early_kernel(table, vert, qs, a0, a2, a1, a3, acc, tops, sums, acc_out, tops_out, sums_out, kv, sems):
+    copies = Copies(sems)
+    load_half(copies, table[META], a0, a2, a1, a3, kv)
+    copies.wait()
+
+    def put(cols, mixed, top, total):
+        acc_out[:, cols], tops_out[:, cols], sums_out[:, cols] = mixed, top, total
+
+    add_listed(table, vert, qs, kv, False, acc, tops, sums, put)
+
+
+def project(att, w, blocks, core, keeps, give):
+    def rows(block, side):
+        start = pl.multiple_of(block * ROWS + side * HALF, HALF)
+        return att[pl.ds(start, HALF), :]
+
+    lhs = jnp.concatenate([rows(b, core) for b in blocks] + [rows(b, 1 - core) for b in blocks], axis=0)
+    tile = 512
+    for n in range(w.shape[1] // tile):
+        cols = slice(n * tile, (n + 1) * tile)
+        out = jnp.dot(lhs, w[:, cols], preferred_element_type=F32).astype(BF16)
+        for i, keep in enumerate(keeps):
+            keep[:, cols] = out[i * HALF:(i + 1) * HALF]
+        give(n * tile, tile, out[len(blocks) * HALF:])
+
+
+def late_kernel(table, vert, qs, w, b0, b2, b1, b3, acc, tops, sums, att, keep, give, kv, sems):
+    copies = Copies(sems)
+    load_half(copies, table[META], b0, b2, b1, b3, kv)
+    copies.wait()
+
+    def put(cols, mixed, top, total):
+        att[:, cols] = (mixed * (1.0 / total)).astype(BF16)
+
+    add_listed(table, vert, qs, kv, True, acc, tops, sums, put)
     project(att, w, [(table[META + 5] + 2) % X], table[META + 1], [keep], functools.partial(store, give))
 
 
@@ -288,7 +297,6 @@
     a0 = jnp.concatenate([mine, z2, z4, z6], axis=1)
     b0 = lax.ppermute(a0, "ctx", [(Y * z + y, Y * (z ^ 1) + y) for z in range(Z) for y in range(Y)])
     a1, a2, a3 = [lax.ppermute(a0, "ctx", y_pairs(f)) for f in (1, 2, 3)]
-    b1, b2, b3 = [lax.ppermute(b0, "ctx", y_pairs(f)) for f in (1, 2, 3)]
 
     width = output_weight.shape[1]
     kv = pltpu.VMEM((2, SLOTS, HALF, HEAD), BF16)
@@ -296,12 +304,17 @@
     part = ((HALF, width), BF16)
     far_queries = pltpu.with_memory_space_constraint(queries, pltpu.HBM)
     far_weight = pltpu.with_memory_space_constraint(output_weight, pltpu.HBM)
+    state = [((TOKENS, HEADS * HEAD), F32)] * 3
     acc, tops, sums, w, q = call(
-        early_kernel, [SMEM] * 4 + [ANY] * 6 + [VMEM, ANY, ANY],
-        [((TOKENS, HEADS * HEAD), F32)] * 3 + [(output_weight.shape, BF16), rows],
-        [kv, pltpu.VMEM((2, 2 * RUNS, ROWS, HEAD), BF16), pltpu.SemaphoreType.DMA((11,))], 8, "early",
-    )(table, vert_blocks, slash_offsets, sink_logits, far_queries, far_weight, a0, a2, a1, a3, prev,
+        band_kernel, [SMEM] * 4 + [ANY] * 2 + [VMEM, ANY, ANY], state + [(output_weight.shape, BF16), rows],
+        [pltpu.VMEM((2, 2 * RUNS, ROWS, HEAD), BF16), pltpu.SemaphoreType.DMA((7,))], 3, "band",
+    )(table, vert_blocks, slash_offsets, sink_logits, far_queries, far_weight, prev,
       *[pltpu.with_memory_space_constraint(a, pltpu.HBM) for a in (keys, values)])
+    b0, acc = lax.optimization_barrier((b0, acc))
+    b1, b2, b3 = [lax.ppermute(b0, "ctx", y_pairs(f)) for f in (1, 2, 3)]
+    acc, tops, sums = call(
+        early_kernel, [SMEM, SMEM, VMEM] + [ANY] * 4 + [VMEM] * 3, state, [kv, pltpu.SemaphoreType.DMA((4,))], 5, "early",
+    )(table, vert_blocks, q, a0, a2, a1, a3, acc, tops, sums)
     att, keep_far, give_far = call(
         late_kernel, [SMEM, SMEM, VMEM, VMEM] + [ANY] * 4 + [VMEM] * 3,
         [rows, part, part], [kv, pltpu.SemaphoreType.DMA((4,))], 0.01, "late",

time: 96.2 us -> 93.2 us (0.969)
  starting transfers between devices: 46.9 us -> 44.3 us
  waiting for transfers between devices: 25.4 us -> 23.5 us
  Pallas kernels: 22 us -> 23.6 us
    ppermute x4, starting transfers between devices: 11.3 us -> 8.64 us  [swap(): return lax.ppermute(a, 'head', CORE_PAIRS)]
    pallas_call x1 -> x2, Pallas kernels: 8.77 us -> 10 us  [the longest x1 5.28 us: per_device(): call(band_kernel, [SMEM] * 4 + [ANY] * 2 + [VMEM, ANY, ANY], state + [(ou...]
  transfers between devices with their start and end apart: 22 -> 22, of which waited for: 11 -> 9; matrix products, arithmetic and copies ran while one was open for 1% -> 2% of each run, Pallas kernels for 14% -> 16%
where the time goes in v9:
time: 93.2 us; the launch traced here: 93 us
  starting transfers between devices  44.3 us (48%)
  Pallas kernels  23.6 us (25%)
  waiting for transfers between devices  23.5 us (25%)
    all_to_all x1, starting transfers between devices, per_device(): lax.all_to_all(spread, 'ctx', 0, 0, tiled=True).reshape(BLOCKS * 8, HEAD)  12 us
    ppermute x6, waiting for transfers between devices, to_x(): return lax.ppermute(a, 'head', x_pairs(step))  11.9 us
    ppermute x4, starting transfers between devices, swap(): return lax.ppermute(a, 'head', CORE_PAIRS)  8.64 us
    all_to_all x1, waiting for transfers between devices, per_device(): lax.all_to_all(spread, 'ctx', 0, 0, tiled=True).reshape(BLOCKS * 8, HEAD)  7.59 us
    ppermute x6, starting transfers between devices, to_x(): return lax.ppermute(a, 'head', x_pairs(step))  6.86 us
    pallas_call x1, Pallas kernels, per_device(): call(late_kernel, [SMEM, SMEM, VMEM, VMEM] + [ANY] * 4 + [VMEM] * 3, [row...  6.06 us
    ppermute x3, starting transfers between devices, from_z(): return lax.ppermute(a, 'ctx', z_pairs(-offset))  5.71 us
    pallas_call x1, Pallas kernels, per_device(): call(band_kernel, [SMEM] * 4 + [ANY] * 2 + [VMEM, ANY, ANY], state + [(ou...  5.28 us
  transfers between devices with their start and end apart: 22, of which 9 were waited for; matrix products, arithmetic and copies ran while one was open for 2% of the time, Pallas kernels for 16%

profile of v9, /device:TPU:1, one launch (start us, length us, event | category | flops | bytes accessed | tf_op | source)
XLA Modules:
  0.0 93.0 jit_solution(16876443397508433110)
XLA Ops:
  0.0 1.7 %spread.1 = bf16[16,2,4,8,128]{4,3,2,1,0:T(8,128)(2,1)} custom-call(bf16[4,16,8,128]{3,2,1,0:T(8,128)(2,1)} %bitcast.18, bf16[4,16,8,128]{3,2,1,0:T(8,128)(2,1)} %bitcast.20), custom_call_target="tpu_custom_call" | custom-call | flops 1000000000 | bytes 1048576 | tf_op jit(solution)/shard_map/spread/pallas_call | solution.py:280
  1.7 12.0 %all-to-all-start = ((bf16[32,32,128]{2,1,0:T(8,128)(2,1)}), bf16[32,32,128]{2,1,0:T(8,128)(2,1)S(1)}, u32[]{:S(2)}, u32[]{:S(2)}) async-start(bf16[32,32,128]{2,1,0:T(8,128)(2,1)} %bitcast.8), calls=%async_computation | async-start | bytes 524288 | tf_op jit(solution)/shard_map/all_to_all | solution.py:285
  13.7 3.1 %collective-permute-start = (bf16[32,32,128]{2,1,0:T(8,128)(2,1)}, bf16[32,32,128]{2,1,0:T(8,128)(2,1)S(1)}, u32[]{:S(2)}, u32[]{:S(2)}) collective-permute-start(bf16[32,32,128]{2,1,0:T(8,128)(2,1)} %bitcast.8), channel_id=1, source_target_pairs={{0,8},{8,16},{16,24},{24,32},{32,40},{40,48},{48,56},{56,64},{64,7... | collective-permute-start | bytes 786440 | tf_op jit(solution)/shard_map/ppermute | solution.py:284
  17.3 7.6 %all-to-all-done = bf16[32,32,128]{2,1,0:T(8,128)(2,1)S(1)} async-done(((bf16[32,32,128]{2,1,0:T(8,128)(2,1)}), bf16[32,32,128]{2,1,0:T(8,128)(2,1)S(1)}, u32[]{:S(2)}, u32[]{:S(2)}) %all-to-all-start) | async-done | bytes 262176 | tf_op jit(solution)/shard_map/all_to_all | solution.py:285
  25.3 1.6 %collective-permute-start.3 = (bf16[24,8,128]{2,1,0:T(8,128)(2,1)S(1)}, bf16[24,8,128]{2,1,0:T(8,128)(2,1)S(1)}, u32[]{:S(2)}, u32[]{:S(2)}) collective-permute-start(bf16[24,8,128]{2,1,0:T(8,128)(2,1)S(1)} %fusion), channel_id=1, source_target_pairs={{0,64},{8,72},{16,80},{24,88},{32,96},{40,104},{48,112},{56,120},{... | collective-permute-start | bytes 147464 | tf_op jit(solution)/shard_map/ppermute | solution.py:293
  26.9 2.1 %collective-permute-start.2 = (bf16[24,8,128]{2,1,0:T(8,128)(2,1)S(1)}, bf16[24,8,128]{2,1,0:T(8,128)(2,1)S(1)}, u32[]{:S(2)}, u32[]{:S(2)}) collective-permute-start(bf16[24,8,128]{2,1,0:T(8,128)(2,1)S(1)} %fusion), channel_id=1, source_target_pairs={{0,128},{8,136},{16,144},{24,152},{32,160},{40,168},{48,176},{56,1... | collective-permute-start | bytes 147464 | tf_op jit(solution)/shard_map/ppermute | solution.py:293
  29.0 2.0 %collective-permute-start.1 = (bf16[24,8,128]{2,1,0:T(8,128)(2,1)S(1)}, bf16[24,8,128]{2,1,0:T(8,128)(2,1)S(1)}, u32[]{:S(2)}, u32[]{:S(2)}) collective-permute-start(bf16[24,8,128]{2,1,0:T(8,128)(2,1)S(1)} %fusion), channel_id=1, source_target_pairs={{0,192},{8,200},{16,208},{24,216},{32,224},{40,232},{48,240},{56,2... | collective-permute-start | bytes 147464 | tf_op jit(solution)/shard_map/ppermute | solution.py:293
  31.2 3.0 %collective-permute-done.2 = bf16[24,8,128]{2,1,0:T(8,128)(2,1)S(1)} collective-permute-done((bf16[24,8,128]{2,1,0:T(8,128)(2,1)S(1)}, bf16[24,8,128]{2,1,0:T(8,128)(2,1)S(1)}, u32[]{:S(2)}, u32[]{:S(2)}) %collective-permute-start.2) | collective-permute-done | bytes 49184 | tf_op jit(solution)/shard_map/ppermute | solution.py:293
  34.8 1.4 %collective-permute-start.10 = (bf16[24,32,128]{2,1,0:T(8,128)(2,1)S(1)}, bf16[24,32,128]{2,1,0:T(8,128)(2,1)S(1)}, u32[]{:S(2)}, u32[]{:S(2)}) collective-permute-start(bf16[24,32,128]{2,1,0:T(8,128)(2,1)S(1)} %pad_maximum_fusion.a0), channel_id=1, source_target_pairs={{0,24},{8,16},{16,8},{24,0},{32,56},{40,48},{48,40},{56,32},{64,88... | collective-permute-start | bytes 589832 | tf_op jit(solution)/shard_map/ppermute | solution.py:299
  36.2 2.6 %collective-permute-start.8 = (bf16[24,32,128]{2,1,0:T(8,128)(2,1)S(1)}, bf16[24,32,128]{2,1,0:T(8,128)(2,1)S(1)}, u32[]{:S(2)}, u32[]{:S(2)}) collective-permute-start(bf16[24,32,128]{2,1,0:T(8,128)(2,1)S(1)} %pad_maximum_fusion.a0), channel_id=1, source_target_pairs={{0,16},{8,24},{16,0},{24,8},{32,48},{40,56},{48,32},{56,40},{64,80... | collective-permute-start | bytes 589832 | tf_op jit(solution)/shard_map/ppermute | solution.py:299
  38.7 5.3 %band.1 = (f32[512,1024]{1,0:T(8,128)S(1)}, f32[512,1024]{1,0:T(8,128)S(1)}, f32[512,1024]{1,0:T(8,128)S(1)}, bf16[1024,4096]{1,0:T(8,128)(2,1)S(1)}, bf16[512,1024]{1,0:T(8,128)(2,1)S(1)}) custom-call(s32[134]{0:T(256)S(1)} %concatenate.6.table, s32[8,8]{1,0:T(8,128)S(1)} %copy-done, s32[8,3]{1,0:T(8,128)S(1)} %copy.10.slash, f32[8]{0:T(128)S(1)} %copy-done.1, ...), custom_call_target="tpu_custom_call" | custom-call | flops 3000000000 | bytes 3145728 | tf_op jit(solution)/shard_map/band/pallas_call | solution.py:308
  44.0 1.4 %collective-permute-start.7 = (bf16[24,32,128]{2,1,0:T(8,128)(2,1)S(1)}, bf16[24,32,128]{2,1,0:T(8,128)(2,1)S(1)}, u32[]{:S(2)}, u32[]{:S(2)}) collective-permute-start(bf16[24,32,128]{2,1,0:T(8,128)(2,1)S(1)} %collective-permute-done.4.b0), channel_id=1, source_target_pairs={{0,24},{8,16},{16,8},{24,0},{32,56},{40,48},{48,40},{56,32},{64,88... | collective-permute-start | bytes 589832 | tf_op jit(solution)/shard_map/ppermute | solution.py:314
  45.4 2.6 %collective-permute-start.5 = (bf16[24,32,128]{2,1,0:T(8,128)(2,1)S(1)}, bf16[24,32,128]{2,1,0:T(8,128)(2,1)S(1)}, u32[]{:S(2)}, u32[]{:S(2)}) collective-permute-start(bf16[24,32,128]{2,1,0:T(8,128)(2,1)S(1)} %collective-permute-done.4.b0), channel_id=1, source_target_pairs={{0,16},{8,24},{16,0},{24,8},{32,48},{40,56},{48,32},{56,40},{64,80... | collective-permute-start | bytes 589832 | tf_op jit(solution)/shard_map/ppermute | solution.py:314
  48.0 4.7 %early.1 = (f32[512,1024]{1,0:T(8,128)S(1)}, f32[512,1024]{1,0:T(8,128)S(1)}, f32[512,1024]{1,0:T(8,128)S(1)}) custom-call(s32[134]{0:T(256)S(1)} %concatenate.6.table, s32[8,8]{1,0:T(8,128)S(1)} %copy-done, bf16[512,1024]{1,0:T(8,128)(2,1)S(1)} %get-tuple-element.34.qs, bf16[24,32,128]{2,1,0:T(8,128)(2,1)S(1)} %pad_maximum_fusion.a0, ...), custom_call_target="tpu_custom_call" | custom-call | flops 5000000000 | bytes 5242880 | tf_op jit(solution)/shard_map/early/pallas_call | solution.py:315
  53.1 6.1 %late.1 = (bf16[512,1024]{1,0:T(8,128)(2,1)S(1)}, bf16[64,4096]{1,0:T(8,128)(2,1)S(1)}, bf16[64,4096]{1,0:T(8,128)(2,1)S(1)}) custom-call(s32[134]{0:T(256)S(1)} %concatenate.6.table, s32[8,8]{1,0:T(8,128)S(1)} %copy-done, bf16[512,1024]{1,0:T(8,128)(2,1)S(1)} %get-tuple-element.34.qs, bf16[1024,4096]{1,0:T(8,128)(2,1)S(1)} %get-tuple-element.35.w, ...), custom_call_target="tpu_custom_call" | custom-call | flops 10000000 | bytes 10485 | tf_op jit(solution)/shard_map/late/pallas_call | solution.py:318
  59.2 6.8 %collective-permute-start.14 = (bf16[64,4096]{1,0:T(8,128)(2,1)S(1)}, bf16[64,4096]{1,0:T(8,128)(2,1)S(1)}, u32[]{:S(2)}, u32[]{:S(2)}) collective-permute-start(bf16[64,4096]{1,0:T(8,128)(2,1)S(1)} %get-tuple-element.55), channel_id=1, source_target_pairs={{0,1},{1,0},{2,3},{3,2},{4,5},{5,4},{6,7},{7,6},{8,9},{9,8},{10,11... | collective-permute-start | bytes 1572872 | tf_op jit(solution)/shard_map/ppermute | solution.py:327
  66.0 2.9 %sides.1 = (bf16[64,4096]{1,0:T(8,128)(2,1)S(1)}, bf16[64,4096]{1,0:T(8,128)(2,1)S(1)}, bf16[128,2048]{1,0:T(8,128)(2,1)S(1)}, bf16[128,2048]{1,0:T(8,128)(2,1)S(1)}) custom-call(s32[134]{0:T(256)S(1)} %concatenate.6.table, bf16[512,1024]{1,0:T(8,128)(2,1)S(1)} %get-tuple-element.47.att, bf16[1024,4096]{1,0:T(8,128)(2,1)S(1)} %get-tuple-element.35.w), custom_call_target="tpu_custom_call" | custom-call | flops 10000000 | bytes 10485 | tf_op jit(solution)/shard_map/sides/pallas_call | solution.py:323
  69.6 2.6 %collective-permute-start.16 = (bf16[64,2048]{1,0:T(8,128)(2,1)S(1)}, bf16[64,2048]{1,0:T(8,128)(2,1)S(1)}, u32[]{:S(2)}, u32[]{:S(2)}) collective-permute-start(bf16[64,2048]{1,0:T(8,128)(2,1)S(1)} %get-tuple-element.61), channel_id=1, source_target_pairs={{0,6},{1,7},{2,0},{3,1},{4,2},{5,3},{6,4},{7,5},{8,14},{9,15},{10,... | collective-permute-start | bytes 786440 | tf_op jit(solution)/shard_map/ppermute | solution.py:330
  72.3 2.8 %collective-permute-start.18 = (bf16[64,2048]{1,0:T(8,128)(2,1)S(1)}, bf16[64,2048]{1,0:T(8,128)(2,1)S(1)}, u32[]{:S(2)}, u32[]{:S(2)}) collective-permute-start(bf16[64,2048]{1,0:T(8,128)(2,1)S(1)} %get-tuple-element.65), channel_id=1, source_target_pairs={{0,6},{1,7},{2,0},{3,1},{4,2},{5,3},{6,4},{7,5},{8,14},{9,15},{10,... | collective-permute-start | bytes 786440 | tf_op jit(solution)/shard_map/ppermute | solution.py:330
  75.1 1.8 %own.1 = (bf16[64,4096]{1,0:T(8,128)(2,1)S(1)}, bf16[64,4096]{1,0:T(8,128)(2,1)S(1)}) custom-call(s32[134]{0:T(256)S(1)} %concatenate.6.table, bf16[512,1024]{1,0:T(8,128)(2,1)S(1)} %get-tuple-element.47.att, bf16[1024,4096]{1,0:T(8,128)(2,1)S(1)} %get-tuple-element.35.w, bf16[64,2048]{1,0:T(8,128)(2,1)S(1)} %get-tuple-element.66.after), custom_call_target="tpu_custom_call" | custom-call | flops 10000000 | bytes 10485 | tf_op jit(solution)/shard_map/own/pallas_call | solution.py:340
  78.2 2.5 %collective-permute-done.15 = bf16[64,2048]{1,0:T(8,128)(2,1)S(1)} collective-permute-done((bf16[64,2048]{1,0:T(8,128)(2,1)S(1)}, bf16[64,2048]{1,0:T(8,128)(2,1)S(1)}, u32[]{:S(2)}, u32[]{:S(2)}) %collective-permute-start.15) | collective-permute-done | bytes 262176 | tf_op jit(solution)/shard_map/ppermute | solution.py:330
  83.2 3.1 %collective-permute-done.19.right_below = bf16[64,2048]{1,0:T(8,128)(2,1)S(1)} collective-permute-done((bf16[64,2048]{1,0:T(8,128)(2,1)S(1)}, bf16[64,2048]{1,0:T(8,128)(2,1)S(1)}, u32[]{:S(2)}, u32[]{:S(2)}) %collective-permute-start.19) | collective-permute-done | bytes 262176 | tf_op jit(solution)/shard_map/ppermute | solution.py:330
  86.3 2.5 %collective-permute-done.20.right_above = bf16[64,2048]{1,0:T(8,128)(2,1)S(1)} collective-permute-done((bf16[64,2048]{1,0:T(8,128)(2,1)S(1)}, bf16[64,2048]{1,0:T(8,128)(2,1)S(1)}, u32[]{:S(2)}, u32[]{:S(2)}) %collective-permute-start.20) | collective-permute-done | bytes 262176 | tf_op jit(solution)/shard_map/ppermute | solution.py:330
  88.8 3.1 %collective-permute-done.17.left_below = bf16[64,2048]{1,0:T(8,128)(2,1)S(1)} collective-permute-done((bf16[64,2048]{1,0:T(8,128)(2,1)S(1)}, bf16[64,2048]{1,0:T(8,128)(2,1)S(1)}, u32[]{:S(2)}, u32[]{:S(2)}) %collective-permute-start.17) | collective-permute-done | bytes 262176 | tf_op jit(solution)/shard_map/ppermute | solution.py:330
  (48 shorter events, 7.6 us)
Async XLA Ops:
  0.0 31.0 %copy-start.2 = (s32[8,3]{0,1:T(4,128)S(1)}, s32[8,3]{0,1:T(4,128)}, u32[]{:S(2)}) copy-start(s32[8,3]{0,1:T(4,128)} %param.12) | copy-start | bytes 292
  0.0 38.7 %copy-start.1 = (f32[8]{0:T(128)S(1)}, f32[8]{0:T(128)}, u32[]{:S(2)}) copy-start(f32[8]{0:T(128)} %sink.1) | copy-start | bytes 100
  1.7 23.2 %all-to-all-start = ((bf16[32,32,128]{2,1,0:T(8,128)(2,1)}), bf16[32,32,128]{2,1,0:T(8,128)(2,1)S(1)}, u32[]{:S(2)}, u32[]{:S(2)}) async-start(bf16[32,32,128]{2,1,0:T(8,128)(2,1)} %bitcast.8), calls=%async_computation | async-start | bytes 524288 | tf_op jit(solution)/shard_map/all_to_all | solution.py:285
  13.7 17.4 %collective-permute-start = (bf16[32,32,128]{2,1,0:T(8,128)(2,1)}, bf16[32,32,128]{2,1,0:T(8,128)(2,1)S(1)}, u32[]{:S(2)}, u32[]{:S(2)}) collective-permute-start(bf16[32,32,128]{2,1,0:T(8,128)(2,1)} %bitcast.8), channel_id=1, source_target_pairs={{0,8},{8,16},{16,24},{24,32},{32,40},{40,48},{48,56},{56,64},{64,7... | collective-permute-start | bytes 786440 | tf_op jit(solution)/shard_map/ppermute | solution.py:284
  25.3 5.9 %collective-permute-start.3 = (bf16[24,8,128]{2,1,0:T(8,128)(2,1)S(1)}, bf16[24,8,128]{2,1,0:T(8,128)(2,1)S(1)}, u32[]{:S(2)}, u32[]{:S(2)}) collective-permute-start(bf16[24,8,128]{2,1,0:T(8,128)(2,1)S(1)} %fusion), channel_id=1, source_target_pairs={{0,64},{8,72},{16,80},{24,88},{32,96},{40,104},{48,112},{56,120},{... | collective-permute-start | bytes 147464 | tf_op jit(solution)/shard_map/ppermute | solution.py:293
  26.9 7.3 %collective-permute-start.2 = (bf16[24,8,128]{2,1,0:T(8,128)(2,1)S(1)}, bf16[24,8,128]{2,1,0:T(8,128)(2,1)S(1)}, u32[]{:S(2)}, u32[]{:S(2)}) collective-permute-start(bf16[24,8,128]{2,1,0:T(8,128)(2,1)S(1)} %fusion), channel_id=1, source_target_pairs={{0,128},{8,136},{16,144},{24,152},{32,160},{40,168},{48,176},{56,1... | collective-permute-start | bytes 147464 | tf_op jit(solution)/shard_map/ppermute | solution.py:293
  29.0 5.7 %collective-permute-start.1 = (bf16[24,8,128]{2,1,0:T(8,128)(2,1)S(1)}, bf16[24,8,128]{2,1,0:T(8,128)(2,1)S(1)}, u32[]{:S(2)}, u32[]{:S(2)}) collective-permute-start(bf16[24,8,128]{2,1,0:T(8,128)(2,1)S(1)} %fusion), channel_id=1, source_target_pairs={{0,192},{8,200},{16,208},{24,216},{32,224},{40,232},{48,240},{56,2... | collective-permute-start | bytes 147464 | tf_op jit(solution)/shard_map/ppermute | solution.py:293
  34.8 10.6 %collective-permute-start.10 = (bf16[24,32,128]{2,1,0:T(8,128)(2,1)S(1)}, bf16[24,32,128]{2,1,0:T(8,128)(2,1)S(1)}, u32[]{:S(2)}, u32[]{:S(2)}) collective-permute-start(bf16[24,32,128]{2,1,0:T(8,128)(2,1)S(1)} %pad_maximum_fusion.a0), channel_id=1, source_target_pairs={{0,24},{8,16},{16,8},{24,0},{32,56},{40,48},{48,40},{56,32},{64,88... | collective-permute-start | bytes 589832 | tf_op jit(solution)/shard_map/ppermute | solution.py:299
  36.1 11.8 %collective-permute-start.9 = (bf16[24,32,128]{2,1,0:T(8,128)(2,1)S(1)}, bf16[24,32,128]{2,1,0:T(8,128)(2,1)S(1)}, u32[]{:S(2)}, u32[]{:S(2)}) collective-permute-start(bf16[24,32,128]{2,1,0:T(8,128)(2,1)S(1)} %pad_maximum_fusion.a0), channel_id=1, source_target_pairs={{0,8},{8,0},{16,24},{24,16},{32,40},{40,32},{48,56},{56,48},{64,72... | collective-permute-start | bytes 589832 | tf_op jit(solution)/shard_map/ppermute | solution.py:299
  36.2 11.8 %collective-permute-start.8 = (bf16[24,32,128]{2,1,0:T(8,128)(2,1)S(1)}, bf16[24,32,128]{2,1,0:T(8,128)(2,1)S(1)}, u32[]{:S(2)}, u32[]{:S(2)}) collective-permute-start(bf16[24,32,128]{2,1,0:T(8,128)(2,1)S(1)} %pad_maximum_fusion.a0), channel_id=1, source_target_pairs={{0,16},{8,24},{16,0},{24,8},{32,48},{40,56},{48,32},{56,40},{64,80... | collective-permute-start | bytes 589832 | tf_op jit(solution)/shard_map/ppermute | solution.py:299
  38.7 5.3 %collective-permute-start.4 = (bf16[24,32,128]{2,1,0:T(8,128)(2,1)S(1)}, bf16[24,32,128]{2,1,0:T(8,128)(2,1)S(1)}, u32[]{:S(2)}, u32[]{:S(2)}) collective-permute-start(bf16[24,32,128]{2,1,0:T(8,128)(2,1)S(1)} %pad_maximum_fusion.a0), channel_id=1, source_target_pairs={{0,32},{8,40},{16,48},{24,56},{32,0},{40,8},{48,16},{56,24},{64,96... | collective-permute-start | bytes 589832 | tf_op jit(solution)/shard_map/ppermute | solution.py:298
  44.0 8.7 %collective-permute-start.7 = (bf16[24,32,128]{2,1,0:T(8,128)(2,1)S(1)}, bf16[24,32,128]{2,1,0:T(8,128)(2,1)S(1)}, u32[]{:S(2)}, u32[]{:S(2)}) collective-permute-start(bf16[24,32,128]{2,1,0:T(8,128)(2,1)S(1)} %collective-permute-done.4.b0), channel_id=1, source_target_pairs={{0,24},{8,16},{16,8},{24,0},{32,56},{40,48},{48,40},{56,32},{64,88... | collective-permute-start | bytes 589832 | tf_op jit(solution)/shard_map/ppermute | solution.py:314
  45.4 7.3 %collective-permute-start.6 = (bf16[24,32,128]{2,1,0:T(8,128)(2,1)S(1)}, bf16[24,32,128]{2,1,0:T(8,128)(2,1)S(1)}, u32[]{:S(2)}, u32[]{:S(2)}) collective-permute-start(bf16[24,32,128]{2,1,0:T(8,128)(2,1)S(1)} %collective-permute-done.4.b0), channel_id=1, source_target_pairs={{0,8},{8,0},{16,24},{24,16},{32,40},{40,32},{48,56},{56,48},{64,72... | collective-permute-start | bytes 589832 | tf_op jit(solution)/shard_map/ppermute | solution.py:314
  45.4 7.7 %collective-permute-start.5 = (bf16[24,32,128]{2,1,0:T(8,128)(2,1)S(1)}, bf16[24,32,128]{2,1,0:T(8,128)(2,1)S(1)}, u32[]{:S(2)}, u32[]{:S(2)}) collective-permute-start(bf16[24,32,128]{2,1,0:T(8,128)(2,1)S(1)} %collective-permute-done.4.b0), channel_id=1, source_target_pairs={{0,16},{8,24},{16,0},{24,8},{32,48},{40,56},{48,32},{56,40},{64,80... | collective-permute-start | bytes 589832 | tf_op jit(solution)/shard_map/ppermute | solution.py:314
  59.2 10.3 %collective-permute-start.14 = (bf16[64,4096]{1,0:T(8,128)(2,1)S(1)}, bf16[64,4096]{1,0:T(8,128)(2,1)S(1)}, u32[]{:S(2)}, u32[]{:S(2)}) collective-permute-start(bf16[64,4096]{1,0:T(8,128)(2,1)S(1)} %get-tuple-element.55), channel_id=1, source_target_pairs={{0,1},{1,0},{2,3},{3,2},{4,5},{5,4},{6,7},{7,6},{8,9},{9,8},{10,11... | collective-permute-start | bytes 1572872 | tf_op jit(solution)/shard_map/ppermute | solution.py:327
  68.9 3.3 %collective-permute-start.11 = (bf16[128,2048]{1,0:T(8,128)(2,1)S(1)}, bf16[128,2048]{1,0:T(8,128)(2,1)S(1)}, u32[]{:S(2)}, u32[]{:S(2)}) collective-permute-start(bf16[128,2048]{1,0:T(8,128)(2,1)S(1)} %get-tuple-element.49), channel_id=1, source_target_pairs={{0,1},{1,0},{2,3},{3,2},{4,5},{5,4},{6,7},{7,6},{8,9},{9,8},{10,11... | collective-permute-start | bytes 1572872 | tf_op jit(solution)/shard_map/ppermute | solution.py:327
  69.0 7.9 %collective-permute-start.13 = (bf16[128,2048]{1,0:T(8,128)(2,1)S(1)}, bf16[128,2048]{1,0:T(8,128)(2,1)S(1)}, u32[]{:S(2)}, u32[]{:S(2)}) collective-permute-start(bf16[128,2048]{1,0:T(8,128)(2,1)S(1)} %get-tuple-element.53), channel_id=1, source_target_pairs={{0,1},{1,0},{2,3},{3,2},{4,5},{5,4},{6,7},{7,6},{8,9},{9,8},{10,11... | collective-permute-start | bytes 1572872 | tf_op jit(solution)/shard_map/ppermute | solution.py:327
  69.6 8.6 %collective-permute-start.16 = (bf16[64,2048]{1,0:T(8,128)(2,1)S(1)}, bf16[64,2048]{1,0:T(8,128)(2,1)S(1)}, u32[]{:S(2)}, u32[]{:S(2)}) collective-permute-start(bf16[64,2048]{1,0:T(8,128)(2,1)S(1)} %get-tuple-element.61), channel_id=1, source_target_pairs={{0,6},{1,7},{2,0},{3,1},{4,2},{5,3},{6,4},{7,5},{8,14},{9,15},{10,... | collective-permute-start | bytes 786440 | tf_op jit(solution)/shard_map/ppermute | solution.py:330
  72.2 8.5 %collective-permute-start.15 = (bf16[64,2048]{1,0:T(8,128)(2,1)S(1)}, bf16[64,2048]{1,0:T(8,128)(2,1)S(1)}, u32[]{:S(2)}, u32[]{:S(2)}) collective-permute-start(bf16[64,2048]{1,0:T(8,128)(2,1)S(1)} %get-tuple-element.62), channel_id=1, source_target_pairs={{0,2},{1,3},{2,4},{3,5},{4,6},{5,7},{6,0},{7,1},{8,10},{9,11},{10,... | collective-permute-start | bytes 786440 | tf_op jit(solution)/shard_map/ppermute | solution.py:330
  72.3 10.8 %collective-permute-start.18 = (bf16[64,2048]{1,0:T(8,128)(2,1)S(1)}, bf16[64,2048]{1,0:T(8,128)(2,1)S(1)}, u32[]{:S(2)}, u32[]{:S(2)}) collective-permute-start(bf16[64,2048]{1,0:T(8,128)(2,1)S(1)} %get-tuple-element.65), channel_id=1, source_target_pairs={{0,6},{1,7},{2,0},{3,1},{4,2},{5,3},{6,4},{7,5},{8,14},{9,15},{10,... | collective-permute-start | bytes 786440 | tf_op jit(solution)/shard_map/ppermute | solution.py:330
  75.1 11.2 %collective-permute-start.19 = (bf16[64,2048]{1,0:T(8,128)(2,1)S(1)}, bf16[64,2048]{1,0:T(8,128)(2,1)S(1)}, u32[]{:S(2)}, u32[]{:S(2)}) collective-permute-start(bf16[64,2048]{1,0:T(8,128)(2,1)S(1)} %get-tuple-element.66.after), channel_id=1, source_target_pairs={{0,2},{1,3},{2,4},{3,5},{4,6},{5,7},{6,0},{7,1},{8,10},{9,11},{10,... | collective-permute-start | bytes 786440 | tf_op jit(solution)/shard_map/ppermute | solution.py:330
  76.9 15.0 %collective-permute-start.12 = (bf16[64,4096]{1,0:T(8,128)(2,1)S(1)}, bf16[64,4096]{1,0:T(8,128)(2,1)S(1)}, u32[]{:S(2)}, u32[]{:S(2)}) collective-permute-start(bf16[64,4096]{1,0:T(8,128)(2,1)S(1)} %get-tuple-element.51), channel_id=1, source_target_pairs={{0,1},{1,0},{2,3},{3,2},{4,5},{5,4},{6,7},{7,6},{8,9},{9,8},{10,11... | collective-permute-start | bytes 1572872 | tf_op jit(solution)/shard_map/ppermute | solution.py:327
  80.9 7.9 %collective-permute-start.20 = (bf16[64,2048]{1,0:T(8,128)(2,1)S(1)}, bf16[64,2048]{1,0:T(8,128)(2,1)S(1)}, u32[]{:S(2)}, u32[]{:S(2)}) collective-permute-start(bf16[64,2048]{1,0:T(8,128)(2,1)S(1)} %get-tuple-element.63), channel_id=1, source_target_pairs={{0,6},{1,7},{2,0},{3,1},{4,2},{5,3},{6,4},{7,5},{8,14},{9,15},{10,... | collective-permute-start | bytes 786440 | tf_op jit(solution)/shard_map/ppermute | solution.py:330
  81.5 10.4 %collective-permute-start.17 = (bf16[64,2048]{1,0:T(8,128)(2,1)S(1)}, bf16[64,2048]{1,0:T(8,128)(2,1)S(1)}, u32[]{:S(2)}, u32[]{:S(2)}) collective-permute-start(bf16[64,2048]{1,0:T(8,128)(2,1)S(1)} %get-tuple-element.64), channel_id=1, source_target_pairs={{0,2},{1,3},{2,4},{3,5},{4,6},{5,7},{6,0},{7,1},{8,10},{9,11},{10,... | collective-permute-start | bytes 786440 | tf_op jit(solution)/shard_map/ppermute | solution.py:330
  (1 other events, 16.9 us)

commit v10 on v9

--- a/solution.py
+++ b/solution.py
@@ -24,6 +24,8 @@
 Z, Y, X = 8, 4, 4
 BF16, F32 = jnp.bfloat16, jnp.float32
 META = BLOCKS
+VERT = META + 6
+SLASH = VERT + HEADS * LISTED
 
 
 def z_pairs(step):
@@ -70,24 +72,27 @@
             copies.start(part, kv.at[kind, :, pl.ds(32 * p, 32)])
 
 
-def slots_of(table, vert, h):
-    return [table[jnp.maximum(vert[h, e], 0)] for e in range(LISTED)]
+def ids_of(table, h):
+    return [table[VERT + h * LISTED + e] for e in range(LISTED)]
+
+
+def slots_of(table, h):
+    return [table[jnp.maximum(i, 0)] for i in ids_of(table, h)]
 
 
 def listed(kv, kind, slots):
     return jnp.concatenate([kv[kind, slot] for slot in slots], axis=0)
 
 
-def limits(vert, places, h):
-    ids = [vert[h, e] for e in range(LISTED)]
-    return jnp.concatenate([places + jnp.where(i >= 0, i * ROWS, NEVER) for i in ids], axis=1)
-
-
-def near_base(table, vert, slash, h, run, j):
-    block = table[META + 2] + run - slash[h, j]
+def limits(table, places, h):
+    return jnp.concatenate([places + jnp.where(i >= 0, i * ROWS, NEVER) for i in ids_of(table, h)], axis=1)
+
+
+def near_base(table, ids, run, offset):
+    block = table[META + 2] + run - offset
     use = block >= 0
-    for e in range(LISTED):
-        use = jnp.logical_and(use, vert[h, e] != block)
+    for i in ids:
+        use = jnp.logical_and(use, i != block)
     return jnp.where(use, block * ROWS, NEVER)
 
 
@@ -103,7 +108,7 @@
     return jnp.concatenate([column_block] * count, axis=1)
 
 
-def band_kernel(table, vert, slash, sink, q, w, prev, kc, vc, acc, tops, sums, w_out, qs, band, sems):
+def band_kernel(table, sink, q, w, prev, kc, vc, acc, tops, sums, w_out, qs, band, sems):
     copies = Copies(sems)
     copies.start(q, qs)
     for kind, cur in enumerate((kc, vc)):
@@ -121,36 +126,38 @@
     within = lax.broadcasted_iota(jnp.int32, (1, ROWS), 1)
     for h in range(HEADS):
         cols = slice(h * HEAD, (h + 1) * HEAD)
-        raw_sink = sink[h] * (1.0 / SCALE)
+        raw_sink = sink[h:h + 1, :]
+        ids = ids_of(table, h)
+        offsets = [table[SLASH + h * BANDS + j] for j in range(BANDS)]
         score = []
         for run in range(RUNS):
             rows = slice(run * ROWS, (run + 1) * ROWS)
-            keys = jnp.concatenate([band[0, RUNS + run - slash[h, j]] for j in range(BANDS)], axis=0)
+            keys = jnp.concatenate([band[0, RUNS + run - offset] for offset in offsets], axis=0)
             limit = jnp.concatenate(
-                [within + near_base(table, vert, slash, h, run, j) for j in range(BANDS)], axis=1)
+                [within + near_base(table, ids, run, offset) for offset in offsets], axis=1)
             score.append(jnp.where(token[rows] >= limit, product(qs[rows, cols], keys), LOW))
         score = jnp.concatenate(score, axis=0)
-        top = jnp.maximum(jnp.max(score, axis=1, keepdims=True), raw_sink)
-        weight = jnp.exp2((score - top) * FACTOR)
-        total = jnp.sum(weight, axis=1, keepdims=True) + jnp.exp2((raw_sink - top) * FACTOR)
+        top = jnp.maximum(wide(jnp.max(score, axis=1, keepdims=True)), raw_sink)
+        weight = jnp.exp2((score - across(top, BANDS)) * FACTOR)
+        total = wide(jnp.sum(weight, axis=1, keepdims=True)) + jnp.exp2((raw_sink - top) * FACTOR)
         weight = weight.astype(BF16)
         for run in range(RUNS):
             rows = slice(run * ROWS, (run + 1) * ROWS)
-            vals = jnp.concatenate([band[1, RUNS + run - slash[h, j]] for j in range(BANDS)], axis=0)
+            vals = jnp.concatenate([band[1, RUNS + run - offset] for offset in offsets], axis=0)
             acc[rows, cols] = jnp.dot(weight[rows], vals, preferred_element_type=F32)
-        tops[:, cols] = wide(top)
-        sums[:, cols] = wide(total)
+        tops[:, cols] = top
+        sums[:, cols] = total
     copies.wait()
 
 
-def add_listed(table, vert, qs, kv, late, acc, tops, sums, put):
+def add_listed(table, qs, kv, late, acc, tops, sums, put):
     token = TOKENS // RUNS * table[META + 2] + lax.broadcasted_iota(jnp.int32, (TOKENS, 1), 0)
     places = key_places(table, late)
     for h in range(HEADS):
         cols = slice(h * HEAD, (h + 1) * HEAD)
-        slots = slots_of(table, vert, h)
+        slots = slots_of(table, h)
         score = product(qs[:, cols], listed(kv, 0, slots))
-        score = jnp.where(token >= limits(vert, places, h), score, LOW)
+        score = jnp.where(token >= limits(table, places, h), score, LOW)
         before = tops[:, cols]
         top = jnp.maximum(wide(jnp.max(score, axis=1, keepdims=True)), before)
         weight = jnp.exp2((score - across(top, LISTED * HALF // HEAD)) * FACTOR)
@@ -160,7 +167,7 @@
         put(cols, mixed + acc[:, cols] * fade, top, total)
 
 
-def early_kernel(table, vert, qs, a0, a2, a1, a3, acc, tops, sums, acc_out, tops_out, sums_out, kv, sems):
+def early_kernel(table, qs, a0, a2, a1, a3, acc, tops, sums, acc_out, tops_out, sums_out, kv, sems):
     copies = Copies(sems)
     load_half(copies, table[META], a0, a2, a1, a3, kv)
     copies.wait()
@@ -168,7 +175,7 @@
     def put(cols, mixed, top, total):
         acc_out[:, cols], tops_out[:, cols], sums_out[:, cols] = mixed, top, total
 
-    add_listed(table, vert, qs, kv, False, acc, tops, sums, put)
+    add_listed(table, qs, kv, False, acc, tops, sums, put)
 
 
 def project(att, w, blocks, core, keeps, give):
@@ -186,7 +193,7 @@
         give(n * tile, tile, out[len(blocks) * HALF:])
 
 
-def late_kernel(table, vert, qs, w, b0, b2, b1, b3, acc, tops, sums, att, keep, give, kv, sems):
+def late_kernel(table, qs, w, b0, b2, b1, b3, acc, tops, sums, att, keep, give, kv, sems):
     copies = Copies(sems)
     load_half(copies, table[META], b0, b2, b1, b3, kv)
     copies.wait()
@@ -194,7 +201,7 @@
     def put(cols, mixed, top, total):
         att[:, cols] = (mixed * (1.0 / total)).astype(BF16)
 
-    add_listed(table, vert, qs, kv, True, acc, tops, sums, put)
+    add_listed(table, qs, kv, True, acc, tops, sums, put)
     project(att, w, [(table[META + 5] + 2) % X], table[META + 1], [keep], functools.partial(store, give))
 
 
@@ -252,12 +259,13 @@
     return functools.reduce(lambda a, b: a + b, [t.astype(F32) for t in terms]).astype(BF16)
 
 
-def tables(c, x, core, vert_blocks):
+def tables(c, x, core, vert_blocks, slash_offsets):
     block = jnp.arange(BLOCKS, dtype=jnp.int32)
     present = jnp.any(vert_blocks[:, :, None] == block, axis=(0, 1)).astype(jnp.int32)
     rank = jnp.sum(jnp.where(block[:, None] > block[None, :], present[None, :], 0), axis=1)
     meta = jnp.stack([c % 2, core, RUNS * c, c // Y, (c % Y) // 2, x]).astype(jnp.int32)
-    return jnp.where(present > 0, rank, -1), jnp.concatenate([rank, meta])
+    table = jnp.concatenate([rank, meta, vert_blocks.reshape(-1), slash_offsets.reshape(-1)])
+    return jnp.where(present > 0, rank, -1), table
 
 
 def spread_kernel(keys, values, out, sems):
@@ -274,7 +282,8 @@
     x, core = h // 2, h % 2
     keys = keys.reshape(RUNS, ROWS, HEAD)
     values = values.reshape(RUNS, ROWS, HEAD)
-    place, table = tables(c, x, core, vert_blocks)
+    place, table = tables(c, x, core, vert_blocks, slash_offsets)
+    sink = jnp.broadcast_to(sink_logits[:, None] * (1.0 / SCALE), (HEADS, HEAD))
     far_keys, far_values = [pltpu.with_memory_space_constraint(a.reshape(RUNS, 16, 8, HEAD), pltpu.HBM)
                             for a in (keys, values)]
     (spread,) = call(
@@ -283,6 +292,7 @@
     spread = spread.reshape(Z * Y, RUNS * 8, HEAD)
     prev = lax.ppermute(spread, "ctx", [(s, s + 1) for s in range(Z * Y - 1)]).reshape(16, 2, RUNS, 8, HEAD)
     got = lax.all_to_all(spread, "ctx", 0, 0, tiled=True).reshape(BLOCKS * 8, HEAD)
+    place, table, sink = lax.optimization_barrier((place, table, sink))
     r = jnp.arange(SLOTS * 8, dtype=jnp.int32)[:, None]
     col = jnp.arange(BLOCKS * 8, dtype=jnp.int32)[None, :]
     pick = (jnp.repeat(place, 8)[None, :] == r // 8) & (col % 8 == r % 8)
@@ -306,19 +316,19 @@
     far_weight = pltpu.with_memory_space_constraint(output_weight, pltpu.HBM)
     state = [((TOKENS, HEADS * HEAD), F32)] * 3
     acc, tops, sums, w, q = call(
-        band_kernel, [SMEM] * 4 + [ANY] * 2 + [VMEM, ANY, ANY], state + [(output_weight.shape, BF16), rows],
+        band_kernel, [SMEM, VMEM] + [ANY] * 2 + [VMEM, ANY, ANY], state + [(output_weight.shape, BF16), rows],
         [pltpu.VMEM((2, 2 * RUNS, ROWS, HEAD), BF16), pltpu.SemaphoreType.DMA((7,))], 3, "band",
-    )(table, vert_blocks, slash_offsets, sink_logits, far_queries, far_weight, prev,
+    )(table, sink, far_queries, far_weight, prev,
       *[pltpu.with_memory_space_constraint(a, pltpu.HBM) for a in (keys, values)])
     b0, acc = lax.optimization_barrier((b0, acc))
     b1, b2, b3 = [lax.ppermute(b0, "ctx", y_pairs(f)) for f in (1, 2, 3)]
     acc, tops, sums = call(
-        early_kernel, [SMEM, SMEM, VMEM] + [ANY] * 4 + [VMEM] * 3, state, [kv, pltpu.SemaphoreType.DMA((4,))], 5, "early",
-    )(table, vert_blocks, q, a0, a2, a1, a3, acc, tops, sums)
+        early_kernel, [SMEM, VMEM] + [ANY] * 4 + [VMEM] * 3, state, [kv, pltpu.SemaphoreType.DMA((4,))], 5, "early",
+    )(table, q, a0, a2, a1, a3, acc, tops, sums)
     att, keep_far, give_far = call(
-        late_kernel, [SMEM, SMEM, VMEM, VMEM] + [ANY] * 4 + [VMEM] * 3,
+        late_kernel, [SMEM, VMEM, VMEM] + [ANY] * 4 + [VMEM] * 3,
         [rows, part, part], [kv, pltpu.SemaphoreType.DMA((4,))], 0.01, "late",
-    )(table, vert_blocks, q, w, b0, b2, b1, b3, acc, tops, sums)
+    )(table, q, w, b0, b2, b1, b3, acc, tops, sums)
     halves = ((2 * HALF, width // 2), BF16)
     keep_below, keep_above, give_direct, give_relayed = call(
         sides_kernel, [SMEM, VMEM, VMEM], [part, part, halves, halves], [], 0.01, "sides",

time: 93.2 us -> 93.1 us (level)
  no operation moved by 1% of the time
where the time goes in v10:
time: 93.1 us; the launch traced here: 92.9 us
  starting transfers between devices  44.4 us (48%)
  Pallas kernels  23.4 us (25%)
  waiting for transfers between devices  23.2 us (25%)
    all_to_all x1, starting transfers between devices, per_device(): lax.all_to_all(spread, 'ctx', 0, 0, tiled=True).reshape(BLOCKS * 8, HEAD)  12 us
    ppermute x6, waiting for transfers between devices, to_x(): return lax.ppermute(a, 'head', x_pairs(step))  11.9 us
    ppermute x4, starting transfers between devices, swap(): return lax.ppermute(a, 'head', CORE_PAIRS)  8.75 us
    all_to_all x1, waiting for transfers between devices, per_device(): lax.all_to_all(spread, 'ctx', 0, 0, tiled=True).reshape(BLOCKS * 8, HEAD)  7.13 us
    ppermute x6, starting transfers between devices, to_x(): return lax.ppermute(a, 'head', x_pairs(step))  6.86 us
    pallas_call x1, Pallas kernels, per_device(): call(late_kernel, [SMEM, VMEM, VMEM] + [ANY] * 4 + [VMEM] * 3, [rows, par...  6 us
    ppermute x3, starting transfers between devices, from_z(): return lax.ppermute(a, 'ctx', z_pairs(-offset))  5.71 us
    pallas_call x1, Pallas kernels, per_device(): call(band_kernel, [SMEM, VMEM] + [ANY] * 2 + [VMEM, ANY, ANY], state + [(...  5.18 us
  transfers between devices with their start and end apart: 22, of which 9 were waited for; matrix products, arithmetic and copies ran while one was open for 2% of the time, Pallas kernels for 16%

profile of v10, /device:TPU:1, one launch (start us, length us, event | category | flops | bytes accessed | tf_op | source)
XLA Modules:
  0.0 92.9 jit_solution(3321075183309914321)
XLA Ops:
  0.0 1.7 %spread.1 = bf16[16,2,4,8,128]{4,3,2,1,0:T(8,128)(2,1)} custom-call(bf16[4,16,8,128]{3,2,1,0:T(8,128)(2,1)} %bitcast.18, bf16[4,16,8,128]{3,2,1,0:T(8,128)(2,1)} %bitcast.20), custom_call_target="tpu_custom_call" | custom-call | flops 1000000000 | bytes 1048576 | tf_op jit(solution)/shard_map/spread/pallas_call | solution.py:289
  1.7 12.0 %all-to-all-start = ((bf16[32,32,128]{2,1,0:T(8,128)(2,1)}), bf16[32,32,128]{2,1,0:T(8,128)(2,1)S(1)}, u32[]{:S(2)}, u32[]{:S(2)}) async-start(bf16[32,32,128]{2,1,0:T(8,128)(2,1)} %bitcast.8), calls=%async_computation | async-start | bytes 524288 | tf_op jit(solution)/shard_map/all_to_all | solution.py:294
  13.7 3.1 %collective-permute-start = (bf16[32,32,128]{2,1,0:T(8,128)(2,1)}, bf16[32,32,128]{2,1,0:T(8,128)(2,1)S(1)}, u32[]{:S(2)}, u32[]{:S(2)}) collective-permute-start(bf16[32,32,128]{2,1,0:T(8,128)(2,1)} %bitcast.8), channel_id=1, source_target_pairs={{0,8},{8,16},{16,24},{24,32},{32,40},{40,48},{48,56},{56,64},{64,7... | collective-permute-start | bytes 786440 | tf_op jit(solution)/shard_map/ppermute | solution.py:293
  17.8 7.1 %all-to-all-done = bf16[32,32,128]{2,1,0:T(8,128)(2,1)S(1)} async-done(((bf16[32,32,128]{2,1,0:T(8,128)(2,1)}), bf16[32,32,128]{2,1,0:T(8,128)(2,1)S(1)}, u32[]{:S(2)}, u32[]{:S(2)}) %all-to-all-start) | async-done | bytes 262176 | tf_op jit(solution)/shard_map/all_to_all | solution.py:294
  25.3 1.6 %collective-permute-start.3 = (bf16[24,8,128]{2,1,0:T(8,128)(2,1)S(1)}, bf16[24,8,128]{2,1,0:T(8,128)(2,1)S(1)}, u32[]{:S(2)}, u32[]{:S(2)}) collective-permute-start(bf16[24,8,128]{2,1,0:T(8,128)(2,1)S(1)} %fusion), channel_id=1, source_target_pairs={{0,64},{8,72},{16,80},{24,88},{32,96},{40,104},{48,112},{56,120},{... | collective-permute-start | bytes 147464 | tf_op jit(solution)/shard_map/ppermute | solution.py:303
  26.9 2.1 %collective-permute-start.2 = (bf16[24,8,128]{2,1,0:T(8,128)(2,1)S(1)}, bf16[24,8,128]{2,1,0:T(8,128)(2,1)S(1)}, u32[]{:S(2)}, u32[]{:S(2)}) collective-permute-start(bf16[24,8,128]{2,1,0:T(8,128)(2,1)S(1)} %fusion), channel_id=1, source_target_pairs={{0,128},{8,136},{16,144},{24,152},{32,160},{40,168},{48,176},{56,1... | collective-permute-start | bytes 147464 | tf_op jit(solution)/shard_map/ppermute | solution.py:303
  29.0 2.0 %collective-permute-start.1 = (bf16[24,8,128]{2,1,0:T(8,128)(2,1)S(1)}, bf16[24,8,128]{2,1,0:T(8,128)(2,1)S(1)}, u32[]{:S(2)}, u32[]{:S(2)}) collective-permute-start(bf16[24,8,128]{2,1,0:T(8,128)(2,1)S(1)} %fusion), channel_id=1, source_target_pairs={{0,192},{8,200},{16,208},{24,216},{32,224},{40,232},{48,240},{56,2... | collective-permute-start | bytes 147464 | tf_op jit(solution)/shard_map/ppermute | solution.py:303
  31.0 3.1 %collective-permute-done.2 = bf16[24,8,128]{2,1,0:T(8,128)(2,1)S(1)} collective-permute-done((bf16[24,8,128]{2,1,0:T(8,128)(2,1)S(1)}, bf16[24,8,128]{2,1,0:T(8,128)(2,1)S(1)}, u32[]{:S(2)}, u32[]{:S(2)}) %collective-permute-start.2) | collective-permute-done | bytes 49184 | tf_op jit(solution)/shard_map/ppermute | solution.py:303
  34.8 1.4 %collective-permute-start.10 = (bf16[24,32,128]{2,1,0:T(8,128)(2,1)S(1)}, bf16[24,32,128]{2,1,0:T(8,128)(2,1)S(1)}, u32[]{:S(2)}, u32[]{:S(2)}) collective-permute-start(bf16[24,32,128]{2,1,0:T(8,128)(2,1)S(1)} %pad_maximum_fusion.a0), channel_id=1, source_target_pairs={{0,24},{8,16},{16,8},{24,0},{32,56},{40,48},{48,40},{56,32},{64,88... | collective-permute-start | bytes 589832 | tf_op jit(solution)/shard_map/ppermute | solution.py:309
  36.2 2.6 %collective-permute-start.8 = (bf16[24,32,128]{2,1,0:T(8,128)(2,1)S(1)}, bf16[24,32,128]{2,1,0:T(8,128)(2,1)S(1)}, u32[]{:S(2)}, u32[]{:S(2)}) collective-permute-start(bf16[24,32,128]{2,1,0:T(8,128)(2,1)S(1)} %pad_maximum_fusion.a0), channel_id=1, source_target_pairs={{0,16},{8,24},{16,0},{24,8},{32,48},{40,56},{48,32},{56,40},{64,80... | collective-permute-start | bytes 589832 | tf_op jit(solution)/shard_map/ppermute | solution.py:309
  38.7 5.2 %band.1 = (f32[512,1024]{1,0:T(8,128)S(1)}, f32[512,1024]{1,0:T(8,128)S(1)}, f32[512,1024]{1,0:T(8,128)S(1)}, bf16[1024,4096]{1,0:T(8,128)(2,1)S(1)}, bf16[512,1024]{1,0:T(8,128)(2,1)S(1)}) custom-call(s32[222]{0:T(256)S(1)} %concatenate.6.table, f32[8,128]{1,0:T(8,128)S(1)} %broadcast_in_dim.35.sink, bf16[512,1024]{1,0:T(8,128)(2,1)} %q.1, ...), custom_call_target="tpu_custom_call" | custom-call | flops 3000000000 | bytes 3145728 | tf_op jit(solution)/shard_map/band/pallas_call | solution.py:318
  43.9 1.4 %collective-permute-start.7 = (bf16[24,32,128]{2,1,0:T(8,128)(2,1)S(1)}, bf16[24,32,128]{2,1,0:T(8,128)(2,1)S(1)}, u32[]{:S(2)}, u32[]{:S(2)}) collective-permute-start(bf16[24,32,128]{2,1,0:T(8,128)(2,1)S(1)} %collective-permute-done.4.b0), channel_id=1, source_target_pairs={{0,24},{8,16},{16,8},{24,0},{32,56},{40,48},{48,40},{56,32},{64,88... | collective-permute-start | bytes 589832 | tf_op jit(solution)/shard_map/ppermute | solution.py:324
  45.3 2.6 %collective-permute-start.5 = (bf16[24,32,128]{2,1,0:T(8,128)(2,1)S(1)}, bf16[24,32,128]{2,1,0:T(8,128)(2,1)S(1)}, u32[]{:S(2)}, u32[]{:S(2)}) collective-permute-start(bf16[24,32,128]{2,1,0:T(8,128)(2,1)S(1)} %collective-permute-done.4.b0), channel_id=1, source_target_pairs={{0,16},{8,24},{16,0},{24,8},{32,48},{40,56},{48,32},{56,40},{64,80... | collective-permute-start | bytes 589832 | tf_op jit(solution)/shard_map/ppermute | solution.py:324
  47.9 4.7 %early.1 = (f32[512,1024]{1,0:T(8,128)S(1)}, f32[512,1024]{1,0:T(8,128)S(1)}, f32[512,1024]{1,0:T(8,128)S(1)}) custom-call(s32[222]{0:T(256)S(1)} %concatenate.6.table, bf16[512,1024]{1,0:T(8,128)(2,1)S(1)} %get-tuple-element.40.qs, bf16[24,32,128]{2,1,0:T(8,128)(2,1)S(1)} %pad_maximum_fusion.a0, bf16[24,32,128]{2,1,0:T(8,128)(2,1)S(1)} %collective-permute-done.8.a2, ...), custom_call_target="tpu_custom_call" | custom-call | flops 5000000000 | bytes 5242880 | tf_op jit(solution)/shard_map/early/pallas_call | solution.py:325
  53.0 6.0 %late.1 = (bf16[512,1024]{1,0:T(8,128)(2,1)S(1)}, bf16[64,4096]{1,0:T(8,128)(2,1)S(1)}, bf16[64,4096]{1,0:T(8,128)(2,1)S(1)}) custom-call(s32[222]{0:T(256)S(1)} %concatenate.6.table, bf16[512,1024]{1,0:T(8,128)(2,1)S(1)} %get-tuple-element.40.qs, bf16[1024,4096]{1,0:T(8,128)(2,1)S(1)} %get-tuple-element.41.w, ...), custom_call_target="tpu_custom_call" | custom-call | flops 10000000 | bytes 10485 | tf_op jit(solution)/shard_map/late/pallas_call | solution.py:328
  59.0 6.9 %collective-permute-start.14 = (bf16[64,4096]{1,0:T(8,128)(2,1)S(1)}, bf16[64,4096]{1,0:T(8,128)(2,1)S(1)}, u32[]{:S(2)}, u32[]{:S(2)}) collective-permute-start(bf16[64,4096]{1,0:T(8,128)(2,1)S(1)} %get-tuple-element.61), channel_id=1, source_target_pairs={{0,1},{1,0},{2,3},{3,2},{4,5},{5,4},{6,7},{7,6},{8,9},{9,8},{10,11... | collective-permute-start | bytes 1572872 | tf_op jit(solution)/shard_map/ppermute | solution.py:337
  65.9 2.9 %sides.1 = (bf16[64,4096]{1,0:T(8,128)(2,1)S(1)}, bf16[64,4096]{1,0:T(8,128)(2,1)S(1)}, bf16[128,2048]{1,0:T(8,128)(2,1)S(1)}, bf16[128,2048]{1,0:T(8,128)(2,1)S(1)}) custom-call(s32[222]{0:T(256)S(1)} %concatenate.6.table, bf16[512,1024]{1,0:T(8,128)(2,1)S(1)} %get-tuple-element.53.att, bf16[1024,4096]{1,0:T(8,128)(2,1)S(1)} %get-tuple-element.41.w), custom_call_target="tpu_custom_call" | custom-call | flops 10000000 | bytes 10485 | tf_op jit(solution)/shard_map/sides/pallas_call | solution.py:333
  69.6 2.6 %collective-permute-start.16 = (bf16[64,2048]{1,0:T(8,128)(2,1)S(1)}, bf16[64,2048]{1,0:T(8,128)(2,1)S(1)}, u32[]{:S(2)}, u32[]{:S(2)}) collective-permute-start(bf16[64,2048]{1,0:T(8,128)(2,1)S(1)} %get-tuple-element.67), channel_id=1, source_target_pairs={{0,6},{1,7},{2,0},{3,1},{4,2},{5,3},{6,4},{7,5},{8,14},{9,15},{10,... | collective-permute-start | bytes 786440 | tf_op jit(solution)/shard_map/ppermute | solution.py:340
  72.3 2.8 %collective-permute-start.18 = (bf16[64,2048]{1,0:T(8,128)(2,1)S(1)}, bf16[64,2048]{1,0:T(8,128)(2,1)S(1)}, u32[]{:S(2)}, u32[]{:S(2)}) collective-permute-start(bf16[64,2048]{1,0:T(8,128)(2,1)S(1)} %get-tuple-element.71), channel_id=1, source_target_pairs={{0,6},{1,7},{2,0},{3,1},{4,2},{5,3},{6,4},{7,5},{8,14},{9,15},{10,... | collective-permute-start | bytes 786440 | tf_op jit(solution)/shard_map/ppermute | solution.py:340
  75.0 1.8 %own.1 = (bf16[64,4096]{1,0:T(8,128)(2,1)S(1)}, bf16[64,4096]{1,0:T(8,128)(2,1)S(1)}) custom-call(s32[222]{0:T(256)S(1)} %concatenate.6.table, bf16[512,1024]{1,0:T(8,128)(2,1)S(1)} %get-tuple-element.53.att, bf16[1024,4096]{1,0:T(8,128)(2,1)S(1)} %get-tuple-element.41.w, bf16[64,2048]{1,0:T(8,128)(2,1)S(1)} %get-tuple-element.72.after), custom_call_target="tpu_custom_call" | custom-call | flops 10000000 | bytes 10485 | tf_op jit(solution)/shard_map/own/pallas_call | solution.py:350
  78.1 2.5 %collective-permute-done.15 = bf16[64,2048]{1,0:T(8,128)(2,1)S(1)} collective-permute-done((bf16[64,2048]{1,0:T(8,128)(2,1)S(1)}, bf16[64,2048]{1,0:T(8,128)(2,1)S(1)}, u32[]{:S(2)}, u32[]{:S(2)}) %collective-permute-start.15) | collective-permute-done | bytes 262176 | tf_op jit(solution)/shard_map/ppermute | solution.py:340
  83.1 3.1 %collective-permute-done.19.right_below = bf16[64,2048]{1,0:T(8,128)(2,1)S(1)} collective-permute-done((bf16[64,2048]{1,0:T(8,128)(2,1)S(1)}, bf16[64,2048]{1,0:T(8,128)(2,1)S(1)}, u32[]{:S(2)}, u32[]{:S(2)}) %collective-permute-start.19) | collective-permute-done | bytes 262176 | tf_op jit(solution)/shard_map/ppermute | solution.py:340
  86.2 2.5 %collective-permute-done.20.right_above = bf16[64,2048]{1,0:T(8,128)(2,1)S(1)} collective-permute-done((bf16[64,2048]{1,0:T(8,128)(2,1)S(1)}, bf16[64,2048]{1,0:T(8,128)(2,1)S(1)}, u32[]{:S(2)}, u32[]{:S(2)}) %collective-permute-start.20) | collective-permute-done | bytes 262176 | tf_op jit(solution)/shard_map/ppermute | solution.py:340
  88.7 3.1 %collective-permute-done.17.left_below = bf16[64,2048]{1,0:T(8,128)(2,1)S(1)} collective-permute-done((bf16[64,2048]{1,0:T(8,128)(2,1)S(1)}, bf16[64,2048]{1,0:T(8,128)(2,1)S(1)}, u32[]{:S(2)}, u32[]{:S(2)}) %collective-permute-start.17) | collective-permute-done | bytes 262176 | tf_op jit(solution)/shard_map/ppermute | solution.py:340
  (52 shorter events, 7.8 us)
Async XLA Ops:
  0.0 17.1 %copy-start.2 = (f32[8]{0:T(128)S(1)}, f32[8]{0:T(128)}, u32[]{:S(2)}) copy-start(f32[8]{0:T(128)} %param.10) | copy-start | bytes 100
  0.0 17.1 %copy-start.1 = (s32[8,3]{0,1:T(4,128)S(1)}, s32[8,3]{0,1:T(4,128)}, u32[]{:S(2)}) copy-start(s32[8,3]{0,1:T(4,128)} %param.12) | copy-start | bytes 292
  1.7 23.2 %all-to-all-start = ((bf16[32,32,128]{2,1,0:T(8,128)(2,1)}), bf16[32,32,128]{2,1,0:T(8,128)(2,1)S(1)}, u32[]{:S(2)}, u32[]{:S(2)}) async-start(bf16[32,32,128]{2,1,0:T(8,128)(2,1)} %bitcast.8), calls=%async_computation | async-start | bytes 524288 | tf_op jit(solution)/shard_map/all_to_all | solution.py:294
  13.7 17.3 %collective-permute-start = (bf16[32,32,128]{2,1,0:T(8,128)(2,1)}, bf16[32,32,128]{2,1,0:T(8,128)(2,1)S(1)}, u32[]{:S(2)}, u32[]{:S(2)}) collective-permute-start(bf16[32,32,128]{2,1,0:T(8,128)(2,1)} %bitcast.8), channel_id=1, source_target_pairs={{0,8},{8,16},{16,24},{24,32},{32,40},{40,48},{48,56},{56,64},{64,7... | collective-permute-start | bytes 786440 | tf_op jit(solution)/shard_map/ppermute | solution.py:293
  25.3 5.7 %collective-permute-start.3 = (bf16[24,8,128]{2,1,0:T(8,128)(2,1)S(1)}, bf16[24,8,128]{2,1,0:T(8,128)(2,1)S(1)}, u32[]{:S(2)}, u32[]{:S(2)}) collective-permute-start(bf16[24,8,128]{2,1,0:T(8,128)(2,1)S(1)} %fusion), channel_id=1, source_target_pairs={{0,64},{8,72},{16,80},{24,88},{32,96},{40,104},{48,112},{56,120},{... | collective-permute-start | bytes 147464 | tf_op jit(solution)/shard_map/ppermute | solution.py:303
  26.9 7.3 %collective-permute-start.2 = (bf16[24,8,128]{2,1,0:T(8,128)(2,1)S(1)}, bf16[24,8,128]{2,1,0:T(8,128)(2,1)S(1)}, u32[]{:S(2)}, u32[]{:S(2)}) collective-permute-start(bf16[24,8,128]{2,1,0:T(8,128)(2,1)S(1)} %fusion), channel_id=1, source_target_pairs={{0,128},{8,136},{16,144},{24,152},{32,160},{40,168},{48,176},{56,1... | collective-permute-start | bytes 147464 | tf_op jit(solution)/shard_map/ppermute | solution.py:303
  29.0 5.7 %collective-permute-start.1 = (bf16[24,8,128]{2,1,0:T(8,128)(2,1)S(1)}, bf16[24,8,128]{2,1,0:T(8,128)(2,1)S(1)}, u32[]{:S(2)}, u32[]{:S(2)}) collective-permute-start(bf16[24,8,128]{2,1,0:T(8,128)(2,1)S(1)} %fusion), channel_id=1, source_target_pairs={{0,192},{8,200},{16,208},{24,216},{32,224},{40,232},{48,240},{56,2... | collective-permute-start | bytes 147464 | tf_op jit(solution)/shard_map/ppermute | solution.py:303
  34.8 10.5 %collective-permute-start.10 = (bf16[24,32,128]{2,1,0:T(8,128)(2,1)S(1)}, bf16[24,32,128]{2,1,0:T(8,128)(2,1)S(1)}, u32[]{:S(2)}, u32[]{:S(2)}) collective-permute-start(bf16[24,32,128]{2,1,0:T(8,128)(2,1)S(1)} %pad_maximum_fusion.a0), channel_id=1, source_target_pairs={{0,24},{8,16},{16,8},{24,0},{32,56},{40,48},{48,40},{56,32},{64,88... | collective-permute-start | bytes 589832 | tf_op jit(solution)/shard_map/ppermute | solution.py:309
  36.1 11.7 %collective-permute-start.9 = (bf16[24,32,128]{2,1,0:T(8,128)(2,1)S(1)}, bf16[24,32,128]{2,1,0:T(8,128)(2,1)S(1)}, u32[]{:S(2)}, u32[]{:S(2)}) collective-permute-start(bf16[24,32,128]{2,1,0:T(8,128)(2,1)S(1)} %pad_maximum_fusion.a0), channel_id=1, source_target_pairs={{0,8},{8,0},{16,24},{24,16},{32,40},{40,32},{48,56},{56,48},{64,72... | collective-permute-start | bytes 589832 | tf_op jit(solution)/shard_map/ppermute | solution.py:309
  36.2 11.7 %collective-permute-start.8 = (bf16[24,32,128]{2,1,0:T(8,128)(2,1)S(1)}, bf16[24,32,128]{2,1,0:T(8,128)(2,1)S(1)}, u32[]{:S(2)}, u32[]{:S(2)}) collective-permute-start(bf16[24,32,128]{2,1,0:T(8,128)(2,1)S(1)} %pad_maximum_fusion.a0), channel_id=1, source_target_pairs={{0,16},{8,24},{16,0},{24,8},{32,48},{40,56},{48,32},{56,40},{64,80... | collective-permute-start | bytes 589832 | tf_op jit(solution)/shard_map/ppermute | solution.py:309
  38.7 5.2 %collective-permute-start.4 = (bf16[24,32,128]{2,1,0:T(8,128)(2,1)S(1)}, bf16[24,32,128]{2,1,0:T(8,128)(2,1)S(1)}, u32[]{:S(2)}, u32[]{:S(2)}) collective-permute-start(bf16[24,32,128]{2,1,0:T(8,128)(2,1)S(1)} %pad_maximum_fusion.a0), channel_id=1, source_target_pairs={{0,32},{8,40},{16,48},{24,56},{32,0},{40,8},{48,16},{56,24},{64,96... | collective-permute-start | bytes 589832 | tf_op jit(solution)/shard_map/ppermute | solution.py:308
  43.9 8.7 %collective-permute-start.7 = (bf16[24,32,128]{2,1,0:T(8,128)(2,1)S(1)}, bf16[24,32,128]{2,1,0:T(8,128)(2,1)S(1)}, u32[]{:S(2)}, u32[]{:S(2)}) collective-permute-start(bf16[24,32,128]{2,1,0:T(8,128)(2,1)S(1)} %collective-permute-done.4.b0), channel_id=1, source_target_pairs={{0,24},{8,16},{16,8},{24,0},{32,56},{40,48},{48,40},{56,32},{64,88... | collective-permute-start | bytes 589832 | tf_op jit(solution)/shard_map/ppermute | solution.py:324
  45.3 7.3 %collective-permute-start.6 = (bf16[24,32,128]{2,1,0:T(8,128)(2,1)S(1)}, bf16[24,32,128]{2,1,0:T(8,128)(2,1)S(1)}, u32[]{:S(2)}, u32[]{:S(2)}) collective-permute-start(bf16[24,32,128]{2,1,0:T(8,128)(2,1)S(1)} %collective-permute-done.4.b0), channel_id=1, source_target_pairs={{0,8},{8,0},{16,24},{24,16},{32,40},{40,32},{48,56},{56,48},{64,72... | collective-permute-start | bytes 589832 | tf_op jit(solution)/shard_map/ppermute | solution.py:324
  45.3 7.7 %collective-permute-start.5 = (bf16[24,32,128]{2,1,0:T(8,128)(2,1)S(1)}, bf16[24,32,128]{2,1,0:T(8,128)(2,1)S(1)}, u32[]{:S(2)}, u32[]{:S(2)}) collective-permute-start(bf16[24,32,128]{2,1,0:T(8,128)(2,1)S(1)} %collective-permute-done.4.b0), channel_id=1, source_target_pairs={{0,16},{8,24},{16,0},{24,8},{32,48},{40,56},{48,32},{56,40},{64,80... | collective-permute-start | bytes 589832 | tf_op jit(solution)/shard_map/ppermute | solution.py:324
  59.0 10.4 %collective-permute-start.14 = (bf16[64,4096]{1,0:T(8,128)(2,1)S(1)}, bf16[64,4096]{1,0:T(8,128)(2,1)S(1)}, u32[]{:S(2)}, u32[]{:S(2)}) collective-permute-start(bf16[64,4096]{1,0:T(8,128)(2,1)S(1)} %get-tuple-element.61), channel_id=1, source_target_pairs={{0,1},{1,0},{2,3},{3,2},{4,5},{5,4},{6,7},{7,6},{8,9},{9,8},{10,11... | collective-permute-start | bytes 1572872 | tf_op jit(solution)/shard_map/ppermute | solution.py:337
  68.8 3.3 %collective-permute-start.11 = (bf16[128,2048]{1,0:T(8,128)(2,1)S(1)}, bf16[128,2048]{1,0:T(8,128)(2,1)S(1)}, u32[]{:S(2)}, u32[]{:S(2)}) collective-permute-start(bf16[128,2048]{1,0:T(8,128)(2,1)S(1)} %get-tuple-element.55), channel_id=1, source_target_pairs={{0,1},{1,0},{2,3},{3,2},{4,5},{5,4},{6,7},{7,6},{8,9},{9,8},{10,11... | collective-permute-start | bytes 1572872 | tf_op jit(solution)/shard_map/ppermute | solution.py:337
  68.9 7.9 %collective-permute-start.13 = (bf16[128,2048]{1,0:T(8,128)(2,1)S(1)}, bf16[128,2048]{1,0:T(8,128)(2,1)S(1)}, u32[]{:S(2)}, u32[]{:S(2)}) collective-permute-start(bf16[128,2048]{1,0:T(8,128)(2,1)S(1)} %get-tuple-element.59), channel_id=1, source_target_pairs={{0,1},{1,0},{2,3},{3,2},{4,5},{5,4},{6,7},{7,6},{8,9},{9,8},{10,11... | collective-permute-start | bytes 1572872 | tf_op jit(solution)/shard_map/ppermute | solution.py:337
  69.6 8.5 %collective-permute-start.16 = (bf16[64,2048]{1,0:T(8,128)(2,1)S(1)}, bf16[64,2048]{1,0:T(8,128)(2,1)S(1)}, u32[]{:S(2)}, u32[]{:S(2)}) collective-permute-start(bf16[64,2048]{1,0:T(8,128)(2,1)S(1)} %get-tuple-element.67), channel_id=1, source_target_pairs={{0,6},{1,7},{2,0},{3,1},{4,2},{5,3},{6,4},{7,5},{8,14},{9,15},{10,... | collective-permute-start | bytes 786440 | tf_op jit(solution)/shard_map/ppermute | solution.py:340
  72.1 8.5 %collective-permute-start.15 = (bf16[64,2048]{1,0:T(8,128)(2,1)S(1)}, bf16[64,2048]{1,0:T(8,128)(2,1)S(1)}, u32[]{:S(2)}, u32[]{:S(2)}) collective-permute-start(bf16[64,2048]{1,0:T(8,128)(2,1)S(1)} %get-tuple-element.68), channel_id=1, source_target_pairs={{0,2},{1,3},{2,4},{3,5},{4,6},{5,7},{6,0},{7,1},{8,10},{9,11},{10,... | collective-permute-start | bytes 786440 | tf_op jit(solution)/shard_map/ppermute | solution.py:340
  72.3 10.9 %collective-permute-start.18 = (bf16[64,2048]{1,0:T(8,128)(2,1)S(1)}, bf16[64,2048]{1,0:T(8,128)(2,1)S(1)}, u32[]{:S(2)}, u32[]{:S(2)}) collective-permute-start(bf16[64,2048]{1,0:T(8,128)(2,1)S(1)} %get-tuple-element.71), channel_id=1, source_target_pairs={{0,6},{1,7},{2,0},{3,1},{4,2},{5,3},{6,4},{7,5},{8,14},{9,15},{10,... | collective-permute-start | bytes 786440 | tf_op jit(solution)/shard_map/ppermute | solution.py:340
  75.0 11.2 %collective-permute-start.19 = (bf16[64,2048]{1,0:T(8,128)(2,1)S(1)}, bf16[64,2048]{1,0:T(8,128)(2,1)S(1)}, u32[]{:S(2)}, u32[]{:S(2)}) collective-permute-start(bf16[64,2048]{1,0:T(8,128)(2,1)S(1)} %get-tuple-element.72.after), channel_id=1, source_target_pairs={{0,2},{1,3},{2,4},{3,5},{4,6},{5,7},{6,0},{7,1},{8,10},{9,11},{10,... | collective-permute-start | bytes 786440 | tf_op jit(solution)/shard_map/ppermute | solution.py:340
  76.9 15.0 %collective-permute-start.12 = (bf16[64,4096]{1,0:T(8,128)(2,1)S(1)}, bf16[64,4096]{1,0:T(8,128)(2,1)S(1)}, u32[]{:S(2)}, u32[]{:S(2)}) collective-permute-start(bf16[64,4096]{1,0:T(8,128)(2,1)S(1)} %get-tuple-element.57), channel_id=1, source_target_pairs={{0,1},{1,0},{2,3},{3,2},{4,5},{5,4},{6,7},{7,6},{8,9},{9,8},{10,11... | collective-permute-start | bytes 1572872 | tf_op jit(solution)/shard_map/ppermute | solution.py:337
  80.8 7.9 %collective-permute-start.20 = (bf16[64,2048]{1,0:T(8,128)(2,1)S(1)}, bf16[64,2048]{1,0:T(8,128)(2,1)S(1)}, u32[]{:S(2)}, u32[]{:S(2)}) collective-permute-start(bf16[64,2048]{1,0:T(8,128)(2,1)S(1)} %get-tuple-element.69), channel_id=1, source_target_pairs={{0,6},{1,7},{2,0},{3,1},{4,2},{5,3},{6,4},{7,5},{8,14},{9,15},{10,... | collective-permute-start | bytes 786440 | tf_op jit(solution)/shard_map/ppermute | solution.py:340
  81.4 10.4 %collective-permute-start.17 = (bf16[64,2048]{1,0:T(8,128)(2,1)S(1)}, bf16[64,2048]{1,0:T(8,128)(2,1)S(1)}, u32[]{:S(2)}, u32[]{:S(2)}) collective-permute-start(bf16[64,2048]{1,0:T(8,128)(2,1)S(1)} %get-tuple-element.70), channel_id=1, source_target_pairs={{0,2},{1,3},{2,4},{3,5},{4,6},{5,7},{6,0},{7,1},{8,10},{9,11},{10,... | collective-permute-start | bytes 786440 | tf_op jit(solution)/shard_map/ppermute | solution.py:340
  (1 other events, 16.9 us)

commit v11 on v10

--- a/solution.py
+++ b/solution.py
@@ -108,20 +108,23 @@
     return jnp.concatenate([column_block] * count, axis=1)
 
 
-def band_kernel(table, sink, q, w, prev, kc, vc, acc, tops, sums, w_out, qs, band, sems):
+def fetch_kernel(q, w, kc, vc, spread, qs, w_out, own, sems):
     copies = Copies(sems)
     copies.start(q, qs)
     for kind, cur in enumerate((kc, vc)):
-        copies.start(cur, band.at[kind, pl.ds(RUNS, RUNS)])
-    first = len(copies.made)
+        copies.start(cur, own.at[kind])
     depth = w.shape[0] // 4
     for n in range(4):
         copies.start(w.at[pl.ds(n * depth, depth)], w_out.at[pl.ds(n * depth, depth)])
+    copies.wait()
+
+
+def band_kernel(table, sink, qs, prev, own, acc, tops, sums, band):
     for kind in range(2):
         for b in range(RUNS):
             rows = [prev[r, kind, b].astype(F32) for r in range(16)]
             band[kind, b] = jnp.concatenate(rows, axis=0).astype(BF16)
-    copies.wait(first)
+            band[kind, RUNS + b] = own[kind, b]
     token = TOKENS // RUNS * table[META + 2] + lax.broadcasted_iota(jnp.int32, (TOKENS, 1), 0)
     within = lax.broadcasted_iota(jnp.int32, (1, ROWS), 1)
     for h in range(HEADS):
@@ -147,7 +150,6 @@
             acc[rows, cols] = jnp.dot(weight[rows], vals, preferred_element_type=F32)
         tops[:, cols] = top
         sums[:, cols] = total
-    copies.wait()
 
 
 def add_listed(table, qs, kv, late, acc, tops, sums, put):
@@ -292,7 +294,12 @@
     spread = spread.reshape(Z * Y, RUNS * 8, HEAD)
     prev = lax.ppermute(spread, "ctx", [(s, s + 1) for s in range(Z * Y - 1)]).reshape(16, 2, RUNS, 8, HEAD)
     got = lax.all_to_all(spread, "ctx", 0, 0, tiled=True).reshape(BLOCKS * 8, HEAD)
-    place, table, sink = lax.optimization_barrier((place, table, sink))
+    rows = ((TOKENS, HEADS * HEAD), BF16)
+    q, w, own = call(
+        fetch_kernel, [ANY] * 5, [rows, (output_weight.shape, BF16), ((2, RUNS, ROWS, HEAD), BF16)],
+        [pltpu.SemaphoreType.DMA((7,))], 4, "fetch",
+    )(*[pltpu.with_memory_space_constraint(a, pltpu.HBM) for a in (queries, output_weight, keys, values)], spread)
+    place, table, sink, q, w, own = lax.optimization_barrier((place, table, sink, q, w, own))
     r = jnp.arange(SLOTS * 8, dtype=jnp.int32)[:, None]
     col = jnp.arange(BLOCKS * 8, dtype=jnp.int32)[None, :]
     pick = (jnp.repeat(place, 8)[None, :] == r // 8) & (col % 8 == r % 8)
@@ -310,16 +317,11 @@
 
     width = output_weight.shape[1]
     kv = pltpu.VMEM((2, SLOTS, HALF, HEAD), BF16)
-    rows = ((TOKENS, HEADS * HEAD), BF16)
     part = ((HALF, width), BF16)
-    far_queries = pltpu.with_memory_space_constraint(queries, pltpu.HBM)
-    far_weight = pltpu.with_memory_space_constraint(output_weight, pltpu.HBM)
     state = [((TOKENS, HEADS * HEAD), F32)] * 3
-    acc, tops, sums, w, q = call(
-        band_kernel, [SMEM, VMEM] + [ANY] * 2 + [VMEM, ANY, ANY], state + [(output_weight.shape, BF16), rows],
-        [pltpu.VMEM((2, 2 * RUNS, ROWS, HEAD), BF16), pltpu.SemaphoreType.DMA((7,))], 3, "band",
-    )(table, sink, far_queries, far_weight, prev,
-      *[pltpu.with_memory_space_constraint(a, pltpu.HBM) for a in (keys, values)])
+    acc, tops, sums = call(
+        band_kernel, [SMEM] + [VMEM] * 4, state, [pltpu.VMEM((2, 2 * RUNS, ROWS, HEAD), BF16)], 3, "band",
+    )(table, sink, q, prev, own)
     b0, acc = lax.optimization_barrier((b0, acc))
     b1, b2, b3 = [lax.ppermute(b0, "ctx", y_pairs(f)) for f in (1, 2, 3)]
     acc, tops, sums = call(

time: 93.1 us -> 93.2 us (level)
  waiting for transfers between devices: 23.2 us -> 14.3 us
  local copies, waits for them, and re-layouts: 0.59 us -> 3.85 us
  starting transfers between devices: 44.4 us -> 47.4 us
  Pallas kernels: 23.4 us -> 26 us
    all_to_all x1, waiting for transfers between devices: 7.13 us -> 0.01 us  [per_device(): lax.all_to_all(spread, 'ctx', 0, 0, tiled=True).reshape(BLOCKS * 8, HEAD)]
    unnamed x7 -> x13, local copies, waits for them, and re-layouts: 0.09 us -> 3.36 us
    ppermute x3, starting transfers between devices: 5.71 us -> 8.74 us  [from_z(): return lax.ppermute(a, 'ctx', z_pairs(-offset))]
    pallas_call x1 -> x2, Pallas kernels: 5.18 us -> 7.87 us  [the longest x1 3.95 us: per_device(): call(band_kernel, [SMEM] + [VMEM] * 4, state, [pltpu.VMEM((2, 2 * RUNS, R...]
    ppermute x3, waiting for transfers between devices: 3.72 us -> 1.93 us  [from_z(): return lax.ppermute(a, 'ctx', z_pairs(-offset))]
    ppermute x4, starting transfers between devices: 8.75 us -> 7.09 us  [swap(): return lax.ppermute(a, 'head', CORE_PAIRS)]
    ppermute x1, starting transfers between devices: 0.01 us -> 1.59 us  [per_device(): lax.ppermute(a0, 'ctx', [(Y * z + y, Y * (z ^ 1) + y) for z in range(Z) f...]
  transfers between devices with their start and end apart: 22 -> 22, of which waited for: 9 -> 8; matrix products, arithmetic and copies ran while one was open for 2% -> 2% of each run, Pallas kernels for 16% -> 19%
where the time goes in v11:
time: 93.2 us; the launch traced here: 93 us
  starting transfers between devices  47.4 us (51%)
  Pallas kernels  26 us (28%)
  waiting for transfers between devices  14.3 us (15%)
  local copies, waits for them, and re-layouts  3.85 us (4%)
    all_to_all x1, starting transfers between devices, per_device(): lax.all_to_all(spread, 'ctx', 0, 0, tiled=True).reshape(BLOCKS * 8, HEAD)  12 us
    ppermute x6, waiting for transfers between devices, to_x(): return lax.ppermute(a, 'head', x_pairs(step))  11.9 us
    ppermute x3, starting transfers between devices, from_z(): return lax.ppermute(a, 'ctx', z_pairs(-offset))  8.74 us
    ppermute x4, starting transfers between devices, swap(): return lax.ppermute(a, 'head', CORE_PAIRS)  7.09 us
    ppermute x6, starting transfers between devices, to_x(): return lax.ppermute(a, 'head', x_pairs(step))  6.86 us
    pallas_call x1, Pallas kernels, per_device(): call(late_kernel, [SMEM, VMEM, VMEM] + [ANY] * 4 + [VMEM] * 3, [rows, par...  5.94 us
    pallas_call x1, Pallas kernels, per_device(): call(early_kernel, [SMEM, VMEM] + [ANY] * 4 + [VMEM] * 3, state, [kv, plt...  4.79 us
    pallas_call x1, Pallas kernels, per_device(): call(band_kernel, [SMEM] + [VMEM] * 4, state, [pltpu.VMEM((2, 2 * RUNS, R...  3.95 us
  transfers between devices with their start and end apart: 22, of which 8 were waited for; matrix products, arithmetic and copies ran while one was open for 2% of the time, Pallas kernels for 19%

profile of v11, /device:TPU:1, one launch (start us, length us, event | category | flops | bytes accessed | tf_op | source)
XLA Modules:
  0.0 93.0 jit_solution(15043960156077351846)
XLA Ops:
  0.0 1.7 %spread.1 = bf16[16,2,4,8,128]{4,3,2,1,0:T(8,128)(2,1)} custom-call(bf16[4,16,8,128]{3,2,1,0:T(8,128)(2,1)} %bitcast.20, bf16[4,16,8,128]{3,2,1,0:T(8,128)(2,1)} %bitcast.22), custom_call_target="tpu_custom_call" | custom-call | flops 1000000000 | bytes 1048576 | tf_op jit(solution)/shard_map/spread/pallas_call | solution.py:291
  1.7 12.0 %all-to-all-start = ((bf16[32,32,128]{2,1,0:T(8,128)(2,1)}), bf16[32,32,128]{2,1,0:T(8,128)(2,1)S(1)}, u32[]{:S(2)}, u32[]{:S(2)}) async-start(bf16[32,32,128]{2,1,0:T(8,128)(2,1)} %bitcast.10.spread), calls=%async_computation | async-start | bytes 524288 | tf_op jit(solution)/shard_map/all_to_all | solution.py:296
  13.7 3.1 %collective-permute-start = (bf16[32,32,128]{2,1,0:T(8,128)(2,1)}, bf16[32,32,128]{2,1,0:T(8,128)(2,1)S(1)}, u32[]{:S(2)}, u32[]{:S(2)}) collective-permute-start(bf16[32,32,128]{2,1,0:T(8,128)(2,1)} %bitcast.10.spread), channel_id=1, source_target_pairs={{0,8},{8,16},{16,24},{24,32},{32,40},{40,48},{48,56},{56,64},{64,7... | collective-permute-start | bytes 786440 | tf_op jit(solution)/shard_map/ppermute | solution.py:295
  17.3 3.9 %fetch.1 = (bf16[512,1024]{1,0:T(8,128)(2,1)S(1)}, bf16[1024,4096]{1,0:T(8,128)(2,1)S(1)}, bf16[2,4,128,128]{3,2,1,0:T(8,128)(2,1)S(1)}) custom-call(bf16[512,1024]{1,0:T(8,128)(2,1)} %q.1, bf16[1024,4096]{1,0:T(8,128)(2,1)} %w.1, bf16[4,128,128]{2,1,0:T(8,128)(2,1)} %bitcast.21, bf16[4,128,128]{2,1,0:T(8,128)(2,1)} %bitcast.23, ...), custom_call_target="tpu_custom_call" | custom-call | flops 4000000000 | bytes 4194304 | tf_op jit(solution)/shard_map/fetch/pallas_call | solution.py:298
  21.3 3.3 %copy-done = bf16[1024,4096]{1,0:T(8,128)(2,1)} copy-done((bf16[1024,4096]{1,0:T(8,128)(2,1)}, bf16[1024,4096]{1,0:T(8,128)(2,1)S(1)}, u32[]{:S(2)}) %copy-start) | copy-done | bytes 8388632
  25.4 2.2 %collective-permute-start.3 = (bf16[24,8,128]{2,1,0:T(8,128)(2,1)S(1)}, bf16[24,8,128]{2,1,0:T(8,128)(2,1)S(1)}, u32[]{:S(2)}, u32[]{:S(2)}) collective-permute-start(bf16[24,8,128]{2,1,0:T(8,128)(2,1)S(1)} %fusion), channel_id=1, source_target_pairs={{0,64},{8,72},{16,80},{24,88},{32,96},{40,104},{48,112},{56,120},{... | collective-permute-start | bytes 147464 | tf_op jit(solution)/shard_map/ppermute | solution.py:310
  27.5 3.3 %collective-permute-start.2 = (bf16[24,8,128]{2,1,0:T(8,128)(2,1)S(1)}, bf16[24,8,128]{2,1,0:T(8,128)(2,1)S(1)}, u32[]{:S(2)}, u32[]{:S(2)}) collective-permute-start(bf16[24,8,128]{2,1,0:T(8,128)(2,1)S(1)} %fusion), channel_id=1, source_target_pairs={{0,128},{8,136},{16,144},{24,152},{32,160},{40,168},{48,176},{56,1... | collective-permute-start | bytes 147464 | tf_op jit(solution)/shard_map/ppermute | solution.py:310
  30.8 3.2 %collective-permute-start.1 = (bf16[24,8,128]{2,1,0:T(8,128)(2,1)S(1)}, bf16[24,8,128]{2,1,0:T(8,128)(2,1)S(1)}, u32[]{:S(2)}, u32[]{:S(2)}) collective-permute-start(bf16[24,8,128]{2,1,0:T(8,128)(2,1)S(1)} %fusion), channel_id=1, source_target_pairs={{0,192},{8,200},{16,208},{24,216},{32,224},{40,232},{48,240},{56,2... | collective-permute-start | bytes 147464 | tf_op jit(solution)/shard_map/ppermute | solution.py:310
  36.1 1.4 %collective-permute-start.10 = (bf16[24,32,128]{2,1,0:T(8,128)(2,1)S(1)}, bf16[24,32,128]{2,1,0:T(8,128)(2,1)S(1)}, u32[]{:S(2)}, u32[]{:S(2)}) collective-permute-start(bf16[24,32,128]{2,1,0:T(8,128)(2,1)S(1)} %pad_maximum_fusion.a0), channel_id=1, source_target_pairs={{0,24},{8,16},{16,8},{24,0},{32,56},{40,48},{48,40},{56,32},{64,88... | collective-permute-start | bytes 589832 | tf_op jit(solution)/shard_map/ppermute | solution.py:316
  38.3 1.7 %collective-permute-start.8 = (bf16[24,32,128]{2,1,0:T(8,128)(2,1)S(1)}, bf16[24,32,128]{2,1,0:T(8,128)(2,1)S(1)}, u32[]{:S(2)}, u32[]{:S(2)}) collective-permute-start(bf16[24,32,128]{2,1,0:T(8,128)(2,1)S(1)} %pad_maximum_fusion.a0), channel_id=1, source_target_pairs={{0,16},{8,24},{16,0},{24,8},{32,48},{40,56},{48,32},{56,40},{64,80... | collective-permute-start | bytes 589832 | tf_op jit(solution)/shard_map/ppermute | solution.py:316
  40.0 1.6 %collective-permute-start.4 = (bf16[24,32,128]{2,1,0:T(8,128)(2,1)S(1)}, bf16[24,32,128]{2,1,0:T(8,128)(2,1)S(1)}, u32[]{:S(2)}, u32[]{:S(2)}) collective-permute-start(bf16[24,32,128]{2,1,0:T(8,128)(2,1)S(1)} %pad_maximum_fusion.a0), channel_id=1, source_target_pairs={{0,32},{8,40},{16,48},{24,56},{32,0},{40,8},{48,16},{56,24},{64,96... | collective-permute-start | bytes 589832 | tf_op jit(solution)/shard_map/ppermute | solution.py:315
  41.6 4.0 %band.1 = (f32[512,1024]{1,0:T(8,128)S(1)}, f32[512,1024]{1,0:T(8,128)S(1)}, f32[512,1024]{1,0:T(8,128)S(1)}) custom-call(s32[222]{0:T(256)S(1)} %concatenate.6.table, f32[8,128]{1,0:T(8,128)S(1)} %broadcast_in_dim.35.sink, bf16[512,1024]{1,0:T(8,128)(2,1)S(1)} %get-tuple-element.44.qs, bf16[16,2,4,8,128]{4,3,2,1,0:T(8,128)(2,1)S(1)} %bitcast.18, ...), custom_call_target="tpu_custom_call" | custom-call | flops 3000000000 | bytes 3145728 | tf_op jit(solution)/shard_map/band/pallas_call | solution.py:322
  45.6 2.7 %collective-permute-start.7 = (bf16[24,32,128]{2,1,0:T(8,128)(2,1)S(1)}, bf16[24,32,128]{2,1,0:T(8,128)(2,1)S(1)}, u32[]{:S(2)}, u32[]{:S(2)}) collective-permute-start(bf16[24,32,128]{2,1,0:T(8,128)(2,1)S(1)} %collective-permute-done.4.b0), channel_id=1, source_target_pairs={{0,24},{8,16},{16,8},{24,0},{32,56},{40,48},{48,40},{56,32},{64,88... | collective-permute-start | bytes 589832 | tf_op jit(solution)/shard_map/ppermute | solution.py:326
  49.6 4.8 %early.1 = (f32[512,1024]{1,0:T(8,128)S(1)}, f32[512,1024]{1,0:T(8,128)S(1)}, f32[512,1024]{1,0:T(8,128)S(1)}) custom-call(s32[222]{0:T(256)S(1)} %concatenate.6.table, bf16[512,1024]{1,0:T(8,128)(2,1)S(1)} %get-tuple-element.44.qs, bf16[24,32,128]{2,1,0:T(8,128)(2,1)S(1)} %pad_maximum_fusion.a0, bf16[24,32,128]{2,1,0:T(8,128)(2,1)S(1)} %collective-permute-done.8.a2, ...), custom_call_target="tpu_custom_call" | custom-call | flops 5000000000 | bytes 5242880 | tf_op jit(solution)/shard_map/early/pallas_call | solution.py:327
  54.8 5.9 %late.1 = (bf16[512,1024]{1,0:T(8,128)(2,1)S(1)}, bf16[64,4096]{1,0:T(8,128)(2,1)S(1)}, bf16[64,4096]{1,0:T(8,128)(2,1)S(1)}) custom-call(s32[222]{0:T(256)S(1)} %concatenate.6.table, bf16[512,1024]{1,0:T(8,128)(2,1)S(1)} %get-tuple-element.44.qs, bf16[1024,4096]{1,0:T(8,128)(2,1)S(1)} %bitcast.17, bf16[24,32,128]{2,1,0:T(8,128)(2,1)S(1)} %collective-permute-done.4.b0, ...), custom_call_target="tpu_custom_call" | custom-call | flops 10000000 | bytes 10485 | tf_op jit(solution)/shard_map/late/pallas_call | solution.py:330
  60.8 5.2 %collective-permute-start.14 = (bf16[64,4096]{1,0:T(8,128)(2,1)S(1)}, bf16[64,4096]{1,0:T(8,128)(2,1)S(1)}, u32[]{:S(2)}, u32[]{:S(2)}) collective-permute-start(bf16[64,4096]{1,0:T(8,128)(2,1)S(1)} %get-tuple-element.69), channel_id=1, source_target_pairs={{0,1},{1,0},{2,3},{3,2},{4,5},{5,4},{6,7},{7,6},{8,9},{9,8},{10,11... | collective-permute-start | bytes 1572872 | tf_op jit(solution)/shard_map/ppermute | solution.py:339
  66.0 2.9 %sides.1 = (bf16[64,4096]{1,0:T(8,128)(2,1)S(1)}, bf16[64,4096]{1,0:T(8,128)(2,1)S(1)}, bf16[128,2048]{1,0:T(8,128)(2,1)S(1)}, bf16[128,2048]{1,0:T(8,128)(2,1)S(1)}) custom-call(s32[222]{0:T(256)S(1)} %concatenate.6.table, bf16[512,1024]{1,0:T(8,128)(2,1)S(1)} %get-tuple-element.61.att, bf16[1024,4096]{1,0:T(8,128)(2,1)S(1)} %bitcast.17), custom_call_target="tpu_custom_call" | custom-call | flops 10000000 | bytes 10485 | tf_op jit(solution)/shard_map/sides/pallas_call | solution.py:335
  69.6 2.6 %collective-permute-start.16 = (bf16[64,2048]{1,0:T(8,128)(2,1)S(1)}, bf16[64,2048]{1,0:T(8,128)(2,1)S(1)}, u32[]{:S(2)}, u32[]{:S(2)}) collective-permute-start(bf16[64,2048]{1,0:T(8,128)(2,1)S(1)} %get-tuple-element.75), channel_id=1, source_target_pairs={{0,6},{1,7},{2,0},{3,1},{4,2},{5,3},{6,4},{7,5},{8,14},{9,15},{10,... | collective-permute-start | bytes 786440 | tf_op jit(solution)/shard_map/ppermute | solution.py:342
  72.3 2.8 %collective-permute-start.18 = (bf16[64,2048]{1,0:T(8,128)(2,1)S(1)}, bf16[64,2048]{1,0:T(8,128)(2,1)S(1)}, u32[]{:S(2)}, u32[]{:S(2)}) collective-permute-start(bf16[64,2048]{1,0:T(8,128)(2,1)S(1)} %get-tuple-element.79), channel_id=1, source_target_pairs={{0,6},{1,7},{2,0},{3,1},{4,2},{5,3},{6,4},{7,5},{8,14},{9,15},{10,... | collective-permute-start | bytes 786440 | tf_op jit(solution)/shard_map/ppermute | solution.py:342
  75.1 1.8 %own.1 = (bf16[64,4096]{1,0:T(8,128)(2,1)S(1)}, bf16[64,4096]{1,0:T(8,128)(2,1)S(1)}) custom-call(s32[222]{0:T(256)S(1)} %concatenate.6.table, bf16[512,1024]{1,0:T(8,128)(2,1)S(1)} %get-tuple-element.61.att, bf16[1024,4096]{1,0:T(8,128)(2,1)S(1)} %bitcast.17, bf16[64,2048]{1,0:T(8,128)(2,1)S(1)} %get-tuple-element.80.after), custom_call_target="tpu_custom_call" | custom-call | flops 10000000 | bytes 10485 | tf_op jit(solution)/shard_map/own/pallas_call | solution.py:352
  78.2 2.5 %collective-permute-done.15 = bf16[64,2048]{1,0:T(8,128)(2,1)S(1)} collective-permute-done((bf16[64,2048]{1,0:T(8,128)(2,1)S(1)}, bf16[64,2048]{1,0:T(8,128)(2,1)S(1)}, u32[]{:S(2)}, u32[]{:S(2)}) %collective-permute-start.15) | collective-permute-done | bytes 262176 | tf_op jit(solution)/shard_map/ppermute | solution.py:342
  83.2 3.1 %collective-permute-done.19.right_below = bf16[64,2048]{1,0:T(8,128)(2,1)S(1)} collective-permute-done((bf16[64,2048]{1,0:T(8,128)(2,1)S(1)}, bf16[64,2048]{1,0:T(8,128)(2,1)S(1)}, u32[]{:S(2)}, u32[]{:S(2)}) %collective-permute-start.19) | collective-permute-done | bytes 262176 | tf_op jit(solution)/shard_map/ppermute | solution.py:342
  86.3 2.5 %collective-permute-done.20.right_above = bf16[64,2048]{1,0:T(8,128)(2,1)S(1)} collective-permute-done((bf16[64,2048]{1,0:T(8,128)(2,1)S(1)}, bf16[64,2048]{1,0:T(8,128)(2,1)S(1)}, u32[]{:S(2)}, u32[]{:S(2)}) %collective-permute-start.20) | collective-permute-done | bytes 262176 | tf_op jit(solution)/shard_map/ppermute | solution.py:342
  88.8 3.1 %collective-permute-done.17.left_below = bf16[64,2048]{1,0:T(8,128)(2,1)S(1)} collective-permute-done((bf16[64,2048]{1,0:T(8,128)(2,1)S(1)}, bf16[64,2048]{1,0:T(8,128)(2,1)S(1)}, u32[]{:S(2)}, u32[]{:S(2)}) %collective-permute-start.17) | collective-permute-done | bytes 262176 | tf_op jit(solution)/shard_map/ppermute | solution.py:342
  (60 shorter events, 11.3 us)
Async XLA Ops:
  0.0 17.1 %copy-start.3 = (f32[8]{0:T(128)S(1)}, f32[8]{0:T(128)}, u32[]{:S(2)}) copy-start(f32[8]{0:T(128)} %param.10) | copy-start | bytes 100
  0.0 17.1 %copy-start.2 = (s32[8,3]{0,1:T(4,128)S(1)}, s32[8,3]{0,1:T(4,128)}, u32[]{:S(2)}) copy-start(s32[8,3]{0,1:T(4,128)} %param.12) | copy-start | bytes 292
  1.7 23.3 %all-to-all-start = ((bf16[32,32,128]{2,1,0:T(8,128)(2,1)}), bf16[32,32,128]{2,1,0:T(8,128)(2,1)S(1)}, u32[]{:S(2)}, u32[]{:S(2)}) async-start(bf16[32,32,128]{2,1,0:T(8,128)(2,1)} %bitcast.10.spread), calls=%async_computation | async-start | bytes 524288 | tf_op jit(solution)/shard_map/all_to_all | solution.py:296
  13.7 20.4 %collective-permute-start = (bf16[32,32,128]{2,1,0:T(8,128)(2,1)}, bf16[32,32,128]{2,1,0:T(8,128)(2,1)S(1)}, u32[]{:S(2)}, u32[]{:S(2)}) collective-permute-start(bf16[32,32,128]{2,1,0:T(8,128)(2,1)} %bitcast.10.spread), channel_id=1, source_target_pairs={{0,8},{8,16},{16,24},{24,32},{32,40},{40,48},{48,56},{56,64},{64,7... | collective-permute-start | bytes 786440 | tf_op jit(solution)/shard_map/ppermute | solution.py:295
  25.4 8.7 %collective-permute-start.3 = (bf16[24,8,128]{2,1,0:T(8,128)(2,1)S(1)}, bf16[24,8,128]{2,1,0:T(8,128)(2,1)S(1)}, u32[]{:S(2)}, u32[]{:S(2)}) collective-permute-start(bf16[24,8,128]{2,1,0:T(8,128)(2,1)S(1)} %fusion), channel_id=1, source_target_pairs={{0,64},{8,72},{16,80},{24,88},{32,96},{40,104},{48,112},{56,120},{... | collective-permute-start | bytes 147464 | tf_op jit(solution)/shard_map/ppermute | solution.py:310
  27.5 8.0 %collective-permute-start.2 = (bf16[24,8,128]{2,1,0:T(8,128)(2,1)S(1)}, bf16[24,8,128]{2,1,0:T(8,128)(2,1)S(1)}, u32[]{:S(2)}, u32[]{:S(2)}) collective-permute-start(bf16[24,8,128]{2,1,0:T(8,128)(2,1)S(1)} %fusion), channel_id=1, source_target_pairs={{0,128},{8,136},{16,144},{24,152},{32,160},{40,168},{48,176},{56,1... | collective-permute-start | bytes 147464 | tf_op jit(solution)/shard_map/ppermute | solution.py:310
  30.8 5.2 %collective-permute-start.1 = (bf16[24,8,128]{2,1,0:T(8,128)(2,1)S(1)}, bf16[24,8,128]{2,1,0:T(8,128)(2,1)S(1)}, u32[]{:S(2)}, u32[]{:S(2)}) collective-permute-start(bf16[24,8,128]{2,1,0:T(8,128)(2,1)S(1)} %fusion), channel_id=1, source_target_pairs={{0,192},{8,200},{16,208},{24,216},{32,224},{40,232},{48,240},{56,2... | collective-permute-start | bytes 147464 | tf_op jit(solution)/shard_map/ppermute | solution.py:310
  36.1 12.2 %collective-permute-start.10 = (bf16[24,32,128]{2,1,0:T(8,128)(2,1)S(1)}, bf16[24,32,128]{2,1,0:T(8,128)(2,1)S(1)}, u32[]{:S(2)}, u32[]{:S(2)}) collective-permute-start(bf16[24,32,128]{2,1,0:T(8,128)(2,1)S(1)} %pad_maximum_fusion.a0), channel_id=1, source_target_pairs={{0,24},{8,16},{16,8},{24,0},{32,56},{40,48},{48,40},{56,32},{64,88... | collective-permute-start | bytes 589832 | tf_op jit(solution)/shard_map/ppermute | solution.py:316
  37.5 12.0 %collective-permute-start.9 = (bf16[24,32,128]{2,1,0:T(8,128)(2,1)S(1)}, bf16[24,32,128]{2,1,0:T(8,128)(2,1)S(1)}, u32[]{:S(2)}, u32[]{:S(2)}) collective-permute-start(bf16[24,32,128]{2,1,0:T(8,128)(2,1)S(1)} %pad_maximum_fusion.a0), channel_id=1, source_target_pairs={{0,8},{8,0},{16,24},{24,16},{32,40},{40,32},{48,56},{56,48},{64,72... | collective-permute-start | bytes 589832 | tf_op jit(solution)/shard_map/ppermute | solution.py:316
  38.3 11.2 %collective-permute-start.8 = (bf16[24,32,128]{2,1,0:T(8,128)(2,1)S(1)}, bf16[24,32,128]{2,1,0:T(8,128)(2,1)S(1)}, u32[]{:S(2)}, u32[]{:S(2)}) collective-permute-start(bf16[24,32,128]{2,1,0:T(8,128)(2,1)S(1)} %pad_maximum_fusion.a0), channel_id=1, source_target_pairs={{0,16},{8,24},{16,0},{24,8},{32,48},{40,56},{48,32},{56,40},{64,80... | collective-permute-start | bytes 589832 | tf_op jit(solution)/shard_map/ppermute | solution.py:316
  40.0 5.6 %collective-permute-start.4 = (bf16[24,32,128]{2,1,0:T(8,128)(2,1)S(1)}, bf16[24,32,128]{2,1,0:T(8,128)(2,1)S(1)}, u32[]{:S(2)}, u32[]{:S(2)}) collective-permute-start(bf16[24,32,128]{2,1,0:T(8,128)(2,1)S(1)} %pad_maximum_fusion.a0), channel_id=1, source_target_pairs={{0,32},{8,40},{16,48},{24,56},{32,0},{40,8},{48,16},{56,24},{64,96... | collective-permute-start | bytes 589832 | tf_op jit(solution)/shard_map/ppermute | solution.py:315
  45.6 8.8 %collective-permute-start.7 = (bf16[24,32,128]{2,1,0:T(8,128)(2,1)S(1)}, bf16[24,32,128]{2,1,0:T(8,128)(2,1)S(1)}, u32[]{:S(2)}, u32[]{:S(2)}) collective-permute-start(bf16[24,32,128]{2,1,0:T(8,128)(2,1)S(1)} %collective-permute-done.4.b0), channel_id=1, source_target_pairs={{0,24},{8,16},{16,8},{24,0},{32,56},{40,48},{48,40},{56,32},{64,88... | collective-permute-start | bytes 589832 | tf_op jit(solution)/shard_map/ppermute | solution.py:326
  48.2 6.1 %collective-permute-start.6 = (bf16[24,32,128]{2,1,0:T(8,128)(2,1)S(1)}, bf16[24,32,128]{2,1,0:T(8,128)(2,1)S(1)}, u32[]{:S(2)}, u32[]{:S(2)}) collective-permute-start(bf16[24,32,128]{2,1,0:T(8,128)(2,1)S(1)} %collective-permute-done.4.b0), channel_id=1, source_target_pairs={{0,8},{8,0},{16,24},{24,16},{32,40},{40,32},{48,56},{56,48},{64,72... | collective-permute-start | bytes 589832 | tf_op jit(solution)/shard_map/ppermute | solution.py:326
  48.3 6.5 %collective-permute-start.5 = (bf16[24,32,128]{2,1,0:T(8,128)(2,1)S(1)}, bf16[24,32,128]{2,1,0:T(8,128)(2,1)S(1)}, u32[]{:S(2)}, u32[]{:S(2)}) collective-permute-start(bf16[24,32,128]{2,1,0:T(8,128)(2,1)S(1)} %collective-permute-done.4.b0), channel_id=1, source_target_pairs={{0,16},{8,24},{16,0},{24,8},{32,48},{40,56},{48,32},{56,40},{64,80... | collective-permute-start | bytes 589832 | tf_op jit(solution)/shard_map/ppermute | solution.py:326
  60.8 8.8 %collective-permute-start.14 = (bf16[64,4096]{1,0:T(8,128)(2,1)S(1)}, bf16[64,4096]{1,0:T(8,128)(2,1)S(1)}, u32[]{:S(2)}, u32[]{:S(2)}) collective-permute-start(bf16[64,4096]{1,0:T(8,128)(2,1)S(1)} %get-tuple-element.69), channel_id=1, source_target_pairs={{0,1},{1,0},{2,3},{3,2},{4,5},{5,4},{6,7},{7,6},{8,9},{9,8},{10,11... | collective-permute-start | bytes 1572872 | tf_op jit(solution)/shard_map/ppermute | solution.py:339
  68.9 3.3 %collective-permute-start.11 = (bf16[128,2048]{1,0:T(8,128)(2,1)S(1)}, bf16[128,2048]{1,0:T(8,128)(2,1)S(1)}, u32[]{:S(2)}, u32[]{:S(2)}) collective-permute-start(bf16[128,2048]{1,0:T(8,128)(2,1)S(1)} %get-tuple-element.63), channel_id=1, source_target_pairs={{0,1},{1,0},{2,3},{3,2},{4,5},{5,4},{6,7},{7,6},{8,9},{9,8},{10,11... | collective-permute-start | bytes 1572872 | tf_op jit(solution)/shard_map/ppermute | solution.py:339
  69.0 7.9 %collective-permute-start.13 = (bf16[128,2048]{1,0:T(8,128)(2,1)S(1)}, bf16[128,2048]{1,0:T(8,128)(2,1)S(1)}, u32[]{:S(2)}, u32[]{:S(2)}) collective-permute-start(bf16[128,2048]{1,0:T(8,128)(2,1)S(1)} %get-tuple-element.67), channel_id=1, source_target_pairs={{0,1},{1,0},{2,3},{3,2},{4,5},{5,4},{6,7},{7,6},{8,9},{9,8},{10,11... | collective-permute-start | bytes 1572872 | tf_op jit(solution)/shard_map/ppermute | solution.py:339
  69.6 8.5 %collective-permute-start.16 = (bf16[64,2048]{1,0:T(8,128)(2,1)S(1)}, bf16[64,2048]{1,0:T(8,128)(2,1)S(1)}, u32[]{:S(2)}, u32[]{:S(2)}) collective-permute-start(bf16[64,2048]{1,0:T(8,128)(2,1)S(1)} %get-tuple-element.75), channel_id=1, source_target_pairs={{0,6},{1,7},{2,0},{3,1},{4,2},{5,3},{6,4},{7,5},{8,14},{9,15},{10,... | collective-permute-start | bytes 786440 | tf_op jit(solution)/shard_map/ppermute | solution.py:342
  72.2 8.5 %collective-permute-start.15 = (bf16[64,2048]{1,0:T(8,128)(2,1)S(1)}, bf16[64,2048]{1,0:T(8,128)(2,1)S(1)}, u32[]{:S(2)}, u32[]{:S(2)}) collective-permute-start(bf16[64,2048]{1,0:T(8,128)(2,1)S(1)} %get-tuple-element.76), channel_id=1, source_target_pairs={{0,2},{1,3},{2,4},{3,5},{4,6},{5,7},{6,0},{7,1},{8,10},{9,11},{10,... | collective-permute-start | bytes 786440 | tf_op jit(solution)/shard_map/ppermute | solution.py:342
  72.3 10.9 %collective-permute-start.18 = (bf16[64,2048]{1,0:T(8,128)(2,1)S(1)}, bf16[64,2048]{1,0:T(8,128)(2,1)S(1)}, u32[]{:S(2)}, u32[]{:S(2)}) collective-permute-start(bf16[64,2048]{1,0:T(8,128)(2,1)S(1)} %get-tuple-element.79), channel_id=1, source_target_pairs={{0,6},{1,7},{2,0},{3,1},{4,2},{5,3},{6,4},{7,5},{8,14},{9,15},{10,... | collective-permute-start | bytes 786440 | tf_op jit(solution)/shard_map/ppermute | solution.py:342
  75.1 11.2 %collective-permute-start.19 = (bf16[64,2048]{1,0:T(8,128)(2,1)S(1)}, bf16[64,2048]{1,0:T(8,128)(2,1)S(1)}, u32[]{:S(2)}, u32[]{:S(2)}) collective-permute-start(bf16[64,2048]{1,0:T(8,128)(2,1)S(1)} %get-tuple-element.80.after), channel_id=1, source_target_pairs={{0,2},{1,3},{2,4},{3,5},{4,6},{5,7},{6,0},{7,1},{8,10},{9,11},{10,... | collective-permute-start | bytes 786440 | tf_op jit(solution)/shard_map/ppermute | solution.py:342
  76.9 15.0 %collective-permute-start.12 = (bf16[64,4096]{1,0:T(8,128)(2,1)S(1)}, bf16[64,4096]{1,0:T(8,128)(2,1)S(1)}, u32[]{:S(2)}, u32[]{:S(2)}) collective-permute-start(bf16[64,4096]{1,0:T(8,128)(2,1)S(1)} %get-tuple-element.65), channel_id=1, source_target_pairs={{0,1},{1,0},{2,3},{3,2},{4,5},{5,4},{6,7},{7,6},{8,9},{9,8},{10,11... | collective-permute-start | bytes 1572872 | tf_op jit(solution)/shard_map/ppermute | solution.py:339
  80.9 7.9 %collective-permute-start.20 = (bf16[64,2048]{1,0:T(8,128)(2,1)S(1)}, bf16[64,2048]{1,0:T(8,128)(2,1)S(1)}, u32[]{:S(2)}, u32[]{:S(2)}) collective-permute-start(bf16[64,2048]{1,0:T(8,128)(2,1)S(1)} %get-tuple-element.77), channel_id=1, source_target_pairs={{0,6},{1,7},{2,0},{3,1},{4,2},{5,3},{6,4},{7,5},{8,14},{9,15},{10,... | collective-permute-start | bytes 786440 | tf_op jit(solution)/shard_map/ppermute | solution.py:342
  81.5 10.4 %collective-permute-start.17 = (bf16[64,2048]{1,0:T(8,128)(2,1)S(1)}, bf16[64,2048]{1,0:T(8,128)(2,1)S(1)}, u32[]{:S(2)}, u32[]{:S(2)}) collective-permute-start(bf16[64,2048]{1,0:T(8,128)(2,1)S(1)} %get-tuple-element.78), channel_id=1, source_target_pairs={{0,2},{1,3},{2,4},{3,5},{4,6},{5,7},{6,0},{7,1},{8,10},{9,11},{10,... | collective-permute-start | bytes 786440 | tf_op jit(solution)/shard_map/ppermute | solution.py:342
  (4 other events, 30.7 us)

commit v12 on v11

--- a/solution.py
+++ b/solution.py
@@ -108,14 +108,13 @@
     return jnp.concatenate([column_block] * count, axis=1)
 
 
-def fetch_kernel(q, w, kc, vc, spread, qs, w_out, own, sems):
+def fetch_kernel(q, kc, vc, spread, qs, own, sems):
     copies = Copies(sems)
-    copies.start(q, qs)
+    half = q.shape[0] // 2
+    for n in range(2):
+        copies.start(q.at[pl.ds(n * half, half)], qs.at[pl.ds(n * half, half)])
     for kind, cur in enumerate((kc, vc)):
         copies.start(cur, own.at[kind])
-    depth = w.shape[0] // 4
-    for n in range(4):
-        copies.start(w.at[pl.ds(n * depth, depth)], w_out.at[pl.ds(n * depth, depth)])
     copies.wait()
 
 
@@ -169,15 +168,20 @@
         put(cols, mixed + acc[:, cols] * fade, top, total)
 
 
-def early_kernel(table, qs, a0, a2, a1, a3, acc, tops, sums, acc_out, tops_out, sums_out, kv, sems):
+def early_kernel(table, qs, w, a0, a2, a1, a3, acc, tops, sums, acc_out, tops_out, sums_out, w_out, kv, sems):
     copies = Copies(sems)
     load_half(copies, table[META], a0, a2, a1, a3, kv)
-    copies.wait()
+    first = len(copies.made)
+    depth = w.shape[0] // 4
+    for n in range(4):
+        copies.start(w.at[pl.ds(n * depth, depth)], w_out.at[pl.ds(n * depth, depth)])
+    copies.wait(first)
 
     def put(cols, mixed, top, total):
         acc_out[:, cols], tops_out[:, cols], sums_out[:, cols] = mixed, top, total
 
     add_listed(table, qs, kv, False, acc, tops, sums, put)
+    copies.wait()
 
 
 def project(att, w, blocks, core, keeps, give):
@@ -295,11 +299,10 @@
     prev = lax.ppermute(spread, "ctx", [(s, s + 1) for s in range(Z * Y - 1)]).reshape(16, 2, RUNS, 8, HEAD)
     got = lax.all_to_all(spread, "ctx", 0, 0, tiled=True).reshape(BLOCKS * 8, HEAD)
     rows = ((TOKENS, HEADS * HEAD), BF16)
-    q, w, own = call(
-        fetch_kernel, [ANY] * 5, [rows, (output_weight.shape, BF16), ((2, RUNS, ROWS, HEAD), BF16)],
-        [pltpu.SemaphoreType.DMA((7,))], 4, "fetch",
-    )(*[pltpu.with_memory_space_constraint(a, pltpu.HBM) for a in (queries, output_weight, keys, values)], spread)
-    place, table, sink, q, w, own = lax.optimization_barrier((place, table, sink, q, w, own))
+    q, own = call(
+        fetch_kernel, [ANY] * 4, [rows, ((2, RUNS, ROWS, HEAD), BF16)], [pltpu.SemaphoreType.DMA((4,))], 1, "fetch",
+    )(*[pltpu.with_memory_space_constraint(a, pltpu.HBM) for a in (queries, keys, values)], spread)
+    place, table, sink, q, own = lax.optimization_barrier((place, table, sink, q, own))
     r = jnp.arange(SLOTS * 8, dtype=jnp.int32)[:, None]
     col = jnp.arange(BLOCKS * 8, dtype=jnp.int32)[None, :]
     pick = (jnp.repeat(place, 8)[None, :] == r // 8) & (col % 8 == r % 8)
@@ -324,9 +327,10 @@
     )(table, sink, q, prev, own)
     b0, acc = lax.optimization_barrier((b0, acc))
     b1, b2, b3 = [lax.ppermute(b0, "ctx", y_pairs(f)) for f in (1, 2, 3)]
-    acc, tops, sums = call(
-        early_kernel, [SMEM, VMEM] + [ANY] * 4 + [VMEM] * 3, state, [kv, pltpu.SemaphoreType.DMA((4,))], 5, "early",
-    )(table, q, a0, a2, a1, a3, acc, tops, sums)
+    acc, tops, sums, w = call(
+        early_kernel, [SMEM, VMEM] + [ANY] * 5 + [VMEM] * 3, state + [(output_weight.shape, BF16)],
+        [kv, pltpu.SemaphoreType.DMA((8,))], 5, "early",
+    )(table, q, pltpu.with_memory_space_constraint(output_weight, pltpu.HBM), a0, a2, a1, a3, acc, tops, sums)
     att, keep_far, give_far = call(
         late_kernel, [SMEM, VMEM, VMEM] + [ANY] * 4 + [VMEM] * 3,
         [rows, part, part], [kv, pltpu.SemaphoreType.DMA((4,))], 0.01, "late",

time: 93.2 us -> 89.8 us (0.964)
  waiting for transfers between devices: 14.3 us -> 21.9 us
  starting transfers between devices: 47.4 us -> 42.1 us
  local copies, waits for them, and re-layouts: 3.85 us -> 0.58 us
  Pallas kernels: 26 us -> 23.3 us
    all_to_all x1, waiting for transfers between devices: 0.01 us -> 5.8 us  [per_device(): lax.all_to_all(spread, 'ctx', 0, 0, tiled=True).reshape(BLOCKS * 8, HEAD)]
    ppermute x3, starting transfers between devices: 8.74 us -> 4.9 us  [from_z(): return lax.ppermute(a, 'ctx', z_pairs(-offset))]
    ppermute x6, waiting for transfers between devices: 11.9 us -> 8.35 us  [to_x(): return lax.ppermute(a, 'head', x_pairs(step))]
    ppermute x3, waiting for transfers between devices: 1.93 us -> 5.47 us  [from_z(): return lax.ppermute(a, 'ctx', z_pairs(-offset))]
    unnamed x13 -> x7, local copies, waits for them, and re-layouts: 3.36 us -> 0.09 us
    pallas_call x2, Pallas kernels: 8.71 us -> 6.01 us  [the longest x1 4.72 us: per_device(): call(early_kernel, [SMEM, VMEM] + [ANY] * 5 + [VMEM] * 3, state + [(outpu...]
    ppermute x3, waiting for transfers between devices: 0.42 us -> 2.28 us  [per_device(): b1, b2, b3 = [lax.ppermute(b0, 'ctx', y_pairs(f)) for f in (1, 2, 3)]]
    ppermute x1, starting transfers between devices: 1.59 us -> 0.09 us  [per_device(): lax.ppermute(a0, 'ctx', [(Y * z + y, Y * (z ^ 1) + y) for z in range(Z) f...]
  transfers between devices with their start and end apart: 22 -> 22, of which waited for: 8 -> 7; matrix products, arithmetic and copies ran while one was open for 2% -> 2% of each run, Pallas kernels for 19% -> 16%
where the time goes in v12:
time: 89.8 us; the launch traced here: 89.3 us
  starting transfers between devices  42.1 us (47%)
  Pallas kernels  23.3 us (26%)
  waiting for transfers between devices  21.9 us (24%)
    all_to_all x1, starting transfers between devices, per_device(): lax.all_to_all(spread, 'ctx', 0, 0, tiled=True).reshape(BLOCKS * 8, HEAD)  12 us
    ppermute x6, waiting for transfers between devices, to_x(): return lax.ppermute(a, 'head', x_pairs(step))  8.35 us
    ppermute x6, starting transfers between devices, to_x(): return lax.ppermute(a, 'head', x_pairs(step))  8.29 us
    ppermute x4, starting transfers between devices, swap(): return lax.ppermute(a, 'head', CORE_PAIRS)  6.96 us
    pallas_call x1, Pallas kernels, per_device(): call(late_kernel, [SMEM, VMEM, VMEM] + [ANY] * 4 + [VMEM] * 3, [rows, par...  5.94 us
    all_to_all x1, waiting for transfers between devices, per_device(): lax.all_to_all(spread, 'ctx', 0, 0, tiled=True).reshape(BLOCKS * 8, HEAD)  5.8 us
    ppermute x3, waiting for transfers between devices, from_z(): return lax.ppermute(a, 'ctx', z_pairs(-offset))  5.47 us
    ppermute x3, starting transfers between devices, from_z(): return lax.ppermute(a, 'ctx', z_pairs(-offset))  4.9 us
  transfers between devices with their start and end apart: 22, of which 7 were waited for; matrix products, arithmetic and copies ran while one was open for 2% of the time, Pallas kernels for 16%

profile of v12, /device:TPU:1, one launch (start us, length us, event | category | flops | bytes accessed | tf_op | source)
XLA Modules:
  0.0 89.3 jit_solution(805132721237420803)
XLA Ops:
  0.0 1.7 %spread.1 = bf16[16,2,4,8,128]{4,3,2,1,0:T(8,128)(2,1)} custom-call(bf16[4,16,8,128]{3,2,1,0:T(8,128)(2,1)} %bitcast.18, bf16[4,16,8,128]{3,2,1,0:T(8,128)(2,1)} %bitcast.20), custom_call_target="tpu_custom_call" | custom-call | flops 1000000000 | bytes 1048576 | tf_op jit(solution)/shard_map/spread/pallas_call | solution.py:295
  1.7 12.0 %all-to-all-start = ((bf16[32,32,128]{2,1,0:T(8,128)(2,1)}), bf16[32,32,128]{2,1,0:T(8,128)(2,1)S(1)}, u32[]{:S(2)}, u32[]{:S(2)}) async-start(bf16[32,32,128]{2,1,0:T(8,128)(2,1)} %bitcast.10.spread), calls=%async_computation | async-start | bytes 524288 | tf_op jit(solution)/shard_map/all_to_all | solution.py:300
  13.7 3.1 %collective-permute-start = (bf16[32,32,128]{2,1,0:T(8,128)(2,1)}, bf16[32,32,128]{2,1,0:T(8,128)(2,1)S(1)}, u32[]{:S(2)}, u32[]{:S(2)}) collective-permute-start(bf16[32,32,128]{2,1,0:T(8,128)(2,1)} %bitcast.10.spread), channel_id=1, source_target_pairs={{0,8},{8,16},{16,24},{24,32},{32,40},{40,48},{48,56},{56,64},{64,7... | collective-permute-start | bytes 786440 | tf_op jit(solution)/shard_map/ppermute | solution.py:299
  17.5 1.3 %fetch.1 = (bf16[512,1024]{1,0:T(8,128)(2,1)S(1)}, bf16[2,4,128,128]{3,2,1,0:T(8,128)(2,1)S(1)}) custom-call(bf16[512,1024]{1,0:T(8,128)(2,1)} %q.1, bf16[4,128,128]{2,1,0:T(8,128)(2,1)} %bitcast.19, bf16[4,128,128]{2,1,0:T(8,128)(2,1)} %bitcast.21, bf16[32,32,128]{2,1,0:T(8,128)(2,1)} %bitcast.10.spread), custom_call_target="tpu_custom_call" | custom-call | flops 1000000000 | bytes 1048576 | tf_op jit(solution)/shard_map/fetch/pallas_call | solution.py:302
  19.1 5.8 %all-to-all-done = bf16[32,32,128]{2,1,0:T(8,128)(2,1)S(1)} async-done(((bf16[32,32,128]{2,1,0:T(8,128)(2,1)}), bf16[32,32,128]{2,1,0:T(8,128)(2,1)S(1)}, u32[]{:S(2)}, u32[]{:S(2)}) %all-to-all-start) | async-done | bytes 262176 | tf_op jit(solution)/shard_map/all_to_all | solution.py:300
  25.3 1.6 %collective-permute-start.1 = (bf16[24,8,128]{2,1,0:T(8,128)(2,1)S(1)}, bf16[24,8,128]{2,1,0:T(8,128)(2,1)S(1)}, u32[]{:S(2)}, u32[]{:S(2)}) collective-permute-start(bf16[24,8,128]{2,1,0:T(8,128)(2,1)S(1)} %fusion), channel_id=1, source_target_pairs={{0,192},{8,200},{16,208},{24,216},{32,224},{40,232},{48,240},{56,2... | collective-permute-start | bytes 147464 | tf_op jit(solution)/shard_map/ppermute | solution.py:313
  26.9 3.3 %collective-permute-start.2 = (bf16[24,8,128]{2,1,0:T(8,128)(2,1)S(1)}, bf16[24,8,128]{2,1,0:T(8,128)(2,1)S(1)}, u32[]{:S(2)}, u32[]{:S(2)}) collective-permute-start(bf16[24,8,128]{2,1,0:T(8,128)(2,1)S(1)} %fusion), channel_id=1, source_target_pairs={{0,128},{8,136},{16,144},{24,152},{32,160},{40,168},{48,176},{56,1... | collective-permute-start | bytes 147464 | tf_op jit(solution)/shard_map/ppermute | solution.py:313
  30.2 3.6 %collective-permute-done.2 = bf16[24,8,128]{2,1,0:T(8,128)(2,1)S(1)} collective-permute-done((bf16[24,8,128]{2,1,0:T(8,128)(2,1)S(1)}, bf16[24,8,128]{2,1,0:T(8,128)(2,1)S(1)}, u32[]{:S(2)}, u32[]{:S(2)}) %collective-permute-start.2) | collective-permute-done | bytes 49184 | tf_op jit(solution)/shard_map/ppermute | solution.py:313
  33.8 1.9 %collective-permute-done.3 = bf16[24,8,128]{2,1,0:T(8,128)(2,1)S(1)} collective-permute-done((bf16[24,8,128]{2,1,0:T(8,128)(2,1)S(1)}, bf16[24,8,128]{2,1,0:T(8,128)(2,1)S(1)}, u32[]{:S(2)}, u32[]{:S(2)}) %collective-permute-start.3) | collective-permute-done | bytes 49184 | tf_op jit(solution)/shard_map/ppermute | solution.py:313
  35.8 2.4 %collective-permute-start.4 = (bf16[24,32,128]{2,1,0:T(8,128)(2,1)S(1)}, bf16[24,32,128]{2,1,0:T(8,128)(2,1)S(1)}, u32[]{:S(2)}, u32[]{:S(2)}) collective-permute-start(bf16[24,32,128]{2,1,0:T(8,128)(2,1)S(1)} %pad_maximum_fusion.a0), channel_id=1, source_target_pairs={{0,16},{8,24},{16,0},{24,8},{32,48},{40,56},{48,32},{56,40},{64,80... | collective-permute-start | bytes 589832 | tf_op jit(solution)/shard_map/ppermute | solution.py:319
  39.1 3.9 %band.1 = (f32[512,1024]{1,0:T(8,128)S(1)}, f32[512,1024]{1,0:T(8,128)S(1)}, f32[512,1024]{1,0:T(8,128)S(1)}) custom-call(s32[222]{0:T(256)S(1)} %concatenate.6.table, f32[8,128]{1,0:T(8,128)S(1)} %broadcast_in_dim.35.sink, bf16[512,1024]{1,0:T(8,128)(2,1)S(1)} %get-tuple-element.42.qs, bf16[16,2,4,8,128]{4,3,2,1,0:T(8,128)(2,1)S(1)} %bitcast.16, ...), custom_call_target="tpu_custom_call" | custom-call | flops 3000000000 | bytes 3145728 | tf_op jit(solution)/shard_map/band/pallas_call | solution.py:325
  43.1 2.1 %collective-permute-start.10 = (bf16[24,32,128]{2,1,0:T(8,128)(2,1)S(1)}, bf16[24,32,128]{2,1,0:T(8,128)(2,1)S(1)}, u32[]{:S(2)}, u32[]{:S(2)}) collective-permute-start(bf16[24,32,128]{2,1,0:T(8,128)(2,1)S(1)} %collective-permute-done.7.b0), channel_id=1, source_target_pairs={{0,24},{8,16},{16,8},{24,0},{32,56},{40,48},{48,40},{56,32},{64,88... | collective-permute-start | bytes 589832 | tf_op jit(solution)/shard_map/ppermute | solution.py:329
  46.4 4.7 %early.1 = (f32[512,1024]{1,0:T(8,128)S(1)}, f32[512,1024]{1,0:T(8,128)S(1)}, f32[512,1024]{1,0:T(8,128)S(1)}, bf16[1024,4096]{1,0:T(8,128)(2,1)S(1)}) custom-call(s32[222]{0:T(256)S(1)} %concatenate.6.table, bf16[512,1024]{1,0:T(8,128)(2,1)S(1)} %get-tuple-element.42.qs, bf16[1024,4096]{1,0:T(8,128)(2,1)} %w.1, ...), custom_call_target="tpu_custom_call" | custom-call | flops 5000000000 | bytes 5242880 | tf_op jit(solution)/shard_map/early/pallas_call | solution.py:330
  51.1 2.3 %collective-permute-done.10.b3 = bf16[24,32,128]{2,1,0:T(8,128)(2,1)S(1)} collective-permute-done((bf16[24,32,128]{2,1,0:T(8,128)(2,1)S(1)}, bf16[24,32,128]{2,1,0:T(8,128)(2,1)S(1)}, u32[]{:S(2)}, u32[]{:S(2)}) %collective-permute-start.10) | collective-permute-done | bytes 196640 | tf_op jit(solution)/shard_map/ppermute | solution.py:329
  53.4 5.9 %late.1 = (bf16[512,1024]{1,0:T(8,128)(2,1)S(1)}, bf16[64,4096]{1,0:T(8,128)(2,1)S(1)}, bf16[64,4096]{1,0:T(8,128)(2,1)S(1)}) custom-call(s32[222]{0:T(256)S(1)} %concatenate.6.table, bf16[512,1024]{1,0:T(8,128)(2,1)S(1)} %get-tuple-element.42.qs, bf16[1024,4096]{1,0:T(8,128)(2,1)S(1)} %get-tuple-element.54.w, ...), custom_call_target="tpu_custom_call" | custom-call | flops 10000000 | bytes 10485 | tf_op jit(solution)/shard_map/late/pallas_call | solution.py:334
  59.4 5.2 %collective-permute-start.14 = (bf16[64,4096]{1,0:T(8,128)(2,1)S(1)}, bf16[64,4096]{1,0:T(8,128)(2,1)S(1)}, u32[]{:S(2)}, u32[]{:S(2)}) collective-permute-start(bf16[64,4096]{1,0:T(8,128)(2,1)S(1)} %get-tuple-element.67), channel_id=1, source_target_pairs={{0,1},{1,0},{2,3},{3,2},{4,5},{5,4},{6,7},{7,6},{8,9},{9,8},{10,11... | collective-permute-start | bytes 1572872 | tf_op jit(solution)/shard_map/ppermute | solution.py:343
  64.5 2.9 %sides.1 = (bf16[64,4096]{1,0:T(8,128)(2,1)S(1)}, bf16[64,4096]{1,0:T(8,128)(2,1)S(1)}, bf16[128,2048]{1,0:T(8,128)(2,1)S(1)}, bf16[128,2048]{1,0:T(8,128)(2,1)S(1)}) custom-call(s32[222]{0:T(256)S(1)} %concatenate.6.table, bf16[512,1024]{1,0:T(8,128)(2,1)S(1)} %get-tuple-element.59.att, bf16[1024,4096]{1,0:T(8,128)(2,1)S(1)} %get-tuple-element.54.w), custom_call_target="tpu_custom_call" | custom-call | flops 10000000 | bytes 10485 | tf_op jit(solution)/shard_map/sides/pallas_call | solution.py:339
  68.2 1.3 %collective-permute-start.15 = (bf16[64,2048]{1,0:T(8,128)(2,1)S(1)}, bf16[64,2048]{1,0:T(8,128)(2,1)S(1)}, u32[]{:S(2)}, u32[]{:S(2)}) collective-permute-start(bf16[64,2048]{1,0:T(8,128)(2,1)S(1)} %get-tuple-element.74), channel_id=1, source_target_pairs={{0,2},{1,3},{2,4},{3,5},{4,6},{5,7},{6,0},{7,1},{8,10},{9,11},{10,... | collective-permute-start | bytes 786440 | tf_op jit(solution)/shard_map/ppermute | solution.py:346
  69.4 1.5 %collective-permute-start.16 = (bf16[64,2048]{1,0:T(8,128)(2,1)S(1)}, bf16[64,2048]{1,0:T(8,128)(2,1)S(1)}, u32[]{:S(2)}, u32[]{:S(2)}) collective-permute-start(bf16[64,2048]{1,0:T(8,128)(2,1)S(1)} %get-tuple-element.73), channel_id=1, source_target_pairs={{0,6},{1,7},{2,0},{3,1},{4,2},{5,3},{6,4},{7,5},{8,14},{9,15},{10,... | collective-permute-start | bytes 786440 | tf_op jit(solution)/shard_map/ppermute | solution.py:346
  71.1 1.8 %own.1 = (bf16[64,4096]{1,0:T(8,128)(2,1)S(1)}, bf16[64,4096]{1,0:T(8,128)(2,1)S(1)}) custom-call(s32[222]{0:T(256)S(1)} %concatenate.6.table, bf16[512,1024]{1,0:T(8,128)(2,1)S(1)} %get-tuple-element.59.att, bf16[1024,4096]{1,0:T(8,128)(2,1)S(1)} %get-tuple-element.54.w, bf16[64,2048]{1,0:T(8,128)(2,1)S(1)} %get-tuple-element.78.after), custom_call_target="tpu_custom_call" | custom-call | flops 10000000 | bytes 10485 | tf_op jit(solution)/shard_map/own/pallas_call | solution.py:356
  74.2 2.7 %collective-permute-start.18 = (bf16[64,2048]{1,0:T(8,128)(2,1)S(1)}, bf16[64,2048]{1,0:T(8,128)(2,1)S(1)}, u32[]{:S(2)}, u32[]{:S(2)}) collective-permute-start(bf16[64,2048]{1,0:T(8,128)(2,1)S(1)} %get-tuple-element.77), channel_id=1, source_target_pairs={{0,6},{1,7},{2,0},{3,1},{4,2},{5,3},{6,4},{7,5},{8,14},{9,15},{10,... | collective-permute-start | bytes 786440 | tf_op jit(solution)/shard_map/ppermute | solution.py:346
  78.2 1.8 %collective-permute-start.20 = (bf16[64,2048]{1,0:T(8,128)(2,1)S(1)}, bf16[64,2048]{1,0:T(8,128)(2,1)S(1)}, u32[]{:S(2)}, u32[]{:S(2)}) collective-permute-start(bf16[64,2048]{1,0:T(8,128)(2,1)S(1)} %get-tuple-element.75), channel_id=1, source_target_pairs={{0,6},{1,7},{2,0},{3,1},{4,2},{5,3},{6,4},{7,5},{8,14},{9,15},{10,... | collective-permute-start | bytes 786440 | tf_op jit(solution)/shard_map/ppermute | solution.py:346
  80.0 2.6 %collective-permute-done.18.left_above = bf16[64,2048]{1,0:T(8,128)(2,1)S(1)} collective-permute-done((bf16[64,2048]{1,0:T(8,128)(2,1)S(1)}, bf16[64,2048]{1,0:T(8,128)(2,1)S(1)}, u32[]{:S(2)}, u32[]{:S(2)}) %collective-permute-start.18) | collective-permute-done | bytes 262176 | tf_op jit(solution)/shard_map/ppermute | solution.py:346
  82.6 5.6 %collective-permute-done.17.left_below = bf16[64,2048]{1,0:T(8,128)(2,1)S(1)} collective-permute-done((bf16[64,2048]{1,0:T(8,128)(2,1)S(1)}, bf16[64,2048]{1,0:T(8,128)(2,1)S(1)}, u32[]{:S(2)}, u32[]{:S(2)}) %collective-permute-start.17) | collective-permute-done | bytes 262176 | tf_op jit(solution)/shard_map/ppermute | solution.py:346
  (53 shorter events, 8.1 us)
Async XLA Ops:
  0.0 17.2 %copy-start.1 = (s32[8,3]{0,1:T(4,128)S(1)}, s32[8,3]{0,1:T(4,128)}, u32[]{:S(2)}) copy-start(s32[8,3]{0,1:T(4,128)} %param.12) | copy-start | bytes 292
  0.0 17.4 %copy-start.2 = (f32[8]{0:T(128)S(1)}, f32[8]{0:T(128)}, u32[]{:S(2)}) copy-start(f32[8]{0:T(128)} %param.10) | copy-start | bytes 100
  1.7 23.2 %all-to-all-start = ((bf16[32,32,128]{2,1,0:T(8,128)(2,1)}), bf16[32,32,128]{2,1,0:T(8,128)(2,1)S(1)}, u32[]{:S(2)}, u32[]{:S(2)}) async-start(bf16[32,32,128]{2,1,0:T(8,128)(2,1)} %bitcast.10.spread), calls=%async_computation | async-start | bytes 524288 | tf_op jit(solution)/shard_map/all_to_all | solution.py:300
  13.7 16.4 %collective-permute-start = (bf16[32,32,128]{2,1,0:T(8,128)(2,1)}, bf16[32,32,128]{2,1,0:T(8,128)(2,1)S(1)}, u32[]{:S(2)}, u32[]{:S(2)}) collective-permute-start(bf16[32,32,128]{2,1,0:T(8,128)(2,1)} %bitcast.10.spread), channel_id=1, source_target_pairs={{0,8},{8,16},{16,24},{24,32},{32,40},{40,48},{48,56},{56,64},{64,7... | collective-permute-start | bytes 786440 | tf_op jit(solution)/shard_map/ppermute | solution.py:299
  25.3 4.9 %collective-permute-start.1 = (bf16[24,8,128]{2,1,0:T(8,128)(2,1)S(1)}, bf16[24,8,128]{2,1,0:T(8,128)(2,1)S(1)}, u32[]{:S(2)}, u32[]{:S(2)}) collective-permute-start(bf16[24,8,128]{2,1,0:T(8,128)(2,1)S(1)} %fusion), channel_id=1, source_target_pairs={{0,192},{8,200},{16,208},{24,216},{32,224},{40,232},{48,240},{56,2... | collective-permute-start | bytes 147464 | tf_op jit(solution)/shard_map/ppermute | solution.py:313
  26.9 6.9 %collective-permute-start.2 = (bf16[24,8,128]{2,1,0:T(8,128)(2,1)S(1)}, bf16[24,8,128]{2,1,0:T(8,128)(2,1)S(1)}, u32[]{:S(2)}, u32[]{:S(2)}) collective-permute-start(bf16[24,8,128]{2,1,0:T(8,128)(2,1)S(1)} %fusion), channel_id=1, source_target_pairs={{0,128},{8,136},{16,144},{24,152},{32,160},{40,168},{48,176},{56,1... | collective-permute-start | bytes 147464 | tf_op jit(solution)/shard_map/ppermute | solution.py:313
  30.2 5.5 %collective-permute-start.3 = (bf16[24,8,128]{2,1,0:T(8,128)(2,1)S(1)}, bf16[24,8,128]{2,1,0:T(8,128)(2,1)S(1)}, u32[]{:S(2)}, u32[]{:S(2)}) collective-permute-start(bf16[24,8,128]{2,1,0:T(8,128)(2,1)S(1)} %fusion), channel_id=1, source_target_pairs={{0,64},{8,72},{16,80},{24,88},{32,96},{40,104},{48,112},{56,120},{... | collective-permute-start | bytes 147464 | tf_op jit(solution)/shard_map/ppermute | solution.py:313
  35.7 7.3 %collective-permute-start.7 = (bf16[24,32,128]{2,1,0:T(8,128)(2,1)S(1)}, bf16[24,32,128]{2,1,0:T(8,128)(2,1)S(1)}, u32[]{:S(2)}, u32[]{:S(2)}) collective-permute-start(bf16[24,32,128]{2,1,0:T(8,128)(2,1)S(1)} %pad_maximum_fusion.a0), channel_id=1, source_target_pairs={{0,32},{8,40},{16,48},{24,56},{32,0},{40,8},{48,16},{56,24},{64,96... | collective-permute-start | bytes 589832 | tf_op jit(solution)/shard_map/ppermute | solution.py:318
  35.8 9.7 %collective-permute-start.4 = (bf16[24,32,128]{2,1,0:T(8,128)(2,1)S(1)}, bf16[24,32,128]{2,1,0:T(8,128)(2,1)S(1)}, u32[]{:S(2)}, u32[]{:S(2)}) collective-permute-start(bf16[24,32,128]{2,1,0:T(8,128)(2,1)S(1)} %pad_maximum_fusion.a0), channel_id=1, source_target_pairs={{0,16},{8,24},{16,0},{24,8},{32,48},{40,56},{48,32},{56,40},{64,80... | collective-permute-start | bytes 589832 | tf_op jit(solution)/shard_map/ppermute | solution.py:319
  38.2 8.2 %collective-permute-start.5 = (bf16[24,32,128]{2,1,0:T(8,128)(2,1)S(1)}, bf16[24,32,128]{2,1,0:T(8,128)(2,1)S(1)}, u32[]{:S(2)}, u32[]{:S(2)}) collective-permute-start(bf16[24,32,128]{2,1,0:T(8,128)(2,1)S(1)} %pad_maximum_fusion.a0), channel_id=1, source_target_pairs={{0,8},{8,0},{16,24},{24,16},{32,40},{40,32},{48,56},{56,48},{64,72... | collective-permute-start | bytes 589832 | tf_op jit(solution)/shard_map/ppermute | solution.py:319
  38.5 7.9 %collective-permute-start.6 = (bf16[24,32,128]{2,1,0:T(8,128)(2,1)S(1)}, bf16[24,32,128]{2,1,0:T(8,128)(2,1)S(1)}, u32[]{:S(2)}, u32[]{:S(2)}) collective-permute-start(bf16[24,32,128]{2,1,0:T(8,128)(2,1)S(1)} %pad_maximum_fusion.a0), channel_id=1, source_target_pairs={{0,24},{8,16},{16,8},{24,0},{32,56},{40,48},{48,40},{56,32},{64,88... | collective-permute-start | bytes 589832 | tf_op jit(solution)/shard_map/ppermute | solution.py:319
  43.1 10.4 %collective-permute-start.10 = (bf16[24,32,128]{2,1,0:T(8,128)(2,1)S(1)}, bf16[24,32,128]{2,1,0:T(8,128)(2,1)S(1)}, u32[]{:S(2)}, u32[]{:S(2)}) collective-permute-start(bf16[24,32,128]{2,1,0:T(8,128)(2,1)S(1)} %collective-permute-done.7.b0), channel_id=1, source_target_pairs={{0,24},{8,16},{16,8},{24,0},{32,56},{40,48},{48,40},{56,32},{64,88... | collective-permute-start | bytes 589832 | tf_op jit(solution)/shard_map/ppermute | solution.py:329
  45.2 8.2 %collective-permute-start.8 = (bf16[24,32,128]{2,1,0:T(8,128)(2,1)S(1)}, bf16[24,32,128]{2,1,0:T(8,128)(2,1)S(1)}, u32[]{:S(2)}, u32[]{:S(2)}) collective-permute-start(bf16[24,32,128]{2,1,0:T(8,128)(2,1)S(1)} %collective-permute-done.7.b0), channel_id=1, source_target_pairs={{0,16},{8,24},{16,0},{24,8},{32,48},{40,56},{48,32},{56,40},{64,80... | collective-permute-start | bytes 589832 | tf_op jit(solution)/shard_map/ppermute | solution.py:329
  45.6 7.9 %collective-permute-start.9 = (bf16[24,32,128]{2,1,0:T(8,128)(2,1)S(1)}, bf16[24,32,128]{2,1,0:T(8,128)(2,1)S(1)}, u32[]{:S(2)}, u32[]{:S(2)}) collective-permute-start(bf16[24,32,128]{2,1,0:T(8,128)(2,1)S(1)} %collective-permute-done.7.b0), channel_id=1, source_target_pairs={{0,8},{8,0},{16,24},{24,16},{32,40},{40,32},{48,56},{56,48},{64,72... | collective-permute-start | bytes 589832 | tf_op jit(solution)/shard_map/ppermute | solution.py:329
  59.4 8.7 %collective-permute-start.14 = (bf16[64,4096]{1,0:T(8,128)(2,1)S(1)}, bf16[64,4096]{1,0:T(8,128)(2,1)S(1)}, u32[]{:S(2)}, u32[]{:S(2)}) collective-permute-start(bf16[64,4096]{1,0:T(8,128)(2,1)S(1)} %get-tuple-element.67), channel_id=1, source_target_pairs={{0,1},{1,0},{2,3},{3,2},{4,5},{5,4},{6,7},{7,6},{8,9},{9,8},{10,11... | collective-permute-start | bytes 1572872 | tf_op jit(solution)/shard_map/ppermute | solution.py:343
  67.4 3.5 %collective-permute-start.11 = (bf16[128,2048]{1,0:T(8,128)(2,1)S(1)}, bf16[128,2048]{1,0:T(8,128)(2,1)S(1)}, u32[]{:S(2)}, u32[]{:S(2)}) collective-permute-start(bf16[128,2048]{1,0:T(8,128)(2,1)S(1)} %get-tuple-element.61), channel_id=1, source_target_pairs={{0,1},{1,0},{2,3},{3,2},{4,5},{5,4},{6,7},{7,6},{8,9},{9,8},{10,11... | collective-permute-start | bytes 1572872 | tf_op jit(solution)/shard_map/ppermute | solution.py:343
  67.5 6.7 %collective-permute-start.13 = (bf16[128,2048]{1,0:T(8,128)(2,1)S(1)}, bf16[128,2048]{1,0:T(8,128)(2,1)S(1)}, u32[]{:S(2)}, u32[]{:S(2)}) collective-permute-start(bf16[128,2048]{1,0:T(8,128)(2,1)S(1)} %get-tuple-element.65), channel_id=1, source_target_pairs={{0,1},{1,0},{2,3},{3,2},{4,5},{5,4},{6,7},{7,6},{8,9},{9,8},{10,11... | collective-permute-start | bytes 1572872 | tf_op jit(solution)/shard_map/ppermute | solution.py:343
  68.2 8.9 %collective-permute-start.15 = (bf16[64,2048]{1,0:T(8,128)(2,1)S(1)}, bf16[64,2048]{1,0:T(8,128)(2,1)S(1)}, u32[]{:S(2)}, u32[]{:S(2)}) collective-permute-start(bf16[64,2048]{1,0:T(8,128)(2,1)S(1)} %get-tuple-element.74), channel_id=1, source_target_pairs={{0,2},{1,3},{2,4},{3,5},{4,6},{5,7},{6,0},{7,1},{8,10},{9,11},{10,... | collective-permute-start | bytes 786440 | tf_op jit(solution)/shard_map/ppermute | solution.py:346
  69.4 7.6 %collective-permute-start.16 = (bf16[64,2048]{1,0:T(8,128)(2,1)S(1)}, bf16[64,2048]{1,0:T(8,128)(2,1)S(1)}, u32[]{:S(2)}, u32[]{:S(2)}) collective-permute-start(bf16[64,2048]{1,0:T(8,128)(2,1)S(1)} %get-tuple-element.73), channel_id=1, source_target_pairs={{0,6},{1,7},{2,0},{3,1},{4,2},{5,3},{6,4},{7,5},{8,14},{9,15},{10,... | collective-permute-start | bytes 786440 | tf_op jit(solution)/shard_map/ppermute | solution.py:346
  71.0 11.6 %collective-permute-start.19 = (bf16[64,2048]{1,0:T(8,128)(2,1)S(1)}, bf16[64,2048]{1,0:T(8,128)(2,1)S(1)}, u32[]{:S(2)}, u32[]{:S(2)}) collective-permute-start(bf16[64,2048]{1,0:T(8,128)(2,1)S(1)} %get-tuple-element.78.after), channel_id=1, source_target_pairs={{0,2},{1,3},{2,4},{3,5},{4,6},{5,7},{6,0},{7,1},{8,10},{9,11},{10,... | collective-permute-start | bytes 786440 | tf_op jit(solution)/shard_map/ppermute | solution.py:346
  73.0 15.3 %collective-permute-start.12 = (bf16[64,4096]{1,0:T(8,128)(2,1)S(1)}, bf16[64,4096]{1,0:T(8,128)(2,1)S(1)}, u32[]{:S(2)}, u32[]{:S(2)}) collective-permute-start(bf16[64,4096]{1,0:T(8,128)(2,1)S(1)} %get-tuple-element.63), channel_id=1, source_target_pairs={{0,1},{1,0},{2,3},{3,2},{4,5},{5,4},{6,7},{7,6},{8,9},{9,8},{10,11... | collective-permute-start | bytes 1572872 | tf_op jit(solution)/shard_map/ppermute | solution.py:343
  74.2 8.4 %collective-permute-start.18 = (bf16[64,2048]{1,0:T(8,128)(2,1)S(1)}, bf16[64,2048]{1,0:T(8,128)(2,1)S(1)}, u32[]{:S(2)}, u32[]{:S(2)}) collective-permute-start(bf16[64,2048]{1,0:T(8,128)(2,1)S(1)} %get-tuple-element.77), channel_id=1, source_target_pairs={{0,6},{1,7},{2,0},{3,1},{4,2},{5,3},{6,4},{7,5},{8,14},{9,15},{10,... | collective-permute-start | bytes 786440 | tf_op jit(solution)/shard_map/ppermute | solution.py:346
  77.3 11.0 %collective-permute-start.17 = (bf16[64,2048]{1,0:T(8,128)(2,1)S(1)}, bf16[64,2048]{1,0:T(8,128)(2,1)S(1)}, u32[]{:S(2)}, u32[]{:S(2)}) collective-permute-start(bf16[64,2048]{1,0:T(8,128)(2,1)S(1)} %get-tuple-element.76), channel_id=1, source_target_pairs={{0,2},{1,3},{2,4},{3,5},{4,6},{5,7},{6,0},{7,1},{8,10},{9,11},{10,... | collective-permute-start | bytes 786440 | tf_op jit(solution)/shard_map/ppermute | solution.py:346
  78.2 10.0 %collective-permute-start.20 = (bf16[64,2048]{1,0:T(8,128)(2,1)S(1)}, bf16[64,2048]{1,0:T(8,128)(2,1)S(1)}, u32[]{:S(2)}, u32[]{:S(2)}) collective-permute-start(bf16[64,2048]{1,0:T(8,128)(2,1)S(1)} %get-tuple-element.75), channel_id=1, source_target_pairs={{0,6},{1,7},{2,0},{3,1},{4,2},{5,3},{6,4},{7,5},{8,14},{9,15},{10,... | collective-permute-start | bytes 786440 | tf_op jit(solution)/shard_map/ppermute | solution.py:346
  (1 other events, 16.9 us)

commit v13 on v12

--- a/solution.py
+++ b/solution.py
@@ -315,7 +315,8 @@
     z2, z4, z6 = from_z(mine, 2), from_z(mine, 4), from_z(mine, 6)
     prev, z2, z4, z6 = lax.optimization_barrier((prev, z2, z4, z6))
     a0 = jnp.concatenate([mine, z2, z4, z6], axis=1)
-    b0 = lax.ppermute(a0, "ctx", [(Y * z + y, Y * (z ^ 1) + y) for z in range(Z) for y in range(Y)])
+    beside = [(Y * z + y, Y * (z ^ 1) + y) for z in range(Z) for y in range(Y)]
+    b0 = lax.ppermute(a0, "ctx", beside)
     a1, a2, a3 = [lax.ppermute(a0, "ctx", y_pairs(f)) for f in (1, 2, 3)]
 
     width = output_weight.shape[1]
@@ -326,7 +327,8 @@
         band_kernel, [SMEM] + [VMEM] * 4, state, [pltpu.VMEM((2, 2 * RUNS, ROWS, HEAD), BF16)], 3, "band",
     )(table, sink, q, prev, own)
     b0, acc = lax.optimization_barrier((b0, acc))
-    b1, b2, b3 = [lax.ppermute(b0, "ctx", y_pairs(f)) for f in (1, 2, 3)]
+    b1, b3 = [lax.ppermute(b0, "ctx", y_pairs(f)) for f in (1, 3)]
+    b2 = lax.ppermute(a2, "ctx", beside)
     acc, tops, sums, w = call(
         early_kernel, [SMEM, VMEM] + [ANY] * 5 + [VMEM] * 3, state + [(output_weight.shape, BF16)],
         [kv, pltpu.SemaphoreType.DMA((8,))], 5, "early",

time: 89.8 us -> 87.8 us (0.978)
  starting transfers between devices: 42.1 us -> 41.1 us
  waiting for transfers between devices: 21.9 us -> 20.9 us
    ppermute x4, starting transfers between devices: 3.43 us -> 2.31 us  [the longest x2 2.12 us: per_device(): b1, b3 = [lax.ppermute(b0, 'ctx', y_pairs(f)) for f in (1, 3)]]
    ppermute x4, waiting for transfers between devices: 2.29 us -> 1.22 us  [the longest x2 1.21 us: per_device(): b1, b3 = [lax.ppermute(b0, 'ctx', y_pairs(f)) for f in (1, 3)]]
  transfers between devices with their start and end apart: 22 -> 22, of which waited for: 7 -> 7; matrix products, arithmetic and copies ran while one was open for 2% -> 2% of each run, Pallas kernels for 16% -> 17%
where the time goes in v13:
time: 87.8 us; the launch traced here: 87.2 us
  starting transfers between devices  41.1 us (47%)
  Pallas kernels  23.3 us (27%)
  waiting for transfers between devices  20.9 us (24%)
    all_to_all x1, starting transfers between devices, per_device(): lax.all_to_all(spread, 'ctx', 0, 0, tiled=True).reshape(BLOCKS * 8, HEAD)  12 us
    ppermute x6, waiting for transfers between devices, to_x(): return lax.ppermute(a, 'head', x_pairs(step))  8.35 us
    ppermute x6, starting transfers between devices, to_x(): return lax.ppermute(a, 'head', x_pairs(step))  8.27 us
    ppermute x4, starting transfers between devices, swap(): return lax.ppermute(a, 'head', CORE_PAIRS)  7.05 us
    pallas_call x1, Pallas kernels, per_device(): call(late_kernel, [SMEM, VMEM, VMEM] + [ANY] * 4 + [VMEM] * 3, [rows, par...  5.94 us
    all_to_all x1, waiting for transfers between devices, per_device(): lax.all_to_all(spread, 'ctx', 0, 0, tiled=True).reshape(BLOCKS * 8, HEAD)  5.8 us
    ppermute x3, waiting for transfers between devices, from_z(): return lax.ppermute(a, 'ctx', z_pairs(-offset))  5.47 us
    ppermute x3, starting transfers between devices, from_z(): return lax.ppermute(a, 'ctx', z_pairs(-offset))  4.9 us
  transfers between devices with their start and end apart: 22, of which 7 were waited for; matrix products, arithmetic and copies ran while one was open for 2% of the time, Pallas kernels for 17%

profile of v13, /device:TPU:1, one launch (start us, length us, event | category | flops | bytes accessed | tf_op | source)
XLA Modules:
  0.0 87.2 jit_solution(3627223727348464007)
XLA Ops:
  0.0 1.7 %spread.1 = bf16[16,2,4,8,128]{4,3,2,1,0:T(8,128)(2,1)} custom-call(bf16[4,16,8,128]{3,2,1,0:T(8,128)(2,1)} %bitcast.18, bf16[4,16,8,128]{3,2,1,0:T(8,128)(2,1)} %bitcast.20), custom_call_target="tpu_custom_call" | custom-call | flops 1000000000 | bytes 1048576 | tf_op jit(solution)/shard_map/spread/pallas_call | solution.py:295
  1.7 12.0 %all-to-all-start = ((bf16[32,32,128]{2,1,0:T(8,128)(2,1)}), bf16[32,32,128]{2,1,0:T(8,128)(2,1)S(1)}, u32[]{:S(2)}, u32[]{:S(2)}) async-start(bf16[32,32,128]{2,1,0:T(8,128)(2,1)} %bitcast.10.spread), calls=%async_computation | async-start | bytes 524288 | tf_op jit(solution)/shard_map/all_to_all | solution.py:300
  13.7 3.1 %collective-permute-start = (bf16[32,32,128]{2,1,0:T(8,128)(2,1)}, bf16[32,32,128]{2,1,0:T(8,128)(2,1)S(1)}, u32[]{:S(2)}, u32[]{:S(2)}) collective-permute-start(bf16[32,32,128]{2,1,0:T(8,128)(2,1)} %bitcast.10.spread), channel_id=1, source_target_pairs={{0,8},{8,16},{16,24},{24,32},{32,40},{40,48},{48,56},{56,64},{64,7... | collective-permute-start | bytes 786440 | tf_op jit(solution)/shard_map/ppermute | solution.py:299
  17.5 1.3 %fetch.1 = (bf16[512,1024]{1,0:T(8,128)(2,1)S(1)}, bf16[2,4,128,128]{3,2,1,0:T(8,128)(2,1)S(1)}) custom-call(bf16[512,1024]{1,0:T(8,128)(2,1)} %q.1, bf16[4,128,128]{2,1,0:T(8,128)(2,1)} %bitcast.19, bf16[4,128,128]{2,1,0:T(8,128)(2,1)} %bitcast.21, bf16[32,32,128]{2,1,0:T(8,128)(2,1)} %bitcast.10.spread), custom_call_target="tpu_custom_call" | custom-call | flops 1000000000 | bytes 1048576 | tf_op jit(solution)/shard_map/fetch/pallas_call | solution.py:302
  19.1 5.8 %all-to-all-done = bf16[32,32,128]{2,1,0:T(8,128)(2,1)S(1)} async-done(((bf16[32,32,128]{2,1,0:T(8,128)(2,1)}), bf16[32,32,128]{2,1,0:T(8,128)(2,1)S(1)}, u32[]{:S(2)}, u32[]{:S(2)}) %all-to-all-start) | async-done | bytes 262176 | tf_op jit(solution)/shard_map/all_to_all | solution.py:300
  25.3 1.6 %collective-permute-start.1 = (bf16[24,8,128]{2,1,0:T(8,128)(2,1)S(1)}, bf16[24,8,128]{2,1,0:T(8,128)(2,1)S(1)}, u32[]{:S(2)}, u32[]{:S(2)}) collective-permute-start(bf16[24,8,128]{2,1,0:T(8,128)(2,1)S(1)} %fusion), channel_id=1, source_target_pairs={{0,192},{8,200},{16,208},{24,216},{32,224},{40,232},{48,240},{56,2... | collective-permute-start | bytes 147464 | tf_op jit(solution)/shard_map/ppermute | solution.py:313
  26.9 3.3 %collective-permute-start.2 = (bf16[24,8,128]{2,1,0:T(8,128)(2,1)S(1)}, bf16[24,8,128]{2,1,0:T(8,128)(2,1)S(1)}, u32[]{:S(2)}, u32[]{:S(2)}) collective-permute-start(bf16[24,8,128]{2,1,0:T(8,128)(2,1)S(1)} %fusion), channel_id=1, source_target_pairs={{0,128},{8,136},{16,144},{24,152},{32,160},{40,168},{48,176},{56,1... | collective-permute-start | bytes 147464 | tf_op jit(solution)/shard_map/ppermute | solution.py:313
  30.2 3.6 %collective-permute-done.2 = bf16[24,8,128]{2,1,0:T(8,128)(2,1)S(1)} collective-permute-done((bf16[24,8,128]{2,1,0:T(8,128)(2,1)S(1)}, bf16[24,8,128]{2,1,0:T(8,128)(2,1)S(1)}, u32[]{:S(2)}, u32[]{:S(2)}) %collective-permute-start.2) | collective-permute-done | bytes 49184 | tf_op jit(solution)/shard_map/ppermute | solution.py:313
  33.8 1.9 %collective-permute-done.3 = bf16[24,8,128]{2,1,0:T(8,128)(2,1)S(1)} collective-permute-done((bf16[24,8,128]{2,1,0:T(8,128)(2,1)S(1)}, bf16[24,8,128]{2,1,0:T(8,128)(2,1)S(1)}, u32[]{:S(2)}, u32[]{:S(2)}) %collective-permute-start.3) | collective-permute-done | bytes 49184 | tf_op jit(solution)/shard_map/ppermute | solution.py:313
  35.8 2.4 %collective-permute-start.4 = (bf16[24,32,128]{2,1,0:T(8,128)(2,1)S(1)}, bf16[24,32,128]{2,1,0:T(8,128)(2,1)S(1)}, u32[]{:S(2)}, u32[]{:S(2)}) collective-permute-start(bf16[24,32,128]{2,1,0:T(8,128)(2,1)S(1)} %pad_maximum_fusion.a0), channel_id=1, source_target_pairs={{0,16},{8,24},{16,0},{24,8},{32,48},{40,56},{48,32},{56,40},{64,80... | collective-permute-start | bytes 589832 | tf_op jit(solution)/shard_map/ppermute | solution.py:320
  39.1 3.9 %band.1 = (f32[512,1024]{1,0:T(8,128)S(1)}, f32[512,1024]{1,0:T(8,128)S(1)}, f32[512,1024]{1,0:T(8,128)S(1)}) custom-call(s32[222]{0:T(256)S(1)} %concatenate.6.table, f32[8,128]{1,0:T(8,128)S(1)} %broadcast_in_dim.35.sink, bf16[512,1024]{1,0:T(8,128)(2,1)S(1)} %get-tuple-element.42.qs, bf16[16,2,4,8,128]{4,3,2,1,0:T(8,128)(2,1)S(1)} %bitcast.16, ...), custom_call_target="tpu_custom_call" | custom-call | flops 3000000000 | bytes 3145728 | tf_op jit(solution)/shard_map/band/pallas_call | solution.py:326
  43.1 2.1 %collective-permute-start.10 = (bf16[24,32,128]{2,1,0:T(8,128)(2,1)S(1)}, bf16[24,32,128]{2,1,0:T(8,128)(2,1)S(1)}, u32[]{:S(2)}, u32[]{:S(2)}) collective-permute-start(bf16[24,32,128]{2,1,0:T(8,128)(2,1)S(1)} %collective-permute-done.7.b0), channel_id=1, source_target_pairs={{0,24},{8,16},{16,8},{24,0},{32,56},{40,48},{48,40},{56,32},{64,88... | collective-permute-start | bytes 589832 | tf_op jit(solution)/shard_map/ppermute | solution.py:330
  45.3 4.7 %early.1 = (f32[512,1024]{1,0:T(8,128)S(1)}, f32[512,1024]{1,0:T(8,128)S(1)}, f32[512,1024]{1,0:T(8,128)S(1)}, bf16[1024,4096]{1,0:T(8,128)(2,1)S(1)}) custom-call(s32[222]{0:T(256)S(1)} %concatenate.6.table, bf16[512,1024]{1,0:T(8,128)(2,1)S(1)} %get-tuple-element.42.qs, bf16[1024,4096]{1,0:T(8,128)(2,1)} %w.1, ...), custom_call_target="tpu_custom_call" | custom-call | flops 5000000000 | bytes 5242880 | tf_op jit(solution)/shard_map/early/pallas_call | solution.py:332
  51.2 5.9 %late.1 = (bf16[512,1024]{1,0:T(8,128)(2,1)S(1)}, bf16[64,4096]{1,0:T(8,128)(2,1)S(1)}, bf16[64,4096]{1,0:T(8,128)(2,1)S(1)}) custom-call(s32[222]{0:T(256)S(1)} %concatenate.6.table, bf16[512,1024]{1,0:T(8,128)(2,1)S(1)} %get-tuple-element.42.qs, bf16[1024,4096]{1,0:T(8,128)(2,1)S(1)} %get-tuple-element.54.w, ...), custom_call_target="tpu_custom_call" | custom-call | flops 10000000 | bytes 10485 | tf_op jit(solution)/shard_map/late/pallas_call | solution.py:336
  57.2 5.2 %collective-permute-start.14 = (bf16[64,4096]{1,0:T(8,128)(2,1)S(1)}, bf16[64,4096]{1,0:T(8,128)(2,1)S(1)}, u32[]{:S(2)}, u32[]{:S(2)}) collective-permute-start(bf16[64,4096]{1,0:T(8,128)(2,1)S(1)} %get-tuple-element.67), channel_id=1, source_target_pairs={{0,1},{1,0},{2,3},{3,2},{4,5},{5,4},{6,7},{7,6},{8,9},{9,8},{10,11... | collective-permute-start | bytes 1572872 | tf_op jit(solution)/shard_map/ppermute | solution.py:345
  62.4 2.9 %sides.1 = (bf16[64,4096]{1,0:T(8,128)(2,1)S(1)}, bf16[64,4096]{1,0:T(8,128)(2,1)S(1)}, bf16[128,2048]{1,0:T(8,128)(2,1)S(1)}, bf16[128,2048]{1,0:T(8,128)(2,1)S(1)}) custom-call(s32[222]{0:T(256)S(1)} %concatenate.6.table, bf16[512,1024]{1,0:T(8,128)(2,1)S(1)} %get-tuple-element.59.att, bf16[1024,4096]{1,0:T(8,128)(2,1)S(1)} %get-tuple-element.54.w), custom_call_target="tpu_custom_call" | custom-call | flops 10000000 | bytes 10485 | tf_op jit(solution)/shard_map/sides/pallas_call | solution.py:341
  66.0 1.3 %collective-permute-start.15 = (bf16[64,2048]{1,0:T(8,128)(2,1)S(1)}, bf16[64,2048]{1,0:T(8,128)(2,1)S(1)}, u32[]{:S(2)}, u32[]{:S(2)}) collective-permute-start(bf16[64,2048]{1,0:T(8,128)(2,1)S(1)} %get-tuple-element.74), channel_id=1, source_target_pairs={{0,2},{1,3},{2,4},{3,5},{4,6},{5,7},{6,0},{7,1},{8,10},{9,11},{10,... | collective-permute-start | bytes 786440 | tf_op jit(solution)/shard_map/ppermute | solution.py:348
  67.3 1.5 %collective-permute-start.16 = (bf16[64,2048]{1,0:T(8,128)(2,1)S(1)}, bf16[64,2048]{1,0:T(8,128)(2,1)S(1)}, u32[]{:S(2)}, u32[]{:S(2)}) collective-permute-start(bf16[64,2048]{1,0:T(8,128)(2,1)S(1)} %get-tuple-element.73), channel_id=1, source_target_pairs={{0,6},{1,7},{2,0},{3,1},{4,2},{5,3},{6,4},{7,5},{8,14},{9,15},{10,... | collective-permute-start | bytes 786440 | tf_op jit(solution)/shard_map/ppermute | solution.py:348
  69.0 1.8 %own.1 = (bf16[64,4096]{1,0:T(8,128)(2,1)S(1)}, bf16[64,4096]{1,0:T(8,128)(2,1)S(1)}) custom-call(s32[222]{0:T(256)S(1)} %concatenate.6.table, bf16[512,1024]{1,0:T(8,128)(2,1)S(1)} %get-tuple-element.59.att, bf16[1024,4096]{1,0:T(8,128)(2,1)S(1)} %get-tuple-element.54.w, bf16[64,2048]{1,0:T(8,128)(2,1)S(1)} %get-tuple-element.78.after), custom_call_target="tpu_custom_call" | custom-call | flops 10000000 | bytes 10485 | tf_op jit(solution)/shard_map/own/pallas_call | solution.py:358
  70.9 1.2 %collective-permute-start.12 = (bf16[64,4096]{1,0:T(8,128)(2,1)S(1)}, bf16[64,4096]{1,0:T(8,128)(2,1)S(1)}, u32[]{:S(2)}, u32[]{:S(2)}) collective-permute-start(bf16[64,4096]{1,0:T(8,128)(2,1)S(1)} %get-tuple-element.63), channel_id=1, source_target_pairs={{0,1},{1,0},{2,3},{3,2},{4,5},{5,4},{6,7},{7,6},{8,9},{9,8},{10,11... | collective-permute-start | bytes 1572872 | tf_op jit(solution)/shard_map/ppermute | solution.py:345
  72.1 2.7 %collective-permute-start.18 = (bf16[64,2048]{1,0:T(8,128)(2,1)S(1)}, bf16[64,2048]{1,0:T(8,128)(2,1)S(1)}, u32[]{:S(2)}, u32[]{:S(2)}) collective-permute-start(bf16[64,2048]{1,0:T(8,128)(2,1)S(1)} %get-tuple-element.77), channel_id=1, source_target_pairs={{0,6},{1,7},{2,0},{3,1},{4,2},{5,3},{6,4},{7,5},{8,14},{9,15},{10,... | collective-permute-start | bytes 786440 | tf_op jit(solution)/shard_map/ppermute | solution.py:348
  76.1 1.8 %collective-permute-start.20 = (bf16[64,2048]{1,0:T(8,128)(2,1)S(1)}, bf16[64,2048]{1,0:T(8,128)(2,1)S(1)}, u32[]{:S(2)}, u32[]{:S(2)}) collective-permute-start(bf16[64,2048]{1,0:T(8,128)(2,1)S(1)} %get-tuple-element.75), channel_id=1, source_target_pairs={{0,6},{1,7},{2,0},{3,1},{4,2},{5,3},{6,4},{7,5},{8,14},{9,15},{10,... | collective-permute-start | bytes 786440 | tf_op jit(solution)/shard_map/ppermute | solution.py:348
  77.9 2.6 %collective-permute-done.18.left_above = bf16[64,2048]{1,0:T(8,128)(2,1)S(1)} collective-permute-done((bf16[64,2048]{1,0:T(8,128)(2,1)S(1)}, bf16[64,2048]{1,0:T(8,128)(2,1)S(1)}, u32[]{:S(2)}, u32[]{:S(2)}) %collective-permute-start.18) | collective-permute-done | bytes 262176 | tf_op jit(solution)/shard_map/ppermute | solution.py:348
  80.5 5.6 %collective-permute-done.17.left_below = bf16[64,2048]{1,0:T(8,128)(2,1)S(1)} collective-permute-done((bf16[64,2048]{1,0:T(8,128)(2,1)S(1)}, bf16[64,2048]{1,0:T(8,128)(2,1)S(1)}, u32[]{:S(2)}, u32[]{:S(2)}) %collective-permute-start.17) | collective-permute-done | bytes 262176 | tf_op jit(solution)/shard_map/ppermute | solution.py:348
  (53 shorter events, 6.9 us)
Async XLA Ops:
  0.0 17.2 %copy-start.1 = (s32[8,3]{0,1:T(4,128)S(1)}, s32[8,3]{0,1:T(4,128)}, u32[]{:S(2)}) copy-start(s32[8,3]{0,1:T(4,128)} %param.12) | copy-start | bytes 292
  0.0 17.4 %copy-start.2 = (f32[8]{0:T(128)S(1)}, f32[8]{0:T(128)}, u32[]{:S(2)}) copy-start(f32[8]{0:T(128)} %param.10) | copy-start | bytes 100
  1.7 23.2 %all-to-all-start = ((bf16[32,32,128]{2,1,0:T(8,128)(2,1)}), bf16[32,32,128]{2,1,0:T(8,128)(2,1)S(1)}, u32[]{:S(2)}, u32[]{:S(2)}) async-start(bf16[32,32,128]{2,1,0:T(8,128)(2,1)} %bitcast.10.spread), calls=%async_computation | async-start | bytes 524288 | tf_op jit(solution)/shard_map/all_to_all | solution.py:300
  13.7 16.4 %collective-permute-start = (bf16[32,32,128]{2,1,0:T(8,128)(2,1)}, bf16[32,32,128]{2,1,0:T(8,128)(2,1)S(1)}, u32[]{:S(2)}, u32[]{:S(2)}) collective-permute-start(bf16[32,32,128]{2,1,0:T(8,128)(2,1)} %bitcast.10.spread), channel_id=1, source_target_pairs={{0,8},{8,16},{16,24},{24,32},{32,40},{40,48},{48,56},{56,64},{64,7... | collective-permute-start | bytes 786440 | tf_op jit(solution)/shard_map/ppermute | solution.py:299
  25.3 4.9 %collective-permute-start.1 = (bf16[24,8,128]{2,1,0:T(8,128)(2,1)S(1)}, bf16[24,8,128]{2,1,0:T(8,128)(2,1)S(1)}, u32[]{:S(2)}, u32[]{:S(2)}) collective-permute-start(bf16[24,8,128]{2,1,0:T(8,128)(2,1)S(1)} %fusion), channel_id=1, source_target_pairs={{0,192},{8,200},{16,208},{24,216},{32,224},{40,232},{48,240},{56,2... | collective-permute-start | bytes 147464 | tf_op jit(solution)/shard_map/ppermute | solution.py:313
  26.9 6.9 %collective-permute-start.2 = (bf16[24,8,128]{2,1,0:T(8,128)(2,1)S(1)}, bf16[24,8,128]{2,1,0:T(8,128)(2,1)S(1)}, u32[]{:S(2)}, u32[]{:S(2)}) collective-permute-start(bf16[24,8,128]{2,1,0:T(8,128)(2,1)S(1)} %fusion), channel_id=1, source_target_pairs={{0,128},{8,136},{16,144},{24,152},{32,160},{40,168},{48,176},{56,1... | collective-permute-start | bytes 147464 | tf_op jit(solution)/shard_map/ppermute | solution.py:313
  30.2 5.5 %collective-permute-start.3 = (bf16[24,8,128]{2,1,0:T(8,128)(2,1)S(1)}, bf16[24,8,128]{2,1,0:T(8,128)(2,1)S(1)}, u32[]{:S(2)}, u32[]{:S(2)}) collective-permute-start(bf16[24,8,128]{2,1,0:T(8,128)(2,1)S(1)} %fusion), channel_id=1, source_target_pairs={{0,64},{8,72},{16,80},{24,88},{32,96},{40,104},{48,112},{56,120},{... | collective-permute-start | bytes 147464 | tf_op jit(solution)/shard_map/ppermute | solution.py:313
  35.7 7.3 %collective-permute-start.7 = (bf16[24,32,128]{2,1,0:T(8,128)(2,1)S(1)}, bf16[24,32,128]{2,1,0:T(8,128)(2,1)S(1)}, u32[]{:S(2)}, u32[]{:S(2)}) collective-permute-start(bf16[24,32,128]{2,1,0:T(8,128)(2,1)S(1)} %pad_maximum_fusion.a0), channel_id=1, source_target_pairs={{0,32},{8,40},{16,48},{24,56},{32,0},{40,8},{48,16},{56,24},{64,96... | collective-permute-start | bytes 589832 | tf_op jit(solution)/shard_map/ppermute | solution.py:319
  35.8 9.4 %collective-permute-start.4 = (bf16[24,32,128]{2,1,0:T(8,128)(2,1)S(1)}, bf16[24,32,128]{2,1,0:T(8,128)(2,1)S(1)}, u32[]{:S(2)}, u32[]{:S(2)}) collective-permute-start(bf16[24,32,128]{2,1,0:T(8,128)(2,1)S(1)} %pad_maximum_fusion.a0), channel_id=1, source_target_pairs={{0,16},{8,24},{16,0},{24,8},{32,48},{40,56},{48,32},{56,40},{64,80... | collective-permute-start | bytes 589832 | tf_op jit(solution)/shard_map/ppermute | solution.py:320
  38.2 7.1 %collective-permute-start.5 = (bf16[24,32,128]{2,1,0:T(8,128)(2,1)S(1)}, bf16[24,32,128]{2,1,0:T(8,128)(2,1)S(1)}, u32[]{:S(2)}, u32[]{:S(2)}) collective-permute-start(bf16[24,32,128]{2,1,0:T(8,128)(2,1)S(1)} %pad_maximum_fusion.a0), channel_id=1, source_target_pairs={{0,8},{8,0},{16,24},{24,16},{32,40},{40,32},{48,56},{56,48},{64,72... | collective-permute-start | bytes 589832 | tf_op jit(solution)/shard_map/ppermute | solution.py:320
  38.5 6.8 %collective-permute-start.6 = (bf16[24,32,128]{2,1,0:T(8,128)(2,1)S(1)}, bf16[24,32,128]{2,1,0:T(8,128)(2,1)S(1)}, u32[]{:S(2)}, u32[]{:S(2)}) collective-permute-start(bf16[24,32,128]{2,1,0:T(8,128)(2,1)S(1)} %pad_maximum_fusion.a0), channel_id=1, source_target_pairs={{0,24},{8,16},{16,8},{24,0},{32,56},{40,48},{48,40},{56,32},{64,88... | collective-permute-start | bytes 589832 | tf_op jit(solution)/shard_map/ppermute | solution.py:320
  43.1 8.2 %collective-permute-start.10 = (bf16[24,32,128]{2,1,0:T(8,128)(2,1)S(1)}, bf16[24,32,128]{2,1,0:T(8,128)(2,1)S(1)}, u32[]{:S(2)}, u32[]{:S(2)}) collective-permute-start(bf16[24,32,128]{2,1,0:T(8,128)(2,1)S(1)} %collective-permute-done.7.b0), channel_id=1, source_target_pairs={{0,24},{8,16},{16,8},{24,0},{32,56},{40,48},{48,40},{56,32},{64,88... | collective-permute-start | bytes 589832 | tf_op jit(solution)/shard_map/ppermute | solution.py:330
  45.2 6.1 %collective-permute-start.9 = (bf16[24,32,128]{2,1,0:T(8,128)(2,1)S(1)}, bf16[24,32,128]{2,1,0:T(8,128)(2,1)S(1)}, u32[]{:S(2)}, u32[]{:S(2)}) collective-permute-start(bf16[24,32,128]{2,1,0:T(8,128)(2,1)S(1)} %collective-permute-done.7.b0), channel_id=1, source_target_pairs={{0,8},{8,0},{16,24},{24,16},{32,40},{40,32},{48,56},{56,48},{64,72... | collective-permute-start | bytes 589832 | tf_op jit(solution)/shard_map/ppermute | solution.py:330
  45.2 6.1 %collective-permute-start.8 = (bf16[24,32,128]{2,1,0:T(8,128)(2,1)S(1)}, bf16[24,32,128]{2,1,0:T(8,128)(2,1)S(1)}, u32[]{:S(2)}, u32[]{:S(2)}) collective-permute-start(bf16[24,32,128]{2,1,0:T(8,128)(2,1)S(1)} %collective-permute-done.4.a2), channel_id=1, source_target_pairs={{0,32},{8,40},{16,48},{24,56},{32,0},{40,8},{48,16},{56,24},{64,96... | collective-permute-start | bytes 589832 | tf_op jit(solution)/shard_map/ppermute | solution.py:331
  57.2 8.7 %collective-permute-start.14 = (bf16[64,4096]{1,0:T(8,128)(2,1)S(1)}, bf16[64,4096]{1,0:T(8,128)(2,1)S(1)}, u32[]{:S(2)}, u32[]{:S(2)}) collective-permute-start(bf16[64,4096]{1,0:T(8,128)(2,1)S(1)} %get-tuple-element.67), channel_id=1, source_target_pairs={{0,1},{1,0},{2,3},{3,2},{4,5},{5,4},{6,7},{7,6},{8,9},{9,8},{10,11... | collective-permute-start | bytes 1572872 | tf_op jit(solution)/shard_map/ppermute | solution.py:345
  65.3 3.5 %collective-permute-start.11 = (bf16[128,2048]{1,0:T(8,128)(2,1)S(1)}, bf16[128,2048]{1,0:T(8,128)(2,1)S(1)}, u32[]{:S(2)}, u32[]{:S(2)}) collective-permute-start(bf16[128,2048]{1,0:T(8,128)(2,1)S(1)} %get-tuple-element.61), channel_id=1, source_target_pairs={{0,1},{1,0},{2,3},{3,2},{4,5},{5,4},{6,7},{7,6},{8,9},{9,8},{10,11... | collective-permute-start | bytes 1572872 | tf_op jit(solution)/shard_map/ppermute | solution.py:345
  65.4 6.7 %collective-permute-start.13 = (bf16[128,2048]{1,0:T(8,128)(2,1)S(1)}, bf16[128,2048]{1,0:T(8,128)(2,1)S(1)}, u32[]{:S(2)}, u32[]{:S(2)}) collective-permute-start(bf16[128,2048]{1,0:T(8,128)(2,1)S(1)} %get-tuple-element.65), channel_id=1, source_target_pairs={{0,1},{1,0},{2,3},{3,2},{4,5},{5,4},{6,7},{7,6},{8,9},{9,8},{10,11... | collective-permute-start | bytes 1572872 | tf_op jit(solution)/shard_map/ppermute | solution.py:345
  66.0 8.9 %collective-permute-start.15 = (bf16[64,2048]{1,0:T(8,128)(2,1)S(1)}, bf16[64,2048]{1,0:T(8,128)(2,1)S(1)}, u32[]{:S(2)}, u32[]{:S(2)}) collective-permute-start(bf16[64,2048]{1,0:T(8,128)(2,1)S(1)} %get-tuple-element.74), channel_id=1, source_target_pairs={{0,2},{1,3},{2,4},{3,5},{4,6},{5,7},{6,0},{7,1},{8,10},{9,11},{10,... | collective-permute-start | bytes 786440 | tf_op jit(solution)/shard_map/ppermute | solution.py:348
  67.3 7.6 %collective-permute-start.16 = (bf16[64,2048]{1,0:T(8,128)(2,1)S(1)}, bf16[64,2048]{1,0:T(8,128)(2,1)S(1)}, u32[]{:S(2)}, u32[]{:S(2)}) collective-permute-start(bf16[64,2048]{1,0:T(8,128)(2,1)S(1)} %get-tuple-element.73), channel_id=1, source_target_pairs={{0,6},{1,7},{2,0},{3,1},{4,2},{5,3},{6,4},{7,5},{8,14},{9,15},{10,... | collective-permute-start | bytes 786440 | tf_op jit(solution)/shard_map/ppermute | solution.py:348
  68.9 11.6 %collective-permute-start.19 = (bf16[64,2048]{1,0:T(8,128)(2,1)S(1)}, bf16[64,2048]{1,0:T(8,128)(2,1)S(1)}, u32[]{:S(2)}, u32[]{:S(2)}) collective-permute-start(bf16[64,2048]{1,0:T(8,128)(2,1)S(1)} %get-tuple-element.78.after), channel_id=1, source_target_pairs={{0,2},{1,3},{2,4},{3,5},{4,6},{5,7},{6,0},{7,1},{8,10},{9,11},{10,... | collective-permute-start | bytes 786440 | tf_op jit(solution)/shard_map/ppermute | solution.py:348
  70.9 15.3 %collective-permute-start.12 = (bf16[64,4096]{1,0:T(8,128)(2,1)S(1)}, bf16[64,4096]{1,0:T(8,128)(2,1)S(1)}, u32[]{:S(2)}, u32[]{:S(2)}) collective-permute-start(bf16[64,4096]{1,0:T(8,128)(2,1)S(1)} %get-tuple-element.63), channel_id=1, source_target_pairs={{0,1},{1,0},{2,3},{3,2},{4,5},{5,4},{6,7},{7,6},{8,9},{9,8},{10,11... | collective-permute-start | bytes 1572872 | tf_op jit(solution)/shard_map/ppermute | solution.py:345
  72.1 8.4 %collective-permute-start.18 = (bf16[64,2048]{1,0:T(8,128)(2,1)S(1)}, bf16[64,2048]{1,0:T(8,128)(2,1)S(1)}, u32[]{:S(2)}, u32[]{:S(2)}) collective-permute-start(bf16[64,2048]{1,0:T(8,128)(2,1)S(1)} %get-tuple-element.77), channel_id=1, source_target_pairs={{0,6},{1,7},{2,0},{3,1},{4,2},{5,3},{6,4},{7,5},{8,14},{9,15},{10,... | collective-permute-start | bytes 786440 | tf_op jit(solution)/shard_map/ppermute | solution.py:348
  75.2 11.0 %collective-permute-start.17 = (bf16[64,2048]{1,0:T(8,128)(2,1)S(1)}, bf16[64,2048]{1,0:T(8,128)(2,1)S(1)}, u32[]{:S(2)}, u32[]{:S(2)}) collective-permute-start(bf16[64,2048]{1,0:T(8,128)(2,1)S(1)} %get-tuple-element.76), channel_id=1, source_target_pairs={{0,2},{1,3},{2,4},{3,5},{4,6},{5,7},{6,0},{7,1},{8,10},{9,11},{10,... | collective-permute-start | bytes 786440 | tf_op jit(solution)/shard_map/ppermute | solution.py:348
  76.1 10.0 %collective-permute-start.20 = (bf16[64,2048]{1,0:T(8,128)(2,1)S(1)}, bf16[64,2048]{1,0:T(8,128)(2,1)S(1)}, u32[]{:S(2)}, u32[]{:S(2)}) collective-permute-start(bf16[64,2048]{1,0:T(8,128)(2,1)S(1)} %get-tuple-element.75), channel_id=1, source_target_pairs={{0,6},{1,7},{2,0},{3,1},{4,2},{5,3},{6,4},{7,5},{8,14},{9,15},{10,... | collective-permute-start | bytes 786440 | tf_op jit(solution)/shard_map/ppermute | solution.py:348
  (1 other events, 16.9 us)

commit v14 on v13

--- a/solution.py
+++ b/solution.py
@@ -357,7 +357,7 @@
     right_below, left_above = to_x(direct_right, 1), to_x(direct_left, -1)
     keep_own, give_own = call(
         own_kernel, [SMEM, VMEM, VMEM, ANY], [part, part], [], 0.01, "own",
-    )(table, att, w, direct_right)
+    )(table, att, w, relayed)
 
     own = swap(give_own)
     keep_below, keep_above, relayed, relay_left, relay_right = lax.optimization_barrier(

time: 87.8 us -> 87.5 us (level)
  waiting for transfers between devices: 20.9 us -> 21.8 us
  starting transfers between devices: 41.1 us -> 40.2 us
    ppermute x6, starting transfers between devices: 8.27 us -> 7.05 us  [to_x(): return lax.ppermute(a, 'head', x_pairs(step))]
    ppermute x6, waiting for transfers between devices: 8.35 us -> 9.3 us  [to_x(): return lax.ppermute(a, 'head', x_pairs(step))]
  transfers between devices with their start and end apart: 22 -> 22, of which waited for: 7 -> 8; matrix products, arithmetic and copies ran while one was open for 2% -> 2% of each run, Pallas kernels for 17% -> 17%
where the time goes in v14:
time: 87.5 us; the launch traced here: 87.2 us
  starting transfers between devices  40.2 us (46%)
  Pallas kernels  23.3 us (27%)
  waiting for transfers between devices  21.8 us (25%)
    all_to_all x1, starting transfers between devices, per_device(): lax.all_to_all(spread, 'ctx', 0, 0, tiled=True).reshape(BLOCKS * 8, HEAD)  12 us
    ppermute x6, waiting for transfers between devices, to_x(): return lax.ppermute(a, 'head', x_pairs(step))  9.3 us
    ppermute x4, starting transfers between devices, swap(): return lax.ppermute(a, 'head', CORE_PAIRS)  7.36 us
    ppermute x6, starting transfers between devices, to_x(): return lax.ppermute(a, 'head', x_pairs(step))  7.05 us
    pallas_call x1, Pallas kernels, per_device(): call(late_kernel, [SMEM, VMEM, VMEM] + [ANY] * 4 + [VMEM] * 3, [rows, par...  5.94 us
    all_to_all x1, waiting for transfers between devices, per_device(): lax.all_to_all(spread, 'ctx', 0, 0, tiled=True).reshape(BLOCKS * 8, HEAD)  5.8 us
    ppermute x3, waiting for transfers between devices, from_z(): return lax.ppermute(a, 'ctx', z_pairs(-offset))  5.47 us
    ppermute x3, starting transfers between devices, from_z(): return lax.ppermute(a, 'ctx', z_pairs(-offset))  4.9 us
  transfers between devices with their start and end apart: 22, of which 8 were waited for; matrix products, arithmetic and copies ran while one was open for 2% of the time, Pallas kernels for 17%

profile of v14, /device:TPU:1, one launch (start us, length us, event | category | flops | bytes accessed | tf_op | source)
XLA Modules:
  0.0 87.2 jit_solution(14753855454592833335)
XLA Ops:
  0.0 1.7 %spread.1 = bf16[16,2,4,8,128]{4,3,2,1,0:T(8,128)(2,1)} custom-call(bf16[4,16,8,128]{3,2,1,0:T(8,128)(2,1)} %bitcast.18, bf16[4,16,8,128]{3,2,1,0:T(8,128)(2,1)} %bitcast.20), custom_call_target="tpu_custom_call" | custom-call | flops 1000000000 | bytes 1048576 | tf_op jit(solution)/shard_map/spread/pallas_call | solution.py:295
  1.7 12.0 %all-to-all-start = ((bf16[32,32,128]{2,1,0:T(8,128)(2,1)}), bf16[32,32,128]{2,1,0:T(8,128)(2,1)S(1)}, u32[]{:S(2)}, u32[]{:S(2)}) async-start(bf16[32,32,128]{2,1,0:T(8,128)(2,1)} %bitcast.10.spread), calls=%async_computation | async-start | bytes 524288 | tf_op jit(solution)/shard_map/all_to_all | solution.py:300
  13.7 3.1 %collective-permute-start = (bf16[32,32,128]{2,1,0:T(8,128)(2,1)}, bf16[32,32,128]{2,1,0:T(8,128)(2,1)S(1)}, u32[]{:S(2)}, u32[]{:S(2)}) collective-permute-start(bf16[32,32,128]{2,1,0:T(8,128)(2,1)} %bitcast.10.spread), channel_id=1, source_target_pairs={{0,8},{8,16},{16,24},{24,32},{32,40},{40,48},{48,56},{56,64},{64,7... | collective-permute-start | bytes 786440 | tf_op jit(solution)/shard_map/ppermute | solution.py:299
  17.5 1.3 %fetch.1 = (bf16[512,1024]{1,0:T(8,128)(2,1)S(1)}, bf16[2,4,128,128]{3,2,1,0:T(8,128)(2,1)S(1)}) custom-call(bf16[512,1024]{1,0:T(8,128)(2,1)} %q.1, bf16[4,128,128]{2,1,0:T(8,128)(2,1)} %bitcast.19, bf16[4,128,128]{2,1,0:T(8,128)(2,1)} %bitcast.21, bf16[32,32,128]{2,1,0:T(8,128)(2,1)} %bitcast.10.spread), custom_call_target="tpu_custom_call" | custom-call | flops 1000000000 | bytes 1048576 | tf_op jit(solution)/shard_map/fetch/pallas_call | solution.py:302
  19.1 5.8 %all-to-all-done = bf16[32,32,128]{2,1,0:T(8,128)(2,1)S(1)} async-done(((bf16[32,32,128]{2,1,0:T(8,128)(2,1)}), bf16[32,32,128]{2,1,0:T(8,128)(2,1)S(1)}, u32[]{:S(2)}, u32[]{:S(2)}) %all-to-all-start) | async-done | bytes 262176 | tf_op jit(solution)/shard_map/all_to_all | solution.py:300
  25.3 1.6 %collective-permute-start.1 = (bf16[24,8,128]{2,1,0:T(8,128)(2,1)S(1)}, bf16[24,8,128]{2,1,0:T(8,128)(2,1)S(1)}, u32[]{:S(2)}, u32[]{:S(2)}) collective-permute-start(bf16[24,8,128]{2,1,0:T(8,128)(2,1)S(1)} %fusion), channel_id=1, source_target_pairs={{0,192},{8,200},{16,208},{24,216},{32,224},{40,232},{48,240},{56,2... | collective-permute-start | bytes 147464 | tf_op jit(solution)/shard_map/ppermute | solution.py:313
  26.9 3.3 %collective-permute-start.2 = (bf16[24,8,128]{2,1,0:T(8,128)(2,1)S(1)}, bf16[24,8,128]{2,1,0:T(8,128)(2,1)S(1)}, u32[]{:S(2)}, u32[]{:S(2)}) collective-permute-start(bf16[24,8,128]{2,1,0:T(8,128)(2,1)S(1)} %fusion), channel_id=1, source_target_pairs={{0,128},{8,136},{16,144},{24,152},{32,160},{40,168},{48,176},{56,1... | collective-permute-start | bytes 147464 | tf_op jit(solution)/shard_map/ppermute | solution.py:313
  30.2 3.6 %collective-permute-done.2 = bf16[24,8,128]{2,1,0:T(8,128)(2,1)S(1)} collective-permute-done((bf16[24,8,128]{2,1,0:T(8,128)(2,1)S(1)}, bf16[24,8,128]{2,1,0:T(8,128)(2,1)S(1)}, u32[]{:S(2)}, u32[]{:S(2)}) %collective-permute-start.2) | collective-permute-done | bytes 49184 | tf_op jit(solution)/shard_map/ppermute | solution.py:313
  33.8 1.9 %collective-permute-done.3 = bf16[24,8,128]{2,1,0:T(8,128)(2,1)S(1)} collective-permute-done((bf16[24,8,128]{2,1,0:T(8,128)(2,1)S(1)}, bf16[24,8,128]{2,1,0:T(8,128)(2,1)S(1)}, u32[]{:S(2)}, u32[]{:S(2)}) %collective-permute-start.3) | collective-permute-done | bytes 49184 | tf_op jit(solution)/shard_map/ppermute | solution.py:313
  35.8 2.4 %collective-permute-start.4 = (bf16[24,32,128]{2,1,0:T(8,128)(2,1)S(1)}, bf16[24,32,128]{2,1,0:T(8,128)(2,1)S(1)}, u32[]{:S(2)}, u32[]{:S(2)}) collective-permute-start(bf16[24,32,128]{2,1,0:T(8,128)(2,1)S(1)} %pad_maximum_fusion.a0), channel_id=1, source_target_pairs={{0,16},{8,24},{16,0},{24,8},{32,48},{40,56},{48,32},{56,40},{64,80... | collective-permute-start | bytes 589832 | tf_op jit(solution)/shard_map/ppermute | solution.py:320
  39.1 3.9 %band.1 = (f32[512,1024]{1,0:T(8,128)S(1)}, f32[512,1024]{1,0:T(8,128)S(1)}, f32[512,1024]{1,0:T(8,128)S(1)}) custom-call(s32[222]{0:T(256)S(1)} %concatenate.6.table, f32[8,128]{1,0:T(8,128)S(1)} %broadcast_in_dim.35.sink, bf16[512,1024]{1,0:T(8,128)(2,1)S(1)} %get-tuple-element.42.qs, bf16[16,2,4,8,128]{4,3,2,1,0:T(8,128)(2,1)S(1)} %bitcast.16, ...), custom_call_target="tpu_custom_call" | custom-call | flops 3000000000 | bytes 3145728 | tf_op jit(solution)/shard_map/band/pallas_call | solution.py:326
  43.1 2.1 %collective-permute-start.10 = (bf16[24,32,128]{2,1,0:T(8,128)(2,1)S(1)}, bf16[24,32,128]{2,1,0:T(8,128)(2,1)S(1)}, u32[]{:S(2)}, u32[]{:S(2)}) collective-permute-start(bf16[24,32,128]{2,1,0:T(8,128)(2,1)S(1)} %collective-permute-done.7.b0), channel_id=1, source_target_pairs={{0,24},{8,16},{16,8},{24,0},{32,56},{40,48},{48,40},{56,32},{64,88... | collective-permute-start | bytes 589832 | tf_op jit(solution)/shard_map/ppermute | solution.py:330
  45.3 4.7 %early.1 = (f32[512,1024]{1,0:T(8,128)S(1)}, f32[512,1024]{1,0:T(8,128)S(1)}, f32[512,1024]{1,0:T(8,128)S(1)}, bf16[1024,4096]{1,0:T(8,128)(2,1)S(1)}) custom-call(s32[222]{0:T(256)S(1)} %concatenate.6.table, bf16[512,1024]{1,0:T(8,128)(2,1)S(1)} %get-tuple-element.42.qs, bf16[1024,4096]{1,0:T(8,128)(2,1)} %w.1, ...), custom_call_target="tpu_custom_call" | custom-call | flops 5000000000 | bytes 5242880 | tf_op jit(solution)/shard_map/early/pallas_call | solution.py:332
  51.2 5.9 %late.1 = (bf16[512,1024]{1,0:T(8,128)(2,1)S(1)}, bf16[64,4096]{1,0:T(8,128)(2,1)S(1)}, bf16[64,4096]{1,0:T(8,128)(2,1)S(1)}) custom-call(s32[222]{0:T(256)S(1)} %concatenate.6.table, bf16[512,1024]{1,0:T(8,128)(2,1)S(1)} %get-tuple-element.42.qs, bf16[1024,4096]{1,0:T(8,128)(2,1)S(1)} %get-tuple-element.54.w, ...), custom_call_target="tpu_custom_call" | custom-call | flops 10000000 | bytes 10485 | tf_op jit(solution)/shard_map/late/pallas_call | solution.py:336
  57.2 5.2 %collective-permute-start.13 = (bf16[64,4096]{1,0:T(8,128)(2,1)S(1)}, bf16[64,4096]{1,0:T(8,128)(2,1)S(1)}, u32[]{:S(2)}, u32[]{:S(2)}) collective-permute-start(bf16[64,4096]{1,0:T(8,128)(2,1)S(1)} %get-tuple-element.66), channel_id=1, source_target_pairs={{0,1},{1,0},{2,3},{3,2},{4,5},{5,4},{6,7},{7,6},{8,9},{9,8},{10,11... | collective-permute-start | bytes 1572872 | tf_op jit(solution)/shard_map/ppermute | solution.py:345
  62.4 2.9 %sides.1 = (bf16[64,4096]{1,0:T(8,128)(2,1)S(1)}, bf16[64,4096]{1,0:T(8,128)(2,1)S(1)}, bf16[128,2048]{1,0:T(8,128)(2,1)S(1)}, bf16[128,2048]{1,0:T(8,128)(2,1)S(1)}) custom-call(s32[222]{0:T(256)S(1)} %concatenate.6.table, bf16[512,1024]{1,0:T(8,128)(2,1)S(1)} %get-tuple-element.59.att, bf16[1024,4096]{1,0:T(8,128)(2,1)S(1)} %get-tuple-element.54.w), custom_call_target="tpu_custom_call" | custom-call | flops 10000000 | bytes 10485 | tf_op jit(solution)/shard_map/sides/pallas_call | solution.py:341
  66.0 1.3 %collective-permute-start.14 = (bf16[64,2048]{1,0:T(8,128)(2,1)S(1)}, bf16[64,2048]{1,0:T(8,128)(2,1)S(1)}, u32[]{:S(2)}, u32[]{:S(2)}) collective-permute-start(bf16[64,2048]{1,0:T(8,128)(2,1)S(1)} %get-tuple-element.74), channel_id=1, source_target_pairs={{0,2},{1,3},{2,4},{3,5},{4,6},{5,7},{6,0},{7,1},{8,10},{9,11},{10,... | collective-permute-start | bytes 786440 | tf_op jit(solution)/shard_map/ppermute | solution.py:348
  67.3 1.5 %collective-permute-start.15 = (bf16[64,2048]{1,0:T(8,128)(2,1)S(1)}, bf16[64,2048]{1,0:T(8,128)(2,1)S(1)}, u32[]{:S(2)}, u32[]{:S(2)}) collective-permute-start(bf16[64,2048]{1,0:T(8,128)(2,1)S(1)} %get-tuple-element.73), channel_id=1, source_target_pairs={{0,6},{1,7},{2,0},{3,1},{4,2},{5,3},{6,4},{7,5},{8,14},{9,15},{10,... | collective-permute-start | bytes 786440 | tf_op jit(solution)/shard_map/ppermute | solution.py:348
  68.9 1.3 %collective-permute-start.18 = (bf16[64,2048]{1,0:T(8,128)(2,1)S(1)}, bf16[64,2048]{1,0:T(8,128)(2,1)S(1)}, u32[]{:S(2)}, u32[]{:S(2)}) collective-permute-start(bf16[64,2048]{1,0:T(8,128)(2,1)S(1)} %get-tuple-element.78), channel_id=1, source_target_pairs={{0,6},{1,7},{2,0},{3,1},{4,2},{5,3},{6,4},{7,5},{8,14},{9,15},{10,... | collective-permute-start | bytes 786440 | tf_op jit(solution)/shard_map/ppermute | solution.py:348
  70.5 1.8 %own.1 = (bf16[64,4096]{1,0:T(8,128)(2,1)S(1)}, bf16[64,4096]{1,0:T(8,128)(2,1)S(1)}) custom-call(s32[222]{0:T(256)S(1)} %concatenate.6.table, bf16[512,1024]{1,0:T(8,128)(2,1)S(1)} %get-tuple-element.59.att, bf16[1024,4096]{1,0:T(8,128)(2,1)S(1)} %get-tuple-element.54.w, bf16[128,2048]{1,0:T(8,128)(2,1)S(1)} %collective-permute-done.11.after), custom_call_target="tpu_custom_call" | custom-call | flops 10000000 | bytes 10485 | tf_op jit(solution)/shard_map/own/pallas_call | solution.py:358
  72.3 1.5 %collective-permute-start.12 = (bf16[64,4096]{1,0:T(8,128)(2,1)S(1)}, bf16[64,4096]{1,0:T(8,128)(2,1)S(1)}, u32[]{:S(2)}, u32[]{:S(2)}) collective-permute-start(bf16[64,4096]{1,0:T(8,128)(2,1)S(1)} %get-tuple-element.62), channel_id=1, source_target_pairs={{0,1},{1,0},{2,3},{3,2},{4,5},{5,4},{6,7},{7,6},{8,9},{9,8},{10,11... | collective-permute-start | bytes 1572872 | tf_op jit(solution)/shard_map/ppermute | solution.py:345
  76.1 1.8 %collective-permute-start.20 = (bf16[64,2048]{1,0:T(8,128)(2,1)S(1)}, bf16[64,2048]{1,0:T(8,128)(2,1)S(1)}, u32[]{:S(2)}, u32[]{:S(2)}) collective-permute-start(bf16[64,2048]{1,0:T(8,128)(2,1)S(1)} %get-tuple-element.75), channel_id=1, source_target_pairs={{0,6},{1,7},{2,0},{3,1},{4,2},{5,3},{6,4},{7,5},{8,14},{9,15},{10,... | collective-permute-start | bytes 786440 | tf_op jit(solution)/shard_map/ppermute | solution.py:348
  77.9 2.3 %collective-permute-done.18.left_above = bf16[64,2048]{1,0:T(8,128)(2,1)S(1)} collective-permute-done((bf16[64,2048]{1,0:T(8,128)(2,1)S(1)}, bf16[64,2048]{1,0:T(8,128)(2,1)S(1)}, u32[]{:S(2)}, u32[]{:S(2)}) %collective-permute-start.18) | collective-permute-done | bytes 262176 | tf_op jit(solution)/shard_map/ppermute | solution.py:348
  80.5 5.6 %collective-permute-done.16.left_below = bf16[64,2048]{1,0:T(8,128)(2,1)S(1)} collective-permute-done((bf16[64,2048]{1,0:T(8,128)(2,1)S(1)}, bf16[64,2048]{1,0:T(8,128)(2,1)S(1)}, u32[]{:S(2)}, u32[]{:S(2)}) %collective-permute-start.16) | collective-permute-done | bytes 262176 | tf_op jit(solution)/shard_map/ppermute | solution.py:348
  (53 shorter events, 8.3 us)
Async XLA Ops:
  0.0 17.2 %copy-start.1 = (s32[8,3]{0,1:T(4,128)S(1)}, s32[8,3]{0,1:T(4,128)}, u32[]{:S(2)}) copy-start(s32[8,3]{0,1:T(4,128)} %param.12) | copy-start | bytes 292
  0.0 17.4 %copy-start.2 = (f32[8]{0:T(128)S(1)}, f32[8]{0:T(128)}, u32[]{:S(2)}) copy-start(f32[8]{0:T(128)} %param.10) | copy-start | bytes 100
  1.7 23.2 %all-to-all-start = ((bf16[32,32,128]{2,1,0:T(8,128)(2,1)}), bf16[32,32,128]{2,1,0:T(8,128)(2,1)S(1)}, u32[]{:S(2)}, u32[]{:S(2)}) async-start(bf16[32,32,128]{2,1,0:T(8,128)(2,1)} %bitcast.10.spread), calls=%async_computation | async-start | bytes 524288 | tf_op jit(solution)/shard_map/all_to_all | solution.py:300
  13.7 16.4 %collective-permute-start = (bf16[32,32,128]{2,1,0:T(8,128)(2,1)}, bf16[32,32,128]{2,1,0:T(8,128)(2,1)S(1)}, u32[]{:S(2)}, u32[]{:S(2)}) collective-permute-start(bf16[32,32,128]{2,1,0:T(8,128)(2,1)} %bitcast.10.spread), channel_id=1, source_target_pairs={{0,8},{8,16},{16,24},{24,32},{32,40},{40,48},{48,56},{56,64},{64,7... | collective-permute-start | bytes 786440 | tf_op jit(solution)/shard_map/ppermute | solution.py:299
  25.3 4.9 %collective-permute-start.1 = (bf16[24,8,128]{2,1,0:T(8,128)(2,1)S(1)}, bf16[24,8,128]{2,1,0:T(8,128)(2,1)S(1)}, u32[]{:S(2)}, u32[]{:S(2)}) collective-permute-start(bf16[24,8,128]{2,1,0:T(8,128)(2,1)S(1)} %fusion), channel_id=1, source_target_pairs={{0,192},{8,200},{16,208},{24,216},{32,224},{40,232},{48,240},{56,2... | collective-permute-start | bytes 147464 | tf_op jit(solution)/shard_map/ppermute | solution.py:313
  26.9 6.9 %collective-permute-start.2 = (bf16[24,8,128]{2,1,0:T(8,128)(2,1)S(1)}, bf16[24,8,128]{2,1,0:T(8,128)(2,1)S(1)}, u32[]{:S(2)}, u32[]{:S(2)}) collective-permute-start(bf16[24,8,128]{2,1,0:T(8,128)(2,1)S(1)} %fusion), channel_id=1, source_target_pairs={{0,128},{8,136},{16,144},{24,152},{32,160},{40,168},{48,176},{56,1... | collective-permute-start | bytes 147464 | tf_op jit(solution)/shard_map/ppermute | solution.py:313
  30.2 5.5 %collective-permute-start.3 = (bf16[24,8,128]{2,1,0:T(8,128)(2,1)S(1)}, bf16[24,8,128]{2,1,0:T(8,128)(2,1)S(1)}, u32[]{:S(2)}, u32[]{:S(2)}) collective-permute-start(bf16[24,8,128]{2,1,0:T(8,128)(2,1)S(1)} %fusion), channel_id=1, source_target_pairs={{0,64},{8,72},{16,80},{24,88},{32,96},{40,104},{48,112},{56,120},{... | collective-permute-start | bytes 147464 | tf_op jit(solution)/shard_map/ppermute | solution.py:313
  35.7 7.3 %collective-permute-start.7 = (bf16[24,32,128]{2,1,0:T(8,128)(2,1)S(1)}, bf16[24,32,128]{2,1,0:T(8,128)(2,1)S(1)}, u32[]{:S(2)}, u32[]{:S(2)}) collective-permute-start(bf16[24,32,128]{2,1,0:T(8,128)(2,1)S(1)} %pad_maximum_fusion.a0), channel_id=1, source_target_pairs={{0,32},{8,40},{16,48},{24,56},{32,0},{40,8},{48,16},{56,24},{64,96... | collective-permute-start | bytes 589832 | tf_op jit(solution)/shard_map/ppermute | solution.py:319
  35.8 9.4 %collective-permute-start.4 = (bf16[24,32,128]{2,1,0:T(8,128)(2,1)S(1)}, bf16[24,32,128]{2,1,0:T(8,128)(2,1)S(1)}, u32[]{:S(2)}, u32[]{:S(2)}) collective-permute-start(bf16[24,32,128]{2,1,0:T(8,128)(2,1)S(1)} %pad_maximum_fusion.a0), channel_id=1, source_target_pairs={{0,16},{8,24},{16,0},{24,8},{32,48},{40,56},{48,32},{56,40},{64,80... | collective-permute-start | bytes 589832 | tf_op jit(solution)/shard_map/ppermute | solution.py:320
  38.2 7.1 %collective-permute-start.5 = (bf16[24,32,128]{2,1,0:T(8,128)(2,1)S(1)}, bf16[24,32,128]{2,1,0:T(8,128)(2,1)S(1)}, u32[]{:S(2)}, u32[]{:S(2)}) collective-permute-start(bf16[24,32,128]{2,1,0:T(8,128)(2,1)S(1)} %pad_maximum_fusion.a0), channel_id=1, source_target_pairs={{0,8},{8,0},{16,24},{24,16},{32,40},{40,32},{48,56},{56,48},{64,72... | collective-permute-start | bytes 589832 | tf_op jit(solution)/shard_map/ppermute | solution.py:320
  38.5 6.8 %collective-permute-start.6 = (bf16[24,32,128]{2,1,0:T(8,128)(2,1)S(1)}, bf16[24,32,128]{2,1,0:T(8,128)(2,1)S(1)}, u32[]{:S(2)}, u32[]{:S(2)}) collective-permute-start(bf16[24,32,128]{2,1,0:T(8,128)(2,1)S(1)} %pad_maximum_fusion.a0), channel_id=1, source_target_pairs={{0,24},{8,16},{16,8},{24,0},{32,56},{40,48},{48,40},{56,32},{64,88... | collective-permute-start | bytes 589832 | tf_op jit(solution)/shard_map/ppermute | solution.py:320
  43.1 8.2 %collective-permute-start.10 = (bf16[24,32,128]{2,1,0:T(8,128)(2,1)S(1)}, bf16[24,32,128]{2,1,0:T(8,128)(2,1)S(1)}, u32[]{:S(2)}, u32[]{:S(2)}) collective-permute-start(bf16[24,32,128]{2,1,0:T(8,128)(2,1)S(1)} %collective-permute-done.7.b0), channel_id=1, source_target_pairs={{0,24},{8,16},{16,8},{24,0},{32,56},{40,48},{48,40},{56,32},{64,88... | collective-permute-start | bytes 589832 | tf_op jit(solution)/shard_map/ppermute | solution.py:330
  45.2 6.1 %collective-permute-start.9 = (bf16[24,32,128]{2,1,0:T(8,128)(2,1)S(1)}, bf16[24,32,128]{2,1,0:T(8,128)(2,1)S(1)}, u32[]{:S(2)}, u32[]{:S(2)}) collective-permute-start(bf16[24,32,128]{2,1,0:T(8,128)(2,1)S(1)} %collective-permute-done.7.b0), channel_id=1, source_target_pairs={{0,8},{8,0},{16,24},{24,16},{32,40},{40,32},{48,56},{56,48},{64,72... | collective-permute-start | bytes 589832 | tf_op jit(solution)/shard_map/ppermute | solution.py:330
  45.2 6.1 %collective-permute-start.8 = (bf16[24,32,128]{2,1,0:T(8,128)(2,1)S(1)}, bf16[24,32,128]{2,1,0:T(8,128)(2,1)S(1)}, u32[]{:S(2)}, u32[]{:S(2)}) collective-permute-start(bf16[24,32,128]{2,1,0:T(8,128)(2,1)S(1)} %collective-permute-done.4.a2), channel_id=1, source_target_pairs={{0,32},{8,40},{16,48},{24,56},{32,0},{40,8},{48,16},{56,24},{64,96... | collective-permute-start | bytes 589832 | tf_op jit(solution)/shard_map/ppermute | solution.py:331
  57.2 8.7 %collective-permute-start.13 = (bf16[64,4096]{1,0:T(8,128)(2,1)S(1)}, bf16[64,4096]{1,0:T(8,128)(2,1)S(1)}, u32[]{:S(2)}, u32[]{:S(2)}) collective-permute-start(bf16[64,4096]{1,0:T(8,128)(2,1)S(1)} %get-tuple-element.66), channel_id=1, source_target_pairs={{0,1},{1,0},{2,3},{3,2},{4,5},{5,4},{6,7},{7,6},{8,9},{9,8},{10,11... | collective-permute-start | bytes 1572872 | tf_op jit(solution)/shard_map/ppermute | solution.py:345
  65.3 3.5 %collective-permute-start.17 = (bf16[128,2048]{1,0:T(8,128)(2,1)S(1)}, bf16[128,2048]{1,0:T(8,128)(2,1)S(1)}, u32[]{:S(2)}, u32[]{:S(2)}) collective-permute-start(bf16[128,2048]{1,0:T(8,128)(2,1)S(1)} %get-tuple-element.70), channel_id=1, source_target_pairs={{0,1},{1,0},{2,3},{3,2},{4,5},{5,4},{6,7},{7,6},{8,9},{9,8},{10,11... | collective-permute-start | bytes 1572872 | tf_op jit(solution)/shard_map/ppermute | solution.py:345
  65.4 5.1 %collective-permute-start.11 = (bf16[128,2048]{1,0:T(8,128)(2,1)S(1)}, bf16[128,2048]{1,0:T(8,128)(2,1)S(1)}, u32[]{:S(2)}, u32[]{:S(2)}) collective-permute-start(bf16[128,2048]{1,0:T(8,128)(2,1)S(1)} %get-tuple-element.60), channel_id=1, source_target_pairs={{0,1},{1,0},{2,3},{3,2},{4,5},{5,4},{6,7},{7,6},{8,9},{9,8},{10,11... | collective-permute-start | bytes 1572872 | tf_op jit(solution)/shard_map/ppermute | solution.py:345
  66.0 8.9 %collective-permute-start.14 = (bf16[64,2048]{1,0:T(8,128)(2,1)S(1)}, bf16[64,2048]{1,0:T(8,128)(2,1)S(1)}, u32[]{:S(2)}, u32[]{:S(2)}) collective-permute-start(bf16[64,2048]{1,0:T(8,128)(2,1)S(1)} %get-tuple-element.74), channel_id=1, source_target_pairs={{0,2},{1,3},{2,4},{3,5},{4,6},{5,7},{6,0},{7,1},{8,10},{9,11},{10,... | collective-permute-start | bytes 786440 | tf_op jit(solution)/shard_map/ppermute | solution.py:348
  67.3 7.6 %collective-permute-start.15 = (bf16[64,2048]{1,0:T(8,128)(2,1)S(1)}, bf16[64,2048]{1,0:T(8,128)(2,1)S(1)}, u32[]{:S(2)}, u32[]{:S(2)}) collective-permute-start(bf16[64,2048]{1,0:T(8,128)(2,1)S(1)} %get-tuple-element.73), channel_id=1, source_target_pairs={{0,6},{1,7},{2,0},{3,1},{4,2},{5,3},{6,4},{7,5},{8,14},{9,15},{10,... | collective-permute-start | bytes 786440 | tf_op jit(solution)/shard_map/ppermute | solution.py:348
  68.9 11.3 %collective-permute-start.18 = (bf16[64,2048]{1,0:T(8,128)(2,1)S(1)}, bf16[64,2048]{1,0:T(8,128)(2,1)S(1)}, u32[]{:S(2)}, u32[]{:S(2)}) collective-permute-start(bf16[64,2048]{1,0:T(8,128)(2,1)S(1)} %get-tuple-element.78), channel_id=1, source_target_pairs={{0,6},{1,7},{2,0},{3,1},{4,2},{5,3},{6,4},{7,5},{8,14},{9,15},{10,... | collective-permute-start | bytes 786440 | tf_op jit(solution)/shard_map/ppermute | solution.py:348
  70.3 10.2 %collective-permute-start.19 = (bf16[64,2048]{1,0:T(8,128)(2,1)S(1)}, bf16[64,2048]{1,0:T(8,128)(2,1)S(1)}, u32[]{:S(2)}, u32[]{:S(2)}) collective-permute-start(bf16[64,2048]{1,0:T(8,128)(2,1)S(1)} %get-tuple-element.77), channel_id=1, source_target_pairs={{0,2},{1,3},{2,4},{3,5},{4,6},{5,7},{6,0},{7,1},{8,10},{9,11},{10,... | collective-permute-start | bytes 786440 | tf_op jit(solution)/shard_map/ppermute | solution.py:348
  72.3 13.8 %collective-permute-start.12 = (bf16[64,4096]{1,0:T(8,128)(2,1)S(1)}, bf16[64,4096]{1,0:T(8,128)(2,1)S(1)}, u32[]{:S(2)}, u32[]{:S(2)}) collective-permute-start(bf16[64,4096]{1,0:T(8,128)(2,1)S(1)} %get-tuple-element.62), channel_id=1, source_target_pairs={{0,1},{1,0},{2,3},{3,2},{4,5},{5,4},{6,7},{7,6},{8,9},{9,8},{10,11... | collective-permute-start | bytes 1572872 | tf_op jit(solution)/shard_map/ppermute | solution.py:345
  75.2 11.0 %collective-permute-start.16 = (bf16[64,2048]{1,0:T(8,128)(2,1)S(1)}, bf16[64,2048]{1,0:T(8,128)(2,1)S(1)}, u32[]{:S(2)}, u32[]{:S(2)}) collective-permute-start(bf16[64,2048]{1,0:T(8,128)(2,1)S(1)} %get-tuple-element.76), channel_id=1, source_target_pairs={{0,2},{1,3},{2,4},{3,5},{4,6},{5,7},{6,0},{7,1},{8,10},{9,11},{10,... | collective-permute-start | bytes 786440 | tf_op jit(solution)/shard_map/ppermute | solution.py:348
  76.1 10.0 %collective-permute-start.20 = (bf16[64,2048]{1,0:T(8,128)(2,1)S(1)}, bf16[64,2048]{1,0:T(8,128)(2,1)S(1)}, u32[]{:S(2)}, u32[]{:S(2)}) collective-permute-start(bf16[64,2048]{1,0:T(8,128)(2,1)S(1)} %get-tuple-element.75), channel_id=1, source_target_pairs={{0,6},{1,7},{2,0},{3,1},{4,2},{5,3},{6,4},{7,5},{8,14},{9,15},{10,... | collective-permute-start | bytes 786440 | tf_op jit(solution)/shard_map/ppermute | solution.py:348
  (1 other events, 16.9 us)

commit v15 on v14

--- a/solution.py
+++ b/solution.py
@@ -313,7 +313,11 @@
         return lax.ppermute(a, "ctx", z_pairs(-offset))
 
     z2, z4, z6 = from_z(mine, 2), from_z(mine, 4), from_z(mine, 6)
-    prev, z2, z4, z6 = lax.optimization_barrier((prev, z2, z4, z6))
+    state = [((TOKENS, HEADS * HEAD), F32)] * 3
+    acc, tops, sums = call(
+        band_kernel, [SMEM] + [VMEM] * 4, state, [pltpu.VMEM((2, 2 * RUNS, ROWS, HEAD), BF16)], 3, "band",
+    )(table, sink, q, prev, own)
+    z2, z4, z6, acc = lax.optimization_barrier((z2, z4, z6, acc))
     a0 = jnp.concatenate([mine, z2, z4, z6], axis=1)
     beside = [(Y * z + y, Y * (z ^ 1) + y) for z in range(Z) for y in range(Y)]
     b0 = lax.ppermute(a0, "ctx", beside)
@@ -322,11 +326,6 @@
     width = output_weight.shape[1]
     kv = pltpu.VMEM((2, SLOTS, HALF, HEAD), BF16)
     part = ((HALF, width), BF16)
-    state = [((TOKENS, HEADS * HEAD), F32)] * 3
-    acc, tops, sums = call(
-        band_kernel, [SMEM] + [VMEM] * 4, state, [pltpu.VMEM((2, 2 * RUNS, ROWS, HEAD), BF16)], 3, "band",
-    )(table, sink, q, prev, own)
-    b0, acc = lax.optimization_barrier((b0, acc))
     b1, b3 = [lax.ppermute(b0, "ctx", y_pairs(f)) for f in (1, 3)]
     b2 = lax.ppermute(a2, "ctx", beside)
     acc, tops, sums, w = call(

time: 87.5 us -> 90.1 us (1.030)
  waiting for transfers between devices: 21.8 us -> 24 us
    ppermute x3, waiting for transfers between devices: 5.47 us -> 1.92 us  [from_z(): return lax.ppermute(a, 'ctx', z_pairs(-offset))]
    all_to_all x1, waiting for transfers between devices: 5.8 us -> 8.45 us  [per_device(): lax.all_to_all(spread, 'ctx', 0, 0, tiled=True).reshape(BLOCKS * 8, HEAD)]
    ppermute x3, waiting for transfers between devices: 0.01 us -> 1.81 us  [per_device(): a1, a2, a3 = [lax.ppermute(a0, 'ctx', y_pairs(f)) for f in (1, 2, 3)]]
    ppermute x2, starting transfers between devices: 2.12 us -> 0.47 us  [per_device(): b1, b3 = [lax.ppermute(b0, 'ctx', y_pairs(f)) for f in (1, 3)]]
    ppermute x1, starting transfers between devices: 0.1 us -> 1.43 us  [per_device(): b2 = lax.ppermute(a2, 'ctx', beside)]
    ppermute x1, waiting for transfers between devices: 0.01 us -> 1.17 us  [per_device(): b0 = lax.ppermute(a0, 'ctx', beside)]
    all_to_all x1, starting transfers between devices: 12 us -> 10.9 us  [per_device(): lax.all_to_all(spread, 'ctx', 0, 0, tiled=True).reshape(BLOCKS * 8, HEAD)]
  transfers between devices with their start and end apart: 22 -> 22, of which waited for: 8 -> 11; matrix products, arithmetic and copies ran while one was open for 2% -> 2% of each run, Pallas kernels for 17% -> 16%
where the time goes in v15:
time: 90.1 us; the launch traced here: 89.8 us
  starting transfers between devices  40.5 us (45%)
  waiting for transfers between devices  24 us (27%)
  Pallas kernels  23.5 us (26%)
    all_to_all x1, starting transfers between devices, per_device(): lax.all_to_all(spread, 'ctx', 0, 0, tiled=True).reshape(BLOCKS * 8, HEAD)  10.9 us
    ppermute x6, waiting for transfers between devices, to_x(): return lax.ppermute(a, 'head', x_pairs(step))  9.3 us
    all_to_all x1, waiting for transfers between devices, per_device(): lax.all_to_all(spread, 'ctx', 0, 0, tiled=True).reshape(BLOCKS * 8, HEAD)  8.45 us
    ppermute x4, starting transfers between devices, swap(): return lax.ppermute(a, 'head', CORE_PAIRS)  7.93 us
    ppermute x6, starting transfers between devices, to_x(): return lax.ppermute(a, 'head', x_pairs(step))  7.05 us
    pallas_call x1, Pallas kernels, per_device(): call(late_kernel, [SMEM, VMEM, VMEM] + [ANY] * 4 + [VMEM] * 3, [rows, par...  5.94 us
    ppermute x3, starting transfers between devices, from_z(): return lax.ppermute(a, 'ctx', z_pairs(-offset))  5.2 us
    pallas_call x1, Pallas kernels, per_device(): call(early_kernel, [SMEM, VMEM] + [ANY] * 5 + [VMEM] * 3, state + [(outpu...  4.82 us
  transfers between devices with their start and end apart: 22, of which 11 were waited for; matrix products, arithmetic and copies ran while one was open for 2% of the time, Pallas kernels for 16%

profile of v15, /device:TPU:1, one launch (start us, length us, event | category | flops | bytes accessed | tf_op | source)
XLA Modules:
  0.0 89.8 jit_solution(4777702195751673209)
XLA Ops:
  0.0 1.7 %spread.1 = bf16[16,2,4,8,128]{4,3,2,1,0:T(8,128)(2,1)} custom-call(bf16[4,16,8,128]{3,2,1,0:T(8,128)(2,1)} %bitcast.18, bf16[4,16,8,128]{3,2,1,0:T(8,128)(2,1)} %bitcast.20), custom_call_target="tpu_custom_call" | custom-call | flops 1000000000 | bytes 1048576 | tf_op jit(solution)/shard_map/spread/pallas_call | solution.py:295
  1.7 4.0 %collective-permute-start.3 = (bf16[32,32,128]{2,1,0:T(8,128)(2,1)}, bf16[32,32,128]{2,1,0:T(8,128)(2,1)S(1)}, u32[]{:S(2)}, u32[]{:S(2)}) collective-permute-start(bf16[32,32,128]{2,1,0:T(8,128)(2,1)} %bitcast.10.spread), channel_id=1, source_target_pairs={{0,8},{8,16},{16,24},{24,32},{32,40},{40,48},{48,56},{56,64},{64,7... | collective-permute-start | bytes 786440 | tf_op jit(solution)/shard_map/ppermute | solution.py:299
  5.7 10.9 %all-to-all-start = ((bf16[32,32,128]{2,1,0:T(8,128)(2,1)}), bf16[32,32,128]{2,1,0:T(8,128)(2,1)S(1)}, u32[]{:S(2)}, u32[]{:S(2)}) async-start(bf16[32,32,128]{2,1,0:T(8,128)(2,1)} %bitcast.10.spread), calls=%async_computation | async-start | bytes 524288 | tf_op jit(solution)/shard_map/all_to_all | solution.py:300
  16.9 1.3 %fetch.1 = (bf16[512,1024]{1,0:T(8,128)(2,1)S(1)}, bf16[2,4,128,128]{3,2,1,0:T(8,128)(2,1)S(1)}) custom-call(bf16[512,1024]{1,0:T(8,128)(2,1)} %q.1, bf16[4,128,128]{2,1,0:T(8,128)(2,1)} %bitcast.19, bf16[4,128,128]{2,1,0:T(8,128)(2,1)} %bitcast.21, bf16[32,32,128]{2,1,0:T(8,128)(2,1)} %bitcast.10.spread), custom_call_target="tpu_custom_call" | custom-call | flops 1000000000 | bytes 1048576 | tf_op jit(solution)/shard_map/fetch/pallas_call | solution.py:302
  18.9 8.5 %all-to-all-done = bf16[32,32,128]{2,1,0:T(8,128)(2,1)S(1)} async-done(((bf16[32,32,128]{2,1,0:T(8,128)(2,1)}), bf16[32,32,128]{2,1,0:T(8,128)(2,1)S(1)}, u32[]{:S(2)}, u32[]{:S(2)}) %all-to-all-start) | async-done | bytes 262176 | tf_op jit(solution)/shard_map/all_to_all | solution.py:300
  27.7 1.9 %collective-permute-start = (bf16[24,8,128]{2,1,0:T(8,128)(2,1)S(1)}, bf16[24,8,128]{2,1,0:T(8,128)(2,1)S(1)}, u32[]{:S(2)}, u32[]{:S(2)}) collective-permute-start(bf16[24,8,128]{2,1,0:T(8,128)(2,1)S(1)} %fusion), channel_id=1, source_target_pairs={{0,192},{8,200},{16,208},{24,216},{32,224},{40,232},{48,240},{56,2... | collective-permute-start | bytes 147464 | tf_op jit(solution)/shard_map/ppermute | solution.py:313
  29.6 3.3 %collective-permute-start.1 = (bf16[24,8,128]{2,1,0:T(8,128)(2,1)S(1)}, bf16[24,8,128]{2,1,0:T(8,128)(2,1)S(1)}, u32[]{:S(2)}, u32[]{:S(2)}) collective-permute-start(bf16[24,8,128]{2,1,0:T(8,128)(2,1)S(1)} %fusion), channel_id=1, source_target_pairs={{0,128},{8,136},{16,144},{24,152},{32,160},{40,168},{48,176},{56,1... | collective-permute-start | bytes 147464 | tf_op jit(solution)/shard_map/ppermute | solution.py:313
  32.9 4.0 %band.1 = (f32[512,1024]{1,0:T(8,128)S(1)}, f32[512,1024]{1,0:T(8,128)S(1)}, f32[512,1024]{1,0:T(8,128)S(1)}) custom-call(s32[222]{0:T(256)S(1)} %concatenate.6.table, f32[8,128]{1,0:T(8,128)S(1)} %broadcast_in_dim.35.sink, bf16[512,1024]{1,0:T(8,128)(2,1)S(1)} %get-tuple-element.40.qs, bf16[16,2,4,8,128]{4,3,2,1,0:T(8,128)(2,1)S(1)} %bitcast.16, ...), custom_call_target="tpu_custom_call" | custom-call | flops 3000000000 | bytes 3145728 | tf_op jit(solution)/shard_map/band/pallas_call | solution.py:317
  36.9 1.9 %collective-permute-done.2 = bf16[24,8,128]{2,1,0:T(8,128)(2,1)S(1)} collective-permute-done((bf16[24,8,128]{2,1,0:T(8,128)(2,1)S(1)}, bf16[24,8,128]{2,1,0:T(8,128)(2,1)S(1)}, u32[]{:S(2)}, u32[]{:S(2)}) %collective-permute-start.2) | collective-permute-done | bytes 49184 | tf_op jit(solution)/shard_map/ppermute | solution.py:313
  38.9 2.0 %collective-permute-start.4 = (bf16[24,32,128]{2,1,0:T(8,128)(2,1)S(1)}, bf16[24,32,128]{2,1,0:T(8,128)(2,1)S(1)}, u32[]{:S(2)}, u32[]{:S(2)}) collective-permute-start(bf16[24,32,128]{2,1,0:T(8,128)(2,1)S(1)} %pad_maximum_fusion.a0), channel_id=1, source_target_pairs={{0,16},{8,24},{16,0},{24,8},{32,48},{40,56},{48,32},{56,40},{64,80... | collective-permute-start | bytes 589832 | tf_op jit(solution)/shard_map/ppermute | solution.py:324
  45.1 1.4 %collective-permute-start.8 = (bf16[24,32,128]{2,1,0:T(8,128)(2,1)S(1)}, bf16[24,32,128]{2,1,0:T(8,128)(2,1)S(1)}, u32[]{:S(2)}, u32[]{:S(2)}) collective-permute-start(bf16[24,32,128]{2,1,0:T(8,128)(2,1)S(1)} %collective-permute-done.4.a2), channel_id=1, source_target_pairs={{0,32},{8,40},{16,48},{24,56},{32,0},{40,8},{48,16},{56,24},{64,96... | collective-permute-start | bytes 589832 | tf_op jit(solution)/shard_map/ppermute | solution.py:330
  47.1 4.8 %early.1 = (f32[512,1024]{1,0:T(8,128)S(1)}, f32[512,1024]{1,0:T(8,128)S(1)}, f32[512,1024]{1,0:T(8,128)S(1)}, bf16[1024,4096]{1,0:T(8,128)(2,1)S(1)}) custom-call(s32[222]{0:T(256)S(1)} %concatenate.6.table, bf16[512,1024]{1,0:T(8,128)(2,1)S(1)} %get-tuple-element.40.qs, bf16[1024,4096]{1,0:T(8,128)(2,1)} %w.1, ...), custom_call_target="tpu_custom_call" | custom-call | flops 5000000000 | bytes 5242880 | tf_op jit(solution)/shard_map/early/pallas_call | solution.py:331
  52.0 1.3 %collective-permute-done.10.b3 = bf16[24,32,128]{2,1,0:T(8,128)(2,1)S(1)} collective-permute-done((bf16[24,32,128]{2,1,0:T(8,128)(2,1)S(1)}, bf16[24,32,128]{2,1,0:T(8,128)(2,1)S(1)}, u32[]{:S(2)}, u32[]{:S(2)}) %collective-permute-start.10) | collective-permute-done | bytes 196640 | tf_op jit(solution)/shard_map/ppermute | solution.py:329
  53.3 5.9 %late.1 = (bf16[512,1024]{1,0:T(8,128)(2,1)S(1)}, bf16[64,4096]{1,0:T(8,128)(2,1)S(1)}, bf16[64,4096]{1,0:T(8,128)(2,1)S(1)}) custom-call(s32[222]{0:T(256)S(1)} %concatenate.6.table, bf16[512,1024]{1,0:T(8,128)(2,1)S(1)} %get-tuple-element.40.qs, bf16[1024,4096]{1,0:T(8,128)(2,1)S(1)} %get-tuple-element.51.w, ...), custom_call_target="tpu_custom_call" | custom-call | flops 10000000 | bytes 10485 | tf_op jit(solution)/shard_map/late/pallas_call | solution.py:335
  59.2 5.8 %collective-permute-start.13 = (bf16[64,4096]{1,0:T(8,128)(2,1)S(1)}, bf16[64,4096]{1,0:T(8,128)(2,1)S(1)}, u32[]{:S(2)}, u32[]{:S(2)}) collective-permute-start(bf16[64,4096]{1,0:T(8,128)(2,1)S(1)} %get-tuple-element.62), channel_id=1, source_target_pairs={{0,1},{1,0},{2,3},{3,2},{4,5},{5,4},{6,7},{7,6},{8,9},{9,8},{10,11... | collective-permute-start | bytes 1572872 | tf_op jit(solution)/shard_map/ppermute | solution.py:344
  65.0 2.9 %sides.1 = (bf16[64,4096]{1,0:T(8,128)(2,1)S(1)}, bf16[64,4096]{1,0:T(8,128)(2,1)S(1)}, bf16[128,2048]{1,0:T(8,128)(2,1)S(1)}, bf16[128,2048]{1,0:T(8,128)(2,1)S(1)}) custom-call(s32[222]{0:T(256)S(1)} %concatenate.6.table, bf16[512,1024]{1,0:T(8,128)(2,1)S(1)} %get-tuple-element.55.att, bf16[1024,4096]{1,0:T(8,128)(2,1)S(1)} %get-tuple-element.51.w), custom_call_target="tpu_custom_call" | custom-call | flops 10000000 | bytes 10485 | tf_op jit(solution)/shard_map/sides/pallas_call | solution.py:340
  68.7 1.3 %collective-permute-start.14 = (bf16[64,2048]{1,0:T(8,128)(2,1)S(1)}, bf16[64,2048]{1,0:T(8,128)(2,1)S(1)}, u32[]{:S(2)}, u32[]{:S(2)}) collective-permute-start(bf16[64,2048]{1,0:T(8,128)(2,1)S(1)} %get-tuple-element.70), channel_id=1, source_target_pairs={{0,2},{1,3},{2,4},{3,5},{4,6},{5,7},{6,0},{7,1},{8,10},{9,11},{10,... | collective-permute-start | bytes 786440 | tf_op jit(solution)/shard_map/ppermute | solution.py:347
  70.0 1.5 %collective-permute-start.15 = (bf16[64,2048]{1,0:T(8,128)(2,1)S(1)}, bf16[64,2048]{1,0:T(8,128)(2,1)S(1)}, u32[]{:S(2)}, u32[]{:S(2)}) collective-permute-start(bf16[64,2048]{1,0:T(8,128)(2,1)S(1)} %get-tuple-element.69), channel_id=1, source_target_pairs={{0,6},{1,7},{2,0},{3,1},{4,2},{5,3},{6,4},{7,5},{8,14},{9,15},{10,... | collective-permute-start | bytes 786440 | tf_op jit(solution)/shard_map/ppermute | solution.py:347
  71.6 1.3 %collective-permute-start.18 = (bf16[64,2048]{1,0:T(8,128)(2,1)S(1)}, bf16[64,2048]{1,0:T(8,128)(2,1)S(1)}, u32[]{:S(2)}, u32[]{:S(2)}) collective-permute-start(bf16[64,2048]{1,0:T(8,128)(2,1)S(1)} %get-tuple-element.74), channel_id=1, source_target_pairs={{0,6},{1,7},{2,0},{3,1},{4,2},{5,3},{6,4},{7,5},{8,14},{9,15},{10,... | collective-permute-start | bytes 786440 | tf_op jit(solution)/shard_map/ppermute | solution.py:347
  73.1 1.8 %own.1 = (bf16[64,4096]{1,0:T(8,128)(2,1)S(1)}, bf16[64,4096]{1,0:T(8,128)(2,1)S(1)}) custom-call(s32[222]{0:T(256)S(1)} %concatenate.6.table, bf16[512,1024]{1,0:T(8,128)(2,1)S(1)} %get-tuple-element.55.att, bf16[1024,4096]{1,0:T(8,128)(2,1)S(1)} %get-tuple-element.51.w, bf16[128,2048]{1,0:T(8,128)(2,1)S(1)} %collective-permute-done.11.after), custom_call_target="tpu_custom_call" | custom-call | flops 10000000 | bytes 10485 | tf_op jit(solution)/shard_map/own/pallas_call | solution.py:357
  75.0 1.5 %collective-permute-start.12 = (bf16[64,4096]{1,0:T(8,128)(2,1)S(1)}, bf16[64,4096]{1,0:T(8,128)(2,1)S(1)}, u32[]{:S(2)}, u32[]{:S(2)}) collective-permute-start(bf16[64,4096]{1,0:T(8,128)(2,1)S(1)} %get-tuple-element.58), channel_id=1, source_target_pairs={{0,1},{1,0},{2,3},{3,2},{4,5},{5,4},{6,7},{7,6},{8,9},{9,8},{10,11... | collective-permute-start | bytes 1572872 | tf_op jit(solution)/shard_map/ppermute | solution.py:344
  78.7 1.8 %collective-permute-start.20 = (bf16[64,2048]{1,0:T(8,128)(2,1)S(1)}, bf16[64,2048]{1,0:T(8,128)(2,1)S(1)}, u32[]{:S(2)}, u32[]{:S(2)}) collective-permute-start(bf16[64,2048]{1,0:T(8,128)(2,1)S(1)} %get-tuple-element.71), channel_id=1, source_target_pairs={{0,6},{1,7},{2,0},{3,1},{4,2},{5,3},{6,4},{7,5},{8,14},{9,15},{10,... | collective-permute-start | bytes 786440 | tf_op jit(solution)/shard_map/ppermute | solution.py:347
  80.6 2.3 %collective-permute-done.18.left_above = bf16[64,2048]{1,0:T(8,128)(2,1)S(1)} collective-permute-done((bf16[64,2048]{1,0:T(8,128)(2,1)S(1)}, bf16[64,2048]{1,0:T(8,128)(2,1)S(1)}, u32[]{:S(2)}, u32[]{:S(2)}) %collective-permute-start.18) | collective-permute-done | bytes 262176 | tf_op jit(solution)/shard_map/ppermute | solution.py:347
  83.2 5.6 %collective-permute-done.16.left_below = bf16[64,2048]{1,0:T(8,128)(2,1)S(1)} collective-permute-done((bf16[64,2048]{1,0:T(8,128)(2,1)S(1)}, bf16[64,2048]{1,0:T(8,128)(2,1)S(1)}, u32[]{:S(2)}, u32[]{:S(2)}) %collective-permute-start.16) | collective-permute-done | bytes 262176 | tf_op jit(solution)/shard_map/ppermute | solution.py:347
  (53 shorter events, 10.7 us)
Async XLA Ops:
  0.0 16.9 %copy-start.2 = (f32[8]{0:T(128)S(1)}, f32[8]{0:T(128)}, u32[]{:S(2)}) copy-start(f32[8]{0:T(128)} %param.10) | copy-start | bytes 100
  1.7 16.7 %copy-start.1 = (s32[8,3]{0,1:T(4,128)S(1)}, s32[8,3]{0,1:T(4,128)}, u32[]{:S(2)}) copy-start(s32[8,3]{0,1:T(4,128)} %param.12) | copy-start | bytes 292
  1.7 31.2 %collective-permute-start.3 = (bf16[32,32,128]{2,1,0:T(8,128)(2,1)}, bf16[32,32,128]{2,1,0:T(8,128)(2,1)S(1)}, u32[]{:S(2)}, u32[]{:S(2)}) collective-permute-start(bf16[32,32,128]{2,1,0:T(8,128)(2,1)} %bitcast.10.spread), channel_id=1, source_target_pairs={{0,8},{8,16},{16,24},{24,32},{32,40},{40,48},{48,56},{56,64},{64,7... | collective-permute-start | bytes 786440 | tf_op jit(solution)/shard_map/ppermute | solution.py:299
  5.7 21.6 %all-to-all-start = ((bf16[32,32,128]{2,1,0:T(8,128)(2,1)}), bf16[32,32,128]{2,1,0:T(8,128)(2,1)S(1)}, u32[]{:S(2)}, u32[]{:S(2)}) async-start(bf16[32,32,128]{2,1,0:T(8,128)(2,1)} %bitcast.10.spread), calls=%async_computation | async-start | bytes 524288 | tf_op jit(solution)/shard_map/all_to_all | solution.py:300
  27.7 9.2 %collective-permute-start = (bf16[24,8,128]{2,1,0:T(8,128)(2,1)S(1)}, bf16[24,8,128]{2,1,0:T(8,128)(2,1)S(1)}, u32[]{:S(2)}, u32[]{:S(2)}) collective-permute-start(bf16[24,8,128]{2,1,0:T(8,128)(2,1)S(1)} %fusion), channel_id=1, source_target_pairs={{0,192},{8,200},{16,208},{24,216},{32,224},{40,232},{48,240},{56,2... | collective-permute-start | bytes 147464 | tf_op jit(solution)/shard_map/ppermute | solution.py:313
  29.6 7.2 %collective-permute-start.1 = (bf16[24,8,128]{2,1,0:T(8,128)(2,1)S(1)}, bf16[24,8,128]{2,1,0:T(8,128)(2,1)S(1)}, u32[]{:S(2)}, u32[]{:S(2)}) collective-permute-start(bf16[24,8,128]{2,1,0:T(8,128)(2,1)S(1)} %fusion), channel_id=1, source_target_pairs={{0,128},{8,136},{16,144},{24,152},{32,160},{40,168},{48,176},{56,1... | collective-permute-start | bytes 147464 | tf_op jit(solution)/shard_map/ppermute | solution.py:313
  32.9 5.9 %collective-permute-start.2 = (bf16[24,8,128]{2,1,0:T(8,128)(2,1)S(1)}, bf16[24,8,128]{2,1,0:T(8,128)(2,1)S(1)}, u32[]{:S(2)}, u32[]{:S(2)}) collective-permute-start(bf16[24,8,128]{2,1,0:T(8,128)(2,1)S(1)} %fusion), channel_id=1, source_target_pairs={{0,64},{8,72},{16,80},{24,88},{32,96},{40,104},{48,112},{56,120},{... | collective-permute-start | bytes 147464 | tf_op jit(solution)/shard_map/ppermute | solution.py:313
  38.8 4.6 %collective-permute-start.7 = (bf16[24,32,128]{2,1,0:T(8,128)(2,1)S(1)}, bf16[24,32,128]{2,1,0:T(8,128)(2,1)S(1)}, u32[]{:S(2)}, u32[]{:S(2)}) collective-permute-start(bf16[24,32,128]{2,1,0:T(8,128)(2,1)S(1)} %pad_maximum_fusion.a0), channel_id=1, source_target_pairs={{0,32},{8,40},{16,48},{24,56},{32,0},{40,8},{48,16},{56,24},{64,96... | collective-permute-start | bytes 589832 | tf_op jit(solution)/shard_map/ppermute | solution.py:323
  38.9 6.2 %collective-permute-start.4 = (bf16[24,32,128]{2,1,0:T(8,128)(2,1)S(1)}, bf16[24,32,128]{2,1,0:T(8,128)(2,1)S(1)}, u32[]{:S(2)}, u32[]{:S(2)}) collective-permute-start(bf16[24,32,128]{2,1,0:T(8,128)(2,1)S(1)} %pad_maximum_fusion.a0), channel_id=1, source_target_pairs={{0,16},{8,24},{16,0},{24,8},{32,48},{40,56},{48,32},{56,40},{64,80... | collective-permute-start | bytes 589832 | tf_op jit(solution)/shard_map/ppermute | solution.py:324
  41.0 5.9 %collective-permute-start.5 = (bf16[24,32,128]{2,1,0:T(8,128)(2,1)S(1)}, bf16[24,32,128]{2,1,0:T(8,128)(2,1)S(1)}, u32[]{:S(2)}, u32[]{:S(2)}) collective-permute-start(bf16[24,32,128]{2,1,0:T(8,128)(2,1)S(1)} %pad_maximum_fusion.a0), channel_id=1, source_target_pairs={{0,8},{8,0},{16,24},{24,16},{32,40},{40,32},{48,56},{56,48},{64,72... | collective-permute-start | bytes 589832 | tf_op jit(solution)/shard_map/ppermute | solution.py:324
  41.0 6.1 %collective-permute-start.6 = (bf16[24,32,128]{2,1,0:T(8,128)(2,1)S(1)}, bf16[24,32,128]{2,1,0:T(8,128)(2,1)S(1)}, u32[]{:S(2)}, u32[]{:S(2)}) collective-permute-start(bf16[24,32,128]{2,1,0:T(8,128)(2,1)S(1)} %pad_maximum_fusion.a0), channel_id=1, source_target_pairs={{0,24},{8,16},{16,8},{24,0},{32,56},{40,48},{48,40},{56,32},{64,88... | collective-permute-start | bytes 589832 | tf_op jit(solution)/shard_map/ppermute | solution.py:324
  43.4 9.9 %collective-permute-start.10 = (bf16[24,32,128]{2,1,0:T(8,128)(2,1)S(1)}, bf16[24,32,128]{2,1,0:T(8,128)(2,1)S(1)}, u32[]{:S(2)}, u32[]{:S(2)}) collective-permute-start(bf16[24,32,128]{2,1,0:T(8,128)(2,1)S(1)} %collective-permute-done.7.b0), channel_id=1, source_target_pairs={{0,24},{8,16},{16,8},{24,0},{32,56},{40,48},{48,40},{56,32},{64,88... | collective-permute-start | bytes 589832 | tf_op jit(solution)/shard_map/ppermute | solution.py:329
  43.7 9.6 %collective-permute-start.9 = (bf16[24,32,128]{2,1,0:T(8,128)(2,1)S(1)}, bf16[24,32,128]{2,1,0:T(8,128)(2,1)S(1)}, u32[]{:S(2)}, u32[]{:S(2)}) collective-permute-start(bf16[24,32,128]{2,1,0:T(8,128)(2,1)S(1)} %collective-permute-done.7.b0), channel_id=1, source_target_pairs={{0,8},{8,0},{16,24},{24,16},{32,40},{40,32},{48,56},{56,48},{64,72... | collective-permute-start | bytes 589832 | tf_op jit(solution)/shard_map/ppermute | solution.py:329
  45.1 8.2 %collective-permute-start.8 = (bf16[24,32,128]{2,1,0:T(8,128)(2,1)S(1)}, bf16[24,32,128]{2,1,0:T(8,128)(2,1)S(1)}, u32[]{:S(2)}, u32[]{:S(2)}) collective-permute-start(bf16[24,32,128]{2,1,0:T(8,128)(2,1)S(1)} %collective-permute-done.4.a2), channel_id=1, source_target_pairs={{0,32},{8,40},{16,48},{24,56},{32,0},{40,8},{48,16},{56,24},{64,96... | collective-permute-start | bytes 589832 | tf_op jit(solution)/shard_map/ppermute | solution.py:330
  59.2 9.3 %collective-permute-start.13 = (bf16[64,4096]{1,0:T(8,128)(2,1)S(1)}, bf16[64,4096]{1,0:T(8,128)(2,1)S(1)}, u32[]{:S(2)}, u32[]{:S(2)}) collective-permute-start(bf16[64,4096]{1,0:T(8,128)(2,1)S(1)} %get-tuple-element.62), channel_id=1, source_target_pairs={{0,1},{1,0},{2,3},{3,2},{4,5},{5,4},{6,7},{7,6},{8,9},{9,8},{10,11... | collective-permute-start | bytes 1572872 | tf_op jit(solution)/shard_map/ppermute | solution.py:344
  68.0 3.5 %collective-permute-start.17 = (bf16[128,2048]{1,0:T(8,128)(2,1)S(1)}, bf16[128,2048]{1,0:T(8,128)(2,1)S(1)}, u32[]{:S(2)}, u32[]{:S(2)}) collective-permute-start(bf16[128,2048]{1,0:T(8,128)(2,1)S(1)} %get-tuple-element.66), channel_id=1, source_target_pairs={{0,1},{1,0},{2,3},{3,2},{4,5},{5,4},{6,7},{7,6},{8,9},{9,8},{10,11... | collective-permute-start | bytes 1572872 | tf_op jit(solution)/shard_map/ppermute | solution.py:344
  68.1 5.1 %collective-permute-start.11 = (bf16[128,2048]{1,0:T(8,128)(2,1)S(1)}, bf16[128,2048]{1,0:T(8,128)(2,1)S(1)}, u32[]{:S(2)}, u32[]{:S(2)}) collective-permute-start(bf16[128,2048]{1,0:T(8,128)(2,1)S(1)} %get-tuple-element.56), channel_id=1, source_target_pairs={{0,1},{1,0},{2,3},{3,2},{4,5},{5,4},{6,7},{7,6},{8,9},{9,8},{10,11... | collective-permute-start | bytes 1572872 | tf_op jit(solution)/shard_map/ppermute | solution.py:344
  68.7 8.9 %collective-permute-start.14 = (bf16[64,2048]{1,0:T(8,128)(2,1)S(1)}, bf16[64,2048]{1,0:T(8,128)(2,1)S(1)}, u32[]{:S(2)}, u32[]{:S(2)}) collective-permute-start(bf16[64,2048]{1,0:T(8,128)(2,1)S(1)} %get-tuple-element.70), channel_id=1, source_target_pairs={{0,2},{1,3},{2,4},{3,5},{4,6},{5,7},{6,0},{7,1},{8,10},{9,11},{10,... | collective-permute-start | bytes 786440 | tf_op jit(solution)/shard_map/ppermute | solution.py:347
  70.0 7.6 %collective-permute-start.15 = (bf16[64,2048]{1,0:T(8,128)(2,1)S(1)}, bf16[64,2048]{1,0:T(8,128)(2,1)S(1)}, u32[]{:S(2)}, u32[]{:S(2)}) collective-permute-start(bf16[64,2048]{1,0:T(8,128)(2,1)S(1)} %get-tuple-element.69), channel_id=1, source_target_pairs={{0,6},{1,7},{2,0},{3,1},{4,2},{5,3},{6,4},{7,5},{8,14},{9,15},{10,... | collective-permute-start | bytes 786440 | tf_op jit(solution)/shard_map/ppermute | solution.py:347
  71.6 11.3 %collective-permute-start.18 = (bf16[64,2048]{1,0:T(8,128)(2,1)S(1)}, bf16[64,2048]{1,0:T(8,128)(2,1)S(1)}, u32[]{:S(2)}, u32[]{:S(2)}) collective-permute-start(bf16[64,2048]{1,0:T(8,128)(2,1)S(1)} %get-tuple-element.74), channel_id=1, source_target_pairs={{0,6},{1,7},{2,0},{3,1},{4,2},{5,3},{6,4},{7,5},{8,14},{9,15},{10,... | collective-permute-start | bytes 786440 | tf_op jit(solution)/shard_map/ppermute | solution.py:347
  72.9 10.2 %collective-permute-start.19 = (bf16[64,2048]{1,0:T(8,128)(2,1)S(1)}, bf16[64,2048]{1,0:T(8,128)(2,1)S(1)}, u32[]{:S(2)}, u32[]{:S(2)}) collective-permute-start(bf16[64,2048]{1,0:T(8,128)(2,1)S(1)} %get-tuple-element.73), channel_id=1, source_target_pairs={{0,2},{1,3},{2,4},{3,5},{4,6},{5,7},{6,0},{7,1},{8,10},{9,11},{10,... | collective-permute-start | bytes 786440 | tf_op jit(solution)/shard_map/ppermute | solution.py:347
  75.0 13.8 %collective-permute-start.12 = (bf16[64,4096]{1,0:T(8,128)(2,1)S(1)}, bf16[64,4096]{1,0:T(8,128)(2,1)S(1)}, u32[]{:S(2)}, u32[]{:S(2)}) collective-permute-start(bf16[64,4096]{1,0:T(8,128)(2,1)S(1)} %get-tuple-element.58), channel_id=1, source_target_pairs={{0,1},{1,0},{2,3},{3,2},{4,5},{5,4},{6,7},{7,6},{8,9},{9,8},{10,11... | collective-permute-start | bytes 1572872 | tf_op jit(solution)/shard_map/ppermute | solution.py:344
  77.8 11.0 %collective-permute-start.16 = (bf16[64,2048]{1,0:T(8,128)(2,1)S(1)}, bf16[64,2048]{1,0:T(8,128)(2,1)S(1)}, u32[]{:S(2)}, u32[]{:S(2)}) collective-permute-start(bf16[64,2048]{1,0:T(8,128)(2,1)S(1)} %get-tuple-element.72), channel_id=1, source_target_pairs={{0,2},{1,3},{2,4},{3,5},{4,6},{5,7},{6,0},{7,1},{8,10},{9,11},{10,... | collective-permute-start | bytes 786440 | tf_op jit(solution)/shard_map/ppermute | solution.py:347
  78.7 10.0 %collective-permute-start.20 = (bf16[64,2048]{1,0:T(8,128)(2,1)S(1)}, bf16[64,2048]{1,0:T(8,128)(2,1)S(1)}, u32[]{:S(2)}, u32[]{:S(2)}) collective-permute-start(bf16[64,2048]{1,0:T(8,128)(2,1)S(1)} %get-tuple-element.71), channel_id=1, source_target_pairs={{0,6},{1,7},{2,0},{3,1},{4,2},{5,3},{6,4},{7,5},{8,14},{9,15},{10,... | collective-permute-start | bytes 786440 | tf_op jit(solution)/shard_map/ppermute | solution.py:347
  (1 other events, 16.7 us)

commit v16 on v14

--- a/solution.py
+++ b/solution.py
@@ -37,7 +37,7 @@
 
 
 def x_pairs(step):
-    return [(2 * x + k, 2 * ((x + step) % X) + k) for x in range(X) for k in range(2)]
+    return [(2 * x + k, 2 * ((x + step * (1 - 2 * k)) % X) + k) for x in range(X) for k in range(2)]
 
 
 CORE_PAIRS = [(h, h ^ 1) for h in range(HEADS)]
@@ -215,32 +215,23 @@
     give[:, start:start + size] = rows
 
 
-def sides_kernel(table, att, w, keep_below, keep_above, direct, relayed):
-    x, mid = table[META + 5], w.shape[1] // 2
+def sides_kernel(table, att, w, keep_next, keep_prev, direct, relayed):
+    x, step = table[META + 5], 1 - 2 * table[META + 1]
 
     def give(start, size, rows):
-        below, above = rows[:HALF], rows[HALF:]
-        at = slice(start % mid, start % mid + size)
-        if start < mid:
-            relayed[:HALF, at], direct[HALF:, at] = below, above
-        else:
-            direct[:HALF, at], relayed[HALF:, at] = below, above
-
-    project(att, w, [(x + 1) % X, (x + 3) % X], table[META + 1], [keep_below, keep_above], give)
+        direct[:, start:start + size] = rows[:HALF]
+        relayed[:, start:start + size] = rows[HALF:]
+
+    project(att, w, [(x + step + X) % X, (x - step + X) % X], table[META + 1], [keep_next, keep_prev], give)
 
 
 def own_kernel(table, att, w, after, keep, give):
     project(att, w, [table[META + 5]], table[META + 1], [keep], functools.partial(store, give))
 
 
-def final_kernel(keep, swapped, left_below, left_above, right_below, right_above, out):
-    mid = out.shape[1] // 2
-    for start, pair in ((0, (left_below, left_above)), (mid, (right_below, right_above))):
-        cols = slice(start, start + mid)
-        total = keep[:, cols].astype(F32) + swapped[:, cols].astype(F32)
-        for part in pair:
-            total = total + part[...].astype(F32)
-        out[:, cols] = total.astype(BF16)
+def final_kernel(keep, swapped, direct, last, out):
+    total = keep[...].astype(F32) + swapped[...].astype(F32)
+    out[...] = (total + direct[...].astype(F32) + last[...].astype(F32)).astype(BF16)
 
 
 SMEM = pl.BlockSpec(memory_space=pltpu.SMEM)
@@ -337,10 +328,10 @@
         late_kernel, [SMEM, VMEM, VMEM] + [ANY] * 4 + [VMEM] * 3,
         [rows, part, part], [kv, pltpu.SemaphoreType.DMA((4,))], 0.01, "late",
     )(table, q, w, b0, b2, b1, b3, acc, tops, sums)
-    halves = ((2 * HALF, width // 2), BF16)
-    keep_below, keep_above, give_direct, give_relayed = call(
-        sides_kernel, [SMEM, VMEM, VMEM], [part, part, halves, halves], [], 0.01, "sides",
+    keep_next, keep_prev, give_direct, give_relayed = call(
+        sides_kernel, [SMEM, VMEM, VMEM], [part] * 4, [], 0.01, "sides",
     )(table, att, w)
+
     def swap(a):
         return lax.ppermute(a, "head", CORE_PAIRS)
 
@@ -348,30 +339,23 @@
         return lax.ppermute(a, "head", x_pairs(step))
 
     far, direct, relayed = swap(give_far), swap(give_direct), swap(give_relayed)
-    mid = width // 2
-    far_left = total_of(keep_far[:, :mid], far[:, :mid])
-    far_right = total_of(keep_far[:, mid:], far[:, mid:])
-    relay_left, relay_right = to_x(far_left, 1), to_x(far_right, -1)
-    direct_right = total_of(keep_below[:, mid:], direct[:HALF])
-    direct_left = total_of(keep_above[:, :mid], direct[HALF:])
-    right_below, left_above = to_x(direct_right, 1), to_x(direct_left, -1)
+    relay = to_x(total_of(keep_far, far), 1)
+    from_direct = to_x(total_of(keep_prev, direct), -1)
     keep_own, give_own = call(
         own_kernel, [SMEM, VMEM, VMEM, ANY], [part, part], [], 0.01, "own",
     )(table, att, w, relayed)
 
     own = swap(give_own)
-    keep_below, keep_above, relayed, relay_left, relay_right = lax.optimization_barrier(
-        (keep_below, keep_above, relayed, relay_left, relay_right))
-    left_below = to_x(total_of(keep_below[:, :mid], relayed[:HALF], relay_left), 1)
-    right_above = to_x(total_of(keep_above[:, mid:], relayed[HALF:], relay_right), -1)
+    keep_next, relayed, relay = lax.optimization_barrier((keep_next, relayed, relay))
+    from_last = to_x(total_of(keep_next, relayed, relay), 1)
     return pl.pallas_call(
         final_kernel,
         out_shape=jax.ShapeDtypeStruct((HALF, width), BF16),
-        in_specs=[VMEM] * 6,
+        in_specs=[VMEM] * 4,
         out_specs=VMEM,
         compiler_params=pltpu.CompilerParams(vmem_limit_bytes=8 * 2 ** 20),
         name="final",
-    )(keep_own, own, left_below, left_above, right_below, right_above)
+    )(keep_own, own, from_direct, from_last)
 
 
 def solution(mesh):

time: 87.5 us -> 91.1 us (1.041)
  the two profiles are of different devices: /device:TPU:1 before, /device:TPU:16 now
where the time goes in v16:
time: 91.1 us; the launch traced here: 90.8 us
  starting transfers between devices  35.8 us (39%)
  waiting for transfers between devices  29.8 us (33%)
  Pallas kernels  23.3 us (26%)
    ppermute x3, waiting for transfers between devices, to_x(): return lax.ppermute(a, 'head', x_pairs(step))  16.9 us
    all_to_all x1, starting transfers between devices, per_device(): lax.all_to_all(spread, 'ctx', 0, 0, tiled=True).reshape(BLOCKS * 8, HEAD)  11.6 us
    ppermute x3, waiting for transfers between devices, from_z(): return lax.ppermute(a, 'ctx', z_pairs(-offset))  6.71 us
    pallas_call x1, Pallas kernels, per_device(): call(late_kernel, [SMEM, VMEM, VMEM] + [ANY] * 4 + [VMEM] * 3, [rows, par...  5.94 us
    all_to_all x1, waiting for transfers between devices, per_device(): lax.all_to_all(spread, 'ctx', 0, 0, tiled=True).reshape(BLOCKS * 8, HEAD)  5.9 us
    ppermute x3, starting transfers between devices, to_x(): return lax.ppermute(a, 'head', x_pairs(step))  5.3 us
    pallas_call x1, Pallas kernels, per_device(): call(early_kernel, [SMEM, VMEM] + [ANY] * 5 + [VMEM] * 3, state + [(outpu...  4.72 us
    ppermute x3, starting transfers between devices, from_z(): return lax.ppermute(a, 'ctx', z_pairs(-offset))  4.46 us
  transfers between devices with their start and end apart: 19, of which 7 were waited for; matrix products, arithmetic and copies ran while one was open for 2% of the time, Pallas kernels for 16%

profile of v16, /device:TPU:16, one launch (start us, length us, event | category | flops | bytes accessed | tf_op | source)
XLA Modules:
  0.0 90.8 jit_solution(5616640270122940831)
XLA Ops:
  0.0 1.7 %spread.1 = bf16[16,2,4,8,128]{4,3,2,1,0:T(8,128)(2,1)} custom-call(bf16[4,16,8,128]{3,2,1,0:T(8,128)(2,1)} %bitcast.18, bf16[4,16,8,128]{3,2,1,0:T(8,128)(2,1)} %bitcast.20), custom_call_target="tpu_custom_call" | custom-call | flops 1000000000 | bytes 1048576 | tf_op jit(solution)/shard_map/spread/pallas_call | solution.py:286
  1.7 11.6 %all-to-all-start = ((bf16[32,32,128]{2,1,0:T(8,128)(2,1)}), bf16[32,32,128]{2,1,0:T(8,128)(2,1)S(1)}, u32[]{:S(2)}, u32[]{:S(2)}) async-start(bf16[32,32,128]{2,1,0:T(8,128)(2,1)} %bitcast.10.spread), calls=%async_computation | async-start | bytes 524288 | tf_op jit(solution)/shard_map/all_to_all | solution.py:291
  13.3 3.1 %collective-permute-start = (bf16[32,32,128]{2,1,0:T(8,128)(2,1)}, bf16[32,32,128]{2,1,0:T(8,128)(2,1)S(1)}, u32[]{:S(2)}, u32[]{:S(2)}) collective-permute-start(bf16[32,32,128]{2,1,0:T(8,128)(2,1)} %bitcast.10.spread), channel_id=1, source_target_pairs={{0,8},{8,16},{16,24},{24,32},{32,40},{40,48},{48,56},{56,64},{64,7... | collective-permute-start | bytes 786440 | tf_op jit(solution)/shard_map/ppermute | solution.py:290
  17.0 1.3 %fetch.1 = (bf16[512,1024]{1,0:T(8,128)(2,1)S(1)}, bf16[2,4,128,128]{3,2,1,0:T(8,128)(2,1)S(1)}) custom-call(bf16[512,1024]{1,0:T(8,128)(2,1)} %q.1, bf16[4,128,128]{2,1,0:T(8,128)(2,1)} %bitcast.19, bf16[4,128,128]{2,1,0:T(8,128)(2,1)} %bitcast.21, bf16[32,32,128]{2,1,0:T(8,128)(2,1)} %bitcast.10.spread), custom_call_target="tpu_custom_call" | custom-call | flops 1000000000 | bytes 1048576 | tf_op jit(solution)/shard_map/fetch/pallas_call | solution.py:293
  18.6 5.9 %all-to-all-done = bf16[32,32,128]{2,1,0:T(8,128)(2,1)S(1)} async-done(((bf16[32,32,128]{2,1,0:T(8,128)(2,1)}), bf16[32,32,128]{2,1,0:T(8,128)(2,1)S(1)}, u32[]{:S(2)}, u32[]{:S(2)}) %all-to-all-start) | async-done | bytes 262176 | tf_op jit(solution)/shard_map/all_to_all | solution.py:291
  25.5 3.5 %collective-permute-start.2 = (bf16[24,8,128]{2,1,0:T(8,128)(2,1)S(1)}, bf16[24,8,128]{2,1,0:T(8,128)(2,1)S(1)}, u32[]{:S(2)}, u32[]{:S(2)}) collective-permute-start(bf16[24,8,128]{2,1,0:T(8,128)(2,1)S(1)} %fusion), channel_id=1, source_target_pairs={{0,128},{8,136},{16,144},{24,152},{32,160},{40,168},{48,176},{56,1... | collective-permute-start | bytes 147464 | tf_op jit(solution)/shard_map/ppermute | solution.py:304
  29.3 1.7 %collective-permute-done.1 = bf16[24,8,128]{2,1,0:T(8,128)(2,1)S(1)} collective-permute-done((bf16[24,8,128]{2,1,0:T(8,128)(2,1)S(1)}, bf16[24,8,128]{2,1,0:T(8,128)(2,1)S(1)}, u32[]{:S(2)}, u32[]{:S(2)}) %collective-permute-start.1) | collective-permute-done | bytes 49184 | tf_op jit(solution)/shard_map/ppermute | solution.py:304
  31.0 2.8 %collective-permute-done.2 = bf16[24,8,128]{2,1,0:T(8,128)(2,1)S(1)} collective-permute-done((bf16[24,8,128]{2,1,0:T(8,128)(2,1)S(1)}, bf16[24,8,128]{2,1,0:T(8,128)(2,1)S(1)}, u32[]{:S(2)}, u32[]{:S(2)}) %collective-permute-start.2) | collective-permute-done | bytes 49184 | tf_op jit(solution)/shard_map/ppermute | solution.py:304
  33.8 2.2 %collective-permute-done.3 = bf16[24,8,128]{2,1,0:T(8,128)(2,1)S(1)} collective-permute-done((bf16[24,8,128]{2,1,0:T(8,128)(2,1)S(1)}, bf16[24,8,128]{2,1,0:T(8,128)(2,1)S(1)}, u32[]{:S(2)}, u32[]{:S(2)}) %collective-permute-start.3) | collective-permute-done | bytes 49184 | tf_op jit(solution)/shard_map/ppermute | solution.py:304
  36.2 2.9 %collective-permute-start.4 = (bf16[24,32,128]{2,1,0:T(8,128)(2,1)S(1)}, bf16[24,32,128]{2,1,0:T(8,128)(2,1)S(1)}, u32[]{:S(2)}, u32[]{:S(2)}) collective-permute-start(bf16[24,32,128]{2,1,0:T(8,128)(2,1)S(1)} %pad_maximum_fusion.a0), channel_id=1, source_target_pairs={{0,16},{8,24},{16,0},{24,8},{32,48},{40,56},{48,32},{56,40},{64,80... | collective-permute-start | bytes 589832 | tf_op jit(solution)/shard_map/ppermute | solution.py:311
  40.4 3.9 %band.1 = (f32[512,1024]{1,0:T(8,128)S(1)}, f32[512,1024]{1,0:T(8,128)S(1)}, f32[512,1024]{1,0:T(8,128)S(1)}) custom-call(s32[222]{0:T(256)S(1)} %concatenate.6.table, f32[8,128]{1,0:T(8,128)S(1)} %broadcast_in_dim.35.sink, bf16[512,1024]{1,0:T(8,128)(2,1)S(1)} %get-tuple-element.40.qs, bf16[16,2,4,8,128]{4,3,2,1,0:T(8,128)(2,1)S(1)} %bitcast.16, ...), custom_call_target="tpu_custom_call" | custom-call | flops 3000000000 | bytes 3145728 | tf_op jit(solution)/shard_map/band/pallas_call | solution.py:317
  44.3 1.6 %collective-permute-start.10 = (bf16[24,32,128]{2,1,0:T(8,128)(2,1)S(1)}, bf16[24,32,128]{2,1,0:T(8,128)(2,1)S(1)}, u32[]{:S(2)}, u32[]{:S(2)}) collective-permute-start(bf16[24,32,128]{2,1,0:T(8,128)(2,1)S(1)} %collective-permute-done.7.b0), channel_id=1, source_target_pairs={{0,24},{8,16},{16,8},{24,0},{32,56},{40,48},{48,40},{56,32},{64,88... | collective-permute-start | bytes 589832 | tf_op jit(solution)/shard_map/ppermute | solution.py:321
  45.9 2.5 %collective-permute-start.9 = (bf16[24,32,128]{2,1,0:T(8,128)(2,1)S(1)}, bf16[24,32,128]{2,1,0:T(8,128)(2,1)S(1)}, u32[]{:S(2)}, u32[]{:S(2)}) collective-permute-start(bf16[24,32,128]{2,1,0:T(8,128)(2,1)S(1)} %collective-permute-done.7.b0), channel_id=1, source_target_pairs={{0,8},{8,0},{16,24},{24,16},{32,40},{40,32},{48,56},{56,48},{64,72... | collective-permute-start | bytes 589832 | tf_op jit(solution)/shard_map/ppermute | solution.py:321
  48.4 1.9 %collective-permute-start.8 = (bf16[24,32,128]{2,1,0:T(8,128)(2,1)S(1)}, bf16[24,32,128]{2,1,0:T(8,128)(2,1)S(1)}, u32[]{:S(2)}, u32[]{:S(2)}) collective-permute-start(bf16[24,32,128]{2,1,0:T(8,128)(2,1)S(1)} %collective-permute-done.4.a2), channel_id=1, source_target_pairs={{0,32},{8,40},{16,48},{24,56},{32,0},{40,8},{48,16},{56,24},{64,96... | collective-permute-start | bytes 589832 | tf_op jit(solution)/shard_map/ppermute | solution.py:322
  50.2 4.7 %early.1 = (f32[512,1024]{1,0:T(8,128)S(1)}, f32[512,1024]{1,0:T(8,128)S(1)}, f32[512,1024]{1,0:T(8,128)S(1)}, bf16[1024,4096]{1,0:T(8,128)(2,1)S(1)}) custom-call(s32[222]{0:T(256)S(1)} %concatenate.6.table, bf16[512,1024]{1,0:T(8,128)(2,1)S(1)} %get-tuple-element.40.qs, bf16[1024,4096]{1,0:T(8,128)(2,1)} %w.1, ...), custom_call_target="tpu_custom_call" | custom-call | flops 5000000000 | bytes 5242880 | tf_op jit(solution)/shard_map/early/pallas_call | solution.py:323
  55.0 5.9 %late.1 = (bf16[512,1024]{1,0:T(8,128)(2,1)S(1)}, bf16[64,4096]{1,0:T(8,128)(2,1)S(1)}, bf16[64,4096]{1,0:T(8,128)(2,1)S(1)}) custom-call(s32[222]{0:T(256)S(1)} %concatenate.6.table, bf16[512,1024]{1,0:T(8,128)(2,1)S(1)} %get-tuple-element.40.qs, bf16[1024,4096]{1,0:T(8,128)(2,1)S(1)} %get-tuple-element.52.w, ...), custom_call_target="tpu_custom_call" | custom-call | flops 10000000 | bytes 10485 | tf_op jit(solution)/shard_map/late/pallas_call | solution.py:327
  61.0 2.9 %sides.1 = (bf16[64,4096]{1,0:T(8,128)(2,1)S(1)}, bf16[64,4096]{1,0:T(8,128)(2,1)S(1)}, bf16[64,4096]{1,0:T(8,128)(2,1)S(1)}, bf16[64,4096]{1,0:T(8,128)(2,1)S(1)}) custom-call(s32[222]{0:T(256)S(1)} %concatenate.6.table, bf16[512,1024]{1,0:T(8,128)(2,1)S(1)} %get-tuple-element.57.att, bf16[1024,4096]{1,0:T(8,128)(2,1)S(1)} %get-tuple-element.52.w), custom_call_target="tpu_custom_call" | custom-call | flops 10000000 | bytes 10485 | tf_op jit(solution)/shard_map/sides/pallas_call | solution.py:331
  65.0 1.6 %collective-permute-start.16 = (bf16[64,4096]{1,0:T(8,128)(2,1)S(1)}, bf16[64,4096]{1,0:T(8,128)(2,1)S(1)}, u32[]{:S(2)}, u32[]{:S(2)}) collective-permute-start(bf16[64,4096]{1,0:T(8,128)(2,1)S(1)} %add_convert_fusion.1), channel_id=1, source_target_pairs={{0,2},{1,7},{2,4},{3,1},{4,6},{5,3},{6,0},{7,5},{8,10},{9,15},{10,... | collective-permute-start | bytes 1572872 | tf_op jit(solution)/shard_map/ppermute | solution.py:339
  66.9 2.8 %collective-permute-start.14 = (bf16[64,4096]{1,0:T(8,128)(2,1)S(1)}, bf16[64,4096]{1,0:T(8,128)(2,1)S(1)}, u32[]{:S(2)}, u32[]{:S(2)}) collective-permute-start(bf16[64,4096]{1,0:T(8,128)(2,1)S(1)} %add_convert_fusion.2), channel_id=1, source_target_pairs={{0,6},{1,3},{2,0},{3,5},{4,2},{5,7},{6,4},{7,1},{8,14},{9,11},{10,... | collective-permute-start | bytes 1572872 | tf_op jit(solution)/shard_map/ppermute | solution.py:339
  69.8 1.8 %own.1 = (bf16[64,4096]{1,0:T(8,128)(2,1)S(1)}, bf16[64,4096]{1,0:T(8,128)(2,1)S(1)}) custom-call(s32[222]{0:T(256)S(1)} %concatenate.6.table, bf16[512,1024]{1,0:T(8,128)(2,1)S(1)} %get-tuple-element.57.att, bf16[1024,4096]{1,0:T(8,128)(2,1)S(1)} %get-tuple-element.52.w, bf16[64,4096]{1,0:T(8,128)(2,1)S(1)} %collective-permute-done.11.after), custom_call_target="tpu_custom_call" | custom-call | flops 10000000 | bytes 10485 | tf_op jit(solution)/shard_map/own/pallas_call | solution.py:344
  71.7 7.4 %collective-permute-done.16 = bf16[64,4096]{1,0:T(8,128)(2,1)S(1)} collective-permute-done((bf16[64,4096]{1,0:T(8,128)(2,1)S(1)}, bf16[64,4096]{1,0:T(8,128)(2,1)S(1)}, u32[]{:S(2)}, u32[]{:S(2)}) %collective-permute-start.16) | collective-permute-done | bytes 524320 | tf_op jit(solution)/shard_map/ppermute | solution.py:339
  79.3 0.9 %collective-permute-start.17 = (bf16[64,4096]{1,0:T(8,128)(2,1)S(1)}, bf16[64,4096]{1,0:T(8,128)(2,1)S(1)}, u32[]{:S(2)}, u32[]{:S(2)}) collective-permute-start(bf16[64,4096]{1,0:T(8,128)(2,1)S(1)} %add_convert_fusion), channel_id=1, source_target_pairs={{0,2},{1,7},{2,4},{3,1},{4,6},{5,3},{6,0},{7,5},{8,10},{9,15},{10,... | collective-permute-start | bytes 1572872 | tf_op jit(solution)/shard_map/ppermute | solution.py:339
  80.2 9.6 %collective-permute-done.17.last = bf16[64,4096]{1,0:T(8,128)(2,1)S(1)} collective-permute-done((bf16[64,4096]{1,0:T(8,128)(2,1)S(1)}, bf16[64,4096]{1,0:T(8,128)(2,1)S(1)}, u32[]{:S(2)}, u32[]{:S(2)}) %collective-permute-start.17) | collective-permute-done | bytes 524320 | tf_op jit(solution)/shard_map/ppermute | solution.py:339
  89.8 1.1 %final.1 = bf16[64,4096]{1,0:T(8,128)(2,1)} custom-call(bf16[64,4096]{1,0:T(8,128)(2,1)S(1)} %get-tuple-element.59.keep, bf16[64,4096]{1,0:T(8,128)(2,1)S(1)} %collective-permute-done.12.swapped, bf16[64,4096]{1,0:T(8,128)(2,1)S(1)} %collective-permute-done.14.direct, bf16[64,4096]{1,0:T(8,128)(2,1)S(1)} %collective-permute-done.17.last), custom_call_target="tpu_custom_call" | custom-call | tf_op jit(solution)/shard_map/final/pallas_call | solution.py:351
  (47 shorter events, 5.3 us)
Async XLA Ops:
  0.0 16.4 %copy-start = (s32[8,8]{1,0:T(8,128)S(1)}, s32[8,8]{1,0:T(8,128)}, u32[]{:S(2)}) copy-start(s32[8,8]{1,0:T(8,128)} %param.11) | copy-start | bytes 772
  0.0 16.7 %copy-start.1 = (s32[8,3]{0,1:T(4,128)S(1)}, s32[8,3]{0,1:T(4,128)}, u32[]{:S(2)}) copy-start(s32[8,3]{0,1:T(4,128)} %param.12) | copy-start | bytes 292
  0.0 16.9 %copy-start.2 = (f32[8]{0:T(128)S(1)}, f32[8]{0:T(128)}, u32[]{:S(2)}) copy-start(f32[8]{0:T(128)} %param.10) | copy-start | bytes 100
  1.7 22.8 %all-to-all-start = ((bf16[32,32,128]{2,1,0:T(8,128)(2,1)}), bf16[32,32,128]{2,1,0:T(8,128)(2,1)S(1)}, u32[]{:S(2)}, u32[]{:S(2)}) async-start(bf16[32,32,128]{2,1,0:T(8,128)(2,1)} %bitcast.10.spread), calls=%async_computation | async-start | bytes 524288 | tf_op jit(solution)/shard_map/all_to_all | solution.py:291
  13.3 16.0 %collective-permute-start = (bf16[32,32,128]{2,1,0:T(8,128)(2,1)}, bf16[32,32,128]{2,1,0:T(8,128)(2,1)S(1)}, u32[]{:S(2)}, u32[]{:S(2)}) collective-permute-start(bf16[32,32,128]{2,1,0:T(8,128)(2,1)} %bitcast.10.spread), channel_id=1, source_target_pairs={{0,8},{8,16},{16,24},{24,32},{32,40},{40,48},{48,56},{56,64},{64,7... | collective-permute-start | bytes 786440 | tf_op jit(solution)/shard_map/ppermute | solution.py:290
  24.9 6.1 %collective-permute-start.1 = (bf16[24,8,128]{2,1,0:T(8,128)(2,1)S(1)}, bf16[24,8,128]{2,1,0:T(8,128)(2,1)S(1)}, u32[]{:S(2)}, u32[]{:S(2)}) collective-permute-start(bf16[24,8,128]{2,1,0:T(8,128)(2,1)S(1)} %fusion), channel_id=1, source_target_pairs={{0,192},{8,200},{16,208},{24,216},{32,224},{40,232},{48,240},{56,2... | collective-permute-start | bytes 147464 | tf_op jit(solution)/shard_map/ppermute | solution.py:304
  25.5 8.3 %collective-permute-start.2 = (bf16[24,8,128]{2,1,0:T(8,128)(2,1)S(1)}, bf16[24,8,128]{2,1,0:T(8,128)(2,1)S(1)}, u32[]{:S(2)}, u32[]{:S(2)}) collective-permute-start(bf16[24,8,128]{2,1,0:T(8,128)(2,1)S(1)} %fusion), channel_id=1, source_target_pairs={{0,128},{8,136},{16,144},{24,152},{32,160},{40,168},{48,176},{56,1... | collective-permute-start | bytes 147464 | tf_op jit(solution)/shard_map/ppermute | solution.py:304
  29.0 7.0 %collective-permute-start.3 = (bf16[24,8,128]{2,1,0:T(8,128)(2,1)S(1)}, bf16[24,8,128]{2,1,0:T(8,128)(2,1)S(1)}, u32[]{:S(2)}, u32[]{:S(2)}) collective-permute-start(bf16[24,8,128]{2,1,0:T(8,128)(2,1)S(1)} %fusion), channel_id=1, source_target_pairs={{0,64},{8,72},{16,80},{24,88},{32,96},{40,104},{48,112},{56,120},{... | collective-permute-start | bytes 147464 | tf_op jit(solution)/shard_map/ppermute | solution.py:304
  36.1 8.2 %collective-permute-start.7 = (bf16[24,32,128]{2,1,0:T(8,128)(2,1)S(1)}, bf16[24,32,128]{2,1,0:T(8,128)(2,1)S(1)}, u32[]{:S(2)}, u32[]{:S(2)}) collective-permute-start(bf16[24,32,128]{2,1,0:T(8,128)(2,1)S(1)} %pad_maximum_fusion.a0), channel_id=1, source_target_pairs={{0,32},{8,40},{16,48},{24,56},{32,0},{40,8},{48,16},{56,24},{64,96... | collective-permute-start | bytes 589832 | tf_op jit(solution)/shard_map/ppermute | solution.py:310
  36.2 12.2 %collective-permute-start.4 = (bf16[24,32,128]{2,1,0:T(8,128)(2,1)S(1)}, bf16[24,32,128]{2,1,0:T(8,128)(2,1)S(1)}, u32[]{:S(2)}, u32[]{:S(2)}) collective-permute-start(bf16[24,32,128]{2,1,0:T(8,128)(2,1)S(1)} %pad_maximum_fusion.a0), channel_id=1, source_target_pairs={{0,16},{8,24},{16,0},{24,8},{32,48},{40,56},{48,32},{56,40},{64,80... | collective-permute-start | bytes 589832 | tf_op jit(solution)/shard_map/ppermute | solution.py:311
  39.1 11.1 %collective-permute-start.5 = (bf16[24,32,128]{2,1,0:T(8,128)(2,1)S(1)}, bf16[24,32,128]{2,1,0:T(8,128)(2,1)S(1)}, u32[]{:S(2)}, u32[]{:S(2)}) collective-permute-start(bf16[24,32,128]{2,1,0:T(8,128)(2,1)S(1)} %pad_maximum_fusion.a0), channel_id=1, source_target_pairs={{0,8},{8,0},{16,24},{24,16},{32,40},{40,32},{48,56},{56,48},{64,72... | collective-permute-start | bytes 589832 | tf_op jit(solution)/shard_map/ppermute | solution.py:311
  39.8 10.4 %collective-permute-start.6 = (bf16[24,32,128]{2,1,0:T(8,128)(2,1)S(1)}, bf16[24,32,128]{2,1,0:T(8,128)(2,1)S(1)}, u32[]{:S(2)}, u32[]{:S(2)}) collective-permute-start(bf16[24,32,128]{2,1,0:T(8,128)(2,1)S(1)} %pad_maximum_fusion.a0), channel_id=1, source_target_pairs={{0,24},{8,16},{16,8},{24,0},{32,56},{40,48},{48,40},{56,32},{64,88... | collective-permute-start | bytes 589832 | tf_op jit(solution)/shard_map/ppermute | solution.py:311
  44.3 10.7 %collective-permute-start.10 = (bf16[24,32,128]{2,1,0:T(8,128)(2,1)S(1)}, bf16[24,32,128]{2,1,0:T(8,128)(2,1)S(1)}, u32[]{:S(2)}, u32[]{:S(2)}) collective-permute-start(bf16[24,32,128]{2,1,0:T(8,128)(2,1)S(1)} %collective-permute-done.7.b0), channel_id=1, source_target_pairs={{0,24},{8,16},{16,8},{24,0},{32,56},{40,48},{48,40},{56,32},{64,88... | collective-permute-start | bytes 589832 | tf_op jit(solution)/shard_map/ppermute | solution.py:321
  45.9 9.1 %collective-permute-start.9 = (bf16[24,32,128]{2,1,0:T(8,128)(2,1)S(1)}, bf16[24,32,128]{2,1,0:T(8,128)(2,1)S(1)}, u32[]{:S(2)}, u32[]{:S(2)}) collective-permute-start(bf16[24,32,128]{2,1,0:T(8,128)(2,1)S(1)} %collective-permute-done.7.b0), channel_id=1, source_target_pairs={{0,8},{8,0},{16,24},{24,16},{32,40},{40,32},{48,56},{56,48},{64,72... | collective-permute-start | bytes 589832 | tf_op jit(solution)/shard_map/ppermute | solution.py:321
  48.4 6.6 %collective-permute-start.8 = (bf16[24,32,128]{2,1,0:T(8,128)(2,1)S(1)}, bf16[24,32,128]{2,1,0:T(8,128)(2,1)S(1)}, u32[]{:S(2)}, u32[]{:S(2)}) collective-permute-start(bf16[24,32,128]{2,1,0:T(8,128)(2,1)S(1)} %collective-permute-done.4.a2), channel_id=1, source_target_pairs={{0,32},{8,40},{16,48},{24,56},{32,0},{40,8},{48,16},{56,24},{64,96... | collective-permute-start | bytes 589832 | tf_op jit(solution)/shard_map/ppermute | solution.py:322
  60.9 3.9 %collective-permute-start.15 = (bf16[64,4096]{1,0:T(8,128)(2,1)S(1)}, bf16[64,4096]{1,0:T(8,128)(2,1)S(1)}, u32[]{:S(2)}, u32[]{:S(2)}) collective-permute-start(bf16[64,4096]{1,0:T(8,128)(2,1)S(1)} %get-tuple-element.65), channel_id=1, source_target_pairs={{0,1},{1,0},{2,3},{3,2},{4,5},{5,4},{6,7},{7,6},{8,9},{9,8},{10,11... | collective-permute-start | bytes 1572872 | tf_op jit(solution)/shard_map/ppermute | solution.py:336
  63.9 5.8 %collective-permute-start.11 = (bf16[64,4096]{1,0:T(8,128)(2,1)S(1)}, bf16[64,4096]{1,0:T(8,128)(2,1)S(1)}, u32[]{:S(2)}, u32[]{:S(2)}) collective-permute-start(bf16[64,4096]{1,0:T(8,128)(2,1)S(1)} %get-tuple-element.58), channel_id=1, source_target_pairs={{0,1},{1,0},{2,3},{3,2},{4,5},{5,4},{6,7},{7,6},{8,9},{9,8},{10,11... | collective-permute-start | bytes 1572872 | tf_op jit(solution)/shard_map/ppermute | solution.py:336
  64.5 2.3 %collective-permute-start.13 = (bf16[64,4096]{1,0:T(8,128)(2,1)S(1)}, bf16[64,4096]{1,0:T(8,128)(2,1)S(1)}, u32[]{:S(2)}, u32[]{:S(2)}) collective-permute-start(bf16[64,4096]{1,0:T(8,128)(2,1)S(1)} %get-tuple-element.62), channel_id=1, source_target_pairs={{0,1},{1,0},{2,3},{3,2},{4,5},{5,4},{6,7},{7,6},{8,9},{9,8},{10,11... | collective-permute-start | bytes 1572872 | tf_op jit(solution)/shard_map/ppermute | solution.py:336
  65.0 14.1 %collective-permute-start.16 = (bf16[64,4096]{1,0:T(8,128)(2,1)S(1)}, bf16[64,4096]{1,0:T(8,128)(2,1)S(1)}, u32[]{:S(2)}, u32[]{:S(2)}) collective-permute-start(bf16[64,4096]{1,0:T(8,128)(2,1)S(1)} %add_convert_fusion.1), channel_id=1, source_target_pairs={{0,2},{1,7},{2,4},{3,1},{4,6},{5,3},{6,0},{7,5},{8,10},{9,15},{10,... | collective-permute-start | bytes 1572872 | tf_op jit(solution)/shard_map/ppermute | solution.py:339
  66.9 13.3 %collective-permute-start.14 = (bf16[64,4096]{1,0:T(8,128)(2,1)S(1)}, bf16[64,4096]{1,0:T(8,128)(2,1)S(1)}, u32[]{:S(2)}, u32[]{:S(2)}) collective-permute-start(bf16[64,4096]{1,0:T(8,128)(2,1)S(1)} %add_convert_fusion.2), channel_id=1, source_target_pairs={{0,6},{1,3},{2,0},{3,5},{4,2},{5,7},{6,4},{7,1},{8,14},{9,11},{10,... | collective-permute-start | bytes 1572872 | tf_op jit(solution)/shard_map/ppermute | solution.py:339
  71.6 8.6 %collective-permute-start.12 = (bf16[64,4096]{1,0:T(8,128)(2,1)S(1)}, bf16[64,4096]{1,0:T(8,128)(2,1)S(1)}, u32[]{:S(2)}, u32[]{:S(2)}) collective-permute-start(bf16[64,4096]{1,0:T(8,128)(2,1)S(1)} %get-tuple-element.60), channel_id=1, source_target_pairs={{0,1},{1,0},{2,3},{3,2},{4,5},{5,4},{6,7},{7,6},{8,9},{9,8},{10,11... | collective-permute-start | bytes 1572872 | tf_op jit(solution)/shard_map/ppermute | solution.py:336
  79.3 10.5 %collective-permute-start.17 = (bf16[64,4096]{1,0:T(8,128)(2,1)S(1)}, bf16[64,4096]{1,0:T(8,128)(2,1)S(1)}, u32[]{:S(2)}, u32[]{:S(2)}) collective-permute-start(bf16[64,4096]{1,0:T(8,128)(2,1)S(1)} %add_convert_fusion), channel_id=1, source_target_pairs={{0,2},{1,7},{2,4},{3,1},{4,6},{5,3},{6,0},{7,5},{8,10},{9,15},{10,... | collective-permute-start | bytes 1572872 | tf_op jit(solution)/shard_map/ppermute | solution.py:339

commit v17 on v13

--- a/solution.py
+++ b/solution.py
@@ -312,8 +312,8 @@
     def from_z(a, offset):
         return lax.ppermute(a, "ctx", z_pairs(-offset))
 
-    z2, z4, z6 = from_z(mine, 2), from_z(mine, 4), from_z(mine, 6)
-    prev, z2, z4, z6 = lax.optimization_barrier((prev, z2, z4, z6))
+    z4, z2, z6 = from_z(mine, 4), from_z(mine, 2), from_z(mine, 6)
+    prev, z4, z2, z6 = lax.optimization_barrier((prev, z4, z2, z6))
     a0 = jnp.concatenate([mine, z2, z4, z6], axis=1)
     beside = [(Y * z + y, Y * (z ^ 1) + y) for z in range(Z) for y in range(Y)]
     b0 = lax.ppermute(a0, "ctx", beside)

time: 87.8 us -> 87.9 us (level)
  no operation moved by 1% of the time
where the time goes in v17:
time: 87.9 us; the launch traced here: 86.9 us
  starting transfers between devices  41.1 us (47%)
  Pallas kernels  23.3 us (27%)
  waiting for transfers between devices  20.6 us (23%)
    all_to_all x1, starting transfers between devices, per_device(): lax.all_to_all(spread, 'ctx', 0, 0, tiled=True).reshape(BLOCKS * 8, HEAD)  12 us
    ppermute x6, waiting for transfers between devices, to_x(): return lax.ppermute(a, 'head', x_pairs(step))  8.35 us
    ppermute x6, starting transfers between devices, to_x(): return lax.ppermute(a, 'head', x_pairs(step))  8.28 us
    ppermute x4, starting transfers between devices, swap(): return lax.ppermute(a, 'head', CORE_PAIRS)  6.99 us
    pallas_call x1, Pallas kernels, per_device(): call(late_kernel, [SMEM, VMEM, VMEM] + [ANY] * 4 + [VMEM] * 3, [rows, par...  5.94 us
    all_to_all x1, waiting for transfers between devices, per_device(): lax.all_to_all(spread, 'ctx', 0, 0, tiled=True).reshape(BLOCKS * 8, HEAD)  5.8 us
    ppermute x3, waiting for transfers between devices, from_z(): return lax.ppermute(a, 'ctx', z_pairs(-offset))  5.14 us
    ppermute x3, starting transfers between devices, from_z(): return lax.ppermute(a, 'ctx', z_pairs(-offset))  4.91 us
  transfers between devices with their start and end apart: 22, of which 7 were waited for; matrix products, arithmetic and copies ran while one was open for 2% of the time, Pallas kernels for 17%

profile of v17, /device:TPU:1, one launch (start us, length us, event | category | flops | bytes accessed | tf_op | source)
XLA Modules:
  0.0 86.9 jit_solution(1185845710503105880)
XLA Ops:
  0.0 1.7 %spread.1 = bf16[16,2,4,8,128]{4,3,2,1,0:T(8,128)(2,1)} custom-call(bf16[4,16,8,128]{3,2,1,0:T(8,128)(2,1)} %bitcast.18, bf16[4,16,8,128]{3,2,1,0:T(8,128)(2,1)} %bitcast.20), custom_call_target="tpu_custom_call" | custom-call | flops 1000000000 | bytes 1048576 | tf_op jit(solution)/shard_map/spread/pallas_call | solution.py:295
  1.7 12.0 %all-to-all-start = ((bf16[32,32,128]{2,1,0:T(8,128)(2,1)}), bf16[32,32,128]{2,1,0:T(8,128)(2,1)S(1)}, u32[]{:S(2)}, u32[]{:S(2)}) async-start(bf16[32,32,128]{2,1,0:T(8,128)(2,1)} %bitcast.10.spread), calls=%async_computation | async-start | bytes 524288 | tf_op jit(solution)/shard_map/all_to_all | solution.py:300
  13.7 3.1 %collective-permute-start = (bf16[32,32,128]{2,1,0:T(8,128)(2,1)}, bf16[32,32,128]{2,1,0:T(8,128)(2,1)S(1)}, u32[]{:S(2)}, u32[]{:S(2)}) collective-permute-start(bf16[32,32,128]{2,1,0:T(8,128)(2,1)} %bitcast.10.spread), channel_id=1, source_target_pairs={{0,8},{8,16},{16,24},{24,32},{32,40},{40,48},{48,56},{56,64},{64,7... | collective-permute-start | bytes 786440 | tf_op jit(solution)/shard_map/ppermute | solution.py:299
  17.5 1.3 %fetch.1 = (bf16[512,1024]{1,0:T(8,128)(2,1)S(1)}, bf16[2,4,128,128]{3,2,1,0:T(8,128)(2,1)S(1)}) custom-call(bf16[512,1024]{1,0:T(8,128)(2,1)} %q.1, bf16[4,128,128]{2,1,0:T(8,128)(2,1)} %bitcast.19, bf16[4,128,128]{2,1,0:T(8,128)(2,1)} %bitcast.21, bf16[32,32,128]{2,1,0:T(8,128)(2,1)} %bitcast.10.spread), custom_call_target="tpu_custom_call" | custom-call | flops 1000000000 | bytes 1048576 | tf_op jit(solution)/shard_map/fetch/pallas_call | solution.py:302
  19.1 5.8 %all-to-all-done = bf16[32,32,128]{2,1,0:T(8,128)(2,1)S(1)} async-done(((bf16[32,32,128]{2,1,0:T(8,128)(2,1)}), bf16[32,32,128]{2,1,0:T(8,128)(2,1)S(1)}, u32[]{:S(2)}, u32[]{:S(2)}) %all-to-all-start) | async-done | bytes 262176 | tf_op jit(solution)/shard_map/all_to_all | solution.py:300
  25.3 2.1 %collective-permute-start.1 = (bf16[24,8,128]{2,1,0:T(8,128)(2,1)S(1)}, bf16[24,8,128]{2,1,0:T(8,128)(2,1)S(1)}, u32[]{:S(2)}, u32[]{:S(2)}) collective-permute-start(bf16[24,8,128]{2,1,0:T(8,128)(2,1)S(1)} %fusion), channel_id=1, source_target_pairs={{0,128},{8,136},{16,144},{24,152},{32,160},{40,168},{48,176},{56,1... | collective-permute-start | bytes 147464 | tf_op jit(solution)/shard_map/ppermute | solution.py:313
  27.4 2.8 %collective-permute-start.2 = (bf16[24,8,128]{2,1,0:T(8,128)(2,1)S(1)}, bf16[24,8,128]{2,1,0:T(8,128)(2,1)S(1)}, u32[]{:S(2)}, u32[]{:S(2)}) collective-permute-start(bf16[24,8,128]{2,1,0:T(8,128)(2,1)S(1)} %fusion), channel_id=1, source_target_pairs={{0,192},{8,200},{16,208},{24,216},{32,224},{40,232},{48,240},{56,2... | collective-permute-start | bytes 147464 | tf_op jit(solution)/shard_map/ppermute | solution.py:313
  30.2 2.0 %collective-permute-done.1 = bf16[24,8,128]{2,1,0:T(8,128)(2,1)S(1)} collective-permute-done((bf16[24,8,128]{2,1,0:T(8,128)(2,1)S(1)}, bf16[24,8,128]{2,1,0:T(8,128)(2,1)S(1)}, u32[]{:S(2)}, u32[]{:S(2)}) %collective-permute-start.1) | collective-permute-done | bytes 49184 | tf_op jit(solution)/shard_map/ppermute | solution.py:313
  32.2 3.1 %collective-permute-done.3 = bf16[24,8,128]{2,1,0:T(8,128)(2,1)S(1)} collective-permute-done((bf16[24,8,128]{2,1,0:T(8,128)(2,1)S(1)}, bf16[24,8,128]{2,1,0:T(8,128)(2,1)S(1)}, u32[]{:S(2)}, u32[]{:S(2)}) %collective-permute-start.3) | collective-permute-done | bytes 49184 | tf_op jit(solution)/shard_map/ppermute | solution.py:313
  35.6 2.0 %collective-permute-start.4 = (bf16[24,32,128]{2,1,0:T(8,128)(2,1)S(1)}, bf16[24,32,128]{2,1,0:T(8,128)(2,1)S(1)}, u32[]{:S(2)}, u32[]{:S(2)}) collective-permute-start(bf16[24,32,128]{2,1,0:T(8,128)(2,1)S(1)} %pad_maximum_fusion.a0), channel_id=1, source_target_pairs={{0,16},{8,24},{16,0},{24,8},{32,48},{40,56},{48,32},{56,40},{64,80... | collective-permute-start | bytes 589832 | tf_op jit(solution)/shard_map/ppermute | solution.py:320
  38.2 1.4 %collective-permute-start.6 = (bf16[24,32,128]{2,1,0:T(8,128)(2,1)S(1)}, bf16[24,32,128]{2,1,0:T(8,128)(2,1)S(1)}, u32[]{:S(2)}, u32[]{:S(2)}) collective-permute-start(bf16[24,32,128]{2,1,0:T(8,128)(2,1)S(1)} %pad_maximum_fusion.a0), channel_id=1, source_target_pairs={{0,24},{8,16},{16,8},{24,0},{32,56},{40,48},{48,40},{56,32},{64,88... | collective-permute-start | bytes 589832 | tf_op jit(solution)/shard_map/ppermute | solution.py:320
  39.7 3.9 %band.1 = (f32[512,1024]{1,0:T(8,128)S(1)}, f32[512,1024]{1,0:T(8,128)S(1)}, f32[512,1024]{1,0:T(8,128)S(1)}) custom-call(s32[222]{0:T(256)S(1)} %concatenate.6.table, f32[8,128]{1,0:T(8,128)S(1)} %broadcast_in_dim.35.sink, bf16[512,1024]{1,0:T(8,128)(2,1)S(1)} %get-tuple-element.42.qs, bf16[16,2,4,8,128]{4,3,2,1,0:T(8,128)(2,1)S(1)} %bitcast.16, ...), custom_call_target="tpu_custom_call" | custom-call | flops 3000000000 | bytes 3145728 | tf_op jit(solution)/shard_map/band/pallas_call | solution.py:326
  43.6 1.3 %collective-permute-start.10 = (bf16[24,32,128]{2,1,0:T(8,128)(2,1)S(1)}, bf16[24,32,128]{2,1,0:T(8,128)(2,1)S(1)}, u32[]{:S(2)}, u32[]{:S(2)}) collective-permute-start(bf16[24,32,128]{2,1,0:T(8,128)(2,1)S(1)} %collective-permute-done.7.b0), channel_id=1, source_target_pairs={{0,24},{8,16},{16,8},{24,0},{32,56},{40,48},{48,40},{56,32},{64,88... | collective-permute-start | bytes 589832 | tf_op jit(solution)/shard_map/ppermute | solution.py:330
  45.0 4.7 %early.1 = (f32[512,1024]{1,0:T(8,128)S(1)}, f32[512,1024]{1,0:T(8,128)S(1)}, f32[512,1024]{1,0:T(8,128)S(1)}, bf16[1024,4096]{1,0:T(8,128)(2,1)S(1)}) custom-call(s32[222]{0:T(256)S(1)} %concatenate.6.table, bf16[512,1024]{1,0:T(8,128)(2,1)S(1)} %get-tuple-element.42.qs, bf16[1024,4096]{1,0:T(8,128)(2,1)} %w.1, ...), custom_call_target="tpu_custom_call" | custom-call | flops 5000000000 | bytes 5242880 | tf_op jit(solution)/shard_map/early/pallas_call | solution.py:332
  49.7 1.3 %collective-permute-done.10.b3 = bf16[24,32,128]{2,1,0:T(8,128)(2,1)S(1)} collective-permute-done((bf16[24,32,128]{2,1,0:T(8,128)(2,1)S(1)}, bf16[24,32,128]{2,1,0:T(8,128)(2,1)S(1)}, u32[]{:S(2)}, u32[]{:S(2)}) %collective-permute-start.10) | collective-permute-done | bytes 196640 | tf_op jit(solution)/shard_map/ppermute | solution.py:330
  51.0 5.9 %late.1 = (bf16[512,1024]{1,0:T(8,128)(2,1)S(1)}, bf16[64,4096]{1,0:T(8,128)(2,1)S(1)}, bf16[64,4096]{1,0:T(8,128)(2,1)S(1)}) custom-call(s32[222]{0:T(256)S(1)} %concatenate.6.table, bf16[512,1024]{1,0:T(8,128)(2,1)S(1)} %get-tuple-element.42.qs, bf16[1024,4096]{1,0:T(8,128)(2,1)S(1)} %get-tuple-element.54.w, ...), custom_call_target="tpu_custom_call" | custom-call | flops 10000000 | bytes 10485 | tf_op jit(solution)/shard_map/late/pallas_call | solution.py:336
  57.0 5.2 %collective-permute-start.14 = (bf16[64,4096]{1,0:T(8,128)(2,1)S(1)}, bf16[64,4096]{1,0:T(8,128)(2,1)S(1)}, u32[]{:S(2)}, u32[]{:S(2)}) collective-permute-start(bf16[64,4096]{1,0:T(8,128)(2,1)S(1)} %get-tuple-element.67), channel_id=1, source_target_pairs={{0,1},{1,0},{2,3},{3,2},{4,5},{5,4},{6,7},{7,6},{8,9},{9,8},{10,11... | collective-permute-start | bytes 1572872 | tf_op jit(solution)/shard_map/ppermute | solution.py:345
  62.1 2.9 %sides.1 = (bf16[64,4096]{1,0:T(8,128)(2,1)S(1)}, bf16[64,4096]{1,0:T(8,128)(2,1)S(1)}, bf16[128,2048]{1,0:T(8,128)(2,1)S(1)}, bf16[128,2048]{1,0:T(8,128)(2,1)S(1)}) custom-call(s32[222]{0:T(256)S(1)} %concatenate.6.table, bf16[512,1024]{1,0:T(8,128)(2,1)S(1)} %get-tuple-element.59.att, bf16[1024,4096]{1,0:T(8,128)(2,1)S(1)} %get-tuple-element.54.w), custom_call_target="tpu_custom_call" | custom-call | flops 10000000 | bytes 10485 | tf_op jit(solution)/shard_map/sides/pallas_call | solution.py:341
  67.1 1.5 %collective-permute-start.16 = (bf16[64,2048]{1,0:T(8,128)(2,1)S(1)}, bf16[64,2048]{1,0:T(8,128)(2,1)S(1)}, u32[]{:S(2)}, u32[]{:S(2)}) collective-permute-start(bf16[64,2048]{1,0:T(8,128)(2,1)S(1)} %get-tuple-element.73), channel_id=1, source_target_pairs={{0,6},{1,7},{2,0},{3,1},{4,2},{5,3},{6,4},{7,5},{8,14},{9,15},{10,... | collective-permute-start | bytes 786440 | tf_op jit(solution)/shard_map/ppermute | solution.py:348
  68.8 1.8 %own.1 = (bf16[64,4096]{1,0:T(8,128)(2,1)S(1)}, bf16[64,4096]{1,0:T(8,128)(2,1)S(1)}) custom-call(s32[222]{0:T(256)S(1)} %concatenate.6.table, bf16[512,1024]{1,0:T(8,128)(2,1)S(1)} %get-tuple-element.59.att, bf16[1024,4096]{1,0:T(8,128)(2,1)S(1)} %get-tuple-element.54.w, bf16[64,2048]{1,0:T(8,128)(2,1)S(1)} %get-tuple-element.78.after), custom_call_target="tpu_custom_call" | custom-call | flops 10000000 | bytes 10485 | tf_op jit(solution)/shard_map/own/pallas_call | solution.py:358
  71.8 2.7 %collective-permute-start.18 = (bf16[64,2048]{1,0:T(8,128)(2,1)S(1)}, bf16[64,2048]{1,0:T(8,128)(2,1)S(1)}, u32[]{:S(2)}, u32[]{:S(2)}) collective-permute-start(bf16[64,2048]{1,0:T(8,128)(2,1)S(1)} %get-tuple-element.77), channel_id=1, source_target_pairs={{0,6},{1,7},{2,0},{3,1},{4,2},{5,3},{6,4},{7,5},{8,14},{9,15},{10,... | collective-permute-start | bytes 786440 | tf_op jit(solution)/shard_map/ppermute | solution.py:348
  75.8 1.8 %collective-permute-start.20 = (bf16[64,2048]{1,0:T(8,128)(2,1)S(1)}, bf16[64,2048]{1,0:T(8,128)(2,1)S(1)}, u32[]{:S(2)}, u32[]{:S(2)}) collective-permute-start(bf16[64,2048]{1,0:T(8,128)(2,1)S(1)} %get-tuple-element.75), channel_id=1, source_target_pairs={{0,6},{1,7},{2,0},{3,1},{4,2},{5,3},{6,4},{7,5},{8,14},{9,15},{10,... | collective-permute-start | bytes 786440 | tf_op jit(solution)/shard_map/ppermute | solution.py:348
  77.6 2.6 %collective-permute-done.18.left_above = bf16[64,2048]{1,0:T(8,128)(2,1)S(1)} collective-permute-done((bf16[64,2048]{1,0:T(8,128)(2,1)S(1)}, bf16[64,2048]{1,0:T(8,128)(2,1)S(1)}, u32[]{:S(2)}, u32[]{:S(2)}) %collective-permute-start.18) | collective-permute-done | bytes 262176 | tf_op jit(solution)/shard_map/ppermute | solution.py:348
  80.3 5.6 %collective-permute-done.17.left_below = bf16[64,2048]{1,0:T(8,128)(2,1)S(1)} collective-permute-done((bf16[64,2048]{1,0:T(8,128)(2,1)S(1)}, bf16[64,2048]{1,0:T(8,128)(2,1)S(1)}, u32[]{:S(2)}, u32[]{:S(2)}) %collective-permute-start.17) | collective-permute-done | bytes 262176 | tf_op jit(solution)/shard_map/ppermute | solution.py:348
  (53 shorter events, 8.0 us)
Async XLA Ops:
  0.0 17.2 %copy-start.1 = (s32[8,3]{0,1:T(4,128)S(1)}, s32[8,3]{0,1:T(4,128)}, u32[]{:S(2)}) copy-start(s32[8,3]{0,1:T(4,128)} %param.12) | copy-start | bytes 292
  0.0 17.4 %copy-start.2 = (f32[8]{0:T(128)S(1)}, f32[8]{0:T(128)}, u32[]{:S(2)}) copy-start(f32[8]{0:T(128)} %param.10) | copy-start | bytes 100
  1.7 23.2 %all-to-all-start = ((bf16[32,32,128]{2,1,0:T(8,128)(2,1)}), bf16[32,32,128]{2,1,0:T(8,128)(2,1)S(1)}, u32[]{:S(2)}, u32[]{:S(2)}) async-start(bf16[32,32,128]{2,1,0:T(8,128)(2,1)} %bitcast.10.spread), calls=%async_computation | async-start | bytes 524288 | tf_op jit(solution)/shard_map/all_to_all | solution.py:300
  13.7 16.5 %collective-permute-start = (bf16[32,32,128]{2,1,0:T(8,128)(2,1)}, bf16[32,32,128]{2,1,0:T(8,128)(2,1)S(1)}, u32[]{:S(2)}, u32[]{:S(2)}) collective-permute-start(bf16[32,32,128]{2,1,0:T(8,128)(2,1)} %bitcast.10.spread), channel_id=1, source_target_pairs={{0,8},{8,16},{16,24},{24,32},{32,40},{40,48},{48,56},{56,64},{64,7... | collective-permute-start | bytes 786440 | tf_op jit(solution)/shard_map/ppermute | solution.py:299
  25.3 6.9 %collective-permute-start.1 = (bf16[24,8,128]{2,1,0:T(8,128)(2,1)S(1)}, bf16[24,8,128]{2,1,0:T(8,128)(2,1)S(1)}, u32[]{:S(2)}, u32[]{:S(2)}) collective-permute-start(bf16[24,8,128]{2,1,0:T(8,128)(2,1)S(1)} %fusion), channel_id=1, source_target_pairs={{0,128},{8,136},{16,144},{24,152},{32,160},{40,168},{48,176},{56,1... | collective-permute-start | bytes 147464 | tf_op jit(solution)/shard_map/ppermute | solution.py:313
  27.4 4.8 %collective-permute-start.2 = (bf16[24,8,128]{2,1,0:T(8,128)(2,1)S(1)}, bf16[24,8,128]{2,1,0:T(8,128)(2,1)S(1)}, u32[]{:S(2)}, u32[]{:S(2)}) collective-permute-start(bf16[24,8,128]{2,1,0:T(8,128)(2,1)S(1)} %fusion), channel_id=1, source_target_pairs={{0,192},{8,200},{16,208},{24,216},{32,224},{40,232},{48,240},{56,2... | collective-permute-start | bytes 147464 | tf_op jit(solution)/shard_map/ppermute | solution.py:313
  30.2 5.2 %collective-permute-start.3 = (bf16[24,8,128]{2,1,0:T(8,128)(2,1)S(1)}, bf16[24,8,128]{2,1,0:T(8,128)(2,1)S(1)}, u32[]{:S(2)}, u32[]{:S(2)}) collective-permute-start(bf16[24,8,128]{2,1,0:T(8,128)(2,1)S(1)} %fusion), channel_id=1, source_target_pairs={{0,64},{8,72},{16,80},{24,88},{32,96},{40,104},{48,112},{56,120},{... | collective-permute-start | bytes 147464 | tf_op jit(solution)/shard_map/ppermute | solution.py:313
  35.4 8.2 %collective-permute-start.7 = (bf16[24,32,128]{2,1,0:T(8,128)(2,1)S(1)}, bf16[24,32,128]{2,1,0:T(8,128)(2,1)S(1)}, u32[]{:S(2)}, u32[]{:S(2)}) collective-permute-start(bf16[24,32,128]{2,1,0:T(8,128)(2,1)S(1)} %pad_maximum_fusion.a0), channel_id=1, source_target_pairs={{0,32},{8,40},{16,48},{24,56},{32,0},{40,8},{48,16},{56,24},{64,96... | collective-permute-start | bytes 589832 | tf_op jit(solution)/shard_map/ppermute | solution.py:319
  35.6 9.3 %collective-permute-start.4 = (bf16[24,32,128]{2,1,0:T(8,128)(2,1)S(1)}, bf16[24,32,128]{2,1,0:T(8,128)(2,1)S(1)}, u32[]{:S(2)}, u32[]{:S(2)}) collective-permute-start(bf16[24,32,128]{2,1,0:T(8,128)(2,1)S(1)} %pad_maximum_fusion.a0), channel_id=1, source_target_pairs={{0,16},{8,24},{16,0},{24,8},{32,48},{40,56},{48,32},{56,40},{64,80... | collective-permute-start | bytes 589832 | tf_op jit(solution)/shard_map/ppermute | solution.py:320
  37.6 7.4 %collective-permute-start.5 = (bf16[24,32,128]{2,1,0:T(8,128)(2,1)S(1)}, bf16[24,32,128]{2,1,0:T(8,128)(2,1)S(1)}, u32[]{:S(2)}, u32[]{:S(2)}) collective-permute-start(bf16[24,32,128]{2,1,0:T(8,128)(2,1)S(1)} %pad_maximum_fusion.a0), channel_id=1, source_target_pairs={{0,8},{8,0},{16,24},{24,16},{32,40},{40,32},{48,56},{56,48},{64,72... | collective-permute-start | bytes 589832 | tf_op jit(solution)/shard_map/ppermute | solution.py:320
  38.2 6.8 %collective-permute-start.6 = (bf16[24,32,128]{2,1,0:T(8,128)(2,1)S(1)}, bf16[24,32,128]{2,1,0:T(8,128)(2,1)S(1)}, u32[]{:S(2)}, u32[]{:S(2)}) collective-permute-start(bf16[24,32,128]{2,1,0:T(8,128)(2,1)S(1)} %pad_maximum_fusion.a0), channel_id=1, source_target_pairs={{0,24},{8,16},{16,8},{24,0},{32,56},{40,48},{48,40},{56,32},{64,88... | collective-permute-start | bytes 589832 | tf_op jit(solution)/shard_map/ppermute | solution.py:320
  43.6 7.5 %collective-permute-start.10 = (bf16[24,32,128]{2,1,0:T(8,128)(2,1)S(1)}, bf16[24,32,128]{2,1,0:T(8,128)(2,1)S(1)}, u32[]{:S(2)}, u32[]{:S(2)}) collective-permute-start(bf16[24,32,128]{2,1,0:T(8,128)(2,1)S(1)} %collective-permute-done.7.b0), channel_id=1, source_target_pairs={{0,24},{8,16},{16,8},{24,0},{32,56},{40,48},{48,40},{56,32},{64,88... | collective-permute-start | bytes 589832 | tf_op jit(solution)/shard_map/ppermute | solution.py:330
  44.9 6.1 %collective-permute-start.9 = (bf16[24,32,128]{2,1,0:T(8,128)(2,1)S(1)}, bf16[24,32,128]{2,1,0:T(8,128)(2,1)S(1)}, u32[]{:S(2)}, u32[]{:S(2)}) collective-permute-start(bf16[24,32,128]{2,1,0:T(8,128)(2,1)S(1)} %collective-permute-done.7.b0), channel_id=1, source_target_pairs={{0,8},{8,0},{16,24},{24,16},{32,40},{40,32},{48,56},{56,48},{64,72... | collective-permute-start | bytes 589832 | tf_op jit(solution)/shard_map/ppermute | solution.py:330
  44.9 6.1 %collective-permute-start.8 = (bf16[24,32,128]{2,1,0:T(8,128)(2,1)S(1)}, bf16[24,32,128]{2,1,0:T(8,128)(2,1)S(1)}, u32[]{:S(2)}, u32[]{:S(2)}) collective-permute-start(bf16[24,32,128]{2,1,0:T(8,128)(2,1)S(1)} %collective-permute-done.4.a2), channel_id=1, source_target_pairs={{0,32},{8,40},{16,48},{24,56},{32,0},{40,8},{48,16},{56,24},{64,96... | collective-permute-start | bytes 589832 | tf_op jit(solution)/shard_map/ppermute | solution.py:331
  57.0 8.7 %collective-permute-start.14 = (bf16[64,4096]{1,0:T(8,128)(2,1)S(1)}, bf16[64,4096]{1,0:T(8,128)(2,1)S(1)}, u32[]{:S(2)}, u32[]{:S(2)}) collective-permute-start(bf16[64,4096]{1,0:T(8,128)(2,1)S(1)} %get-tuple-element.67), channel_id=1, source_target_pairs={{0,1},{1,0},{2,3},{3,2},{4,5},{5,4},{6,7},{7,6},{8,9},{9,8},{10,11... | collective-permute-start | bytes 1572872 | tf_op jit(solution)/shard_map/ppermute | solution.py:345
  65.0 3.5 %collective-permute-start.11 = (bf16[128,2048]{1,0:T(8,128)(2,1)S(1)}, bf16[128,2048]{1,0:T(8,128)(2,1)S(1)}, u32[]{:S(2)}, u32[]{:S(2)}) collective-permute-start(bf16[128,2048]{1,0:T(8,128)(2,1)S(1)} %get-tuple-element.61), channel_id=1, source_target_pairs={{0,1},{1,0},{2,3},{3,2},{4,5},{5,4},{6,7},{7,6},{8,9},{9,8},{10,11... | collective-permute-start | bytes 1572872 | tf_op jit(solution)/shard_map/ppermute | solution.py:345
  65.1 6.7 %collective-permute-start.13 = (bf16[128,2048]{1,0:T(8,128)(2,1)S(1)}, bf16[128,2048]{1,0:T(8,128)(2,1)S(1)}, u32[]{:S(2)}, u32[]{:S(2)}) collective-permute-start(bf16[128,2048]{1,0:T(8,128)(2,1)S(1)} %get-tuple-element.65), channel_id=1, source_target_pairs={{0,1},{1,0},{2,3},{3,2},{4,5},{5,4},{6,7},{7,6},{8,9},{9,8},{10,11... | collective-permute-start | bytes 1572872 | tf_op jit(solution)/shard_map/ppermute | solution.py:345
  65.8 8.9 %collective-permute-start.15 = (bf16[64,2048]{1,0:T(8,128)(2,1)S(1)}, bf16[64,2048]{1,0:T(8,128)(2,1)S(1)}, u32[]{:S(2)}, u32[]{:S(2)}) collective-permute-start(bf16[64,2048]{1,0:T(8,128)(2,1)S(1)} %get-tuple-element.74), channel_id=1, source_target_pairs={{0,2},{1,3},{2,4},{3,5},{4,6},{5,7},{6,0},{7,1},{8,10},{9,11},{10,... | collective-permute-start | bytes 786440 | tf_op jit(solution)/shard_map/ppermute | solution.py:348
  67.1 7.6 %collective-permute-start.16 = (bf16[64,2048]{1,0:T(8,128)(2,1)S(1)}, bf16[64,2048]{1,0:T(8,128)(2,1)S(1)}, u32[]{:S(2)}, u32[]{:S(2)}) collective-permute-start(bf16[64,2048]{1,0:T(8,128)(2,1)S(1)} %get-tuple-element.73), channel_id=1, source_target_pairs={{0,6},{1,7},{2,0},{3,1},{4,2},{5,3},{6,4},{7,5},{8,14},{9,15},{10,... | collective-permute-start | bytes 786440 | tf_op jit(solution)/shard_map/ppermute | solution.py:348
  68.7 11.6 %collective-permute-start.19 = (bf16[64,2048]{1,0:T(8,128)(2,1)S(1)}, bf16[64,2048]{1,0:T(8,128)(2,1)S(1)}, u32[]{:S(2)}, u32[]{:S(2)}) collective-permute-start(bf16[64,2048]{1,0:T(8,128)(2,1)S(1)} %get-tuple-element.78.after), channel_id=1, source_target_pairs={{0,2},{1,3},{2,4},{3,5},{4,6},{5,7},{6,0},{7,1},{8,10},{9,11},{10,... | collective-permute-start | bytes 786440 | tf_op jit(solution)/shard_map/ppermute | solution.py:348
  70.6 15.3 %collective-permute-start.12 = (bf16[64,4096]{1,0:T(8,128)(2,1)S(1)}, bf16[64,4096]{1,0:T(8,128)(2,1)S(1)}, u32[]{:S(2)}, u32[]{:S(2)}) collective-permute-start(bf16[64,4096]{1,0:T(8,128)(2,1)S(1)} %get-tuple-element.63), channel_id=1, source_target_pairs={{0,1},{1,0},{2,3},{3,2},{4,5},{5,4},{6,7},{7,6},{8,9},{9,8},{10,11... | collective-permute-start | bytes 1572872 | tf_op jit(solution)/shard_map/ppermute | solution.py:345
  71.8 8.4 %collective-permute-start.18 = (bf16[64,2048]{1,0:T(8,128)(2,1)S(1)}, bf16[64,2048]{1,0:T(8,128)(2,1)S(1)}, u32[]{:S(2)}, u32[]{:S(2)}) collective-permute-start(bf16[64,2048]{1,0:T(8,128)(2,1)S(1)} %get-tuple-element.77), channel_id=1, source_target_pairs={{0,6},{1,7},{2,0},{3,1},{4,2},{5,3},{6,4},{7,5},{8,14},{9,15},{10,... | collective-permute-start | bytes 786440 | tf_op jit(solution)/shard_map/ppermute | solution.py:348
  74.9 11.0 %collective-permute-start.17 = (bf16[64,2048]{1,0:T(8,128)(2,1)S(1)}, bf16[64,2048]{1,0:T(8,128)(2,1)S(1)}, u32[]{:S(2)}, u32[]{:S(2)}) collective-permute-start(bf16[64,2048]{1,0:T(8,128)(2,1)S(1)} %get-tuple-element.76), channel_id=1, source_target_pairs={{0,2},{1,3},{2,4},{3,5},{4,6},{5,7},{6,0},{7,1},{8,10},{9,11},{10,... | collective-permute-start | bytes 786440 | tf_op jit(solution)/shard_map/ppermute | solution.py:348
  75.8 10.0 %collective-permute-start.20 = (bf16[64,2048]{1,0:T(8,128)(2,1)S(1)}, bf16[64,2048]{1,0:T(8,128)(2,1)S(1)}, u32[]{:S(2)}, u32[]{:S(2)}) collective-permute-start(bf16[64,2048]{1,0:T(8,128)(2,1)S(1)} %get-tuple-element.75), channel_id=1, source_target_pairs={{0,6},{1,7},{2,0},{3,1},{4,2},{5,3},{6,4},{7,5},{8,14},{9,15},{10,... | collective-permute-start | bytes 786440 | tf_op jit(solution)/shard_map/ppermute | solution.py:348
  (1 other events, 16.9 us)

commit v18 on v13

--- a/solution.py
+++ b/solution.py
@@ -233,14 +233,17 @@
     project(att, w, [table[META + 5]], table[META + 1], [keep], functools.partial(store, give))
 
 
-def final_kernel(keep, swapped, left_below, left_above, right_below, right_above, out):
+def final_kernel(keep, swapped, left_below, left_above, right_below, right_above, out, held, sems):
+    copies = Copies(sems)
     mid = out.shape[1] // 2
     for start, pair in ((0, (left_below, left_above)), (mid, (right_below, right_above))):
         cols = slice(start, start + mid)
         total = keep[:, cols].astype(F32) + swapped[:, cols].astype(F32)
         for part in pair:
             total = total + part[...].astype(F32)
-        out[:, cols] = total.astype(BF16)
+        held[:, cols] = total.astype(BF16)
+        copies.start(held.at[:, pl.ds(start, mid)], out.at[:, pl.ds(start, mid)])
+    copies.wait()
 
 
 SMEM = pl.BlockSpec(memory_space=pltpu.SMEM)
@@ -368,7 +371,8 @@
         final_kernel,
         out_shape=jax.ShapeDtypeStruct((HALF, width), BF16),
         in_specs=[VMEM] * 6,
-        out_specs=VMEM,
+        out_specs=ANY,
+        scratch_shapes=[pltpu.VMEM((HALF, width), BF16), pltpu.SemaphoreType.DMA((2,))],
         compiler_params=pltpu.CompilerParams(vmem_limit_bytes=8 * 2 ** 20),
         name="final",
     )(keep_own, own, left_below, left_above, right_below, right_above)

time: 87.8 us -> 87.9 us (level)
  no operation moved by 1% of the time
where the time goes in v18:
time: 87.9 us; the launch traced here: 87.3 us
  starting transfers between devices  41.1 us (47%)
  Pallas kernels  23.2 us (26%)
  waiting for transfers between devices  20.9 us (24%)
    all_to_all x1, starting transfers between devices, per_device(): lax.all_to_all(spread, 'ctx', 0, 0, tiled=True).reshape(BLOCKS * 8, HEAD)  12 us
    ppermute x6, waiting for transfers between devices, to_x(): return lax.ppermute(a, 'head', x_pairs(step))  8.35 us
    ppermute x6, starting transfers between devices, to_x(): return lax.ppermute(a, 'head', x_pairs(step))  8.27 us
    ppermute x4, starting transfers between devices, swap(): return lax.ppermute(a, 'head', CORE_PAIRS)  7.05 us
    pallas_call x1, Pallas kernels, per_device(): call(late_kernel, [SMEM, VMEM, VMEM] + [ANY] * 4 + [VMEM] * 3, [rows, par...  5.94 us
    all_to_all x1, waiting for transfers between devices, per_device(): lax.all_to_all(spread, 'ctx', 0, 0, tiled=True).reshape(BLOCKS * 8, HEAD)  5.8 us
    ppermute x3, waiting for transfers between devices, from_z(): return lax.ppermute(a, 'ctx', z_pairs(-offset))  5.47 us
    ppermute x3, starting transfers between devices, from_z(): return lax.ppermute(a, 'ctx', z_pairs(-offset))  4.9 us
  transfers between devices with their start and end apart: 22, of which 7 were waited for; matrix products, arithmetic and copies ran while one was open for 2% of the time, Pallas kernels for 17%

profile of v18, /device:TPU:1, one launch (start us, length us, event | category | flops | bytes accessed | tf_op | source)
XLA Modules:
  0.0 87.3 jit_solution(17680728615167627336)
XLA Ops:
  0.0 1.7 %spread.1 = bf16[16,2,4,8,128]{4,3,2,1,0:T(8,128)(2,1)} custom-call(bf16[4,16,8,128]{3,2,1,0:T(8,128)(2,1)} %bitcast.18, bf16[4,16,8,128]{3,2,1,0:T(8,128)(2,1)} %bitcast.20), custom_call_target="tpu_custom_call" | custom-call | flops 1000000000 | bytes 1048576 | tf_op jit(solution)/shard_map/spread/pallas_call | solution.py:298
  1.7 12.0 %all-to-all-start = ((bf16[32,32,128]{2,1,0:T(8,128)(2,1)}), bf16[32,32,128]{2,1,0:T(8,128)(2,1)S(1)}, u32[]{:S(2)}, u32[]{:S(2)}) async-start(bf16[32,32,128]{2,1,0:T(8,128)(2,1)} %bitcast.10.spread), calls=%async_computation | async-start | bytes 524288 | tf_op jit(solution)/shard_map/all_to_all | solution.py:303
  13.7 3.1 %collective-permute-start = (bf16[32,32,128]{2,1,0:T(8,128)(2,1)}, bf16[32,32,128]{2,1,0:T(8,128)(2,1)S(1)}, u32[]{:S(2)}, u32[]{:S(2)}) collective-permute-start(bf16[32,32,128]{2,1,0:T(8,128)(2,1)} %bitcast.10.spread), channel_id=1, source_target_pairs={{0,8},{8,16},{16,24},{24,32},{32,40},{40,48},{48,56},{56,64},{64,7... | collective-permute-start | bytes 786440 | tf_op jit(solution)/shard_map/ppermute | solution.py:302
  17.5 1.3 %fetch.1 = (bf16[512,1024]{1,0:T(8,128)(2,1)S(1)}, bf16[2,4,128,128]{3,2,1,0:T(8,128)(2,1)S(1)}) custom-call(bf16[512,1024]{1,0:T(8,128)(2,1)} %q.1, bf16[4,128,128]{2,1,0:T(8,128)(2,1)} %bitcast.19, bf16[4,128,128]{2,1,0:T(8,128)(2,1)} %bitcast.21, bf16[32,32,128]{2,1,0:T(8,128)(2,1)} %bitcast.10.spread), custom_call_target="tpu_custom_call" | custom-call | flops 1000000000 | bytes 1048576 | tf_op jit(solution)/shard_map/fetch/pallas_call | solution.py:305
  19.1 5.8 %all-to-all-done = bf16[32,32,128]{2,1,0:T(8,128)(2,1)S(1)} async-done(((bf16[32,32,128]{2,1,0:T(8,128)(2,1)}), bf16[32,32,128]{2,1,0:T(8,128)(2,1)S(1)}, u32[]{:S(2)}, u32[]{:S(2)}) %all-to-all-start) | async-done | bytes 262176 | tf_op jit(solution)/shard_map/all_to_all | solution.py:303
  25.3 1.6 %collective-permute-start.1 = (bf16[24,8,128]{2,1,0:T(8,128)(2,1)S(1)}, bf16[24,8,128]{2,1,0:T(8,128)(2,1)S(1)}, u32[]{:S(2)}, u32[]{:S(2)}) collective-permute-start(bf16[24,8,128]{2,1,0:T(8,128)(2,1)S(1)} %fusion), channel_id=1, source_target_pairs={{0,192},{8,200},{16,208},{24,216},{32,224},{40,232},{48,240},{56,2... | collective-permute-start | bytes 147464 | tf_op jit(solution)/shard_map/ppermute | solution.py:316
  26.9 3.3 %collective-permute-start.2 = (bf16[24,8,128]{2,1,0:T(8,128)(2,1)S(1)}, bf16[24,8,128]{2,1,0:T(8,128)(2,1)S(1)}, u32[]{:S(2)}, u32[]{:S(2)}) collective-permute-start(bf16[24,8,128]{2,1,0:T(8,128)(2,1)S(1)} %fusion), channel_id=1, source_target_pairs={{0,128},{8,136},{16,144},{24,152},{32,160},{40,168},{48,176},{56,1... | collective-permute-start | bytes 147464 | tf_op jit(solution)/shard_map/ppermute | solution.py:316
  30.2 3.6 %collective-permute-done.2 = bf16[24,8,128]{2,1,0:T(8,128)(2,1)S(1)} collective-permute-done((bf16[24,8,128]{2,1,0:T(8,128)(2,1)S(1)}, bf16[24,8,128]{2,1,0:T(8,128)(2,1)S(1)}, u32[]{:S(2)}, u32[]{:S(2)}) %collective-permute-start.2) | collective-permute-done | bytes 49184 | tf_op jit(solution)/shard_map/ppermute | solution.py:316
  33.8 1.9 %collective-permute-done.3 = bf16[24,8,128]{2,1,0:T(8,128)(2,1)S(1)} collective-permute-done((bf16[24,8,128]{2,1,0:T(8,128)(2,1)S(1)}, bf16[24,8,128]{2,1,0:T(8,128)(2,1)S(1)}, u32[]{:S(2)}, u32[]{:S(2)}) %collective-permute-start.3) | collective-permute-done | bytes 49184 | tf_op jit(solution)/shard_map/ppermute | solution.py:316
  35.8 2.4 %collective-permute-start.4 = (bf16[24,32,128]{2,1,0:T(8,128)(2,1)S(1)}, bf16[24,32,128]{2,1,0:T(8,128)(2,1)S(1)}, u32[]{:S(2)}, u32[]{:S(2)}) collective-permute-start(bf16[24,32,128]{2,1,0:T(8,128)(2,1)S(1)} %pad_maximum_fusion.a0), channel_id=1, source_target_pairs={{0,16},{8,24},{16,0},{24,8},{32,48},{40,56},{48,32},{56,40},{64,80... | collective-permute-start | bytes 589832 | tf_op jit(solution)/shard_map/ppermute | solution.py:323
  39.1 3.9 %band.1 = (f32[512,1024]{1,0:T(8,128)S(1)}, f32[512,1024]{1,0:T(8,128)S(1)}, f32[512,1024]{1,0:T(8,128)S(1)}) custom-call(s32[222]{0:T(256)S(1)} %concatenate.6.table, f32[8,128]{1,0:T(8,128)S(1)} %broadcast_in_dim.35.sink, bf16[512,1024]{1,0:T(8,128)(2,1)S(1)} %get-tuple-element.42.qs, bf16[16,2,4,8,128]{4,3,2,1,0:T(8,128)(2,1)S(1)} %bitcast.16, ...), custom_call_target="tpu_custom_call" | custom-call | flops 3000000000 | bytes 3145728 | tf_op jit(solution)/shard_map/band/pallas_call | solution.py:329
  43.1 2.1 %collective-permute-start.10 = (bf16[24,32,128]{2,1,0:T(8,128)(2,1)S(1)}, bf16[24,32,128]{2,1,0:T(8,128)(2,1)S(1)}, u32[]{:S(2)}, u32[]{:S(2)}) collective-permute-start(bf16[24,32,128]{2,1,0:T(8,128)(2,1)S(1)} %collective-permute-done.7.b0), channel_id=1, source_target_pairs={{0,24},{8,16},{16,8},{24,0},{32,56},{40,48},{48,40},{56,32},{64,88... | collective-permute-start | bytes 589832 | tf_op jit(solution)/shard_map/ppermute | solution.py:333
  45.3 4.7 %early.1 = (f32[512,1024]{1,0:T(8,128)S(1)}, f32[512,1024]{1,0:T(8,128)S(1)}, f32[512,1024]{1,0:T(8,128)S(1)}, bf16[1024,4096]{1,0:T(8,128)(2,1)S(1)}) custom-call(s32[222]{0:T(256)S(1)} %concatenate.6.table, bf16[512,1024]{1,0:T(8,128)(2,1)S(1)} %get-tuple-element.42.qs, bf16[1024,4096]{1,0:T(8,128)(2,1)} %w.1, ...), custom_call_target="tpu_custom_call" | custom-call | flops 5000000000 | bytes 5242880 | tf_op jit(solution)/shard_map/early/pallas_call | solution.py:335
  51.2 5.9 %late.1 = (bf16[512,1024]{1,0:T(8,128)(2,1)S(1)}, bf16[64,4096]{1,0:T(8,128)(2,1)S(1)}, bf16[64,4096]{1,0:T(8,128)(2,1)S(1)}) custom-call(s32[222]{0:T(256)S(1)} %concatenate.6.table, bf16[512,1024]{1,0:T(8,128)(2,1)S(1)} %get-tuple-element.42.qs, bf16[1024,4096]{1,0:T(8,128)(2,1)S(1)} %get-tuple-element.54.w, ...), custom_call_target="tpu_custom_call" | custom-call | flops 10000000 | bytes 10485 | tf_op jit(solution)/shard_map/late/pallas_call | solution.py:339
  57.2 5.2 %collective-permute-start.14 = (bf16[64,4096]{1,0:T(8,128)(2,1)S(1)}, bf16[64,4096]{1,0:T(8,128)(2,1)S(1)}, u32[]{:S(2)}, u32[]{:S(2)}) collective-permute-start(bf16[64,4096]{1,0:T(8,128)(2,1)S(1)} %get-tuple-element.67), channel_id=1, source_target_pairs={{0,1},{1,0},{2,3},{3,2},{4,5},{5,4},{6,7},{7,6},{8,9},{9,8},{10,11... | collective-permute-start | bytes 1572872 | tf_op jit(solution)/shard_map/ppermute | solution.py:348
  62.4 2.9 %sides.1 = (bf16[64,4096]{1,0:T(8,128)(2,1)S(1)}, bf16[64,4096]{1,0:T(8,128)(2,1)S(1)}, bf16[128,2048]{1,0:T(8,128)(2,1)S(1)}, bf16[128,2048]{1,0:T(8,128)(2,1)S(1)}) custom-call(s32[222]{0:T(256)S(1)} %concatenate.6.table, bf16[512,1024]{1,0:T(8,128)(2,1)S(1)} %get-tuple-element.59.att, bf16[1024,4096]{1,0:T(8,128)(2,1)S(1)} %get-tuple-element.54.w), custom_call_target="tpu_custom_call" | custom-call | flops 10000000 | bytes 10485 | tf_op jit(solution)/shard_map/sides/pallas_call | solution.py:344
  66.0 1.3 %collective-permute-start.15 = (bf16[64,2048]{1,0:T(8,128)(2,1)S(1)}, bf16[64,2048]{1,0:T(8,128)(2,1)S(1)}, u32[]{:S(2)}, u32[]{:S(2)}) collective-permute-start(bf16[64,2048]{1,0:T(8,128)(2,1)S(1)} %get-tuple-element.74), channel_id=1, source_target_pairs={{0,2},{1,3},{2,4},{3,5},{4,6},{5,7},{6,0},{7,1},{8,10},{9,11},{10,... | collective-permute-start | bytes 786440 | tf_op jit(solution)/shard_map/ppermute | solution.py:351
  67.3 1.5 %collective-permute-start.16 = (bf16[64,2048]{1,0:T(8,128)(2,1)S(1)}, bf16[64,2048]{1,0:T(8,128)(2,1)S(1)}, u32[]{:S(2)}, u32[]{:S(2)}) collective-permute-start(bf16[64,2048]{1,0:T(8,128)(2,1)S(1)} %get-tuple-element.73), channel_id=1, source_target_pairs={{0,6},{1,7},{2,0},{3,1},{4,2},{5,3},{6,4},{7,5},{8,14},{9,15},{10,... | collective-permute-start | bytes 786440 | tf_op jit(solution)/shard_map/ppermute | solution.py:351
  69.0 1.8 %own.1 = (bf16[64,4096]{1,0:T(8,128)(2,1)S(1)}, bf16[64,4096]{1,0:T(8,128)(2,1)S(1)}) custom-call(s32[222]{0:T(256)S(1)} %concatenate.6.table, bf16[512,1024]{1,0:T(8,128)(2,1)S(1)} %get-tuple-element.59.att, bf16[1024,4096]{1,0:T(8,128)(2,1)S(1)} %get-tuple-element.54.w, bf16[64,2048]{1,0:T(8,128)(2,1)S(1)} %get-tuple-element.78.after), custom_call_target="tpu_custom_call" | custom-call | flops 10000000 | bytes 10485 | tf_op jit(solution)/shard_map/own/pallas_call | solution.py:361
  70.9 1.2 %collective-permute-start.12 = (bf16[64,4096]{1,0:T(8,128)(2,1)S(1)}, bf16[64,4096]{1,0:T(8,128)(2,1)S(1)}, u32[]{:S(2)}, u32[]{:S(2)}) collective-permute-start(bf16[64,4096]{1,0:T(8,128)(2,1)S(1)} %get-tuple-element.63), channel_id=1, source_target_pairs={{0,1},{1,0},{2,3},{3,2},{4,5},{5,4},{6,7},{7,6},{8,9},{9,8},{10,11... | collective-permute-start | bytes 1572872 | tf_op jit(solution)/shard_map/ppermute | solution.py:348
  72.1 2.7 %collective-permute-start.18 = (bf16[64,2048]{1,0:T(8,128)(2,1)S(1)}, bf16[64,2048]{1,0:T(8,128)(2,1)S(1)}, u32[]{:S(2)}, u32[]{:S(2)}) collective-permute-start(bf16[64,2048]{1,0:T(8,128)(2,1)S(1)} %get-tuple-element.77), channel_id=1, source_target_pairs={{0,6},{1,7},{2,0},{3,1},{4,2},{5,3},{6,4},{7,5},{8,14},{9,15},{10,... | collective-permute-start | bytes 786440 | tf_op jit(solution)/shard_map/ppermute | solution.py:351
  76.1 1.8 %collective-permute-start.20 = (bf16[64,2048]{1,0:T(8,128)(2,1)S(1)}, bf16[64,2048]{1,0:T(8,128)(2,1)S(1)}, u32[]{:S(2)}, u32[]{:S(2)}) collective-permute-start(bf16[64,2048]{1,0:T(8,128)(2,1)S(1)} %get-tuple-element.75), channel_id=1, source_target_pairs={{0,6},{1,7},{2,0},{3,1},{4,2},{5,3},{6,4},{7,5},{8,14},{9,15},{10,... | collective-permute-start | bytes 786440 | tf_op jit(solution)/shard_map/ppermute | solution.py:351
  77.9 2.6 %collective-permute-done.18.left_above = bf16[64,2048]{1,0:T(8,128)(2,1)S(1)} collective-permute-done((bf16[64,2048]{1,0:T(8,128)(2,1)S(1)}, bf16[64,2048]{1,0:T(8,128)(2,1)S(1)}, u32[]{:S(2)}, u32[]{:S(2)}) %collective-permute-start.18) | collective-permute-done | bytes 262176 | tf_op jit(solution)/shard_map/ppermute | solution.py:351
  80.5 5.6 %collective-permute-done.17.left_below = bf16[64,2048]{1,0:T(8,128)(2,1)S(1)} collective-permute-done((bf16[64,2048]{1,0:T(8,128)(2,1)S(1)}, bf16[64,2048]{1,0:T(8,128)(2,1)S(1)}, u32[]{:S(2)}, u32[]{:S(2)}) %collective-permute-start.17) | collective-permute-done | bytes 262176 | tf_op jit(solution)/shard_map/ppermute | solution.py:351
  (53 shorter events, 6.9 us)
Async XLA Ops:
  0.0 17.2 %copy-start.1 = (s32[8,3]{0,1:T(4,128)S(1)}, s32[8,3]{0,1:T(4,128)}, u32[]{:S(2)}) copy-start(s32[8,3]{0,1:T(4,128)} %param.12) | copy-start | bytes 292
  0.0 17.4 %copy-start.2 = (f32[8]{0:T(128)S(1)}, f32[8]{0:T(128)}, u32[]{:S(2)}) copy-start(f32[8]{0:T(128)} %param.10) | copy-start | bytes 100
  1.7 23.2 %all-to-all-start = ((bf16[32,32,128]{2,1,0:T(8,128)(2,1)}), bf16[32,32,128]{2,1,0:T(8,128)(2,1)S(1)}, u32[]{:S(2)}, u32[]{:S(2)}) async-start(bf16[32,32,128]{2,1,0:T(8,128)(2,1)} %bitcast.10.spread), calls=%async_computation | async-start | bytes 524288 | tf_op jit(solution)/shard_map/all_to_all | solution.py:303
  13.7 16.4 %collective-permute-start = (bf16[32,32,128]{2,1,0:T(8,128)(2,1)}, bf16[32,32,128]{2,1,0:T(8,128)(2,1)S(1)}, u32[]{:S(2)}, u32[]{:S(2)}) collective-permute-start(bf16[32,32,128]{2,1,0:T(8,128)(2,1)} %bitcast.10.spread), channel_id=1, source_target_pairs={{0,8},{8,16},{16,24},{24,32},{32,40},{40,48},{48,56},{56,64},{64,7... | collective-permute-start | bytes 786440 | tf_op jit(solution)/shard_map/ppermute | solution.py:302
  25.3 4.9 %collective-permute-start.1 = (bf16[24,8,128]{2,1,0:T(8,128)(2,1)S(1)}, bf16[24,8,128]{2,1,0:T(8,128)(2,1)S(1)}, u32[]{:S(2)}, u32[]{:S(2)}) collective-permute-start(bf16[24,8,128]{2,1,0:T(8,128)(2,1)S(1)} %fusion), channel_id=1, source_target_pairs={{0,192},{8,200},{16,208},{24,216},{32,224},{40,232},{48,240},{56,2... | collective-permute-start | bytes 147464 | tf_op jit(solution)/shard_map/ppermute | solution.py:316
  26.9 6.9 %collective-permute-start.2 = (bf16[24,8,128]{2,1,0:T(8,128)(2,1)S(1)}, bf16[24,8,128]{2,1,0:T(8,128)(2,1)S(1)}, u32[]{:S(2)}, u32[]{:S(2)}) collective-permute-start(bf16[24,8,128]{2,1,0:T(8,128)(2,1)S(1)} %fusion), channel_id=1, source_target_pairs={{0,128},{8,136},{16,144},{24,152},{32,160},{40,168},{48,176},{56,1... | collective-permute-start | bytes 147464 | tf_op jit(solution)/shard_map/ppermute | solution.py:316
  30.2 5.5 %collective-permute-start.3 = (bf16[24,8,128]{2,1,0:T(8,128)(2,1)S(1)}, bf16[24,8,128]{2,1,0:T(8,128)(2,1)S(1)}, u32[]{:S(2)}, u32[]{:S(2)}) collective-permute-start(bf16[24,8,128]{2,1,0:T(8,128)(2,1)S(1)} %fusion), channel_id=1, source_target_pairs={{0,64},{8,72},{16,80},{24,88},{32,96},{40,104},{48,112},{56,120},{... | collective-permute-start | bytes 147464 | tf_op jit(solution)/shard_map/ppermute | solution.py:316
  35.7 7.3 %collective-permute-start.7 = (bf16[24,32,128]{2,1,0:T(8,128)(2,1)S(1)}, bf16[24,32,128]{2,1,0:T(8,128)(2,1)S(1)}, u32[]{:S(2)}, u32[]{:S(2)}) collective-permute-start(bf16[24,32,128]{2,1,0:T(8,128)(2,1)S(1)} %pad_maximum_fusion.a0), channel_id=1, source_target_pairs={{0,32},{8,40},{16,48},{24,56},{32,0},{40,8},{48,16},{56,24},{64,96... | collective-permute-start | bytes 589832 | tf_op jit(solution)/shard_map/ppermute | solution.py:322
  35.8 9.4 %collective-permute-start.4 = (bf16[24,32,128]{2,1,0:T(8,128)(2,1)S(1)}, bf16[24,32,128]{2,1,0:T(8,128)(2,1)S(1)}, u32[]{:S(2)}, u32[]{:S(2)}) collective-permute-start(bf16[24,32,128]{2,1,0:T(8,128)(2,1)S(1)} %pad_maximum_fusion.a0), channel_id=1, source_target_pairs={{0,16},{8,24},{16,0},{24,8},{32,48},{40,56},{48,32},{56,40},{64,80... | collective-permute-start | bytes 589832 | tf_op jit(solution)/shard_map/ppermute | solution.py:323
  38.2 7.1 %collective-permute-start.5 = (bf16[24,32,128]{2,1,0:T(8,128)(2,1)S(1)}, bf16[24,32,128]{2,1,0:T(8,128)(2,1)S(1)}, u32[]{:S(2)}, u32[]{:S(2)}) collective-permute-start(bf16[24,32,128]{2,1,0:T(8,128)(2,1)S(1)} %pad_maximum_fusion.a0), channel_id=1, source_target_pairs={{0,8},{8,0},{16,24},{24,16},{32,40},{40,32},{48,56},{56,48},{64,72... | collective-permute-start | bytes 589832 | tf_op jit(solution)/shard_map/ppermute | solution.py:323
  38.5 6.8 %collective-permute-start.6 = (bf16[24,32,128]{2,1,0:T(8,128)(2,1)S(1)}, bf16[24,32,128]{2,1,0:T(8,128)(2,1)S(1)}, u32[]{:S(2)}, u32[]{:S(2)}) collective-permute-start(bf16[24,32,128]{2,1,0:T(8,128)(2,1)S(1)} %pad_maximum_fusion.a0), channel_id=1, source_target_pairs={{0,24},{8,16},{16,8},{24,0},{32,56},{40,48},{48,40},{56,32},{64,88... | collective-permute-start | bytes 589832 | tf_op jit(solution)/shard_map/ppermute | solution.py:323
  43.1 8.2 %collective-permute-start.10 = (bf16[24,32,128]{2,1,0:T(8,128)(2,1)S(1)}, bf16[24,32,128]{2,1,0:T(8,128)(2,1)S(1)}, u32[]{:S(2)}, u32[]{:S(2)}) collective-permute-start(bf16[24,32,128]{2,1,0:T(8,128)(2,1)S(1)} %collective-permute-done.7.b0), channel_id=1, source_target_pairs={{0,24},{8,16},{16,8},{24,0},{32,56},{40,48},{48,40},{56,32},{64,88... | collective-permute-start | bytes 589832 | tf_op jit(solution)/shard_map/ppermute | solution.py:333
  45.2 6.1 %collective-permute-start.9 = (bf16[24,32,128]{2,1,0:T(8,128)(2,1)S(1)}, bf16[24,32,128]{2,1,0:T(8,128)(2,1)S(1)}, u32[]{:S(2)}, u32[]{:S(2)}) collective-permute-start(bf16[24,32,128]{2,1,0:T(8,128)(2,1)S(1)} %collective-permute-done.7.b0), channel_id=1, source_target_pairs={{0,8},{8,0},{16,24},{24,16},{32,40},{40,32},{48,56},{56,48},{64,72... | collective-permute-start | bytes 589832 | tf_op jit(solution)/shard_map/ppermute | solution.py:333
  45.2 6.1 %collective-permute-start.8 = (bf16[24,32,128]{2,1,0:T(8,128)(2,1)S(1)}, bf16[24,32,128]{2,1,0:T(8,128)(2,1)S(1)}, u32[]{:S(2)}, u32[]{:S(2)}) collective-permute-start(bf16[24,32,128]{2,1,0:T(8,128)(2,1)S(1)} %collective-permute-done.4.a2), channel_id=1, source_target_pairs={{0,32},{8,40},{16,48},{24,56},{32,0},{40,8},{48,16},{56,24},{64,96... | collective-permute-start | bytes 589832 | tf_op jit(solution)/shard_map/ppermute | solution.py:334
  57.2 8.7 %collective-permute-start.14 = (bf16[64,4096]{1,0:T(8,128)(2,1)S(1)}, bf16[64,4096]{1,0:T(8,128)(2,1)S(1)}, u32[]{:S(2)}, u32[]{:S(2)}) collective-permute-start(bf16[64,4096]{1,0:T(8,128)(2,1)S(1)} %get-tuple-element.67), channel_id=1, source_target_pairs={{0,1},{1,0},{2,3},{3,2},{4,5},{5,4},{6,7},{7,6},{8,9},{9,8},{10,11... | collective-permute-start | bytes 1572872 | tf_op jit(solution)/shard_map/ppermute | solution.py:348
  65.3 3.5 %collective-permute-start.11 = (bf16[128,2048]{1,0:T(8,128)(2,1)S(1)}, bf16[128,2048]{1,0:T(8,128)(2,1)S(1)}, u32[]{:S(2)}, u32[]{:S(2)}) collective-permute-start(bf16[128,2048]{1,0:T(8,128)(2,1)S(1)} %get-tuple-element.61), channel_id=1, source_target_pairs={{0,1},{1,0},{2,3},{3,2},{4,5},{5,4},{6,7},{7,6},{8,9},{9,8},{10,11... | collective-permute-start | bytes 1572872 | tf_op jit(solution)/shard_map/ppermute | solution.py:348
  65.4 6.7 %collective-permute-start.13 = (bf16[128,2048]{1,0:T(8,128)(2,1)S(1)}, bf16[128,2048]{1,0:T(8,128)(2,1)S(1)}, u32[]{:S(2)}, u32[]{:S(2)}) collective-permute-start(bf16[128,2048]{1,0:T(8,128)(2,1)S(1)} %get-tuple-element.65), channel_id=1, source_target_pairs={{0,1},{1,0},{2,3},{3,2},{4,5},{5,4},{6,7},{7,6},{8,9},{9,8},{10,11... | collective-permute-start | bytes 1572872 | tf_op jit(solution)/shard_map/ppermute | solution.py:348
  66.0 8.9 %collective-permute-start.15 = (bf16[64,2048]{1,0:T(8,128)(2,1)S(1)}, bf16[64,2048]{1,0:T(8,128)(2,1)S(1)}, u32[]{:S(2)}, u32[]{:S(2)}) collective-permute-start(bf16[64,2048]{1,0:T(8,128)(2,1)S(1)} %get-tuple-element.74), channel_id=1, source_target_pairs={{0,2},{1,3},{2,4},{3,5},{4,6},{5,7},{6,0},{7,1},{8,10},{9,11},{10,... | collective-permute-start | bytes 786440 | tf_op jit(solution)/shard_map/ppermute | solution.py:351
  67.3 7.6 %collective-permute-start.16 = (bf16[64,2048]{1,0:T(8,128)(2,1)S(1)}, bf16[64,2048]{1,0:T(8,128)(2,1)S(1)}, u32[]{:S(2)}, u32[]{:S(2)}) collective-permute-start(bf16[64,2048]{1,0:T(8,128)(2,1)S(1)} %get-tuple-element.73), channel_id=1, source_target_pairs={{0,6},{1,7},{2,0},{3,1},{4,2},{5,3},{6,4},{7,5},{8,14},{9,15},{10,... | collective-permute-start | bytes 786440 | tf_op jit(solution)/shard_map/ppermute | solution.py:351
  68.9 11.6 %collective-permute-start.19 = (bf16[64,2048]{1,0:T(8,128)(2,1)S(1)}, bf16[64,2048]{1,0:T(8,128)(2,1)S(1)}, u32[]{:S(2)}, u32[]{:S(2)}) collective-permute-start(bf16[64,2048]{1,0:T(8,128)(2,1)S(1)} %get-tuple-element.78.after), channel_id=1, source_target_pairs={{0,2},{1,3},{2,4},{3,5},{4,6},{5,7},{6,0},{7,1},{8,10},{9,11},{10,... | collective-permute-start | bytes 786440 | tf_op jit(solution)/shard_map/ppermute | solution.py:351
  70.9 15.3 %collective-permute-start.12 = (bf16[64,4096]{1,0:T(8,128)(2,1)S(1)}, bf16[64,4096]{1,0:T(8,128)(2,1)S(1)}, u32[]{:S(2)}, u32[]{:S(2)}) collective-permute-start(bf16[64,4096]{1,0:T(8,128)(2,1)S(1)} %get-tuple-element.63), channel_id=1, source_target_pairs={{0,1},{1,0},{2,3},{3,2},{4,5},{5,4},{6,7},{7,6},{8,9},{9,8},{10,11... | collective-permute-start | bytes 1572872 | tf_op jit(solution)/shard_map/ppermute | solution.py:348
  72.1 8.4 %collective-permute-start.18 = (bf16[64,2048]{1,0:T(8,128)(2,1)S(1)}, bf16[64,2048]{1,0:T(8,128)(2,1)S(1)}, u32[]{:S(2)}, u32[]{:S(2)}) collective-permute-start(bf16[64,2048]{1,0:T(8,128)(2,1)S(1)} %get-tuple-element.77), channel_id=1, source_target_pairs={{0,6},{1,7},{2,0},{3,1},{4,2},{5,3},{6,4},{7,5},{8,14},{9,15},{10,... | collective-permute-start | bytes 786440 | tf_op jit(solution)/shard_map/ppermute | solution.py:351
  75.2 11.0 %collective-permute-start.17 = (bf16[64,2048]{1,0:T(8,128)(2,1)S(1)}, bf16[64,2048]{1,0:T(8,128)(2,1)S(1)}, u32[]{:S(2)}, u32[]{:S(2)}) collective-permute-start(bf16[64,2048]{1,0:T(8,128)(2,1)S(1)} %get-tuple-element.76), channel_id=1, source_target_pairs={{0,2},{1,3},{2,4},{3,5},{4,6},{5,7},{6,0},{7,1},{8,10},{9,11},{10,... | collective-permute-start | bytes 786440 | tf_op jit(solution)/shard_map/ppermute | solution.py:351
  76.1 10.0 %collective-permute-start.20 = (bf16[64,2048]{1,0:T(8,128)(2,1)S(1)}, bf16[64,2048]{1,0:T(8,128)(2,1)S(1)}, u32[]{:S(2)}, u32[]{:S(2)}) collective-permute-start(bf16[64,2048]{1,0:T(8,128)(2,1)S(1)} %get-tuple-element.75), channel_id=1, source_target_pairs={{0,6},{1,7},{2,0},{3,1},{4,2},{5,3},{6,4},{7,5},{8,14},{9,15},{10,... | collective-permute-start | bytes 786440 | tf_op jit(solution)/shard_map/ppermute | solution.py:351
  (1 other events, 16.9 us)
